TPU v7x, 32 devices: a whole 2x2x4 slice. The times are simulated.
32 devices in a mesh: seg: 4 (over y, x), seq: 8 (over z, core).
Axes of the slice: x: 2, y: 2, z: 4, core: 2. Of those that a mesh axis runs over, the one named last changes fastest.
Arguments:
- sublevel_arguments: bfloat16 [4, 1024, 2048], P('seg', 'seq'), may hold values from -6 to 6
- upstream_derivative: bfloat16 [4, 1024, 2048], P('seg', 'seq'), may hold values from -6 to 6
- piece_starting_memories: float32 [4, 32, 64, 64], P('seg'), may hold values from -6 to 6
- initial_standardize_scaling: bfloat16 [2048], P(('seg', 'seq')), may hold values from 0.099609375 to 1.8984375
- initial_standardize_offset: bfloat16 [2048], P(('seg', 'seq')), may hold values from -1.1953125 to 1.1953125
- acceptor_lerp_fraction: bfloat16 [2048], P(('seg', 'seq')), may hold values from 0 to 1
- lookup_lerp_fraction: bfloat16 [2048], P(('seg', 'seq')), may hold values from 0 to 1
- payload_lerp_fraction: bfloat16 [2048], P(('seg', 'seq')), may hold values from 0 to 1
- valve_lerp_fraction: bfloat16 [2048], P(('seg', 'seq')), may hold values from 0 to 1
- lane_fading_speed: bfloat16 [2048], P(('seg', 'seq')), may hold values from 9.727478e-05 to 0.024902344
- current_step_reward: bfloat16 [2048], P(('seg', 'seq')), may hold values from -2 to 2
- cluster_standardize_scaling: bfloat16 [2048], P(('seg', 'seq')), may hold values from 0.099609375 to 1.8984375
- cluster_standardize_offset: bfloat16 [2048], P(('seg', 'seq')), may hold values from -1.1953125 to 1.1953125
- acceptor_weights: bfloat16 [2048, 2048], P(('seg', 'seq')), may hold values from -0.125 to 0.125
- lookup_weights: bfloat16 [2048, 2048], P(('seg', 'seq')), may hold values from -0.125 to 0.125
- payload_weights: bfloat16 [2048, 2048], P(('seg', 'seq')), may hold values from -0.125 to 0.125
- valve_weights: bfloat16 [2048, 2048], P(('seg', 'seq')), may hold values from -0.125 to 0.125
- emission_weights: bfloat16 [2048, 2048], P(('seg', 'seq')), may hold values from -0.25 to 0.25
- latter_standardize_scaling: bfloat16 [2048], P(('seg', 'seq')), may hold values from 0.099609375 to 1.8984375
- latter_standardize_offset: bfloat16 [2048], P(('seg', 'seq')), may hold values from -1.1953125 to 1.1953125
- feedforward_lookup_lerp: bfloat16 [2048], P(('seg', 'seq')), may hold values from 0 to 1
- feedforward_acceptor_lerp: bfloat16 [2048], P(('seg', 'seq')), may hold values from 0 to 1
- feedforward_lookup_weights: bfloat16 [2048, 7168], P(('seg', 'seq')), may hold values from -0.125 to 0.125
- feedforward_payload_weights: bfloat16 [7168, 2048], P(('seg', 'seq')), may hold values from -0.125 to 0.125
- feedforward_acceptor_weights: bfloat16 [2048, 2048], P(('seg', 'seq')), may hold values from -0.125 to 0.125
Outputs:
- layer_output: bfloat16 [4, 1024, 2048], P('seg', 'seq')
- input_grad: float32 [4, 1024, 2048], P('seg', 'seq')
- final_states: float32 [4, 32, 64, 64], P('seg', 'seq')
- grad_first_gain: float32 [2048], P(('seg', 'seq'))
- grad_first_bias: float32 [2048], P(('seg', 'seq'))
- grad_mix_recept: float32 [2048], P(('seg', 'seq'))
- grad_mix_key: float32 [2048], P(('seg', 'seq'))
- grad_mix_value: float32 [2048], P(('seg', 'seq'))
- grad_mix_gate: float32 [2048], P(('seg', 'seq'))
- grad_decay_rate: float32 [2048], P(('seg', 'seq'))
- grad_current_bonus: float32 [2048], P(('seg', 'seq'))
- grad_group_gain: float32 [2048], P(('seg', 'seq'))
- grad_group_bias: float32 [2048], P(('seg', 'seq'))
- grad_recept_weight: float32 [2048, 2048], P(('seg', 'seq'))
- grad_key_weight: float32 [2048, 2048], P(('seg', 'seq'))
- grad_value_weight: float32 [2048, 2048], P(('seg', 'seq'))
- grad_gate_weight: float32 [2048, 2048], P(('seg', 'seq'))
- grad_output_weight: float32 [2048, 2048], P(('seg', 'seq'))
- grad_second_gain: float32 [2048], P(('seg', 'seq'))
- grad_second_bias: float32 [2048], P(('seg', 'seq'))
- grad_shift_key: float32 [2048], P(('seg', 'seq'))
- grad_shift_recept: float32 [2048], P(('seg', 'seq'))
- grad_channel_key: float32 [2048, 7168], P(('seg', 'seq'))
- grad_channel_value: float32 [7168, 2048], P(('seg', 'seq'))
- grad_channel_recept: float32 [2048, 2048], P(('seg', 'seq'))
All inputs are finite; a program needn't handle non-finite values.
Results may differ from a plain program's by a relative error of at most 0.029.
Values may be sent and summed in bfloat16 or wider, within the bound.
A program may use at most 272 MiB of HBM per device.

v0:
```python
import jax
import jax.numpy as jnp
from jax import lax
from jax.sharding import PartitionSpec as P

BLOCK_LEN = 64


EPS = 1e-05
GROUP_EPS = 0.00064
EXACT_ARITHMETIC = lax.Precision.HIGHEST


def passed_along(block, axis, distance):
    devices = range(lax.axis_size(axis))
    route = [(i - distance, i) for i in devices if i - distance in devices]
    return lax.ppermute(block, axis, route)


def entering(part, axis, combine, identity):
    place = lax.axis_index(axis)
    gathered = jax.tree.map(lambda a: lax.all_gather(a, axis), part)
    state = jax.tree.map(lambda a, e: jnp.zeros_like(a) + jnp.asarray(e, a.dtype), part, identity)

    def one(lap, state):
        return combine(
            state, jax.tree.map(lambda a: lax.dynamic_index_in_dim(a, lap, 0, False), gathered)
        )

    return lax.fori_loop(0, place, one, state)


def carried_in(shard, axis, combine, identity):
    size, place = (lax.axis_size(axis), lax.axis_index(axis))
    everything = jax.tree.map(
        lambda part, kind: lax.all_gather(part.astype(kind), axis),
        shard,
        jax.tree.map(lambda a: jnp.bfloat16 if a.dtype == jnp.float32 else a.dtype, shard),
    )
    start = jax.tree.map(
        lambda part, zero: jnp.broadcast_to(jnp.asarray(zero, part.dtype), part.shape),
        shard,
        identity,
    )

    def lap(k, before):
        at = size - 1 - k
        reached = at > place
        new = combine(
            before, jax.tree.map(lambda part, own: part[at].astype(own.dtype), everything, shard)
        )
        return jax.tree.map(lambda a, b: jnp.where(reached, a, b), new, before)

    return lax.fori_loop(0, size, lap, start)


def layer_norm(values, gain_vec, bias_vec):
    average = jnp.mean(values, axis=-1, keepdims=True)
    centred = values - average
    spread = jnp.mean(centred * centred, axis=-1, keepdims=True)
    return centred * lax.rsqrt(spread + EPS) * gain_vec + bias_vec


def group_norm(values, gain_vec, bias_vec, lane_number):
    row_total = values.shape[0]
    piece_partition = values.reshape(row_total, lane_number, -1)
    average = jnp.mean(piece_partition, axis=-1, keepdims=True)
    centred = piece_partition - average
    spread = jnp.mean(centred * centred, axis=-1, keepdims=True)
    return (centred * lax.rsqrt(spread + GROUP_EPS)).reshape(row_total, -1) * gain_vec + bias_vec


def blend(current, previous, shares):
    return tuple((previous + share * (current - previous) for share in shares))


def widen(items):
    return tuple((item.astype(jnp.float32) if item.ndim == 1 else item for item in items))


def tile_stepping(passed_memory, tile_elements, fading_speeds, reward_array):
    acceptor_tile, lookup_tile, payload_tile = tile_elements
    block_len = acceptor_tile.shape[0]
    offsets = jnp.arange(block_len, dtype=jnp.float32)[:, None, None]
    decayed_recept = acceptor_tile * jnp.exp(-fading_speeds[None] * offsets)
    grown_keys = lookup_tile * jnp.exp(fading_speeds[None] * (offsets + 1.0))
    affinity_table = jnp.einsum(
        "thc,shc->hts", decayed_recept, grown_keys, precision=EXACT_ARITHMETIC
    )
    below_mask = jnp.arange(block_len)[:, None] > jnp.arange(block_len)[None, :]
    affinity_table = jnp.where(below_mask[None], affinity_table, 0.0)
    reward_addend = jnp.sum(
        acceptor_tile * reward_array[None] * lookup_tile, axis=-1, keepdims=True
    )
    sublevel_answer = (
        jnp.einsum("csk,kcd->scd", affinity_table, payload_tile, precision=EXACT_ARITHMETIC)
        + reward_addend * payload_tile
    )
    sublevel_answer = sublevel_answer + jnp.einsum(
        "thc,hcv->thv", decayed_recept, passed_memory, precision=EXACT_ARITHMETIC
    )
    tail_keys = lookup_tile * jnp.exp(-fading_speeds[None] * (block_len - 1.0 - offsets))
    new_state = jnp.exp(-fading_speeds * block_len)[:, :, None] * passed_memory
    new_state = new_state + jnp.einsum(
        "shc,shv->hcv", tail_keys, payload_tile, precision=EXACT_ARITHMETIC
    )
    return (new_state, sublevel_answer)


def tile_traversal(acceptor_numbers, lookup_tile, payload_tile, fading_speeds, reward_array):
    row_total, lane_number, lane_dimension = acceptor_numbers.shape
    shape = (row_total // BLOCK_LEN, BLOCK_LEN, lane_number, lane_dimension)
    empty_state = jnp.zeros((lane_number, lane_dimension, lane_dimension), jnp.float32)

    def stepper(passed_memory, tile_elements):
        return tile_stepping(passed_memory, tile_elements, fading_speeds, reward_array)

    closing_state, outputs = lax.scan(
        stepper,
        empty_state,
        (acceptor_numbers.reshape(shape), lookup_tile.reshape(shape), payload_tile.reshape(shape)),
    )
    return (
        outputs.reshape(row_total, lane_number, lane_dimension),
        closing_state,
        jnp.exp(-fading_speeds * row_total),
    )


def decayed_rows(acceptor_numbers, fading_speeds):
    offsets = jnp.arange(acceptor_numbers.shape[0], dtype=jnp.float32)[:, None, None]
    return acceptor_numbers * jnp.exp(-fading_speeds[None] * offsets)


def complete_state(
    acceptor_numbers, lookup_tile, payload_tile, fading_speeds, reward_array, starting_memory
):
    segment_output, closing_state, decay_factor = tile_traversal(
        acceptor_numbers, lookup_tile, payload_tile, fading_speeds, reward_array
    )
    carried = jnp.einsum(
        "thc,hcv->thv",
        decayed_rows(acceptor_numbers, fading_speeds),
        starting_memory,
        precision=EXACT_ARITHMETIC,
    )
    return (segment_output + carried, closing_state, decay_factor)


def chain_combine(earlier, later):
    return (earlier[0] * later[0], later[1] + later[0][:, :, None] * earlier[1])


def fetch_time(
    initial_standardize_scaling,
    initial_standardize_offset,
    acceptor_lerp_fraction,
    lookup_lerp_fraction,
    payload_lerp_fraction,
    valve_lerp_fraction,
    lane_fading_speed,
    current_step_reward,
    cluster_standardize_scaling,
    cluster_standardize_offset,
    acceptor_weights,
    lookup_weights,
    payload_weights,
    valve_weights,
    emission_weights,
):
    return (
        lax.all_gather(initial_standardize_scaling, ("seg", "seq"), axis=0, tiled=True),
        lax.all_gather(initial_standardize_offset, ("seg", "seq"), axis=0, tiled=True),
        lax.all_gather(acceptor_lerp_fraction, ("seg", "seq"), axis=0, tiled=True),
        lax.all_gather(lookup_lerp_fraction, ("seg", "seq"), axis=0, tiled=True),
        lax.all_gather(payload_lerp_fraction, ("seg", "seq"), axis=0, tiled=True),
        lax.all_gather(valve_lerp_fraction, ("seg", "seq"), axis=0, tiled=True),
        lax.all_gather(lane_fading_speed, ("seg", "seq"), axis=0, tiled=True),
        lax.all_gather(current_step_reward, ("seg", "seq"), axis=0, tiled=True),
        lax.all_gather(cluster_standardize_scaling, ("seg", "seq"), axis=0, tiled=True),
        lax.all_gather(cluster_standardize_offset, ("seg", "seq"), axis=0, tiled=True),
        lax.all_gather(acceptor_weights, ("seg", "seq"), axis=0, tiled=True),
        lax.all_gather(lookup_weights, ("seg", "seq"), axis=0, tiled=True),
        lax.all_gather(payload_weights, ("seg", "seq"), axis=0, tiled=True),
        lax.all_gather(valve_weights, ("seg", "seq"), axis=0, tiled=True),
        lax.all_gather(emission_weights, ("seg", "seq"), axis=0, tiled=True),
    )


def previous_rows(normed_rows):
    incoming = passed_along(normed_rows[-1:], "seq", 1)
    return jnp.concatenate([incoming, normed_rows[:-1]], axis=0)


def previous_back(grad_before):
    incoming = passed_along(grad_before[:1], "seq", -1)
    return jnp.concatenate([grad_before[1:], incoming], axis=0)


def scatter_channel(gain_grad, bias_grad, share_a, share_b, key_grad, value_grad, recept_grad):
    return (
        lax.psum_scatter(gain_grad, ("seg", "seq"), scatter_dimension=0, tiled=True),
        lax.psum_scatter(bias_grad, ("seg", "seq"), scatter_dimension=0, tiled=True),
        lax.psum_scatter(share_a, ("seg", "seq"), scatter_dimension=0, tiled=True),
        lax.psum_scatter(share_b, ("seg", "seq"), scatter_dimension=0, tiled=True),
        lax.psum_scatter(key_grad, ("seg", "seq"), scatter_dimension=0, tiled=True),
        lax.psum_scatter(value_grad, ("seg", "seq"), scatter_dimension=0, tiled=True),
        lax.psum_scatter(recept_grad, ("seg", "seq"), scatter_dimension=0, tiled=True),
    )


def per_device(
    sublevel_arguments,
    upstream_derivative,
    piece_starting_memories,
    initial_standardize_scaling,
    initial_standardize_offset,
    acceptor_lerp_fraction,
    lookup_lerp_fraction,
    payload_lerp_fraction,
    valve_lerp_fraction,
    lane_fading_speed,
    current_step_reward,
    cluster_standardize_scaling,
    cluster_standardize_offset,
    acceptor_weights,
    lookup_weights,
    payload_weights,
    valve_weights,
    emission_weights,
    latter_standardize_scaling,
    latter_standardize_offset,
    feedforward_lookup_lerp,
    feedforward_acceptor_lerp,
    feedforward_lookup_weights,
    feedforward_payload_weights,
    feedforward_acceptor_weights,
):
    time_args = (
        initial_standardize_scaling,
        initial_standardize_offset,
        acceptor_lerp_fraction,
        lookup_lerp_fraction,
        payload_lerp_fraction,
        valve_lerp_fraction,
        lane_fading_speed,
        current_step_reward,
        cluster_standardize_scaling,
        cluster_standardize_offset,
        acceptor_weights,
        lookup_weights,
        payload_weights,
        valve_weights,
        emission_weights,
    )
    inputs = sublevel_arguments[0].astype(jnp.float32)
    row_total = inputs.shape[0]
    lane_number = piece_starting_memories.shape[1]
    lane_dimension = piece_starting_memories.shape[2]
    start_given = piece_starting_memories[0]
    device_count = lax.axis_size("seq")
    position = lax.axis_index("seq")
    own_heads = lane_number // device_count
    time_full = widen(fetch_time(*time_args))
    (
        gain_one,
        bias_one,
        share_recept,
        share_key,
        share_value,
        share_gate,
        rate_flat,
        reward_array_linear,
        group_scale,
        group_shift,
        weight_recept,
        weight_key,
        weight_value,
        weight_gate,
        weight_output,
    ) = time_full
    fading_speeds = rate_flat.reshape(lane_number, lane_dimension)
    reward_array = reward_array_linear.reshape(lane_number, lane_dimension)
    normed_one = layer_norm(inputs, gain_one, bias_one)
    before_one = previous_rows(normed_one)
    shares_one = (share_recept, share_key, share_value, share_gate)
    mixed_one = tuple(
        (item.astype(jnp.bfloat16) for item in blend(normed_one, before_one, shares_one))
    )
    acceptor_numbers = jnp.dot(
        mixed_one[0], weight_recept, preferred_element_type=jnp.float32
    ).astype(jnp.bfloat16)
    lookup_arrays = jnp.dot(mixed_one[1], weight_key, preferred_element_type=jnp.float32).astype(
        jnp.bfloat16
    )
    payload_arrays = jnp.dot(mixed_one[2], weight_value, preferred_element_type=jnp.float32).astype(
        jnp.bfloat16
    )
    gate_pre = jnp.dot(mixed_one[3], weight_gate, preferred_element_type=jnp.float32)
    piece_partition = (row_total, lane_number, lane_dimension)
    acceptor_by_lane = acceptor_numbers.astype(jnp.float32).reshape(piece_partition)
    lookup_by_lane = lookup_arrays.astype(jnp.float32).reshape(piece_partition)
    payload_by_lane = payload_arrays.astype(jnp.float32).reshape(piece_partition)
    segment_output, closing_state, decay_factor = tile_traversal(
        acceptor_by_lane, lookup_by_lane, payload_by_lane, fading_speeds, reward_array
    )
    empty_state = jnp.zeros_like(closing_state)
    whole_lift = jnp.exp(-fading_speeds * float(row_total * device_count))[:, :, None] * start_given
    prefix_factor, prefix_state = entering(
        (decay_factor, closing_state),
        "seq",
        chain_combine,
        (jnp.ones_like(decay_factor), empty_state),
    )
    starting_memory = prefix_state + prefix_factor[:, :, None] * start_given
    lift = jnp.exp(-fading_speeds * (row_total * (device_count - 1 - position)).astype(jnp.float32))
    final_part = lax.psum_scatter(
        (lift[:, :, None] * closing_state).astype(jnp.bfloat16),
        "seq",
        scatter_dimension=0,
        tiled=True,
    ).astype(jnp.float32)
    final_memory = final_part + lax.dynamic_slice_in_dim(
        whole_lift, position * own_heads, own_heads, 0
    )
    decayed_recept = decayed_rows(acceptor_by_lane, fading_speeds)
    mixer_out = segment_output + jnp.einsum(
        "thc,hcv->thv", decayed_recept, starting_memory, precision=EXACT_ARITHMETIC
    )
    blender_emission_linear = mixer_out.reshape(row_total, -1)

    def gate_norm(mixer_rows, gate_rows, scale_vec, shift_vec):
        return group_norm(mixer_rows, scale_vec, shift_vec, lane_number) * jax.nn.silu(gate_rows)

    gated = gate_norm(blender_emission_linear, gate_pre, group_scale, group_shift).astype(
        jnp.bfloat16
    )
    middle = inputs + jnp.dot(gated, weight_output, preferred_element_type=jnp.float32)
    channel_full = widen(
        (
            lax.all_gather(latter_standardize_scaling, ("seg", "seq"), axis=0, tiled=True),
            lax.all_gather(latter_standardize_offset, ("seg", "seq"), axis=0, tiled=True),
            lax.all_gather(feedforward_lookup_lerp, ("seg", "seq"), axis=0, tiled=True),
            lax.all_gather(feedforward_acceptor_lerp, ("seg", "seq"), axis=0, tiled=True),
            lax.all_gather(feedforward_lookup_weights, ("seg", "seq"), axis=0, tiled=True),
            lax.all_gather(feedforward_payload_weights, ("seg", "seq"), axis=0, tiled=True),
            lax.all_gather(feedforward_acceptor_weights, ("seg", "seq"), axis=0, tiled=True),
        )
    )
    gain_two, bias_two, share_ckey, share_crec, weight_ckey, weight_cval, weight_crec = channel_full
    normed_two = layer_norm(middle, gain_two, bias_two)
    before_two = previous_rows(normed_two)
    mixed_two = tuple(
        (
            item.astype(jnp.bfloat16)
            for item in blend(normed_two, before_two, (share_ckey, share_crec))
        )
    )
    pre_act = jnp.dot(mixed_two[0], weight_ckey, preferred_element_type=jnp.float32)
    activation = jnp.square(jax.nn.relu(pre_act)).astype(jnp.bfloat16)
    value_out = jnp.dot(activation, weight_cval, preferred_element_type=jnp.float32)
    pre_gate = jnp.dot(mixed_two[1], weight_crec, preferred_element_type=jnp.float32)
    sigma = jax.nn.sigmoid(pre_gate)
    sublevel_answer = middle + sigma * value_out
    upstream = upstream_derivative[0].astype(jnp.float32)
    d_value = (sigma * upstream).astype(jnp.bfloat16)
    d_pregate = (upstream * value_out * sigma * (1.0 - sigma)).astype(jnp.bfloat16)
    grad_cval = jnp.einsum("tf,td->fd", activation, d_value, preferred_element_type=jnp.float32)
    grad_crec = jnp.einsum("te,td->ed", mixed_two[1], d_pregate, preferred_element_type=jnp.float32)
    d_act = jnp.einsum("td,fd->tf", d_value, weight_cval, preferred_element_type=jnp.float32)
    d_pre = (d_act * 2.0 * jax.nn.relu(pre_act)).astype(jnp.bfloat16)
    grad_ckey = jnp.einsum("td,tf->df", mixed_two[0], d_pre, preferred_element_type=jnp.float32)
    d_mixed_ckey = jnp.einsum("tf,df->td", d_pre, weight_ckey, preferred_element_type=jnp.float32)
    d_mixed_crec = jnp.einsum(
        "te,de->td", d_pregate, weight_crec, preferred_element_type=jnp.float32
    )

    def blend_two(current, previous, first_share, second_share):
        return blend(current, previous, (first_share, second_share))

    unused_slot, pull_blend_two = jax.vjp(blend_two, normed_two, before_two, share_ckey, share_crec)
    d_normed_two, d_before_two, grad_share_ckey, grad_share_crec = pull_blend_two(
        (d_mixed_ckey, d_mixed_crec)
    )
    d_normed_two = d_normed_two + previous_back(d_before_two)
    unused_slot, pull_norm_two = jax.vjp(layer_norm, middle, gain_two, bias_two)
    d_middle, grad_gain_two, grad_bias_two = pull_norm_two(d_normed_two)
    d_middle = d_middle + upstream
    channel_items = (
        grad_gain_two,
        grad_bias_two,
        grad_share_ckey,
        grad_share_crec,
        grad_ckey,
        grad_cval,
        grad_crec,
    )
    time_back = widen(fetch_time(*time_args))
    weight_recept, weight_key, weight_value, weight_gate, weight_output = time_back[10:]
    d_branch = d_middle.astype(jnp.bfloat16)
    grad_wout = jnp.einsum("td,te->de", gated, d_branch, preferred_element_type=jnp.float32)
    d_gated = jnp.einsum("te,de->td", d_branch, weight_output, preferred_element_type=jnp.float32)
    unused_slot, pull_gate = jax.vjp(
        gate_norm, blender_emission_linear, gate_pre, group_scale, group_shift
    )
    d_mixer, d_gate, grad_group_scale, grad_group_shift = pull_gate(d_gated)
    d_gate_low = d_gate.astype(jnp.bfloat16)
    grad_wgate = jnp.einsum(
        "td,te->de", mixed_one[3], d_gate_low, preferred_element_type=jnp.float32
    )
    d_mixer_heads = d_mixer.reshape(piece_partition)
    state_grad = jnp.einsum(
        "thc,thv->hcv", decayed_recept, d_mixer_heads, precision=EXACT_ARITHMETIC
    )
    unused_slot, later_grad = carried_in(
        (decay_factor, state_grad), "seq", chain_combine, (jnp.ones_like(decay_factor), empty_state)
    )
    factor_grad = jnp.sum(later_grad * starting_memory, axis=-1)
    unused_slot, state_pullback = jax.vjp(
        complete_state,
        acceptor_by_lane,
        lookup_by_lane,
        payload_by_lane,
        fading_speeds,
        reward_array,
        starting_memory,
    )
    (
        receptance_gradient,
        key_gradient,
        value_gradient,
        rate_gradient,
        reward_derivative,
        unused_slot,
    ) = state_pullback((d_mixer_heads, later_grad, factor_grad))
    d_recept_low = receptance_gradient.reshape(row_total, -1).astype(jnp.bfloat16)
    d_keys_low = key_gradient.reshape(row_total, -1).astype(jnp.bfloat16)
    d_values_low = value_gradient.reshape(row_total, -1).astype(jnp.bfloat16)
    grad_wrec = jnp.einsum(
        "td,te->de", mixed_one[0], d_recept_low, preferred_element_type=jnp.float32
    )
    grad_wkey = jnp.einsum(
        "td,te->de", mixed_one[1], d_keys_low, preferred_element_type=jnp.float32
    )
    grad_wval = jnp.einsum(
        "td,te->de", mixed_one[2], d_values_low, preferred_element_type=jnp.float32
    )
    d_mixed_rec = jnp.einsum(
        "te,de->td", d_recept_low, weight_recept, preferred_element_type=jnp.float32
    )
    d_mixed_key = jnp.einsum(
        "te,de->td", d_keys_low, weight_key, preferred_element_type=jnp.float32
    )
    d_mixed_val = jnp.einsum(
        "te,de->td", d_values_low, weight_value, preferred_element_type=jnp.float32
    )
    d_mixed_gate = jnp.einsum(
        "te,de->td", d_gate_low, weight_gate, preferred_element_type=jnp.float32
    )

    def blend_one(current, previous, share_a, share_b, share_c, share_d):
        return blend(current, previous, (share_a, share_b, share_c, share_d))

    unused_slot, pull_blend_one = jax.vjp(
        blend_one, normed_one, before_one, share_recept, share_key, share_value, share_gate
    )
    d_normed_one, d_before_one, grad_share_rec, grad_share_key, grad_share_val, grad_share_gate = (
        pull_blend_one((d_mixed_rec, d_mixed_key, d_mixed_val, d_mixed_gate))
    )
    d_normed_one = d_normed_one + previous_back(d_before_one)
    unused_slot, pull_norm_one = jax.vjp(layer_norm, inputs, gain_one, bias_one)
    d_inputs, grad_gain_one, grad_bias_one = pull_norm_one(d_normed_one)
    input_grad = d_inputs + d_middle
    channel_sums = scatter_channel(*channel_items)
    time_sums = (
        lax.psum_scatter(grad_gain_one, ("seg", "seq"), scatter_dimension=0, tiled=True),
        lax.psum_scatter(grad_bias_one, ("seg", "seq"), scatter_dimension=0, tiled=True),
        lax.psum_scatter(grad_share_rec, ("seg", "seq"), scatter_dimension=0, tiled=True),
        lax.psum_scatter(grad_share_key, ("seg", "seq"), scatter_dimension=0, tiled=True),
        lax.psum_scatter(grad_share_val, ("seg", "seq"), scatter_dimension=0, tiled=True),
        lax.psum_scatter(grad_share_gate, ("seg", "seq"), scatter_dimension=0, tiled=True),
        lax.psum_scatter(
            rate_gradient.reshape(-1), ("seg", "seq"), scatter_dimension=0, tiled=True
        ),
        lax.psum_scatter(
            reward_derivative.reshape(-1), ("seg", "seq"), scatter_dimension=0, tiled=True
        ),
        lax.psum_scatter(grad_group_scale, ("seg", "seq"), scatter_dimension=0, tiled=True),
        lax.psum_scatter(grad_group_shift, ("seg", "seq"), scatter_dimension=0, tiled=True),
        lax.psum_scatter(grad_wrec, ("seg", "seq"), scatter_dimension=0, tiled=True),
        lax.psum_scatter(grad_wkey, ("seg", "seq"), scatter_dimension=0, tiled=True),
        lax.psum_scatter(grad_wval, ("seg", "seq"), scatter_dimension=0, tiled=True),
        lax.psum_scatter(grad_wgate, ("seg", "seq"), scatter_dimension=0, tiled=True),
        lax.psum_scatter(grad_wout, ("seg", "seq"), scatter_dimension=0, tiled=True),
    )
    return (
        sublevel_answer.astype(jnp.bfloat16)[None],
        input_grad[None],
        final_memory[None],
        time_sums[0],
        time_sums[1],
        time_sums[2],
        time_sums[3],
        time_sums[4],
        time_sums[5],
        time_sums[6],
        time_sums[7],
        time_sums[8],
        time_sums[9],
        time_sums[10],
        time_sums[11],
        time_sums[12],
        time_sums[13],
        time_sums[14],
        channel_sums[0],
        channel_sums[1],
        channel_sums[2],
        channel_sums[3],
        channel_sums[4],
        channel_sums[5],
        channel_sums[6],
    )


def solution(mesh):
    return jax.shard_map(
        per_device,
        mesh=mesh,
        in_specs=(
            P("seg", "seq", None),
            P("seg", "seq", None),
            P("seg", None, None, None),
            P(("seg", "seq")),
            P(("seg", "seq")),
            P(("seg", "seq")),
            P(("seg", "seq")),
            P(("seg", "seq")),
            P(("seg", "seq")),
            P(("seg", "seq")),
            P(("seg", "seq")),
            P(("seg", "seq")),
            P(("seg", "seq")),
            P(("seg", "seq"), None),
            P(("seg", "seq"), None),
            P(("seg", "seq"), None),
            P(("seg", "seq"), None),
            P(("seg", "seq"), None),
            P(("seg", "seq")),
            P(("seg", "seq")),
            P(("seg", "seq")),
            P(("seg", "seq")),
            P(("seg", "seq"), None),
            P(("seg", "seq"), None),
            P(("seg", "seq"), None),
        ),
        out_specs=(
            P("seg", "seq", None),
            P("seg", "seq", None),
            P("seg", "seq", None, None),
            P(("seg", "seq")),
            P(("seg", "seq")),
            P(("seg", "seq")),
            P(("seg", "seq")),
            P(("seg", "seq")),
            P(("seg", "seq")),
            P(("seg", "seq")),
            P(("seg", "seq")),
            P(("seg", "seq")),
            P(("seg", "seq")),
            P(("seg", "seq"), None),
            P(("seg", "seq"), None),
            P(("seg", "seq"), None),
            P(("seg", "seq"), None),
            P(("seg", "seq"), None),
            P(("seg", "seq")),
            P(("seg", "seq")),
            P(("seg", "seq")),
            P(("seg", "seq")),
            P(("seg", "seq"), None),
            P(("seg", "seq"), None),
            P(("seg", "seq"), None),
        ),
        check_vma=False,
    )
```

profile of v0, /device:TPU:0, one launch (start us, length us, event | category | flops | bytes accessed | tf_op | source)
XLA Modules:
  0.0 3909.7 jit_solution(3256709475409224807)
XLA Ops:
  21.3 43.8 %all-reduce.29 = (bf16[2048]{0:T(1024)(128)(2,1)S(1)}, bf16[2048]{0:T(1024)(128)(2,1)S(1)}, bf16[2048]{0:T(1024)(128)(2,1)S(1)}, bf16[2048]{0:T(1024)(128)(2,1)S...) all-reduce(bf16[2048]{0:T(1024)(128)(2,1)S(1)} %dynamic-update-slic, ...), channel_id=1, replica_groups=mesh['seg'=4,'seq'=8] {'seg','seq'}, use_global_device_ids=true, to_apply=%add | all-reduce | flops 28672 | bytes 114688
  71.1 20.4 all-gather.13.cloned.1.call-done
  91.5 5.9 fusion.137
  103.3 67.0 %all-gather.15.cloned.1.call-done = bf16[2048,2048]{1,0:T(8,128)(2,1)} async-done(((bf16[64,2048]{1,0:T(8,128)(2,1)}), bf16[2048,2048]{1,0:T(8,128)(2,1)}) %all-gather.15.cloned.1.call-update) | async-done | bytes 8388624 | tf_op jit(solution)/shard_map/all_gather | solution.py:184
  170.4 6.4 fusion.136
  179.8 4.2 copy.117
  184.0 65.4 %all-gather.17.cloned.1.call-done = bf16[2048,2048]{1,0:T(8,128)(2,1)} async-done(((bf16[64,2048]{1,0:T(8,128)(2,1)}), bf16[2048,2048]{1,0:T(8,128)(2,1)}) %all-gather.17.cloned.1.call-update) | async-done | bytes 8388624 | tf_op jit(solution)/shard_map/all_gather | solution.py:182
  249.4 6.4 fusion.135
  258.8 4.1 copy.118
  265.2 89.5 %while.99 = (s32[]{:T(128)}, f32[32,64,64]{2,1,0:T(8,128)S(1)}, f32[2,64,32,64]{1,0,3,2:T(2,128)}, f32[32,64,1]{1,0,2:T(8,128)S(1)}, f32[2,64,32,64]{3,1,2,0:T(8...) while((s32[]{:T(128)}, f32[32,64,64]{2,1,0:T(8,128)S(1)}, ...), condition=%wide.region_4.5_spmd.clone, body=%wide.region_2.4_spmd.clone.sunk | while | flops 405020864 | bytes 27419852 | solution.py:118
  265.4 3.7 convolution_bitcast_fusion.11
  284.6 25.5 dynamic_update_slice.118
  310.1 3.7 convolution_bitcast_fusion.11
  329.2 25.5 dynamic_update_slice.118
  359.3 15.4 all_gather.101
  380.6 56.5 %all-gather.29.cloned.1.call-done = f32[256,64,64]{2,1,0:T(8,128)} async-done(((f32[32,64,64]{2,1,0:T(8,128)}), f32[256,64,64]{2,1,0:T(8,128)}) %all-gather.29.cloned.1.call-update) | async-done | bytes 4194320 | tf_op jit(solution)/shard_map/all_gather | solution.py:22
  446.3 69.5 %all-gather.19.cloned.1.call-done = bf16[2048,2048]{1,0:T(8,128)(2,1)} async-done(((bf16[64,2048]{1,0:T(8,128)(2,1)}), bf16[2048,2048]{1,0:T(8,128)(2,1)}) %all-gather.19.cloned.1.call-update) | async-done | bytes 8388624 | tf_op jit(solution)/shard_map/all_gather | solution.py:185
  515.9 6.6 multiply_convert_fusion.2
  522.5 72.2 %all-gather.21.cloned.1.call-done = bf16[2048,2048]{1,0:T(8,128)(2,1)} async-done(((bf16[64,2048]{1,0:T(8,128)(2,1)}), bf16[2048,2048]{1,0:T(8,128)(2,1)}) %all-gather.21.cloned.1.call-update) | async-done | bytes 8388624 | tf_op jit(solution)/shard_map/all_gather | solution.py:186
  594.7 4.7 fusion.230
  609.6 64.2 %all-gather.23.cloned.1.call-done = bf16[2048,2048]{1,0:T(8,128)(2,1)} async-done(((bf16[64,2048]{1,0:T(8,128)(2,1)}), bf16[2048,2048]{1,0:T(8,128)(2,1)}) %all-gather.23.cloned.1.call-update) | async-done | bytes 8388624 | tf_op jit(solution)/shard_map/all_gather | solution.py:347
  673.8 5.9 fusion.134
  679.7 170.4 %all-gather.25.cloned.1.call-done = bf16[2048,7168]{1,0:T(8,128)(2,1)} async-done(((bf16[64,7168]{1,0:T(8,128)(2,1)}), bf16[2048,7168]{1,0:T(8,128)(2,1)}) %all-gather.25.cloned.1.call-update) | async-done | bytes 29360144 | tf_op jit(solution)/shard_map/all_gather | solution.py:345
  850.1 15.7 convolution_maximum_fusion
  865.7 160.3 %all-gather.27.cloned.1.call-done = bf16[7168,2048]{1,0:T(8,128)(2,1)} async-done(((bf16[224,2048]{1,0:T(8,128)(2,1)}), bf16[7168,2048]{1,0:T(8,128)(2,1)}) %all-gather.27.cloned.1.call-update) | async-done | bytes 29360144 | tf_op jit(solution)/shard_map/all_gather | solution.py:346
  1026.0 16.5 fusion.159
  1042.5 15.8 fusion.131
  1058.3 16.4 fusion.233
  1074.7 8.1 multiply_reduce_fusion
  1084.2 14.2 all_gather.118
  1101.8 8.0 fusion.223
  1127.4 20.8 while.101
  1151.6 7.3 fusion.234
  1158.9 8.9 all-gather.31.cloned.1.call-done
  1167.7 21.4 while.100
  1193.1 130.3 %while.102 = (s32[]{:T(128)}, f32[32,64]{1,0:T(8,128)S(1)}, f32[32,64]{1,0:T(8,128)S(1)}, f32[32,64,64]{2,1,0:T(8,128)}, f32[2,64,32,64]{1,0,3,2:T(2,128)}, /*in...) while((s32[]{:T(128)}, f32[32,64]{1,0:T(8,128)S(1)}, ...), condition=%wide.region_27.28_spmd.clone.clone.clone, body=%wide.region_20.27_spmd.clone.clone.clone.sunk | while | flops 810430592 | bytes 74234952 | solution.py:118
  1220.5 4.3 convolution_add_fusion.10
  1228.4 25.5 dynamic_update_slice.125
  1253.9 4.2 fusion.347
  1285.4 4.3 convolution_add_fusion.10
  1293.3 25.5 dynamic_update_slice.125
  1318.8 4.2 fusion.347
  1337.8 6.5 fusion.236
  1344.4 6.7 fusion.235
  1351.2 4.1 negate_add_fusion
  1359.2 4.0 fusion.224
  1366.8 9.2 fusion.239
  1377.0 8.3 fusion.221
  1386.6 8.2 fusion.237
  1396.2 8.3 fusion.172
  1405.5 8.4 fusion.175
  1415.0 8.4 fusion.178
  1424.4 24.1 fusion.238
  1449.9 22.5 fusion.166
  1475.4 23.6 all-reduce.32.cloned.1.call-done
  1516.6 16.4 reduce-scatter.10.cloned.1.call-done
  1534.7 186.2 %reduce-scatter.26.cloned.1.call-done = f32[64,2048]{1,0:T(8,128)} async-done(((f32[2048,2048]{1,0:T(8,128)}), f32[64,2048]{1,0:T(8,128)}) %reduce-scatter.26.cloned.1.call-update) | async-done | bytes 524304 | tf_op jit(solution)/shard_map/reduce_scatter | solution.py:208
  1720.8 187.3 %reduce-scatter.18.cloned.1.call-done = f32[64,2048]{1,0:T(8,128)} async-done(((f32[2048,2048]{1,0:T(8,128)}), f32[64,2048]{1,0:T(8,128)}) %reduce-scatter.18.cloned.1.call-update) | async-done | bytes 524304 | tf_op jit(solution)/shard_map/reduce_scatter | solution.py:493
  1908.1 187.2 %reduce-scatter.20.cloned.1.call-done = f32[64,2048]{1,0:T(8,128)} async-done(((f32[2048,2048]{1,0:T(8,128)}), f32[64,2048]{1,0:T(8,128)}) %reduce-scatter.20.cloned.1.call-update) | async-done | bytes 524304 | tf_op jit(solution)/shard_map/reduce_scatter | solution.py:494
  2095.3 187.2 %reduce-scatter.12.cloned.1.call-done = f32[64,2048]{1,0:T(8,128)} async-done(((f32[2048,2048]{1,0:T(8,128)}), f32[64,2048]{1,0:T(8,128)}) %reduce-scatter.12.cloned.1.call-update) | async-done | bytes 524304 | tf_op jit(solution)/shard_map/reduce_scatter | solution.py:490
  2282.6 187.2 %reduce-scatter.14.cloned.1.call-done = f32[64,2048]{1,0:T(8,128)} async-done(((f32[2048,2048]{1,0:T(8,128)}), f32[64,2048]{1,0:T(8,128)}) %reduce-scatter.14.cloned.1.call-update) | async-done | bytes 524304 | tf_op jit(solution)/shard_map/reduce_scatter | solution.py:491
  2469.8 187.2 %reduce-scatter.16.cloned.1.call-done = f32[64,2048]{1,0:T(8,128)} async-done(((f32[2048,2048]{1,0:T(8,128)}), f32[64,2048]{1,0:T(8,128)}) %reduce-scatter.16.cloned.1.call-update) | async-done | bytes 524304 | tf_op jit(solution)/shard_map/reduce_scatter | solution.py:492
  2657.0 623.5 %reduce-scatter.22.cloned.1.call-done = f32[64,7168]{1,0:T(8,128)} async-done(((f32[2048,7168]{1,0:T(8,128)}), f32[64,7168]{1,0:T(8,128)}) %reduce-scatter.22.cloned.1.call-update) | async-done | bytes 1835024 | tf_op jit(solution)/shard_map/reduce_scatter | solution.py:206
  3280.4 622.1 %reduce-scatter.24.cloned.1.call-done = f32[224,2048]{1,0:T(8,128)} async-done(((f32[7168,2048]{1,0:T(8,128)}), f32[224,2048]{1,0:T(8,128)}) %reduce-scatter.24.cloned.1.call-update) | async-done | bytes 1835024 | tf_op jit(solution)/shard_map/reduce_scatter | solution.py:207
  (505 shorter events, 279.7 us)
Async XLA Ops:
  7.2 60.5 %copy-start.13 = (bf16[1,128,2048]{2,1,0:T(8,128)(2,1)S(1)}, bf16[1,128,2048]{2,1,0:T(8,128)(2,1)}, u32[]{:S(2)}) copy-start(bf16[1,128,2048]{2,1,0:T(8,128)(2,1)} %param.35) | copy-start | bytes 1572868
  7.2 84.3 %all-gather.13.cloned.1.call-start = ((), (), s32[]{:S(2)}) async-start(), calls=%async_computation.9 | async-start | bytes 8650752 | tf_op jit(solution)/shard_map/all_gather | solution.py:183
  7.9 162.4 %all-gather.15.cloned.1.call-start = ((), (), s32[]{:S(2)}) async-start(), calls=%async_computation.10 | async-start | bytes 8650752 | tf_op jit(solution)/shard_map/all_gather | solution.py:184
  8.7 240.7 %all-gather.17.cloned.1.call-start = ((), (), s32[]{:S(2)}) async-start(), calls=%async_computation.11 | async-start | bytes 8650752 | tf_op jit(solution)/shard_map/all_gather | solution.py:182
  9.4 427.7 %all-gather.29.cloned.1.call-start = ((), (), s32[]{:S(2)}) async-start(), calls=%async_computation.26 | async-start | bytes 9437184 | tf_op jit(solution)/shard_map/all_gather | solution.py:22
  65.1 450.7 %copy-start.73 = (f32[2048]{0:T(1024)}, f32[2048]{0:T(1024)S(1)}, u32[]{:S(2)}) copy-start(f32[2048]{0:T(1024)S(1)} %convert_element_type.205) | copy-start | bytes 24580
  65.1 450.7 %copy-start.71 = (f32[2048]{0:T(1024)}, f32[2048]{0:T(1024)S(1)}, u32[]{:S(2)}) copy-start(f32[2048]{0:T(1024)S(1)} %convert_element_type.204) | copy-start | bytes 24580
  66.4 449.5 %copy-start.86 = (f32[128]{0:T(128)}, f32[128]{0:T(128)S(1)}, u32[]{:S(2)}) copy-start(f32[128]{0:T(128)S(1)} %broadcast_multiply_fusion.3) | copy-start | bytes 1540
  67.7 448.1 %copy-start.88 = (f32[128]{0:T(128)}, f32[128]{0:T(128)S(1)}, u32[]{:S(2)}) copy-start(f32[128]{0:T(128)S(1)} %fusion.206) | copy-start | bytes 1540
  68.2 3.0 collective-permute-start
  70.9 26.5 copy-start.42
  71.1 26.3 copy-start.82
  71.1 99.3 %copy-start.80 = (f32[2048]{0:T(1024)}, f32[2048]{0:T(1024)S(1)}, u32[]{:S(2)}) copy-start(f32[2048]{0:T(1024)S(1)} %convert_element_type.209) | copy-start | bytes 24580
  71.1 178.3 %copy-start.76 = (f32[2048]{0:T(1024)}, f32[2048]{0:T(1024)S(1)}, u32[]{:S(2)}) copy-start(f32[2048]{0:T(1024)S(1)} %convert_element_type.212) | copy-start | bytes 24580
  71.1 444.8 %copy-start.78 = (f32[1,2048]{1,0:T(1,128)}, f32[1,2048]{1,0:T(1,128)S(1)}, u32[]{:S(2)}) copy-start(f32[1,2048]{1,0:T(1,128)S(1)} %collective-permute-done) | copy-start | bytes 24580
  355.7 20.2 copy-start.62
  355.8 160.1 %all-gather.19.cloned.1.call-start = ((), (), s32[]{:S(2)}) async-start(), calls=%async_computation.12 | async-start | bytes 8650752 | tf_op jit(solution)/shard_map/all_gather | solution.py:185
  356.3 238.4 %all-gather.21.cloned.1.call-start = ((), (), s32[]{:S(2)}) async-start(), calls=%async_computation.13 | async-start | bytes 8650752 | tf_op jit(solution)/shard_map/all_gather | solution.py:186
  356.9 316.9 %all-gather.23.cloned.1.call-start = ((), (), s32[]{:S(2)}) async-start(), calls=%async_computation.14 | async-start | bytes 8650752 | tf_op jit(solution)/shard_map/all_gather | solution.py:347
  357.7 492.4 %all-gather.25.cloned.1.call-start = ((), (), s32[]{:S(2)}) async-start(), calls=%async_computation.15 | async-start | bytes 30277632 | tf_op jit(solution)/shard_map/all_gather | solution.py:345
  358.4 667.6 %all-gather.27.cloned.1.call-start = ((), (), s32[]{:S(2)}) async-start(), calls=%async_computation.16 | async-start | bytes 30277632 | tf_op jit(solution)/shard_map/all_gather | solution.py:346
  359.2 808.6 %all-gather.31.cloned.1.call-start = ((), (), s32[]{:S(2)}) async-start(), calls=%async_computation.27 | async-start | bytes 4718592 | tf_op jit(solution)/shard_map/all_gather | solution.py:36
  359.3 156.6 %copy-start.84 = (f32[2048]{0:T(1024)}, f32[2048]{0:T(1024)S(1)}, u32[]{:S(2)}) copy-start(f32[2048]{0:T(1024)S(1)} %convert_element_type.219) | copy-start | bytes 24580
  442.6 73.3 %copy-start.14 = (bf16[1,128,2048]{2,1,0:T(8,128)(2,1)S(1)}, bf16[1,128,2048]{2,1,0:T(8,128)(2,1)}, u32[]{:S(2)}) copy-start(bf16[1,128,2048]{2,1,0:T(8,128)(2,1)} %param.35) | copy-start | bytes 1572868
  522.5 76.9 %copy-start.65 = (bf16[128,2048]{1,0:T(8,128)(2,1)}, bf16[128,2048]{1,0:T(8,128)(2,1)S(1)}, u32[]{:S(2)}) copy-start(bf16[128,2048]{1,0:T(8,128)(2,1)S(1)} %get-tuple-element.1849) | copy-start | bytes 1572868
  601.7 4.8 collective-permute-start.1
  1026.0 16.5 copy-start.12
  1026.0 16.5 copy-start.35
  1026.0 16.5 copy-start.40
  1082.8 15.8 copy-start.18
  1082.8 15.8 copy-start.47
  1082.8 15.8 collective-permute-start.2
  1100.2 9.6 copy-start.90
  1101.1 8.7 copy-start.67
  1120.3 378.7 %all-reduce.32.cloned.1.call-start = ((), (), s32[]{:S(2)}) async-start(), calls=%async_computation.28 | async-start | bytes 229376
  1167.7 21.4 copy-start.29
  1201.2 5.0 copy-start.23
  1206.2 5.3 copy-start.21
  1266.0 5.0 copy-start.23
  1271.1 5.3 copy-start.21
  1328.6 6.2 copy-start.26
  1328.6 6.2 copy-start.30
  1328.6 6.2 copy-start.33
  1337.7 13.4 copy-start.60
  1337.7 6.5 copy-start.56
  1337.8 13.4 slice-start
  1344.3 6.8 copy-start.45
  1344.3 6.8 copy-start.44
  1344.3 6.8 slice-start.1
  1344.3 6.8 copy-start.77
  1344.3 6.8 copy-start.81
  1344.3 6.8 copy-start.83
  1344.4 6.8 copy-start.85
  1351.1 4.2 copy-start.46
  1355.3 3.9 collective-permute-start.3
  1365.3 167.7 %reduce-scatter.10.cloned.1.call-start = ((), (), s32[]{:S(2)}) async-start(), calls=%async_computation.17 | async-start | bytes 589824 | tf_op jit(solution)/shard_map/reduce_scatter | solution.py:317
  1366.6 354.3 %reduce-scatter.26.cloned.1.call-start = ((), (), s32[]{:S(2)}) async-start(), calls=%async_computation.25 | async-start | bytes 17301504 | tf_op jit(solution)/shard_map/reduce_scatter | solution.py:208
  1376.0 532.1 %reduce-scatter.18.cloned.1.call-start = ((), (), s32[]{:S(2)}) async-start(), calls=%async_computation.21 | async-start | bytes 17301504 | tf_op jit(solution)/shard_map/reduce_scatter | solution.py:493
  1385.4 709.9 %reduce-scatter.20.cloned.1.call-start = ((), (), s32[]{:S(2)}) async-start(), calls=%async_computation.22 | async-start | bytes 17301504 | tf_op jit(solution)/shard_map/reduce_scatter | solution.py:494
  1394.9 887.7 %reduce-scatter.12.cloned.1.call-start = ((), (), s32[]{:S(2)}) async-start(), calls=%async_computation.18 | async-start | bytes 17301504 | tf_op jit(solution)/shard_map/reduce_scatter | solution.py:490
  1404.5 1065.3 %reduce-scatter.14.cloned.1.call-start = ((), (), s32[]{:S(2)}) async-start(), calls=%async_computation.19 | async-start | bytes 17301504 | tf_op jit(solution)/shard_map/reduce_scatter | solution.py:491
  1414.0 1243.0 %reduce-scatter.16.cloned.1.call-start = ((), (), s32[]{:S(2)}) async-start(), calls=%async_computation.20 | async-start | bytes 17301504 | tf_op jit(solution)/shard_map/reduce_scatter | solution.py:492
  1423.4 1857.1 %reduce-scatter.22.cloned.1.call-start = ((), (), s32[]{:S(2)}) async-start(), calls=%async_computation.23 | async-start | bytes 60555264 | tf_op jit(solution)/shard_map/reduce_scatter | solution.py:206
  1448.5 2454.1 %reduce-scatter.24.cloned.1.call-start = ((), (), s32[]{:S(2)}) async-start(), calls=%async_computation.24 | async-start | bytes 60555264 | tf_op jit(solution)/shard_map/reduce_scatter | solution.py:207
  (75 other events, 168.2 us)
Sparse Core Ops, SparseCore 0:
  11.0 80.4 all-gather.12
  94.5 75.8 all-gather.14
  173.4 75.9 all-gather.16
  355.9 81.2 all-gather.28
  439.9 75.8 all-gather.18
  518.7 75.9 all-gather.20
  597.7 76.0 all-gather.22
  676.7 173.3 all-gather.24
  852.9 173.0 all-gather.26
  1120.4 47.2 all-gather.30
  1365.4 133.5 all-reduce.31
  1501.1 31.8 reduce-scatter.9
  1536.0 184.8 reduce-scatter.25
  1723.7 184.3 reduce-scatter.17
  1910.9 184.3 reduce-scatter.19
  2098.2 184.3 reduce-scatter.11
  2285.4 184.3 reduce-scatter.13
  2472.6 184.3 reduce-scatter.15
  2660.0 620.4 reduce-scatter.21
  3283.3 619.2 reduce-scatter.23
where the time goes:
time: 3920 us; the launch traced here: 3910 us
  waiting for transfers between devices  3170 us (81%)
  matrix products  328 us (8%)
  local copies, waits for them, and re-layouts  244 us (6%)
  blocking collectives  73.4 us (2%)
  other arithmetic  70.6 us (2%)
    reduce_scatter x1, waiting for transfers between devices, scatter_channel(): lax.psum_scatter(key_grad, ('seg', 'seq'), scatter_dimension=0, tiled=True)  623 us
    reduce_scatter x1, waiting for transfers between devices, scatter_channel(): lax.psum_scatter(value_grad, ('seg', 'seq'), scatter_dimension=0, tiled=T...  622 us
    reduce_scatter x1, waiting for transfers between devices, per_device(): lax.psum_scatter(grad_wgate, ('seg', 'seq'), scatter_dimension=0, tiled=T...  187 us
    reduce_scatter x1, waiting for transfers between devices, per_device(): lax.psum_scatter(grad_wrec, ('seg', 'seq'), scatter_dimension=0, tiled=True)  187 us
    reduce_scatter x1, waiting for transfers between devices, per_device(): lax.psum_scatter(grad_wout, ('seg', 'seq'), scatter_dimension=0, tiled=True)  187 us
    reduce_scatter x1, waiting for transfers between devices, per_device(): lax.psum_scatter(grad_wkey, ('seg', 'seq'), scatter_dimension=0, tiled=True)  187 us
    reduce_scatter x1, waiting for transfers between devices, per_device(): lax.psum_scatter(grad_wval, ('seg', 'seq'), scatter_dimension=0, tiled=True)  187 us
    reduce_scatter x1, waiting for transfers between devices, scatter_channel(): lax.psum_scatter(recept_grad, ('seg', 'seq'), scatter_dimension=0, tiled=...  186 us
  transfers between devices with their start and end apart: 24, of which 20 were waited for; matrix products, arithmetic and copies ran while one was open for 6% of the time, Pallas kernels for 0%

commit v1 on v0

v1 whole, which is shorter than its diff:
```python
import jax
import jax.numpy as jnp
from jax import lax
from jax.sharding import Mesh, PartitionSpec as P

TEAM = ("b", "l", "c")
TEAMS = ("a", "h")
SEQ = ("h", "l", "c")
ALL = ("a", "b", "h", "l", "c")
HEAD = 64
CHUNK = 128
EPS = 1e-05
GROUP_EPS = 0.00064
BF = jnp.bfloat16
F32 = jnp.float32


def dot(a, b, dims):
    return lax.dot_general(a, b, (dims, ((), ())), preferred_element_type=F32)


def mm(a, b):
    return dot(a, b, ((1,), (0,)))


def mm_nt(a, b):
    return dot(a, b, ((1,), (1,)))


def mm_tn(a, b):
    return dot(a, b, ((0,), (0,)))


class Layout:
    def __init__(self, mesh_shape):
        self.A, self.B, self.H, self.L, self.C = mesh_shape
        self.team = self.B * self.L * self.C
        self.n = self.team * self.A * self.H

    def spread(self, v, whole):
        w = v.shape[-1] // self.n
        lead = v.shape[:-1]
        if w % whole:
            return v.reshape(*lead, self.team, -1)
        k = len(lead)
        v = v.reshape(*lead, self.A, self.B, self.H, self.L, self.C, w)
        v = v.transpose(*range(k), k + 1, k + 3, k + 4, k, k + 2, k + 5)
        return v.reshape(*lead, self.team, -1)

    def unspread(self, v, whole):
        lead = v.shape[:-2]
        w = v.shape[-1] * self.team // self.n
        if w % whole:
            return v.reshape(*lead, -1)
        k = len(lead)
        v = v.reshape(*lead, self.B, self.L, self.C, self.A, self.H, w)
        v = v.transpose(*range(k), k + 3, k, k + 4, k + 1, k + 2, k + 5)
        return v.reshape(*lead, -1)

    def rows_in(self, g):
        m = g.shape[-1]
        g = g.reshape(self.A, self.H, self.B, self.L, self.C, -1, m)
        return g.transpose(0, 2, 1, 3, 4, 5, 6).reshape(-1, m)

    def rows_out(self, g):
        m = g.shape[-1]
        g = g.reshape(self.A, self.B, self.H, self.L, self.C, -1, m)
        return g.transpose(0, 2, 1, 3, 4, 5, 6).reshape(self.A * self.H, self.team, -1, m)


def column_weights(lay, pieces):
    parts = [lay.spread(w, unit) for w, unit in pieces]
    widths = [p.shape[-1] for p in parts]
    sent = jnp.concatenate(parts, axis=-1)
    got = lax.all_to_all(sent, TEAM, split_axis=1, concat_axis=0, tiled=False)
    full = lay.rows_in(lax.all_gather(got, TEAMS, axis=0))
    out, at = [], 0
    for w in widths:
        out.append(full[:, at : at + w])
        at += w
    return out


def column_grads(lay, pieces):
    sent = jnp.concatenate([g.astype(BF) for g, _ in pieces], axis=1)
    part = lax.psum_scatter(lay.rows_out(sent), TEAMS, scatter_dimension=0, tiled=False)
    got = lax.all_to_all(part, TEAM, split_axis=0, concat_axis=1, tiled=False)
    out, at = [], 0
    for g, unit in pieces:
        w = g.shape[1]
        out.append(lay.unspread(got[:, :, at : at + w], unit).astype(F32))
        at += w
    return out


def from_left(row, n):
    return lax.ppermute(row, SEQ, [(i, i + 1) for i in range(n - 1)])


def from_right(row, n):
    return lax.ppermute(row, SEQ, [(i + 1, i) for i in range(n - 1)])


def normed(v):
    mean = jnp.mean(v, axis=-1, keepdims=True)
    cent = v - mean
    rstd = lax.rsqrt(jnp.mean(cent * cent, axis=-1, keepdims=True) + EPS)
    return cent * rstd, rstd


def norm_back(e, xhat, rstd):
    m1 = jnp.mean(e, axis=-1, keepdims=True)
    m2 = jnp.mean(e * xhat, axis=-1, keepdims=True)
    return (e - m1 - xhat * m2) * rstd


def with_before(rows, halo, segs):
    v = rows.reshape(segs, -1, rows.shape[-1])
    return jnp.concatenate([halo, v[:, :-1]], axis=1).reshape(rows.shape)


def with_after(rows, segs):
    v = rows.reshape(segs, -1, rows.shape[-1])
    return (
        jnp.concatenate([v[:, 1:], jnp.zeros_like(v[:, :1])], axis=1).reshape(rows.shape),
        v[:, :1],
    )


EX = lax.Precision.HIGHEST


def ein(spec, a, b):
    return jnp.einsum(spec, a, b, precision=EX, preferred_element_type=F32)


class Wkv:
    def __init__(self, r, k, v, lam, u):
        c = r.shape[2]
        self.c = c
        i = jnp.arange(c, dtype=F32)[:, None, None]
        self.i = i
        self.down = jnp.exp(-lam[None] * i)
        self.up = jnp.exp(lam[None] * (i + 1.0))
        self.tail = jnp.exp(-lam[None] * (c - 1.0 - i))
        self.span = jnp.exp(-lam * c)
        self.r, self.k, self.v, self.u = r, k, v, u
        self.rd, self.kg, self.kt = r * self.down, k * self.up, k * self.tail
        self.low = jnp.arange(c)[:, None] > jnp.arange(c)[None, :]
        self.add = ein("znsgc,znsgv->zngcv", self.kt, v)

    def closing(self):
        s = 0.0
        for n in range(self.r.shape[1]):
            s = self.span[..., None] * s + self.add[:, n]
        return s

    def forward(self, s):
        states = []
        for n in range(self.r.shape[1]):
            states.append(s)
            s = self.span[..., None] * s + self.add[:, n]
        self.states = jnp.stack(states, 1)
        att = jnp.where(self.low, ein("zntgc,znsgc->zngts", self.rd, self.kg), 0.0)
        self.att = att
        self.diag = jnp.sum(self.r * self.u * self.k, axis=-1, keepdims=True)
        y = ein("zngts,znsgv->zntgv", att, self.v) + self.diag * self.v
        y = y + ein("zntgc,zngcv->zntgv", self.rd, self.states)
        return y, s

    def back_add(self, dy):
        return ein("zntgc,zntgv->zngcv", self.rd, dy)

    def back_closing(self, adds):
        g = 0.0
        for n in reversed(range(self.r.shape[1])):
            g = self.span[..., None] * g + adds[:, n]
        return g

    def backward(self, dy, adds, g):
        ends = []
        for n in reversed(range(self.r.shape[1])):
            ends.append(g)
            g = self.span[..., None] * g + adds[:, n]
        ends = jnp.stack(ends[::-1], 1)
        datt = jnp.where(self.low, ein("zntgv,znsgv->zngts", dy, self.v), 0.0)
        ddiag = jnp.sum(dy * self.v, axis=-1, keepdims=True)
        d_rd = ein("zngts,znsgc->zntgc", datt, self.kg) + ein("zntgv,zngcv->zntgc", dy, self.states)
        d_kg = ein("zngts,zntgc->znsgc", datt, self.rd)
        d_kt = ein("znsgv,zngcv->znsgc", self.v, ends)
        d_v = ein("zngts,zntgv->znsgv", self.att, dy) + self.diag * dy
        d_v = d_v + ein("znsgc,zngcv->znsgv", self.kt, ends)
        d_r = d_rd * self.down + ddiag * self.u * self.k
        d_k = d_kg * self.up + d_kt * self.tail + ddiag * self.u * self.r
        d_u = jnp.sum(ddiag * self.r * self.k, axis=(0, 1, 2))
        i = self.i
        d_l = jnp.sum(
            (i + 1.0) * self.kg * d_kg
            - i * self.rd * d_rd
            - (self.c - 1.0 - i) * self.kt * d_kt,
            axis=(0, 1, 2),
        )
        d_l = d_l - self.c * self.span * jnp.sum(self.states * ends, axis=(0, 1, 4))
        return d_r, d_k, d_v, d_u, d_l


def chain(first, add, span, n, ahead):
    place = lax.axis_index("h")
    state = jnp.where(place == (0 if ahead else n - 1), first, 0.0)
    for i in range(n - 1):
        pairs = [(j, j + 1) for j in range(n - 1)] if ahead else [(j + 1, j) for j in range(n - 1)]
        arrived = lax.ppermute(span * state + add, "h", pairs)
        state = jnp.where(place == (i + 1 if ahead else n - 2 - i), arrived, state)
    return state


def per_device(lay, *args):
    (x_in, up_in, start_in) = args[:3]
    vec = args[3:13]
    w_r, w_k, w_v, w_g, w_o = args[13:18]
    vec2 = args[18:22]
    w_ck, w_cv, w_cr = args[22:]
    rank = (lax.axis_index("b") * lay.L + lax.axis_index("l")) * lay.C + lax.axis_index("c")
    h_at = lax.axis_index("h")
    nseq = lay.H * lay.L * lay.C
    segs = lay.B
    D = x_in.shape[-1]
    x_own = x_in[0]
    rows = x_own.shape[0]
    T = rows * lay.team
    dcol = D // lay.team
    heads = dcol // HEAD
    half = lay.L * lay.C

    stacked = jnp.stack([*vec, *vec2])
    every = lax.all_gather(stacked, ALL, axis=0)
    every = every.transpose(1, 0, 2).reshape(stacked.shape[0], D).astype(F32)
    g1, b1, s_r, s_k, s_v, s_g, lam, bonus, gn_g, gn_b, g2, b2, s_ck, s_cr = every

    def mine(v):
        return lax.dynamic_index_in_dim(lay.spread(v, HEAD), rank, 0, False)

    lam_m, u_m, gs_m, gb_m = (mine(v) for v in (lam, bonus, gn_g, gn_b))

    W_r, W_k, W_v, W_g = column_weights(lay, [(w, HEAD) for w in (w_r, w_k, w_v, w_g)])
    if (D // lay.n) % HEAD:
        W_o = lax.all_gather(w_o, ALL, axis=0, tiled=True)
        W_o = lax.dynamic_slice_in_dim(W_o, rank * dcol, dcol, 0)
    else:
        W_o = lax.all_gather(w_o, TEAMS, axis=0, tiled=True)

    halo_x = from_left(x_own[-1:], nseq)
    xg = lax.all_gather(x_own, TEAM, axis=0, tiled=True).astype(F32)
    halo_all = lax.all_gather(halo_x, TEAM, axis=0)[::half].astype(F32)
    n1 = normed(xg)[0] * g1 + b1
    halo_1 = (normed(halo_all)[0] * g1 + b1) * jnp.where(h_at > 0, 1.0, 0.0)
    before = with_before(n1, halo_1, segs)
    diff1 = n1 - before
    m_r, m_k, m_v, m_g = ((before + s * diff1).astype(BF) for s in (s_r, s_k, s_v, s_g))
    r = mm(m_r, W_r).astype(BF)
    k = mm(m_k, W_k).astype(BF)
    v = mm(m_v, W_v).astype(BF)
    gate = mm(m_g, W_g)
    shape = (segs, T // segs // CHUNK, CHUNK, heads, HEAD)
    lam_h, u_h = lam_m.reshape(heads, HEAD), u_m.reshape(heads, HEAD)
    wkv = Wkv(*(t.astype(F32).reshape(shape) for t in (r, k, v)), lam_h, u_h)
    span_all = jnp.exp(-lam_h * (T // segs))[..., None]
    nh = start_in.shape[1]
    head_ids = jnp.arange(nh * HEAD, dtype=jnp.int32)
    my_heads = lax.dynamic_index_in_dim(lay.spread(head_ids, HEAD), rank, 0, False)[::HEAD] // HEAD
    b_at = lax.axis_index("b")
    other_rank = rank + jnp.where(b_at == 0, 1, -1) * (lay.L * lay.C)
    other_heads = (
        lax.dynamic_index_in_dim(lay.spread(head_ids, HEAD), other_rank, 0, False)[::HEAD] // HEAD
    )
    own_start = jnp.take(start_in[0], my_heads, axis=0)
    got_start = lax.ppermute(jnp.take(start_in[0], other_heads, axis=0), "b", [(0, 1), (1, 0)])
    start = jnp.where(b_at == 0, jnp.stack([own_start, got_start]), jnp.stack([got_start, own_start]))
    s_in = chain(start, wkv.closing(), span_all, lay.H, True)
    mixer, s_out = wkv.forward(s_in)
    mix = mixer.reshape(T, heads, HEAD)
    cent = mix - jnp.mean(mix, axis=-1, keepdims=True)
    g_rstd = lax.rsqrt(jnp.mean(cent * cent, axis=-1, keepdims=True) + GROUP_EPS)
    g_hat = (cent * g_rstd).reshape(T, dcol)
    n_mix = g_hat * gs_m + gb_m
    sig = jax.nn.sigmoid(gate)
    silu = gate * sig
    gated = (n_mix * silu).astype(BF)
    part = mm(gated, W_o).astype(BF)
    out = lax.psum_scatter(part, TEAM, scatter_dimension=0, tiled=True)
    middle = x_own.astype(F32) + out.astype(F32)

    placed = jnp.zeros((segs, nh, HEAD, HEAD), BF)
    s_fin = jnp.where(h_at == lay.H - 1, s_out, 0.0).astype(BF)
    placed = placed.at[:, my_heads].set(s_fin)
    final = lax.psum_scatter(placed, "b", scatter_dimension=0, tiled=True)
    final = lax.psum_scatter(final, SEQ, scatter_dimension=1, tiled=True).astype(F32)

    W_ck, W_cr = column_weights(lay, [(w_ck, 1), (w_cr, D)])
    W_cv = lax.all_gather(w_cv, TEAMS, axis=0, tiled=True)
    hat2, rstd2 = normed(middle)
    n2_own = (hat2 * g2 + b2).astype(BF)
    halo_2 = from_left(n2_own[-1:], nseq)
    n2 = lax.all_gather(n2_own, TEAM, axis=0, tiled=True).astype(F32)
    halo_2 = lax.all_gather(halo_2, TEAM, axis=0)[::half].astype(F32)
    before2 = with_before(n2, halo_2, segs)
    diff2 = n2 - before2
    m_ck, m_cr = ((before2 + s * diff2).astype(BF) for s in (s_ck, s_cr))
    relu = jax.nn.relu(mm(m_ck, W_ck))
    act = (relu * relu).astype(BF)
    vpart = mm(act, W_cv).astype(BF)
    val = lax.psum_scatter(vpart, TEAM, scatter_dimension=1, tiled=True).astype(F32)
    sigma = jax.nn.sigmoid(mm(m_cr, W_cr))
    upc = lax.all_to_all(up_in[0].reshape(rows, lay.team, dcol), TEAM, 1, 0).reshape(T, dcol)
    upc = upc.astype(F32)
    add = (sigma * val).astype(BF).reshape(lay.team, rows, dcol)
    add = lax.all_to_all(add, TEAM, 0, 1).reshape(rows, D)
    layer_output = (middle + add.astype(F32)).astype(BF)

    d_value = (sigma * upc).astype(BF)
    d_pregate = (upc * val * sigma * (1.0 - sigma)).astype(BF)
    d_val = lax.all_gather(d_value, TEAM, axis=1, tiled=True)
    g_cv = mm_tn(act, d_val)
    d_pre = (mm_nt(d_val, W_cv) * 2.0 * relu).astype(BF)
    g_ck = mm_tn(m_ck, d_pre)
    g_cr = mm_tn(m_cr, d_pregate)
    d_mck = mm_nt(d_pre, W_ck)
    d_mcr = mm_nt(d_pregate, W_cr)
    g_s_ck = jnp.sum(d_mck * diff2, axis=0)
    g_s_cr = jnp.sum(d_mcr * diff2, axis=0)
    nxt, first = with_after((1.0 - s_ck) * d_mck + (1.0 - s_cr) * d_mcr, segs)
    dn2_part = (s_ck * d_mck + s_cr * d_mcr + nxt).astype(BF)

    def to_rows(part, first):
        mine = lax.psum_scatter(part, TEAM, scatter_dimension=0, tiled=True).astype(F32)
        spread = jnp.zeros((segs, half, D), BF).at[:, :1].set(first.astype(BF))
        edge = lax.psum_scatter(spread.reshape(-1, D), TEAM, scatter_dimension=0, tiled=True)
        return mine.at[-1:].add(from_right(edge, nseq).astype(F32))

    dn2 = to_rows(dn2_part, first)
    g_g2 = jnp.sum(dn2 * hat2, axis=0)
    g_b2 = jnp.sum(dn2, axis=0)
    d_mid = up_in[0].astype(F32) + norm_back(dn2 * g2, hat2, rstd2)

    d_br = lax.all_gather(d_mid.astype(BF), TEAM, axis=0, tiled=True)
    g_o = mm_tn(gated, d_br)
    d_gated = mm_nt(d_br, W_o)
    dn = d_gated * silu
    g_gs = jnp.sum(dn * g_hat, axis=0)
    g_gb = jnp.sum(dn, axis=0)
    d_gate = (d_gated * n_mix * sig * (1.0 + gate * (1.0 - sig))).astype(BF)
    d_mix = norm_back(
        (dn * gs_m).reshape(T, heads, HEAD), g_hat.reshape(T, heads, HEAD), g_rstd
    ).reshape(shape)
    adds = wkv.back_add(d_mix)
    g_in = chain(0.0, wkv.back_closing(adds), span_all, lay.H, False)
    d_r, d_k, d_v, d_u, d_l = wkv.backward(d_mix, adds, g_in)
    d_r, d_k, d_v = (t.reshape(T, dcol).astype(BF) for t in (d_r, d_k, d_v))
    g_r, g_k, g_v, g_w = (
        mm_tn(m, d) for m, d in ((m_r, d_r), (m_k, d_k), (m_v, d_v), (m_g, d_gate))
    )
    d_m = [mm_nt(d, w) for d, w in ((d_r, W_r), (d_k, W_k), (d_v, W_v), (d_gate, W_g))]
    shares = (s_r, s_k, s_v, s_g)
    g_shares = [jnp.sum(d * diff1, axis=0) for d in d_m]
    nxt, first = with_after(sum((1.0 - s) * d for s, d in zip(shares, d_m)), segs)
    dn1_part = (sum(s * d for s, d in zip(shares, d_m)) + nxt).astype(BF)
    dn1 = to_rows(dn1_part, first)
    hat1, rstd1 = normed(x_own.astype(F32))
    g_g1 = jnp.sum(dn1 * hat1, axis=0)
    g_b1 = jnp.sum(dn1, axis=0)
    input_grad = d_mid + norm_back(dn1 * g1, hat1, rstd1)

    g_r, g_k, g_v, g_w, g_ck, g_cr = column_grads(
        lay, [(g_r, HEAD), (g_k, HEAD), (g_v, HEAD), (g_w, HEAD), (g_ck, 1), (g_cr, D)]
    )
    g_cv = lax.psum_scatter(g_cv.astype(BF), TEAMS, scatter_dimension=0, tiled=True).astype(F32)
    if (D // lay.n) % HEAD:
        g_o = jnp.zeros((D, D), BF).at[rank * dcol + jnp.arange(dcol)].set(g_o.astype(BF))
        g_o = lax.psum_scatter(g_o, ALL, scatter_dimension=0, tiled=True).astype(F32)
    else:
        g_o = lax.psum_scatter(g_o.astype(BF), TEAMS, scatter_dimension=0, tiled=True).astype(F32)

    def in_place(v):
        spread = jnp.where(jnp.arange(lay.team)[:, None] == rank, v.reshape(1, -1), 0.0)
        return lay.unspread(spread, HEAD)

    small = jnp.stack(
        [g_g1, g_b1, *g_shares, in_place(d_l), in_place(d_u), in_place(g_gs), in_place(g_gb)]
        + [g_g2, g_b2, g_s_ck, g_s_cr]
    )
    ns = small.shape[0]
    small = small.reshape(ns, lay.n, D // lay.n).transpose(1, 0, 2).reshape(-1)
    small = lax.psum_scatter(small, ALL, scatter_dimension=0, tiled=True).reshape(ns, -1)
    return (
        layer_output[None],
        input_grad[None],
        final,
        *(small[i] for i in range(10)),
        g_r,
        g_k,
        g_v,
        g_w,
        g_o,
        *(small[i] for i in range(10, 14)),
        g_ck,
        g_cv,
        g_cr,
    )


def solution(mesh):
    n_seg, n_seq = mesh.devices.shape
    shape = (n_seg // 2, 2, n_seq // 4, 2, 2)
    view = Mesh(mesh.devices.reshape(shape), ALL)
    lay = Layout(shape)
    seg = ("a", "b")
    vec, mat = P(ALL), P(ALL, None)
    tok = P(seg, SEQ, None)

    def step(*args):
        return per_device(lay, *args)

    return jax.shard_map(
        step,
        mesh=view,
        in_specs=(tok, tok, P(seg, None, None, None), *[vec] * 10, *[mat] * 5, *[vec] * 4, *[mat] * 3),
        out_specs=(tok, tok, P(seg, SEQ, None, None), *[vec] * 10, *[mat] * 5, *[vec] * 4, *[mat] * 3),
        check_vma=False,
    )
```

time: 3920 us -> 1360 us (0.35)
  waiting for transfers between devices: 3170 us -> 615 us
  matrix products: 328 us -> 177 us
  blocking collectives: 73.4 us -> 206 us
  local copies, waits for them, and re-layouts: 244 us -> 185 us
  other arithmetic: 70.6 us -> 119 us
    reduce_scatter x9, waiting for transfers between devices: 2380 us -> 284 us  [the longest x1 83.5 us: column_grads(): lax.psum_scatter(lay.rows_out(sent), TEAMS, scatter_dimension=0, tiled=Fa...]
    all_gather x10 -> x8, waiting for transfers between devices: 755 us -> 200 us  [the longest x2 86.5 us: column_weights(): full = lay.rows_in(lax.all_gather(got, TEAMS, axis=0))]
    dot_general x55 -> x36, matrix products: 328 us -> 177 us  [the longest x24 146 us: dot(): return lax.dot_general(a, b, (dims, ((), ())), preferred_element_type=F32)]
    dynamic_update_slice x10 -> x0, local copies, waits for them, and re-layouts: 116 us -> none  [tile_traversal(): lax.scan(stepper, empty_state, (acceptor_numbers.reshape(shape), lookup_t...]
    unnamed x21 -> x19, waiting for transfers between devices: 29 us -> 124 us
    all_to_all x0 -> x3, blocking collectives: none -> 85.3 us  [the longest x2 66.2 us: column_weights(): got = lax.all_to_all(sent, TEAM, split_axis=1, concat_axis=0, tiled=False)]
    convert_element_type x26 -> x17, other arithmetic: 4.53 us -> 64.2 us  [the longest x1 18.2 us: per_device(): dn1_part = (sum((s * d for s, d in zip(shares, d_m))) + nxt).astype(BF)]
  transfers between devices with their start and end apart: 24 -> 27, of which waited for: 20 -> 15; matrix products, arithmetic and copies ran while one was open for 6% -> 27% of each run, Pallas kernels for 0% -> 0%
where the time goes in v1:
time: 1360 us; the launch traced here: 1350 us
  waiting for transfers between devices  615 us (45%)
  blocking collectives  206 us (15%)
  local copies, waits for them, and re-layouts  185 us (14%)
  matrix products  177 us (13%)
  other arithmetic  119 us (9%)
  starting transfers between devices  29.5 us (2%)
  between operations  16.6 us (1%)
    dot_general x24, matrix products, dot(): return lax.dot_general(a, b, (dims, ((), ())), preferred_element_type=F32)  146 us
    unnamed x19, waiting for transfers between devices  124 us
    all_gather x2, waiting for transfers between devices, column_weights(): full = lay.rows_in(lax.all_gather(got, TEAMS, axis=0))  86.5 us
    reduce_scatter x1, waiting for transfers between devices, column_grads(): lax.psum_scatter(lay.rows_out(sent), TEAMS, scatter_dimension=0, tiled=Fa...  83.5 us
    reduce_scatter x1, waiting for transfers between devices, per_device(): lax.psum_scatter(g_cv.astype(BF), TEAMS, scatter_dimension=0, tiled=True)  77.9 us
    all_to_all x2, blocking collectives, column_weights(): got = lax.all_to_all(sent, TEAM, split_axis=1, concat_axis=0, tiled=False)  66.2 us
    all_gather x1, waiting for transfers between devices, per_device(): W_cv = lax.all_gather(w_cv, TEAMS, axis=0, tiled=True)  55.5 us
    unnamed x2, blocking collectives  54.3 us
  transfers between devices with their start and end apart: 27, of which 15 were waited for; matrix products, arithmetic and copies ran while one was open for 27% of the time, Pallas kernels for 0%

profile of v1, /device:TPU:0, one launch (start us, length us, event | category | flops | bytes accessed | tf_op | source)
XLA Modules:
  0.0 1348.0 jit_solution(3796809602955540323)
XLA Ops:
  16.5 32.0 %all_to_all.63 = bf16[1,64,8,1024]{3,1,0,2:T(8,128)(2,1)} all-to-all(bf16[1,64,8,1024]{3,1,0,2:T(8,128)(2,1)S(1)} %copy.334), channel_id=1, replica_groups=mesh['a'=2,'b'=2,'h'=2,'l'=2,'c'=2] {'b','l','c'}, dimensions={2} | all-to-all | bytes 2097152 | tf_op jit(solution)/shard_map/all_to_all | solution.py:75
  53.2 41.9 %all-gather.7 = bf16[32,14,64]{2,1,0:T(8,128)(2,1)S(1)} all-gather(bf16[1,14,64]{2,1,0:T(8,128)(2,1)S(1)} %bitcast.567), channel_id=3, replica_groups=mesh['a'=2,'b'=2,'h'=2,'l'=2,'c'=2] {'a','b','h','l','c'}, dimensions={0}, use_global_device_ids=true | all-gather | bytes 59136 | tf_op jit(solution)/shard_map/all_gather | solution.py:236
  100.9 12.2 all-gather.6
  118.2 4.4 fusion.5
  122.7 4.4 pad_maximum_fusion
  130.5 10.5 fusion.13
  149.9 5.0 fusion.67
  165.9 11.1 collective-permute-start.2
  202.3 5.4 multiply_convert_fusion.3
  207.6 4.6 convolution_convert_fusion
  214.1 5.6 reshape.939
  223.1 4.6 reshape.940
  229.3 34.2 %all_to_all.64 = bf16[1,64,8,1152]{3,1,0,2:T(8,128)(2,1)} all-to-all(bf16[1,64,8,1152]{3,1,0,2:T(8,128)(2,1)S(1)} %copy.360), channel_id=1, replica_groups=mesh['a'=2,'b'=2,'h'=2,'l'=2,'c'=2] {'b','l','c'}, dimensions={2} | all-to-all | bytes 2359296 | tf_op jit(solution)/shard_map/all_to_all | solution.py:75
  266.3 9.6 reduce-scatter.10.cloned.1.call-done
  288.1 84.6 %all-gather.32.cloned.1.call-done = bf16[32,1,64,1,1152]{4,2,3,1,0:T(8,128)(2,1)} async-done(((bf16[8,1,64,1,1152]{4,2,3,1,0:T(8,128)(2,1)}), bf16[32,1,64,1,1152]{4,2,3,1,0:T(8,128)(2,1)}) %all-gather.32.cloned.1.call-update) | async-done | bytes 4718608 | tf_op jit(solution)/shard_map/all_gather | solution.py:76
  372.7 5.1 copy.362
  377.8 12.4 all-gather.8
  390.9 12.1 all-gather.20.cloned.1.call-done
  403.0 6.5 slice.323
  409.6 5.2 pad_maximum_fusion.1
  415.1 4.6 fusion.9
  421.8 6.3 fusion.16
  428.1 55.5 %all-gather.22.cloned.1.call-done = bf16[896,2048]{1,0:T(8,128)(2,1)} async-done(((bf16[224,2048]{1,0:T(8,128)(2,1)}), bf16[896,2048]{1,0:T(8,128)(2,1)}) %all-gather.22.cloned.1.call-update) | async-done | bytes 3670032 | tf_op jit(solution)/shard_map/all_gather | solution.py:300
  483.6 9.9 convolution_convert_fusion.1
  495.6 19.0 %all_to_all.65 = bf16[1,128,8,256]{1,3,0,2:T(8,128)(2,1)S(1)} all-to-all(bf16[1,128,8,256]{1,3,0,2:T(8,128)(2,1)} %bitcast.538), channel_id=1, replica_groups=mesh['a'=2,'b'=2,'h'=2,'l'=2,'c'=2] {'b','l','c'}, dimensions={2} | all-to-all | bytes 1048576 | tf_op jit(solution)/shard_map/all_to_all | solution.py:314
  516.3 31.0 %reduce-scatter.12.cloned.1.call-done = bf16[1024,256]{0,1:T(8,128)(2,1)} async-done(((bf16[1024,2048]{0,1:T(8,128)(2,1)}), bf16[1024,256]{0,1:T(8,128)(2,1)}) %reduce-scatter.12.cloned.1.call-update) | async-done | bytes 524304 | tf_op jit(solution)/shard_map/reduce_scatter | solution.py:312
  547.4 5.7 fusion.89
  556.1 25.5 %all-gather.24.cloned.1.call-done = bf16[1024,2048]{0,1:T(8,128)(2,1)} async-done(((bf16[1024,256]{0,1:T(8,128)(2,1)}), bf16[1024,2048]{0,1:T(8,128)(2,1)}) %all-gather.24.cloned.1.call-update) | async-done | bytes 4194320 | tf_op jit(solution)/shard_map/all_gather | solution.py:322
  581.7 8.9 multiply_convert_fusion
  590.6 9.4 fusion.14
  600.1 11.6 multiply_reduce_fusion
  611.7 4.4 slice.326
  617.2 9.2 fusion.7
  630.4 4.2 all-to-all-start.2
  638.7 30.4 %all-reduce.2 = bf16[8,2048]{1,0:T(8,128)(2,1)} all-reduce(bf16[8,2048]{1,0:T(8,128)(2,1)} %reshape.946), channel_id=11, replica_groups=mesh['a'=2,'b'=2,'h'=2,'l'=2,'c'=2] {'b','l','c'}, use_global_device_ids=true, to_apply=%region_12.14.clone | all-reduce | flops 16384 | bytes 65536
  677.4 4.6 reduce-scatter.14.cloned.1.call-done
  689.7 3.9 fusion.162
  701.6 20.3 %all-gather.26.cloned.1.call-done = bf16[1024,2048]{1,0:T(8,128)(2,1)} async-done(((bf16[128,2048]{1,0:T(8,128)(2,1)}), bf16[1024,2048]{1,0:T(8,128)(2,1)}) %all-gather.26.cloned.1.call-update) | async-done | bytes 4194320 | tf_op jit(solution)/shard_map/all_gather | solution.py:345
  722.0 6.3 fusion.158
  743.9 5.2 fusion.52
  752.1 6.9 collective-permute-done.5
  767.7 5.3 subtract_reduce_fusion
  775.7 4.6 fusion.22
  788.6 5.6 convert_dynamic-update-slice_fusion
  796.6 11.8 copy.388
  808.4 7.9 copy.389
  817.0 9.2 convolution_convert_fusion.2
  826.6 4.5 convolution_convert_fusion.8
  831.5 6.0 fusion.123
  837.5 4.6 fusion.117
  842.1 4.6 fusion.120
  846.8 20.8 %multiply_reduce_fusion.2 = (f32[2048]{0:T(1024)S(1)}, f32[2048]{0:T(1024)S(1)}, f32[2048]{0:T(1024)S(1)}, f32[2048]{0:T(1024)S(1)}, f32[1024,2048]{1,0:T(8,128)}, /*index=5*/f32[1024,2048]{1,0:T(8,128)}) fusion(f32[2,512,2048]{2,1,0:T(8,128)} %copy-done.3, f32[2048]{0:T(1024)S(1)} %copy-done.59, f32[2048]{0:T(1024)S(1)} %copy-done.55, ...), kind=kOutput, calls=%fused_computation.33 | convolution fusion | flops 1117773824 | bytes 56188928 | tf_op jit(solution)/shard_map/dot_general | solution.py:19
  867.6 4.4 slice.333
  872.0 3.9 concatenate.35
  875.9 18.2 %fusion.6 = bf16[1024,2048]{1,0:T(8,128)(2,1)} fusion(f32[2,512,2048]{2,1,0:T(8,128)} %concatenate.35, f32[1024,2048]{1,0:T(8,128)} %get-tuple-element.204, f32[1024,2048]{1,0:T(8,128)} %fusion.123, f32[1024,2048]{1,0:T(8,128)} %fusion.117, f32[1024,2048]{1,0:T(8,128)} %fusion.120, f32[2048]{0:T(1024)S(1)} %copy-done.74, f32[2048]{0:T(1024)S(1)} %copy-done.72, ...), kind=kLoop, calls=%fused_computation.14 | loop fusion | flops 18874368 | bytes 46170112 | tf_op jit(solution)/shard_map/convert_element_type | solution.py:366
  894.2 83.5 %reduce-scatter.22.cloned.1.call-done = bf16[1,8,64,2176]{3,2,1,0:T(8,128)(2,1)} async-done(((bf16[4,8,64,2176]{3,2,1,0:T(8,128)(2,1)}), bf16[1,8,64,2176]{3,2,1,0:T(8,128)(2,1)}) %reduce-scatter.22.cloned.1.call-update) | async-done | bytes 2228240 | tf_op jit(solution)/shard_map/reduce_scatter | solution.py:86
  977.7 4.4 all-to-all-start.4
  982.4 30.0 %reduce-scatter.20.cloned.1.call-done = bf16[1,4,64,64]{3,2,1,0:T(8,128)(2,1)} async-done(((bf16[1,32,64,64]{3,2,1,0:T(8,128)(2,1)}), bf16[1,4,64,64]{3,2,1,0:T(8,128)(2,1)}) %reduce-scatter.20.cloned.1.call-update) | async-done | bytes 32784 | tf_op jit(solution)/shard_map/reduce_scatter | solution.py:297
  1014.2 77.9 %reduce-scatter.26.cloned.1.call-done = bf16[224,2048]{1,0:T(8,128)(2,1)} async-done(((bf16[896,2048]{1,0:T(8,128)(2,1)}), bf16[224,2048]{1,0:T(8,128)(2,1)}) %reduce-scatter.26.cloned.1.call-update) | async-done | bytes 917520 | tf_op jit(solution)/shard_map/reduce_scatter | solution.py:376
  1104.3 23.9 %all-reduce.3 = bf16[8,2048]{1,0:T(8,128)(2,1)S(1)} all-reduce(bf16[8,2048]{1,0:T(8,128)(2,1)S(1)} %reshape.952), channel_id=13, replica_groups=mesh['a'=2,'b'=2,'h'=2,'l'=2,'c'=2] {'b','l','c'}, use_global_device_ids=true, to_apply=%region_19.21.clone | all-reduce | flops 16384 | bytes 65536
  1132.5 47.4 %reduce-scatter.16.cloned.1.call-done = bf16[128,2048]{1,0:T(8,128)(2,1)} async-done(((bf16[1024,2048]{1,0:T(8,128)(2,1)}), bf16[128,2048]{1,0:T(8,128)(2,1)}) %reduce-scatter.16.cloned.1.call-update) | async-done | bytes 524304 | tf_op jit(solution)/shard_map/reduce_scatter | solution.py:335
  1184.5 122.1 %all-reduce.7.cloned.1.call-done = f32[28672]{0:T(1024)} async-done(((f32[28672]{0:T(1024)}), f32[28672]{0:T(1024)}) %all-reduce.7.cloned.1.call-update) | async-done | bytes 114704
  1313.3 4.7 reshape.971
  1321.0 5.2 reshape.963
  (538 shorter events, 226.4 us)
Async XLA Ops:
  7.2 43.6 %copy-start = (f32[1,32,64,64]{3,2,1,0:T(8,128)S(1)}, f32[1,32,64,64]{3,2,1,0:T(8,128)}, u32[]{:S(2)}) copy-start(f32[1,32,64,64]{3,2,1,0:T(8,128)} %param.37) | copy-start | bytes 1572868
  7.2 106.3 %all-gather.28.cloned.1.call-start = ((), (), s32[]{:S(2)}) async-start(), calls=%async_computation.28 | async-start | bytes 4718592 | tf_op jit(solution)/shard_map/all_gather | solution.py:253
  8.0 134.9 %all-gather.30.cloned.1.call-start = ((), (), s32[]{:S(2)}) async-start(), calls=%async_computation.29 | async-start | bytes 5242880 | tf_op jit(solution)/shard_map/all_gather | solution.py:76
  15.2 33.3 %copy-start.7 = (bf16[1,128,2048]{2,1,0:T(8,128)(2,1)S(1)}, bf16[1,128,2048]{2,1,0:T(8,128)(2,1)}, u32[]{:S(2)}) copy-start(bf16[1,128,2048]{2,1,0:T(8,128)(2,1)} %param.35) | copy-start | bytes 1572868
  15.6 37.4 %copy-start.108 = (bf16[64]{0:T(256)(128)(2,1)S(1)}, bf16[64]{0:T(256)(128)(2,1)}, u32[]{:S(2)}) copy-start(bf16[64]{0:T(256)(128)(2,1)} %param.38) | copy-start | bytes 388
  15.6 37.4 %copy-start.109 = (bf16[64]{0:T(256)(128)(2,1)S(1)}, bf16[64]{0:T(256)(128)(2,1)}, u32[]{:S(2)}) copy-start(bf16[64]{0:T(256)(128)(2,1)} %param.39) | copy-start | bytes 388
  15.6 37.4 %copy-start.110 = (bf16[64]{0:T(256)(128)(2,1)S(1)}, bf16[64]{0:T(256)(128)(2,1)}, u32[]{:S(2)}) copy-start(bf16[64]{0:T(256)(128)(2,1)} %param.40) | copy-start | bytes 388
  15.6 37.4 %copy-start.111 = (bf16[64]{0:T(256)(128)(2,1)S(1)}, bf16[64]{0:T(256)(128)(2,1)}, u32[]{:S(2)}) copy-start(bf16[64]{0:T(256)(128)(2,1)} %param.41) | copy-start | bytes 388
  15.6 37.4 %copy-start.112 = (bf16[64]{0:T(256)(128)(2,1)S(1)}, bf16[64]{0:T(256)(128)(2,1)}, u32[]{:S(2)}) copy-start(bf16[64]{0:T(256)(128)(2,1)} %param.42) | copy-start | bytes 388
  15.7 37.4 %copy-start.113 = (bf16[64]{0:T(256)(128)(2,1)S(1)}, bf16[64]{0:T(256)(128)(2,1)}, u32[]{:S(2)}) copy-start(bf16[64]{0:T(256)(128)(2,1)} %param.43) | copy-start | bytes 388
  15.7 37.4 %copy-start.114 = (bf16[64]{0:T(256)(128)(2,1)S(1)}, bf16[64]{0:T(256)(128)(2,1)}, u32[]{:S(2)}) copy-start(bf16[64]{0:T(256)(128)(2,1)} %param.44) | copy-start | bytes 388
  15.7 37.4 %copy-start.115 = (bf16[64]{0:T(256)(128)(2,1)S(1)}, bf16[64]{0:T(256)(128)(2,1)}, u32[]{:S(2)}) copy-start(bf16[64]{0:T(256)(128)(2,1)} %param.45) | copy-start | bytes 388
  15.7 37.3 %copy-start.116 = (bf16[64]{0:T(256)(128)(2,1)S(1)}, bf16[64]{0:T(256)(128)(2,1)}, u32[]{:S(2)}) copy-start(bf16[64]{0:T(256)(128)(2,1)} %param.46) | copy-start | bytes 388
  15.7 37.3 %copy-start.117 = (bf16[64]{0:T(256)(128)(2,1)S(1)}, bf16[64]{0:T(256)(128)(2,1)}, u32[]{:S(2)}) copy-start(bf16[64]{0:T(256)(128)(2,1)} %param.47) | copy-start | bytes 388
  15.7 37.3 %copy-start.118 = (bf16[64]{0:T(256)(128)(2,1)S(1)}, bf16[64]{0:T(256)(128)(2,1)}, u32[]{:S(2)}) copy-start(bf16[64]{0:T(256)(128)(2,1)} %param.53) | copy-start | bytes 388
  15.7 37.3 %copy-start.119 = (bf16[64]{0:T(256)(128)(2,1)S(1)}, bf16[64]{0:T(256)(128)(2,1)}, u32[]{:S(2)}) copy-start(bf16[64]{0:T(256)(128)(2,1)} %param.54) | copy-start | bytes 388
  15.7 37.3 %copy-start.120 = (bf16[64]{0:T(256)(128)(2,1)S(1)}, bf16[64]{0:T(256)(128)(2,1)}, u32[]{:S(2)}) copy-start(bf16[64]{0:T(256)(128)(2,1)} %param.55) | copy-start | bytes 388
  15.8 37.3 %copy-start.121 = (bf16[64]{0:T(256)(128)(2,1)S(1)}, bf16[64]{0:T(256)(128)(2,1)}, u32[]{:S(2)}) copy-start(bf16[64]{0:T(256)(128)(2,1)} %param.56) | copy-start | bytes 388
  48.5 159.1 %all-gather.18.cloned.1.call-start = ((), (), s32[]{:S(2)}) async-start(), calls=%async_computation.14 | async-start | bytes 1310720 | tf_op jit(solution)/shard_map/all_gather | solution.py:250
  48.6 52.3 %collective-permute-start = (bf16[1,2048]{1,0:T(2,128)(2,1)S(1)}, bf16[1,2048]{1,0:T(2,128)(2,1)S(1)}, u32[]{:S(2)}, u32[]{:S(2)}) collective-permute-start(bf16[1,2048]{1,0:T(2,128)(2,1)S(1)} %slice_bitcast_fusion.8), channel_id=1, source_target_pairs={{0,1},{1,2},{2,3},{3,4},{4,5},{5,6},{6,7},{8,9},{9,10},{10,11},{11... | collective-permute-start | bytes 12296 | tf_op jit(solution)/shard_map/ppermute | solution.py:97
  50.8 48.3 %copy-start.102 = (s32[4]{0:T(128)}, s32[4]{0:T(128)S(1)}, u32[]{:S(2)}) copy-start(s32[4]{0:T(128)S(1)} %get-tuple-element.208) | copy-start | bytes 52
  52.2 111.3 %collective-permute-start.1 = (f32[4,64,64]{1,2,0:T(8,128)}, f32[4,64,64]{1,2,0:T(8,128)}, u32[]{:S(2)}, u32[]{:S(2)}) collective-permute-start(f32[4,64,64]{1,2,0:T(8,128)} %broadcast_select_fusion), channel_id=1, source_target_pairs={{0,8},{8,0},{1,9},{9,1},{2,10},{10,2},{3,11},{11,3},{4,12},{12,4},... | collective-permute-start | bytes 196616 | tf_op jit(solution)/shard_map/ppermute | solution.py:277
  52.8 223.1 %reduce-scatter.10.cloned.1.call-start = ((), (), s32[]{:S(2)}) async-start(), calls=%async_computation.15 | async-start | bytes 4718592 | tf_op jit(solution)/shard_map/reduce_scatter | solution.py:290
  52.9 46.2 %copy-start.100 = (f32[128]{0:T(128)}, f32[128]{0:T(128)S(1)}, u32[]{:S(2)}) copy-start(f32[128]{0:T(128)S(1)} %get-tuple-element.212) | copy-start | bytes 1540
  52.9 65.3 %copy-start.99 = (f32[128]{0:T(128)}, f32[128]{0:T(128)S(1)}, u32[]{:S(2)}) copy-start(f32[128]{0:T(128)S(1)} %get-tuple-element.211) | copy-start | bytes 1540
  52.9 138.4 %copy-start.50 = (pred[128,128]{1,0:T(8,128)(4,1)}, pred[128,128]{1,0:T(8,128)(4,1)S(1)}, u32[]{:S(2)}) copy-start(pred[128,128]{1,0:T(8,128)(4,1)S(1)} %iota_compare_fusion) | copy-start | bytes 49156
  98.3 86.1 %copy-start.37 = (f32[128,4,64]{0,2,1:T(8,128)}, f32[128,4,64]{0,2,1:T(8,128)S(1)}, u32[]{:S(2)}) copy-start(f32[128,4,64]{0,2,1:T(8,128)S(1)} %multiply_exponential_fusion.1) | copy-start | bytes 393220
  99.2 83.5 %copy-start.45 = (f32[128,4,64]{0,2,1:T(8,128)}, f32[128,4,64]{0,2,1:T(8,128)S(1)}, u32[]{:S(2)}) copy-start(f32[128,4,64]{0,2,1:T(8,128)S(1)} %get-tuple-element.194) | copy-start | bytes 393220
  99.9 27.2 %copy-start.54 = (f32[2048]{0:T(1024)}, f32[2048]{0:T(1024)S(1)}, u32[]{:S(2)}) copy-start(f32[2048]{0:T(1024)S(1)} %mul.764) | copy-start | bytes 24580
  99.9 27.1 %copy-start.58 = (f32[2048]{0:T(1024)}, f32[2048]{0:T(1024)S(1)}, u32[]{:S(2)}) copy-start(f32[2048]{0:T(1024)S(1)} %add.354) | copy-start | bytes 24580
  100.0 27.1 %copy-start.67 = (f32[2048]{0:T(1024)}, f32[2048]{0:T(1024)S(1)}, u32[]{:S(2)}) copy-start(f32[2048]{0:T(1024)S(1)} %mul.774) | copy-start | bytes 24580
  100.1 27.0 %copy-start.69 = (f32[2048]{0:T(1024)}, f32[2048]{0:T(1024)S(1)}, u32[]{:S(2)}) copy-start(f32[2048]{0:T(1024)S(1)} %mul.777) | copy-start | bytes 24580
  165.9 22.0 %collective-permute-start.2 = (f32[2,4,64,64]{2,3,1,0:T(8,128)}, f32[2,4,64,64]{2,3,1,0:T(8,128)}, u32[]{:S(2)}, u32[]{:S(2)}) collective-permute-start(f32[2,4,64,64]{2,3,1,0:T(8,128)} %add_add_fusion), channel_id=1, source_target_pairs={{0,4},{1,5},{2,6},{3,7},{8,12},{9,13},{10,14},{11,15},{16,20},{17,... | collective-permute-start | bytes 393224 | tf_op jit(solution)/shard_map/ppermute | solution.py:212
  212.3 160.4 %all-gather.32.cloned.1.call-start = ((), (), s32[]{:S(2)}) async-start(), calls=%async_computation.30 | async-start | bytes 5898240 | tf_op jit(solution)/shard_map/all_gather | solution.py:76
  263.5 139.5 %all-gather.20.cloned.1.call-start = ((), (), s32[]{:S(2)}) async-start(), calls=%async_computation.16 | async-start | bytes 4718592 | tf_op jit(solution)/shard_map/all_gather | solution.py:304
  281.3 202.4 %all-gather.22.cloned.1.call-start = ((), (), s32[]{:S(2)}) async-start(), calls=%async_computation.17 | async-start | bytes 4587520 | tf_op jit(solution)/shard_map/all_gather | solution.py:300
  282.0 265.3 %reduce-scatter.12.cloned.1.call-start = ((), (), s32[]{:S(2)}) async-start(), calls=%async_computation.18 | async-start | bytes 4718592 | tf_op jit(solution)/shard_map/reduce_scatter | solution.py:312
  283.4 94.4 %collective-permute-start.3 = (bf16[1,2048]{1,0:T(2,128)(2,1)}, bf16[1,2048]{1,0:T(2,128)(2,1)}, u32[]{:S(2)}, u32[]{:S(2)}) collective-permute-start(bf16[1,2048]{1,0:T(2,128)(2,1)} %slice.322), channel_id=1, source_target_pairs={{0,1},{1,2},{2,3},{3,4},{4,5},{5,6},{6,7},{8,9},{9,10},{10,11},{11... | collective-permute-start | bytes 12296 | tf_op jit(solution)/shard_map/ppermute | solution.py:97
  493.5 88.1 %all-gather.24.cloned.1.call-start = ((), (), s32[]{:S(2)}) async-start(), calls=%async_computation.19 | async-start | bytes 4718592 | tf_op jit(solution)/shard_map/all_gather | solution.py:322
  553.1 128.8 %reduce-scatter.14.cloned.1.call-start = ((), (), s32[]{:S(2)}) async-start(), calls=%async_computation.20 | async-start | bytes 4718592 | tf_op jit(solution)/shard_map/reduce_scatter | solution.py:335
  630.4 42.3 %all-to-all-start.2 = ((bf16[8,128,1,256]{1,3,2,0:T(8,128)(2,1)}), bf16[8,128,1,256]{1,3,2,0:T(8,128)(2,1)}, u32[]{:S(2)}, u32[]{:S(2)}) async-start(bf16[8,128,1,256]{1,3,2,0:T(8,128)(2,1)} %copy.365), calls=%async_computation.4 | async-start | bytes 1048576 | tf_op jit(solution)/shard_map/all_to_all | solution.py:317
  634.5 87.5 %all-gather.26.cloned.1.call-start = ((), (), s32[]{:S(2)}) async-start(), calls=%async_computation.21 | async-start | bytes 4718592 | tf_op jit(solution)/shard_map/all_gather | solution.py:345
  671.2 12.0 collective-permute-start.4
  693.6 122.8 %reduce-scatter.18.cloned.1.call-start = ((), (), s32[]{:S(2)}) async-start(), calls=%async_computation.23 | async-start | bytes 1572864 | tf_op jit(solution)/shard_map/reduce_scatter | solution.py:296
  701.6 276.1 %reduce-scatter.22.cloned.1.call-start = ((), (), s32[]{:S(2)}) async-start(), calls=%async_computation.25 | async-start | bytes 11141120 | tf_op jit(solution)/shard_map/reduce_scatter | solution.py:86
  742.2 16.9 %collective-permute-start.5 = (f32[2,4,64,64]{2,3,1,0:T(8,128)S(1)}, f32[2,4,64,64]{2,3,1,0:T(8,128)S(1)}, u32[]{:S(2)}, u32[]{:S(2)}) collective-permute-start(f32[2,4,64,64]{2,3,1,0:T(8,128)S(1)} %fusion.140), channel_id=1, source_target_pairs={{4,0},{5,1},{6,2},{7,3},{12,8},{13,9},{14,10},{15,11},{20,16},{21,... | collective-permute-start | bytes 393224 | tf_op jit(solution)/shard_map/ppermute | solution.py:212
  816.3 196.2 %reduce-scatter.20.cloned.1.call-start = ((), (), s32[]{:S(2)}) async-start(), calls=%async_computation.24 | async-start | bytes 589824 | tf_op jit(solution)/shard_map/reduce_scatter | solution.py:297
  816.9 275.1 %reduce-scatter.26.cloned.1.call-start = ((), (), s32[]{:S(2)}) async-start(), calls=%async_computation.27 | async-start | bytes 4587520 | tf_op jit(solution)/shard_map/reduce_scatter | solution.py:376
  826.2 304.5 %reduce-scatter.24.cloned.1.call-start = ((), (), s32[]{:S(2)}) async-start(), calls=%async_computation.26 | async-start | bytes 1310720 | tf_op jit(solution)/shard_map/reduce_scatter | solution.py:381
  831.1 348.8 %reduce-scatter.16.cloned.1.call-start = ((), (), s32[]{:S(2)}) async-start(), calls=%async_computation.22 | async-start | bytes 4718592 | tf_op jit(solution)/shard_map/reduce_scatter | solution.py:335
  894.1 119.9 %copy-start.89 = (f32[2048]{0:T(1024)S(1)}, f32[2048]{0:T(1024)}, u32[]{:S(2)}) copy-start(f32[2048]{0:T(1024)} %get-tuple-element.78) | copy-start | bytes 24580
  894.1 119.9 %copy-start.88 = (f32[2048]{0:T(1024)S(1)}, f32[2048]{0:T(1024)}, u32[]{:S(2)}) copy-start(f32[2048]{0:T(1024)} %get-tuple-element.79) | copy-start | bytes 24580
  894.2 200.5 %copy-start.87 = (f32[2048]{0:T(1024)S(1)}, f32[2048]{0:T(1024)}, u32[]{:S(2)}) copy-start(f32[2048]{0:T(1024)} %get-tuple-element.80) | copy-start | bytes 24580
  894.2 200.6 %copy-start.86 = (f32[2048]{0:T(1024)S(1)}, f32[2048]{0:T(1024)}, u32[]{:S(2)}) copy-start(f32[2048]{0:T(1024)} %get-tuple-element.86) | copy-start | bytes 24580
  894.2 200.7 %copy-start.107 = (f32[128]{0:T(128)S(1)}, f32[128]{0:T(128)}, u32[]{:S(2)}) copy-start(f32[128]{0:T(128)} %get-tuple-element.92) | copy-start | bytes 1540
  894.2 200.9 %copy-start.105 = (f32[256]{0:T(256)S(1)}, f32[256]{0:T(256)}, u32[]{:S(2)}) copy-start(f32[256]{0:T(256)} %get-tuple-element.87) | copy-start | bytes 3076
  894.2 201.0 %copy-start.104 = (f32[256]{0:T(256)S(1)}, f32[256]{0:T(256)}, u32[]{:S(2)}) copy-start(f32[256]{0:T(256)} %get-tuple-element.88) | copy-start | bytes 3076
  977.7 330.3 %all-to-all-start.4 = ((bf16[8,64,1,2176]{3,1,2,0:T(8,128)(2,1)}), bf16[8,64,1,2176]{3,1,2,0:T(8,128)(2,1)}, u32[]{:S(2)}, u32[]{:S(2)}) async-start(bf16[8,64,1,2176]{3,1,2,0:T(8,128)(2,1)} %bitcast.532), calls=%async_computation.11 | async-start | bytes 4456448 | tf_op jit(solution)/shard_map/all_to_all | solution.py:87
  982.1 324.5 %all-reduce.7.cloned.1.call-start = ((), (), s32[]{:S(2)}) async-start(), calls=%async_computation.31 | async-start | bytes 229376
  1014.2 86.6 %copy-start.20 = (f32[1024,256]{1,0:T(8,128)S(1)}, f32[1024,256]{1,0:T(8,128)}, u32[]{:S(2)}) copy-start(f32[1024,256]{1,0:T(8,128)} %fusion.67) | copy-start | bytes 3145732
  1014.2 86.6 %copy-start.22 = (f32[1024,256]{1,0:T(8,128)S(1)}, f32[1024,256]{1,0:T(8,128)}, u32[]{:S(2)}) copy-start(f32[1024,256]{1,0:T(8,128)} %copy-done.21) | copy-start | bytes 3145732
  1097.5 83.8 %copy-start.101 = (f32[128]{0:T(128)S(1)}, f32[128]{0:T(128)}, u32[]{:S(2)}) copy-start(f32[128]{0:T(128)} %broadcast_multiply_fusion.9) | copy-start | bytes 1540
  1102.2 80.9 %copy-start.23 = (f32[128,2048]{1,0:T(8,128)S(1)}, f32[128,2048]{1,0:T(8,128)}, u32[]{:S(2)}) copy-start(f32[128,2048]{1,0:T(8,128)} %get-tuple-element.119) | copy-start | bytes 3145732
  1128.9 52.2 %collective-permute-start.6 = (bf16[1,2048]{1,0:T(2,128)(2,1)S(1)}, bf16[1,2048]{1,0:T(2,128)(2,1)S(1)}, u32[]{:S(2)}, u32[]{:S(2)}) collective-permute-start(bf16[1,2048]{1,0:T(2,128)(2,1)S(1)} %constant_dynamic-slice_fusion.6), channel_id=1, source_target_pairs={{1,0},{2,1},{3,2},{4,3},{5,4},{6,5},{7,6},{9,8},{10,9},{11,10},{12... | collective-permute-start | bytes 12296 | tf_op jit(solution)/shard_map/ppermute | solution.py:101
  (89 other events, 525.4 us)
Sparse Core Ops, SparseCore 0:
  9.7 43.0 all-gather.27
  54.6 88.2 all-gather.29
  144.7 34.8 all-gather.17
  212.4 63.4 reduce-scatter.9
  277.6 95.0 all-gather.31
  374.7 28.2 all-gather.19
  404.9 78.7 all-gather.21
  493.6 53.6 reduce-scatter.11
  553.3 28.3 all-gather.23
  626.6 55.3 reduce-scatter.13
  693.7 28.2 all-gather.25
  724.1 20.3 reduce-scatter.17
  816.4 161.2 reduce-scatter.21
  979.9 32.5 reduce-scatter.19
  1015.3 76.6 reduce-scatter.25
  1094.8 34.6 reduce-scatter.23
  1131.8 48.0 reduce-scatter.15
  1186.8 119.7 all-reduce.6

commit v2 on v1

--- a/solution.py
+++ b/solution.py
@@ -1,6 +1,8 @@
 import jax
 import jax.numpy as jnp
 from jax import lax
+from jax.experimental import pallas as pl
+from jax.experimental.pallas import tpu as pltpu
 from jax.sharding import Mesh, PartitionSpec as P
 
 TEAM = ("b", "l", "c")
@@ -15,6 +17,621 @@
 F32 = jnp.float32
 
 
+MESH = pl.DeviceIdType.MESH
+DMA = pltpu.SemaphoreType.DMA
+VMEM_BYTES = 56 << 20
+
+
+def coords():
+    return {name: lax.axis_index(name) for name in ALL}
+
+
+def rank_of(b, l, c):
+    return (b * 2 + l) * 2 + c
+
+
+def remote(src, dst, sent, landed, to):
+    return pltpu.make_async_remote_copy(
+        src_ref=src,
+        dst_ref=dst,
+        send_sem=sent,
+        recv_sem=landed,
+        device_id=to,
+        device_id_type=MESH,
+    )
+
+
+def mates(me):
+    for m in range(1, 8):
+        yield m, {"b": me["b"] ^ (m >> 2), "l": me["l"] ^ ((m >> 1) & 1), "c": me["c"] ^ (m & 1)}
+
+
+def greet(me, H, column, across):
+    sem = pltpu.get_barrier_semaphore()
+    count = 0
+    for dh in range(H if column else 1):
+        h = lax.rem(me["h"] + dh, H)
+        for m in range(8):
+            if dh == 0 and m == 0:
+                continue
+            to = {
+                "b": me["b"] ^ (m >> 2),
+                "h": h if column else me["h"],
+                "l": me["l"] ^ ((m >> 1) & 1),
+                "c": me["c"] ^ (m & 1),
+            }
+            pl.semaphore_signal(sem, inc=1, device_id=to, device_id_type=MESH)
+            count += 1
+    if across:
+        pl.semaphore_signal(sem, inc=1, device_id={"a": 1 - me["a"]}, device_id_type=MESH)
+        count += 1
+    pl.semaphore_wait(sem, count)
+
+
+class Copies:
+    def __init__(self, sems):
+        self.sems, self.k, self.open = sems, 0, []
+
+    def go(self, src, dst, landed, to):
+        copy = remote(src, dst, self.sems.at[self.k], landed, to)
+        self.k += 1
+        copy.start()
+        self.open.append(copy)
+
+    def drain(self):
+        for copy in self.open:
+            copy.wait_send()
+
+
+def landed(ref, sem):
+    remote(ref, ref, sem, sem, {"c": 1 - lax.axis_index("c")}).wait_recv()
+
+
+def upper(ref, half):
+    n = ref.shape[0] // 2
+    return ref.at[pl.ds(half * n, n)]
+
+
+class TeamGather:
+    SENDS = 14
+
+    def __init__(self, me, own, view, send, recv):
+        self.me, self.own, self.view, self.recv = me, own, view, recv
+        self.copies = Copies(send)
+        self.tx, self.tz, self.ts = {"b": 1 - me["b"]}, {"l": 1 - me["l"]}, {"c": 1 - me["c"]}
+
+    def put(self, src, p, half, to):
+        self.copies.go(src, upper(self.view(p), half), self.recv.at[p, half], to)
+
+    def start(self):
+        mine = rank_of(self.me["b"], self.me["l"], self.me["c"])
+        for half, to in ((0, self.tx), (1, self.tz), (1, self.tx), (0, self.tz), (0, self.ts), (1, self.ts)):
+            self.put(upper(self.own, half), mine, half, to)
+
+    def finish(self):
+        b, l, c = self.me["b"], self.me["l"], self.me["c"]
+        px, pz, pd = rank_of(1 - b, l, c), rank_of(b, 1 - l, c), rank_of(1 - b, 1 - l, c)
+        for p, half, on in (
+            (px, 0, self.tz),
+            (pz, 1, self.tx),
+            (px, 1, None),
+            (pz, 0, None),
+            (pd, 0, None),
+            (pd, 1, None),
+        ):
+            block = upper(self.view(p), half)
+            landed(block, self.recv.at[p, half])
+            if on is not None:
+                self.put(block, p, half, on)
+            self.put(block, p, half, self.ts)
+        for q in range(4):
+            p = q * 2 + 1 - c
+            for half in range(2):
+                landed(upper(self.view(p), half), self.recv.at[p, half])
+        self.copies.drain()
+
+
+class TeamSum:
+    SENDS = 10
+
+    def __init__(self, me, part, near, acc, mid, far, send, recv):
+        self.me, self.part, self.near, self.acc, self.mid, self.far = me, part, near, acc, mid, far
+        self.recv = recv
+        self.copies = Copies(send)
+
+    def start(self):
+        b, l, c = self.me["b"], self.me["l"], self.me["c"]
+        self.spots = [(b, l), (1 - b, l), (b, 1 - l), (1 - b, 1 - l)]
+        for i in (3, 1, 2, 0):
+            bb, ll = self.spots[i]
+            self.copies.go(
+                self.part(rank_of(bb, ll, 1 - c)), self.near.at[i], self.recv.at[i], {"c": 1 - c}
+            )
+
+    def pair(self, i):
+        bb, ll = self.spots[i]
+        landed(self.near.at[i], self.recv.at[i])
+        return self.part(rank_of(bb, ll, self.me["c"]))[...].astype(F32) + self.near[i].astype(F32)
+
+    def finish(self):
+        b, l = self.me["b"], self.me["l"]
+        tx, tz = {"b": 1 - b}, {"l": 1 - l}
+        acc, mid, far, recv, go = self.acc, self.mid, self.far, self.recv, self.copies.go
+        for i in (3, 1, 2):
+            acc[i - 1] = self.pair(i).astype(BF)
+            if i == 3:
+                go(upper(acc.at[2], 0), mid.at[0], recv.at[4], tx)
+                go(upper(acc.at[2], 1), mid.at[1], recv.at[5], tz)
+            elif i == 1:
+                go(upper(acc.at[0], 0), upper(far.at[0], 0), recv.at[6], tx)
+            else:
+                go(upper(acc.at[1], 1), upper(far.at[1], 1), recv.at[7], tz)
+        n = mid.shape[1]
+        landed(mid.at[0], recv.at[4])
+        acc[1, :n] = (acc[1, :n].astype(F32) + mid[0].astype(F32)).astype(BF)
+        go(upper(acc.at[1], 0), upper(far.at[1], 0), recv.at[8], tz)
+        landed(mid.at[1], recv.at[5])
+        acc[0, n:] = (acc[0, n:].astype(F32) + mid[1].astype(F32)).astype(BF)
+        go(upper(acc.at[0], 1), upper(far.at[0], 1), recv.at[9], tx)
+        own = self.pair(0)
+        landed(upper(far.at[0], 0), recv.at[6])
+        landed(upper(far.at[1], 1), recv.at[7])
+        landed(upper(far.at[1], 0), recv.at[8])
+        landed(upper(far.at[0], 1), recv.at[9])
+        total = own + far[0].astype(F32) + far[1].astype(F32)
+        self.copies.drain()
+        return total
+
+    @staticmethod
+    def scratch(R, C):
+        return [
+            pltpu.VMEM((4, R, C), BF),
+            pltpu.VMEM((3, R, C), BF),
+            pltpu.VMEM((2, R // 2, C), BF),
+            pltpu.VMEM((2, R, C), BF),
+            DMA((10,)),
+            DMA((10,)),
+        ]
+
+
+class TeamsGather:
+    def __init__(self, me, H, source, out, send, near, far):
+        self.me, self.H, self.source, self.out = me, H, source, out
+        self.near, self.far = near, far
+        self.copies = Copies(send)
+
+    @staticmethod
+    def sems(H):
+        return [DMA((9 + 4 * (H - 1),)), DMA((8,)), DMA((2 * H, 2))]
+
+    def start(self):
+        me = self.me
+        a, b, h, l, c = (me[n] for n in ALL)
+        mine = rank_of(b, l, c)
+        for m, to in mates(me):
+            p = rank_of(to["b"], to["l"], to["c"])
+            self.copies.go(self.source(p), self.out.at[a, b, h, l, c], self.near.at[mine], to)
+
+    def spread(self, local):
+        me = self.me
+        a, b, h, l, c = (me[n] for n in ALL)
+        local.wait()
+        for g in range(2):
+            bb = b if g == 0 else 1 - b
+            for m in range(4):
+                if g == 0 and m == 0:
+                    continue
+                ll, cc = l ^ (m >> 1), c ^ (m & 1)
+                landed(self.out.at[a, bb, h, ll, cc], self.near.at[rank_of(bb, ll, cc)])
+            block = self.out.at[a, bb, h]
+            for dh in range(1, self.H):
+                to = lax.rem(h + dh, self.H)
+                self.copies.go(block, block, self.far.at[dh, g], {"h": to})
+            self.copies.go(block, block, self.far.at[0, g], {"a": 1 - a})
+
+    def forward(self):
+        me = self.me
+        a, b, h, l, c = (me[n] for n in ALL)
+        H = self.H
+        for g in range(2):
+            bb = b if g == 0 else 1 - b
+            for dh in range(1, H):
+                came = lax.rem(h - dh + H, H)
+                block = self.out.at[a, bb, came]
+                landed(block, self.far.at[dh, g])
+                self.copies.go(block, block, self.far.at[H - 1 + dh, g], {"a": 1 - a})
+
+    def finish(self):
+        me = self.me
+        a, b, h, l, c = (me[n] for n in ALL)
+        H = self.H
+        for g in range(2):
+            bb = b if g == 0 else 1 - b
+            landed(self.out.at[1 - a, bb, h], self.far.at[0, g])
+            for dh in range(1, H):
+                came = lax.rem(h - dh + H, H)
+                landed(self.out.at[1 - a, bb, came], self.far.at[H - 1 + dh, g])
+        self.copies.drain()
+
+
+class Halo:
+    def __init__(self, me, H, own, out, send, recv):
+        self.me, self.H, self.own, self.out, self.send, self.recv = me, H, own, out, send, recv
+        self.last = (me["l"] == 1) & (me["c"] == 1) & (me["h"] < H - 1)
+
+    def each(self):
+        me = self.me
+        n = self.own.shape[0]
+        for p in range(8):
+            to = {
+                "b": p >> 2,
+                "h": jnp.minimum(me["h"] + 1, self.H - 1),
+                "l": (p >> 1) & 1,
+                "c": p & 1,
+            }
+            src = self.own.at[pl.ds(n - 16, 16)]
+            yield remote(src, self.out.at[me["b"]], self.send.at[p], self.recv.at[me["b"]], to)
+
+    def start(self):
+        if self.H == 1:
+            return
+
+        @pl.when(self.last)
+        def _():
+            for copy in self.each():
+                copy.start()
+
+    def finish(self):
+        if self.H == 1:
+            return
+
+        @pl.when(self.me["h"] > 0)
+        def _():
+            for b in range(2):
+                landed(self.out.at[b], self.recv.at[b])
+
+        @pl.when(self.last)
+        def _():
+            for copy in self.each():
+                copy.wait_send()
+
+
+class Edge:
+    def __init__(self, me, H, first, got, send, recv):
+        self.me, self.H, self.first, self.got, self.send, self.recv = me, H, first, got, send, recv
+
+    def each(self):
+        me = self.me
+        mine = rank_of(me["b"], me["l"], me["c"])
+        for b in range(2):
+            to = {"b": b, "h": jnp.maximum(me["h"] - 1, 0), "l": 1, "c": 1}
+            yield remote(self.first.at[b], self.got.at[mine], self.send.at[b], self.recv.at[mine], to)
+
+    def start(self):
+        if self.H == 1:
+            return
+
+        @pl.when(self.me["h"] > 0)
+        def _():
+            for copy in self.each():
+                copy.start()
+
+    def finish(self, out):
+        if self.H == 1:
+            return
+        me = self.me
+
+        @pl.when((me["l"] == 1) & (me["c"] == 1) & (me["h"] < self.H - 1))
+        def _():
+            for p in range(8):
+                landed(self.got.at[p], self.recv.at[p])
+            total = self.got[0, 0:1].astype(F32)
+            for p in range(1, 8):
+                total = total + self.got[p, 0:1].astype(F32)
+            n = out.shape[0]
+            out[n - 1 : n] = out[n - 1 : n] + total
+
+        @pl.when(me["h"] > 0)
+        def _():
+            for copy in self.each():
+                copy.wait_send()
+
+
+class Exchange:
+    def __init__(self, me, source, out, send, recv):
+        self.me, self.source, self.out, self.recv = me, source, out, recv
+        self.copies = Copies(send)
+
+    def start(self):
+        mine = rank_of(self.me["b"], self.me["l"], self.me["c"])
+        for m, to in mates(self.me):
+            p = rank_of(to["b"], to["l"], to["c"])
+            self.copies.go(self.source(p), self.out(mine), self.recv.at[mine], to)
+
+    def finish(self):
+        for m, to in mates(self.me):
+            p = rank_of(to["b"], to["l"], to["c"])
+            landed(self.out(p), self.recv.at[p])
+        self.copies.drain()
+
+
+ANY = pl.BlockSpec(memory_space=pl.ANY)
+VM = pl.BlockSpec(memory_space=pltpu.VMEM)
+
+
+def comm_call(body, outs, in_specs, out_specs, scratch, cid):
+    return pl.pallas_call(
+        body,
+        out_shape=outs,
+        in_specs=in_specs,
+        out_specs=out_specs,
+        scratch_shapes=scratch,
+        compiler_params=pltpu.CompilerParams(
+            collective_id=cid, has_side_effects=True, vmem_limit_bytes=VMEM_BYTES
+        ),
+    )
+
+
+def opening(H, vecs, x, up, w, later):
+    A = lax.axis_size("a")
+    grid = (A, 2, H, 2, 2)
+    rows, D = x.shape
+    dcol = D // 8
+
+    def body(
+        vecs, x, up, w, later, va, xg, halo, upc, wa, team, *sems
+    ):
+        vs, vn, vf, xs, xr, hs, hr, us, ur, ws, wn, wf, qs, qr, ls = sems
+        me = coords()
+        a, b, h, l, c = (me[n] for n in ALL)
+        mine = rank_of(b, l, c)
+        local = [
+            pltpu.make_async_copy(w.at[mine], wa.at[a, b, h, l, c], ls.at[0]),
+            pltpu.make_async_copy(vecs, va.at[a, b, h, l, c], ls.at[1]),
+            pltpu.make_async_copy(x, xg.at[mine], ls.at[2]),
+            pltpu.make_async_copy(
+                up.at[:, pl.ds(pl.multiple_of(mine * dcol, dcol), dcol)], upc.at[mine], ls.at[3]
+            ),
+            pltpu.make_async_copy(later.at[mine], team.at[mine], ls.at[4]),
+        ]
+        for copy in local:
+            copy.start()
+        greet(me, H, True, True)
+        gw = TeamsGather(me, H, lambda p: w.at[p], wa, ws, wn, wf)
+        gv = TeamsGather(me, H, lambda p: vecs, va, vs, vn, vf)
+        gx = TeamGather(me, x, lambda p: xg.at[p], xs, xr)
+        gh = Halo(me, H, x, halo, hs, hr)
+        gu = Exchange(
+            me,
+            lambda p: up.at[:, pl.ds(pl.multiple_of(p * dcol, dcol), dcol)],
+            lambda p: upc.at[p],
+            us,
+            ur,
+        )
+        gq = Exchange(me, lambda p: later.at[p], lambda p: team.at[p], qs, qr)
+        gv.start()
+        gw.start()
+        gx.start()
+        gh.start()
+        gw.spread(local[0])
+        gv.spread(local[1])
+        gx.finish()
+        gu.start()
+        gq.start()
+        gv.forward()
+        gw.forward()
+        gu.finish()
+        gh.finish()
+        gv.finish()
+        gw.finish()
+        gq.finish()
+        for copy in local[2:]:
+            copy.wait()
+
+    gsems = TeamsGather.sems(H)
+    return comm_call(
+        body,
+        (
+            jax.ShapeDtypeStruct((*grid, *vecs.shape), BF),
+            jax.ShapeDtypeStruct((8, rows, D), BF),
+            jax.ShapeDtypeStruct((2, 16, D), BF),
+            jax.ShapeDtypeStruct((8, rows, dcol), BF),
+            jax.ShapeDtypeStruct((*grid, *w.shape[1:]), BF),
+            jax.ShapeDtypeStruct(later.shape, BF),
+        ),
+        [ANY] * 5,
+        [ANY] * 6,
+        [*gsems, DMA((14,)), DMA((8, 2)), DMA((8,)), DMA((2,)), DMA((7,)), DMA((8,)), *gsems]
+        + [DMA((7,)), DMA((8,)), DMA((5,))],
+        0,
+    )(vecs, x, up, w, later)
+
+
+def gather_rows(H, x, cid, with_halo, move=None):
+    rows, D = x.shape
+
+    def body(*refs):
+        refs = list(refs)
+        x = refs.pop(0)
+        src = refs.pop(0) if move is not None else None
+        out = refs.pop(0)
+        halo = refs.pop(0) if with_halo else None
+        moved = refs.pop(0) if move is not None else None
+        xs, xr, ls = refs[:3]
+        rest = refs[3:]
+        me = coords()
+        mine = rank_of(me["b"], me["l"], me["c"])
+        local = pltpu.make_async_copy(x, out.at[mine], ls.at[0])
+        local.start()
+        if move is not None:
+            keep = pltpu.make_async_copy(src.at[mine], moved.at[mine], ls.at[1])
+            keep.start()
+        greet(me, H, with_halo, False)
+        gx = TeamGather(me, x, lambda p: out.at[p], xs, xr)
+        gx.start()
+        if with_halo:
+            gh = Halo(me, H, x, halo, rest[0], rest[1])
+            gh.start()
+        if move is not None:
+            gm = Exchange(me, lambda p: src.at[p], lambda p: moved.at[p], rest[-2], rest[-1])
+            gm.start()
+        gx.finish()
+        if with_halo:
+            gh.finish()
+        if move is not None:
+            gm.finish()
+            keep.wait()
+        local.wait()
+
+    outs = [jax.ShapeDtypeStruct((8, rows, D), BF)]
+    scratch = [DMA((14,)), DMA((8, 2)), DMA((2,))]
+    args = [x]
+    if with_halo:
+        outs.append(jax.ShapeDtypeStruct((2, 16, D), BF))
+        scratch += [DMA((8,)), DMA((2,))]
+    if move is not None:
+        outs.append(jax.ShapeDtypeStruct(move.shape, BF))
+        scratch += [DMA((7,)), DMA((8,))]
+        args.append(move)
+    out = comm_call(body, tuple(outs), [ANY] * len(args), [ANY] * len(outs), scratch, cid)(*args)
+    return out if len(outs) > 1 else out[0]
+
+
+def gather_columns(x, cid):
+    T, m = x.shape
+
+    def body(x, out, xs, xr, ls):
+        me = coords()
+        mine = rank_of(me["b"], me["l"], me["c"])
+
+        def view(p):
+            return out.at[:, pl.ds(pl.multiple_of(p * m, m), m)]
+
+        local = pltpu.make_async_copy(x, view(mine), ls)
+        local.start()
+        greet(me, 1, False, False)
+        gx = TeamGather(me, x, view, xs, xr)
+        gx.start()
+        gx.finish()
+        local.wait()
+
+    return comm_call(
+        body,
+        jax.ShapeDtypeStruct((T, 8 * m), BF),
+        [ANY],
+        ANY,
+        [DMA((14,)), DMA((8, 2)), DMA],
+        cid,
+    )(x)
+
+
+def sum_rows(H, part, first, cid):
+    _, rows, D = part.shape
+    n = len(TeamSum.scratch(rows, D))
+
+    def body(*refs):
+        refs = list(refs)
+        part = refs.pop(0)
+        fst = refs.pop(0) if first is not None else None
+        out = refs.pop(0)
+        me = coords()
+        greet(me, H, first is not None, False)
+        s = TeamSum(me, lambda p: part.at[p], *refs[:n])
+        s.start()
+        if first is not None:
+            e = Edge(me, H, fst, *refs[n:])
+            e.start()
+        out[...] = s.finish()
+        if first is not None:
+            e.finish(out)
+
+    scratch = TeamSum.scratch(rows, D)
+    args = [part]
+    if first is not None:
+        scratch += [pltpu.VMEM((8, 16, D), BF), DMA((2,)), DMA((8,))]
+        args.append(first)
+    return comm_call(
+        body, jax.ShapeDtypeStruct((rows, D), F32), [VM] * len(args), VM, scratch, cid
+    )(*args)
+
+
+def sum_columns(part, cid):
+    T, m = part.shape[0], part.shape[1] // 8
+
+    def body(part, out, *scratch):
+        me = coords()
+        greet(me, 1, False, False)
+        s = TeamSum(
+            me, lambda p: part.at[:, pl.ds(pl.multiple_of(p * m, m), m)], *scratch
+        )
+        s.start()
+        out[...] = s.finish()
+
+    return comm_call(
+        body, jax.ShapeDtypeStruct((T, m), F32), [VM], VM, TeamSum.scratch(T, m), cid
+    )(part)
+
+
+def closing(H, small, cols):
+    A = lax.axis_size("a")
+    n = small.shape[0]
+    grid = (A, 2, H, 2, 2)
+
+    def body(small, cols, total, moved, got, ss, sr, ms, mr, ls):
+        me = coords()
+        a, b, h, l, c = (me[k] for k in ALL)
+        mine = rank_of(b, l, c)
+        keep = pltpu.make_async_copy(cols.at[mine], moved.at[mine], ls)
+        keep.start()
+        sem = pltpu.get_barrier_semaphore()
+        others = []
+        for i in range(1, n):
+            k = i
+            dc, k = k % 2, k // 2
+            dl, k = k % 2, k // 2
+            dh, k = k % H, k // H
+            db, da = k % 2, k // 2
+            to = {
+                "a": lax.rem(a + da, A),
+                "b": b ^ db,
+                "h": lax.rem(h + dh, H),
+                "l": l ^ dl,
+                "c": c ^ dc,
+            }
+            others.append((i, to))
+            pl.semaphore_signal(sem, inc=1, device_id=to, device_id_type=MESH)
+        pl.semaphore_wait(sem, n - 1)
+        copies = Copies(ss)
+
+        def at(d):
+            return (((d["a"] * 2 + d["b"]) * H + d["h"]) * 2 + d["l"]) * 2 + d["c"]
+
+        for i, to in others:
+            copies.go(small.at[at(to)], got.at[i], sr.at[i], to)
+        gm = Exchange(me, lambda p: cols.at[p], lambda p: moved.at[p], ms, mr)
+        gm.start()
+        acc = small[at(me)]
+        for i, _ in others:
+            landed(got.at[i], sr.at[i])
+            acc = acc + got[i]
+        total[...] = acc
+        copies.drain()
+        gm.finish()
+        keep.wait()
+
+    return comm_call(
+        body,
+        (
+            jax.ShapeDtypeStruct(small.shape[1:], F32),
+            jax.ShapeDtypeStruct(cols.shape, BF),
+        ),
+        [VM, ANY],
+        [VM, ANY],
+        [pltpu.VMEM(small.shape, F32), DMA((n,)), DMA((n,)), DMA((7,)), DMA((8,)), DMA],
+        15,
+    )(small, cols)
+
+
 def dot(a, b, dims):
     return lax.dot_general(a, b, (dims, ((), ())), preferred_element_type=F32)
 
@@ -66,39 +683,6 @@
         m = g.shape[-1]
         g = g.reshape(self.A, self.B, self.H, self.L, self.C, -1, m)
         return g.transpose(0, 2, 1, 3, 4, 5, 6).reshape(self.A * self.H, self.team, -1, m)
-
-
-def column_weights(lay, pieces):
-    parts = [lay.spread(w, unit) for w, unit in pieces]
-    widths = [p.shape[-1] for p in parts]
-    sent = jnp.concatenate(parts, axis=-1)
-    got = lax.all_to_all(sent, TEAM, split_axis=1, concat_axis=0, tiled=False)
-    full = lay.rows_in(lax.all_gather(got, TEAMS, axis=0))
-    out, at = [], 0
-    for w in widths:
-        out.append(full[:, at : at + w])
-        at += w
-    return out
-
-
-def column_grads(lay, pieces):
-    sent = jnp.concatenate([g.astype(BF) for g, _ in pieces], axis=1)
-    part = lax.psum_scatter(lay.rows_out(sent), TEAMS, scatter_dimension=0, tiled=False)
-    got = lax.all_to_all(part, TEAM, split_axis=0, concat_axis=1, tiled=False)
-    out, at = [], 0
-    for g, unit in pieces:
-        w = g.shape[1]
-        out.append(lay.unspread(got[:, :, at : at + w], unit).astype(F32))
-        at += w
-    return out
-
-
-def from_left(row, n):
-    return lax.ppermute(row, SEQ, [(i, i + 1) for i in range(n - 1)])
-
-
-def from_right(row, n):
-    return lax.ppermute(row, SEQ, [(i + 1, i) for i in range(n - 1)])
 
 
 def normed(v):
@@ -214,15 +798,67 @@
     return state
 
 
+def swap(v, axis):
+    return lax.ppermute(v, axis, [(0, 1), (1, 0)])
+
+
+def shifted(v, dh, H):
+    return lax.ppermute(v, "h", [(i, (i + dh) % H) for i in range(H)])
+
+
+def in_order(near, far, lay):
+    a, h = lax.axis_index("a"), lax.axis_index("h")
+    out = []
+    for i in range(lay.A):
+        for j in range(lay.H):
+            pick = lambda group: lax.select_n(lax.rem(h - j + lay.H, lay.H), *group)
+            if lay.H == 2:
+                pick = lambda group: jnp.where(h == j, group[0], group[1])
+            elif lay.H > 2:
+                pick = lambda group: lax.dynamic_index_in_dim(
+                    jnp.stack(group), lax.rem(h - j + lay.H, lay.H), 0, False
+                )
+            out.append(jnp.where(a == i, pick(near), pick(far)))
+    return jnp.stack(out)
+
+
+def teams_gather(v, lay):
+    near = [v] + [shifted(v, dh, lay.H) for dh in range(1, lay.H)]
+    far = [swap(n, "a") for n in near]
+    return in_order(near, far, lay)
+
+
+def teams_sum(g, lay):
+    a, h = lax.axis_index("a"), lax.axis_index("h")
+    g = g.reshape(lay.A, lay.H, *g.shape[1:])
+    keep = lax.dynamic_index_in_dim(g, a, 0, False)
+    got = swap(lax.dynamic_index_in_dim(g, 1 - a, 0, False), "a")
+    part = (keep.astype(F32) + got.astype(F32)).astype(BF)
+    total = lax.dynamic_index_in_dim(part, h, 0, False).astype(F32)
+    for dh in range(1, lay.H):
+        sent = lax.dynamic_index_in_dim(part, lax.rem(h + dh, lay.H), 0, False)
+        total = total + shifted(sent, dh, lay.H).astype(F32)
+    return total.astype(BF)
+
+
+def swap_blocks(v, rank):
+    got = [lax.dynamic_index_in_dim(v, rank, 0, False)]
+    for m in range(1, 8):
+        sent = lax.dynamic_index_in_dim(v, rank ^ m, 0, False)
+        got.append(lax.ppermute(sent, TEAM, [(i, i ^ m) for i in range(8)]))
+    got = jnp.stack(got)
+    return jnp.stack([lax.dynamic_index_in_dim(got, rank ^ p, 0, False) for p in range(8)])
+
+
 def per_device(lay, *args):
     (x_in, up_in, start_in) = args[:3]
     vec = args[3:13]
     w_r, w_k, w_v, w_g, w_o = args[13:18]
     vec2 = args[18:22]
     w_ck, w_cv, w_cr = args[22:]
-    rank = (lax.axis_index("b") * lay.L + lax.axis_index("l")) * lay.C + lax.axis_index("c")
-    h_at = lax.axis_index("h")
-    nseq = lay.H * lay.L * lay.C
+    a_at, b_at, h_at = (lax.axis_index(n) for n in ("a", "b", "h"))
+    rank = (b_at * lay.L + lax.axis_index("l")) * lay.C + lax.axis_index("c")
+    H = lay.H
     segs = lay.B
     D = x_in.shape[-1]
     x_own = x_in[0]
@@ -231,29 +867,42 @@
     dcol = D // lay.team
     heads = dcol // HEAD
     half = lay.L * lay.C
+    w_row = D // lay.n
+    hid = w_ck.shape[1] // lay.team
 
     stacked = jnp.stack([*vec, *vec2])
-    every = lax.all_gather(stacked, ALL, axis=0)
-    every = every.transpose(1, 0, 2).reshape(stacked.shape[0], D).astype(F32)
+    nv = stacked.shape[0]
+    stacked = jnp.pad(stacked, ((0, 16 - nv), (0, 128 - w_row)))
+    spread4 = jnp.concatenate(
+        [lay.spread(w, HEAD) for w in (w_r, w_k, w_v, w_g)], axis=-1
+    ).transpose(1, 0, 2)
+    ffn = jnp.concatenate([lay.spread(w_ck, 1), lay.spread(w_cr, D)], axis=-1).transpose(1, 0, 2)
+    va, xg, halo_x, upc, W4, ffn_got = opening(H, stacked, x_own, up_in[0], spread4, ffn)
+    every = va.reshape(lay.n, 16, 128)[:, :nv, :w_row].transpose(1, 0, 2).reshape(nv, D).astype(F32)
     g1, b1, s_r, s_k, s_v, s_g, lam, bonus, gn_g, gn_b, g2, b2, s_ck, s_cr = every
-
-    def mine(v):
-        return lax.dynamic_index_in_dim(lay.spread(v, HEAD), rank, 0, False)
-
-    lam_m, u_m, gs_m, gb_m = (mine(v) for v in (lam, bonus, gn_g, gn_b))
-
-    W_r, W_k, W_v, W_g = column_weights(lay, [(w, HEAD) for w in (w_r, w_k, w_v, w_g)])
-    if (D // lay.n) % HEAD:
+    W4 = W4.reshape(D, 4 * dcol)
+    W_r, W_k, W_v, W_g = (W4[:, i * dcol : (i + 1) * dcol] for i in range(4))
+    w_o, w_cv, ffn_got, xg = lax.optimization_barrier((w_o, w_cv, ffn_got, xg))
+    if w_row % HEAD:
         W_o = lax.all_gather(w_o, ALL, axis=0, tiled=True)
         W_o = lax.dynamic_slice_in_dim(W_o, rank * dcol, dcol, 0)
     else:
-        W_o = lax.all_gather(w_o, TEAMS, axis=0, tiled=True)
-
-    halo_x = from_left(x_own[-1:], nseq)
-    xg = lax.all_gather(x_own, TEAM, axis=0, tiled=True).astype(F32)
-    halo_all = lax.all_gather(halo_x, TEAM, axis=0)[::half].astype(F32)
-    n1 = normed(xg)[0] * g1 + b1
-    halo_1 = (normed(halo_all)[0] * g1 + b1) * jnp.where(h_at > 0, 1.0, 0.0)
+        W_o = teams_gather(w_o, lay).reshape(dcol, D)
+    ffn_all = lay.rows_in(teams_gather(ffn_got, lay))
+    W_ck, W_cr = ffn_all[:, :hid], ffn_all[:, hid:]
+    W_cv = teams_gather(w_cv, lay).reshape(hid, D)
+
+    def mine(v):
+        return lax.dynamic_index_in_dim(lay.spread(v, HEAD), rank, 0, False)
+
+    lam_m, u_m, gs_m, gb_m = (mine(v) for v in (lam, bonus, gn_g, gn_b))
+
+    def halo_rows(halo):
+        return jnp.where(h_at > 0, halo[:, -1:].astype(F32), 0.0)
+
+    xf = xg.reshape(T, D).astype(F32)
+    n1 = normed(xf)[0] * g1 + b1
+    halo_1 = jnp.where(h_at > 0, normed(halo_rows(halo_x))[0] * g1 + b1, 0.0)
     before = with_before(n1, halo_1, segs)
     diff1 = n1 - before
     m_r, m_k, m_v, m_g = ((before + s * diff1).astype(BF) for s in (s_r, s_k, s_v, s_g))
@@ -267,14 +916,14 @@
     span_all = jnp.exp(-lam_h * (T // segs))[..., None]
     nh = start_in.shape[1]
     head_ids = jnp.arange(nh * HEAD, dtype=jnp.int32)
-    my_heads = lax.dynamic_index_in_dim(lay.spread(head_ids, HEAD), rank, 0, False)[::HEAD] // HEAD
-    b_at = lax.axis_index("b")
-    other_rank = rank + jnp.where(b_at == 0, 1, -1) * (lay.L * lay.C)
-    other_heads = (
-        lax.dynamic_index_in_dim(lay.spread(head_ids, HEAD), other_rank, 0, False)[::HEAD] // HEAD
-    )
+
+    def heads_of(p):
+        ids = lax.dynamic_index_in_dim(lay.spread(head_ids, HEAD), p, 0, False)
+        return ids[::HEAD] // HEAD
+
+    my_heads = heads_of(rank)
     own_start = jnp.take(start_in[0], my_heads, axis=0)
-    got_start = lax.ppermute(jnp.take(start_in[0], other_heads, axis=0), "b", [(0, 1), (1, 0)])
+    got_start = swap(jnp.take(start_in[0], heads_of(rank ^ 4), axis=0), "b")
     start = jnp.where(b_at == 0, jnp.stack([own_start, got_start]), jnp.stack([got_start, own_start]))
     s_in = chain(start, wkv.closing(), span_all, lay.H, True)
     mixer, s_out = wkv.forward(s_in)
@@ -286,9 +935,8 @@
     sig = jax.nn.sigmoid(gate)
     silu = gate * sig
     gated = (n_mix * silu).astype(BF)
-    part = mm(gated, W_o).astype(BF)
-    out = lax.psum_scatter(part, TEAM, scatter_dimension=0, tiled=True)
-    middle = x_own.astype(F32) + out.astype(F32)
+    part = mm(gated, W_o).astype(BF).reshape(8, rows, D)
+    middle = x_own.astype(F32) + sum_rows(H, part, None, 1)
 
     placed = jnp.zeros((segs, nh, HEAD, HEAD), BF)
     s_fin = jnp.where(h_at == lay.H - 1, s_out, 0.0).astype(BF)
@@ -296,30 +944,23 @@
     final = lax.psum_scatter(placed, "b", scatter_dimension=0, tiled=True)
     final = lax.psum_scatter(final, SEQ, scatter_dimension=1, tiled=True).astype(F32)
 
-    W_ck, W_cr = column_weights(lay, [(w_ck, 1), (w_cr, D)])
-    W_cv = lax.all_gather(w_cv, TEAMS, axis=0, tiled=True)
     hat2, rstd2 = normed(middle)
     n2_own = (hat2 * g2 + b2).astype(BF)
-    halo_2 = from_left(n2_own[-1:], nseq)
-    n2 = lax.all_gather(n2_own, TEAM, axis=0, tiled=True).astype(F32)
-    halo_2 = lax.all_gather(halo_2, TEAM, axis=0)[::half].astype(F32)
-    before2 = with_before(n2, halo_2, segs)
+    n2, halo_2 = gather_rows(H, n2_own, 2, True)
+    n2 = n2.reshape(T, D).astype(F32)
+    before2 = with_before(n2, halo_rows(halo_2), segs)
     diff2 = n2 - before2
     m_ck, m_cr = ((before2 + s * diff2).astype(BF) for s in (s_ck, s_cr))
     relu = jax.nn.relu(mm(m_ck, W_ck))
     act = (relu * relu).astype(BF)
-    vpart = mm(act, W_cv).astype(BF)
-    val = lax.psum_scatter(vpart, TEAM, scatter_dimension=1, tiled=True).astype(F32)
+    val = sum_columns(mm(act, W_cv).astype(BF), 3)
     sigma = jax.nn.sigmoid(mm(m_cr, W_cr))
-    upc = lax.all_to_all(up_in[0].reshape(rows, lay.team, dcol), TEAM, 1, 0).reshape(T, dcol)
-    upc = upc.astype(F32)
+    upc = upc.reshape(T, dcol).astype(F32)
     add = (sigma * val).astype(BF).reshape(lay.team, rows, dcol)
-    add = lax.all_to_all(add, TEAM, 0, 1).reshape(rows, D)
-    layer_output = (middle + add.astype(F32)).astype(BF)
 
     d_value = (sigma * upc).astype(BF)
     d_pregate = (upc * val * sigma * (1.0 - sigma)).astype(BF)
-    d_val = lax.all_gather(d_value, TEAM, axis=1, tiled=True)
+    d_val = gather_columns(d_value, 4)
     g_cv = mm_tn(act, d_val)
     d_pre = (mm_nt(d_val, W_cv) * 2.0 * relu).astype(BF)
     g_ck = mm_tn(m_ck, d_pre)
@@ -331,18 +972,17 @@
     nxt, first = with_after((1.0 - s_ck) * d_mck + (1.0 - s_cr) * d_mcr, segs)
     dn2_part = (s_ck * d_mck + s_cr * d_mcr + nxt).astype(BF)
 
-    def to_rows(part, first):
-        mine = lax.psum_scatter(part, TEAM, scatter_dimension=0, tiled=True).astype(F32)
-        spread = jnp.zeros((segs, half, D), BF).at[:, :1].set(first.astype(BF))
-        edge = lax.psum_scatter(spread.reshape(-1, D), TEAM, scatter_dimension=0, tiled=True)
-        return mine.at[-1:].add(from_right(edge, nseq).astype(F32))
-
-    dn2 = to_rows(dn2_part, first)
+    def edge_rows(first):
+        return jnp.pad(first.astype(BF), ((0, 0), (0, 15), (0, 0)))
+
+    dn2 = sum_rows(H, dn2_part.reshape(8, rows, D), edge_rows(first), 5)
     g_g2 = jnp.sum(dn2 * hat2, axis=0)
     g_b2 = jnp.sum(dn2, axis=0)
     d_mid = up_in[0].astype(F32) + norm_back(dn2 * g2, hat2, rstd2)
 
-    d_br = lax.all_gather(d_mid.astype(BF), TEAM, axis=0, tiled=True)
+    d_br, moved = gather_rows(H, d_mid.astype(BF), 6, False, add)
+    layer_output = (middle + moved.transpose(1, 0, 2).reshape(rows, D).astype(F32)).astype(BF)
+    d_br = d_br.reshape(T, D)
     g_o = mm_tn(gated, d_br)
     d_gated = mm_nt(d_br, W_o)
     dn = d_gated * silu
@@ -364,21 +1004,25 @@
     g_shares = [jnp.sum(d * diff1, axis=0) for d in d_m]
     nxt, first = with_after(sum((1.0 - s) * d for s, d in zip(shares, d_m)), segs)
     dn1_part = (sum(s * d for s, d in zip(shares, d_m)) + nxt).astype(BF)
-    dn1 = to_rows(dn1_part, first)
+    dn1 = sum_rows(H, dn1_part.reshape(8, rows, D), edge_rows(first), 7)
     hat1, rstd1 = normed(x_own.astype(F32))
     g_g1 = jnp.sum(dn1 * hat1, axis=0)
     g_b1 = jnp.sum(dn1, axis=0)
     input_grad = d_mid + norm_back(dn1 * g1, hat1, rstd1)
 
-    g_r, g_k, g_v, g_w, g_ck, g_cr = column_grads(
-        lay, [(g_r, HEAD), (g_k, HEAD), (g_v, HEAD), (g_w, HEAD), (g_ck, 1), (g_cr, D)]
-    )
-    g_cv = lax.psum_scatter(g_cv.astype(BF), TEAMS, scatter_dimension=0, tiled=True).astype(F32)
-    if (D // lay.n) % HEAD:
+    g_cv = teams_sum(g_cv.astype(BF).reshape(lay.A * H, -1, D), lay).astype(F32)
+    if w_row % HEAD:
         g_o = jnp.zeros((D, D), BF).at[rank * dcol + jnp.arange(dcol)].set(g_o.astype(BF))
         g_o = lax.psum_scatter(g_o, ALL, scatter_dimension=0, tiled=True).astype(F32)
     else:
-        g_o = lax.psum_scatter(g_o.astype(BF), TEAMS, scatter_dimension=0, tiled=True).astype(F32)
+        g_o = teams_sum(g_o.astype(BF).reshape(lay.A * H, -1, D), lay).astype(F32)
+
+    def shares_out(pieces):
+        whole = jnp.concatenate([g.astype(BF) for g in pieces], axis=1)
+        return teams_sum(lay.rows_out(whole), lay)
+
+    g_ffn = swap_blocks(shares_out([g_ck, g_cr]), rank)
+    g_4 = shares_out([g_r, g_k, g_v, g_w])
 
     def in_place(v):
         spread = jnp.where(jnp.arange(lay.team)[:, None] == rank, v.reshape(1, -1), 0.0)
@@ -388,9 +1032,16 @@
         [g_g1, g_b1, *g_shares, in_place(d_l), in_place(d_u), in_place(g_gs), in_place(g_gb)]
         + [g_g2, g_b2, g_s_ck, g_s_cr]
     )
-    ns = small.shape[0]
-    small = small.reshape(ns, lay.n, D // lay.n).transpose(1, 0, 2).reshape(-1)
-    small = lax.psum_scatter(small, ALL, scatter_dimension=0, tiled=True).reshape(ns, -1)
+    small = small.reshape(nv, lay.n, w_row).transpose(1, 0, 2)
+    small = jnp.pad(small, ((0, 0), (0, 16 - nv), (0, 128 - w_row)))
+    small, g_4 = closing(H, small, g_4)
+    small = small[:nv, :w_row]
+
+    def columns(got, lo, hi, unit):
+        return lay.unspread(got[:, :, lo:hi].transpose(1, 0, 2), unit).astype(F32)
+
+    g_r, g_k, g_v, g_w = (columns(g_4, i * dcol, (i + 1) * dcol, HEAD) for i in range(4))
+    g_ck, g_cr = columns(g_ffn, 0, hid, 1), columns(g_ffn, hid, hid + dcol, D)
     return (
         layer_output[None],
         input_grad[None],

time: 1360 us -> 1070 us (0.79)
  waiting for transfers between devices: 615 us -> 154 us
  Pallas kernels: 0 us -> 343 us
  blocking collectives: 206 us -> 0 us
  other arithmetic: 119 us -> 168 us
  matrix products: 177 us -> 161 us
    pallas_call x0 -> x9, Pallas kernels: none -> 343 us  [the longest x3 112 us: sum_rows(): comm_call(body, jax.ShapeDtypeStruct((rows, D), F32), [VM] * len(args), V...]
    reduce_scatter x7 -> x0, waiting for transfers between devices: 254 us -> none  [the longest x1 83.5 us: column_grads(): lax.psum_scatter(lay.rows_out(sent), TEAMS, scatter_dimension=0, tiled=Fa...]
    all_gather x8 -> x0, waiting for transfers between devices: 200 us -> none  [the longest x2 86.5 us: column_weights(): full = lay.rows_in(lax.all_gather(got, TEAMS, axis=0))]
    ppermute x5 -> x25, waiting for transfers between devices: 0.01 us -> 131 us  [the longest x7 108 us: shifted(): return lax.ppermute(v, 'h', [(i, (i + dh) % H) for i in range(H)])]
    unnamed x19 -> x2, waiting for transfers between devices: 124 us -> 0.03 us
    all_to_all x3 -> x0, blocking collectives: 85.3 us -> none  [the longest x2 66.2 us: column_weights(): got = lax.all_to_all(sent, TEAM, split_axis=1, concat_axis=0, tiled=False)]
    all_gather x3 -> x0, blocking collectives: 66.5 us -> none  [the longest x1 41.9 us: per_device(): every = lax.all_gather(stacked, ALL, axis=0)]
    unnamed x2 -> x0, blocking collectives: 54.3 us -> none
  transfers between devices with their start and end apart: 27 -> 29, of which waited for: 15 -> 8; matrix products, arithmetic and copies ran while one was open for 27% -> 33% of each run, Pallas kernels for 0% -> 14%
where the time goes in v2:
time: 1070 us; the launch traced here: 1060 us
  Pallas kernels  343 us (32%)
  local copies, waits for them, and re-layouts  185 us (17%)
  other arithmetic  168 us (16%)
  matrix products  161 us (15%)
  waiting for transfers between devices  154 us (14%)
  starting transfers between devices  29.5 us (3%)
  between operations  17.1 us (2%)
    dot_general x24, matrix products, dot(): return lax.dot_general(a, b, (dims, ((), ())), preferred_element_type=F32)  127 us
    pallas_call x3, Pallas kernels, sum_rows(): comm_call(body, jax.ShapeDtypeStruct((rows, D), F32), [VM] * len(args), V...  112 us
    ppermute x7, waiting for transfers between devices, shifted(): return lax.ppermute(v, 'h', [(i, (i + dh) % H) for i in range(H)])  108 us
    pallas_call x1, Pallas kernels, opening(): comm_call(body, (jax.ShapeDtypeStruct((*grid, *vecs.shape), BF), jax.Shap...  89.3 us
    pallas_call x2, Pallas kernels, gather_rows(): comm_call(body, tuple(outs), [ANY] * len(args), [ANY] * len(outs), scratc...  53.3 us
    convert_element_type x16, local copies, waits for them, and re-layouts, columns(): return lay.unspread(got[:, :, lo:hi].transpose(1, 0, 2), unit).astype(F32)  40.2 us
    pallas_call x1, Pallas kernels, closing(): comm_call(body, (jax.ShapeDtypeStruct(small.shape[1:], F32), jax.ShapeDty...  39.5 us
    dot_general x12, matrix products, ein(): return jnp.einsum(spec, a, b, precision=EX, preferred_element_type=F32)  34.8 us
  transfers between devices with their start and end apart: 29, of which 8 were waited for; matrix products, arithmetic and copies ran while one was open for 33% of the time, Pallas kernels for 14%

profile of v2, /device:TPU:0, one launch (start us, length us, event | category | flops | bytes accessed | tf_op | source)
XLA Modules:
  0.0 1058.0 jit_solution(16653678245956878936)
XLA Ops:
  16.7 4.8 reshape.1202
  28.2 89.3 %shard_map.432 = (bf16[2,2,2,2,2,16,128]{6,5,4,3,2,1,0:T(8,128)(2,1)}, bf16[8,128,2048]{2,1,0:T(8,128)(2,1)}, bf16[2,16,2048]{2,1,0:T(8,128)(2,1)}, bf16[8,128,2...) custom-call(bf16[16,128]{1,0:T(8,128)(2,1)} %pad.17.vecs, ...), custom_call_target="tpu_custom_call" | custom-call | tf_op jit(solution)/shard_map/pallas_call | solution.py:432
  131.6 6.6 convert_element_type.566
  142.8 7.2 fusion.14
  151.7 7.7 add_convert_fusion.2
  159.4 9.3 fusion.10
  176.3 4.1 fusion.67
  187.7 4.6 convolution_convert_fusion.12
  192.3 3.1 reshape.1314
  200.5 9.9 add_convert_fusion.1
  211.0 4.8 fusion.128
  238.1 3.2 reshape.1311
  250.2 6.1 multiply_convert_fusion.4
  259.9 3.3 convolution_convert_fusion
  263.3 51.6 %shard_map.433 = f32[128,2048]{1,0:T(8,128)} custom-call(bf16[8,128,2048]{2,1,0:T(8,128)(2,1)} %bitcast.575), custom_call_target="tpu_custom_call" | custom-call | tf_op jit(solution)/shard_map/pallas_call | solution.py:553
  317.8 23.1 %shard_map.434 = (bf16[8,128,2048]{2,1,0:T(8,128)(2,1)}, bf16[2,16,2048]{2,1,0:T(8,128)(2,1)}) custom-call(bf16[128,2048]{1,0:T(8,128)(2,1)} %add_convert_fusion.4.refs_0_), custom_call_target="tpu_custom_call" | custom-call | tf_op jit(solution)/shard_map/pallas_call | solution.py:496
  340.8 3.2 slice_convert_fusion
  345.0 4.3 pad_maximum_fusion.1
  349.8 7.9 fusion.3
  359.9 23.2 %reduce-scatter.5.cloned.1.call-done = bf16[1,4,64,64]{3,2,1,0:T(8,128)(2,1)} async-done(((bf16[1,32,64,64]{3,2,1,0:T(8,128)(2,1)}), bf16[1,4,64,64]{3,2,1,0:T(8,128)(2,1)}) %reduce-scatter.5.cloned.1.call-update) | async-done | bytes 32784 | tf_op jit(solution)/shard_map/reduce_scatter | solution.py:945
  387.5 10.1 collective-permute-done.7
  401.5 3.4 copy-done.53
  404.8 4.5 fusion.20
  411.1 6.5 convolution_convert_fusion.1.part
  417.6 25.8 %shard_map.436 = f32[1024,256]{1,0:T(8,128)} custom-call(bf16[1024,2048]{1,0:T(8,128)(2,1)} %convolution_convert_fusion.1.part), custom_call_target="tpu_custom_call" | custom-call | tf_op jit(solution)/shard_map/pallas_call | solution.py:570
  443.4 5.1 multiply_convert_fusion.3
  448.5 23.0 %shard_map.435 = bf16[1024,2048]{1,0:T(8,128)(2,1)} custom-call(bf16[1024,256]{1,0:T(8,128)(2,1)} %get-tuple-element.120.x), custom_call_target="tpu_custom_call" | custom-call | tf_op jit(solution)/shard_map/pallas_call | solution.py:518
  471.6 8.3 convolution_convert_fusion.2
  479.9 4.5 multiply_convert_fusion.1
  484.5 5.5 convolution_convert_fusion.3
  490.0 7.0 fusion.18
  499.4 11.3 %multiply_reduce_fusion = (f32[2048]{0:T(1024)}, f32[2048]{0:T(1024)}, f32[1024,2048]{1,0:T(8,128)}, f32[1024,2048]{1,0:T(8,128)}) fusion(f32[2,512,2048]{2,1,0:T(8,128)S(1)} %bitcast.568, bf16[8,128,2048]{2,1,0:T(8,128)(2,1)} %get-tuple-element.50, f32[1024,2048]{1,0:T(8,128)} %fusion.18, f32[2048]{0:T(1024)S(1)} %copy-done.130, f32[2048]{0:T(1024)S(1)} %copy-done.129, ...), kind=kOutput, calls=%fused_computation.34 | convolution fusion | flops 1092612096 | bytes 39354368 | tf_op jit(solution)/shard_map/dot_general | solution.py:636
  510.7 4.4 slice.241
  517.9 9.3 fusion.1
  527.2 30.3 %shard_map.437 = f32[128,2048]{1,0:T(8,128)} custom-call(bf16[8,128,2048]{2,1,0:T(8,128)(2,1)} %bitcast.583, bf16[2,16,2048]{2,1,0:T(8,128)(2,1)} %fusion.144.refs_1_), custom_call_target="tpu_custom_call" | custom-call | tf_op jit(solution)/shard_map/pallas_call | solution.py:553
  562.8 30.2 %shard_map.438 = (bf16[8,128,2048]{2,1,0:T(8,128)(2,1)}, bf16[8,128,256]{2,1,0:T(8,128)(2,1)}) custom-call(bf16[128,2048]{1,0:T(8,128)(2,1)} %get-tuple-element.86.refs_0_, bf16[8,128,256]{2,1,0:T(8,128)(2,1)} %bitcast.636), custom_call_target="tpu_custom_call" | custom-call | tf_op jit(solution)/shard_map/pallas_call | solution.py:496
  593.0 4.6 convolution_convert_fusion.8
  597.7 4.6 fusion.160
  615.7 3.2 fusion.166
  626.4 6.7 copy.223
  643.2 3.0 fusion.57
  646.2 5.2 fusion.54
  654.7 3.2 mul.954.clone
  657.9 3.4 reshape.1313
  681.9 3.8 fusion.63
  687.3 6.0 fusion.118
  693.3 4.7 fusion.121
  698.1 5.1 fusion.115
  703.2 19.7 %multiply_reduce_fusion.2 = (f32[2048]{0:T(1024)S(1)}, f32[2048]{0:T(1024)S(1)}, f32[2048]{0:T(1024)S(1)}, f32[2048]{0:T(1024)S(1)}, f32[1024,2048]{1,0:T(8,128)}, /*index=5*/f32[1024,2048]{1,0:T(8,128)}) fusion(f32[2,512,2048]{2,1,0:T(8,128)} %copy-done.2, f32[2048]{0:T(1024)S(1)} %copy-done.87, f32[2048]{0:T(1024)S(1)} %copy-done.80, ...), kind=kOutput, calls=%fused_computation.36 | convolution fusion | flops 1117773824 | bytes 56188928 | tf_op jit(solution)/shard_map/dot_general | solution.py:636
  723.0 8.7 slice.247
  740.7 6.4 copy.217
  755.6 7.9 concatenate.30
  763.5 17.9 %fusion = bf16[1024,2048]{1,0:T(8,128)(2,1)} fusion(f32[2,512,2048]{2,1,0:T(8,128)} %concatenate.30, f32[1024,2048]{1,0:T(8,128)} %get-tuple-element.199, f32[1024,2048]{1,0:T(8,128)} %fusion.121, f32[1024,2048]{1,0:T(8,128)} %fusion.115, f32[1024,2048]{1,0:T(8,128)} %fusion.118, f32[2048]{0:T(1024)S(1)} %copy-done.106, f32[2048]{0:T(1024)S(1)} %copy-done.99, ...), kind=kLoop, calls=%fused_computation.7 | loop fusion | flops 18874368 | bytes 46170112 | tf_op jit(solution)/shard_map/convert_element_type | solution.py:1006
  781.5 30.4 %shard_map.439 = f32[128,2048]{1,0:T(8,128)} custom-call(bf16[8,128,2048]{2,1,0:T(8,128)(2,1)} %bitcast.582, bf16[2,16,2048]{2,1,0:T(8,128)(2,1)} %fusion.145.refs_1_), custom_call_target="tpu_custom_call" | custom-call | tf_op jit(solution)/shard_map/pallas_call | solution.py:553
  815.6 3.1 fusion.77
  834.6 68.6 %collective-permute-done.15 = bf16[64,2048]{1,0:T(8,128)(2,1)S(1)} collective-permute-done((bf16[64,2048]{1,0:T(8,128)(2,1)S(1)}, bf16[64,2048]{1,0:T(8,128)(2,1)S(1)}, u32[]{:S(2)}, u32[]{:S(2)}) %collective-permute-start.15) | collective-permute-done | bytes 262176 | tf_op jit(solution)/shard_map/ppermute | solution.py:806
  904.0 18.8 %collective-permute-done.26 = bf16[224,2048]{1,0:T(8,128)(2,1)S(1)} collective-permute-done((bf16[224,2048]{1,0:T(8,128)(2,1)S(1)}, bf16[224,2048]{1,0:T(8,128)(2,1)S(1)}, u32[]{:S(2)}, u32[]{:S(2)}) %collective-permute-start.26) | collective-permute-done | bytes 917536 | tf_op jit(solution)/shard_map/ppermute | solution.py:806
  924.4 20.9 %collective-permute-done.13 = bf16[8,64,1024]{2,1,0:T(8,128)(2,1)S(1)} collective-permute-done((bf16[8,64,1024]{2,1,0:T(8,128)(2,1)S(1)}, bf16[8,64,1024]{2,1,0:T(8,128)(2,1)S(1)}, u32[]{:S(2)}, u32[]{:S(2)}) %collective-permute-start.13) | collective-permute-done | bytes 1048608 | tf_op jit(solution)/shard_map/ppermute | solution.py:806
  946.7 39.5 %shard_map.440 = (f32[16,128]{1,0:T(8,128)}, bf16[8,64,1024]{2,1,0:T(8,128)(2,1)}) custom-call(f32[32,16,128]{2,1,0:T(8,128)} %pad.20.small, bf16[8,64,1024]{2,1,0:T(8,128)(2,1)} %fusion.23.cols), custom_call_target="tpu_custom_call" | custom-call | tf_op jit(solution)/shard_map/pallas_call | solution.py:622
  1005.2 3.0 reshape.1265
  1011.6 3.0 reshape.1266
  1026.0 7.9 collective-permute-done.22
  1036.4 4.7 reshape.1279
  1044.1 4.9 reshape.1271
  (675 shorter events, 255.0 us)
Async XLA Ops:
  7.2 116.6 %copy-start = (f32[1,32,64,64]{3,2,1,0:T(8,128)S(1)}, f32[1,32,64,64]{3,2,1,0:T(8,128)}, u32[]{:S(2)}) copy-start(f32[1,32,64,64]{3,2,1,0:T(8,128)} %param.29) | copy-start | bytes 1572868
  7.2 342.5 %reduce-scatter.3.cloned.1.call-start = ((), (), s32[]{:S(2)}) async-start(), calls=%async_computation.2 | async-start | bytes 1572864 | tf_op jit(solution)/shard_map/reduce_scatter | solution.py:944
  117.5 131.8 %collective-permute-start.2 = (bf16[64,2048]{1,0:T(8,128)(2,1)}, bf16[64,2048]{1,0:T(8,128)(2,1)}, u32[]{:S(2)}, u32[]{:S(2)}) collective-permute-start(bf16[64,2048]{1,0:T(8,128)(2,1)} %param.44), channel_id=1, source_target_pairs={{0,4},{4,0},{1,5},{5,1},{2,6},{6,2},{3,7},{7,3},{8,12},{12,8},{9,1... | collective-permute-start | bytes 786440 | tf_op jit(solution)/shard_map/ppermute | solution.py:806
  117.9 138.4 %collective-permute-start.3 = (bf16[64,2048]{1,0:T(8,128)(2,1)}, bf16[64,2048]{1,0:T(8,128)(2,1)}, u32[]{:S(2)}, u32[]{:S(2)}) collective-permute-start(bf16[64,2048]{1,0:T(8,128)(2,1)} %param.44), channel_id=1, source_target_pairs={{0,16},{16,0},{1,17},{17,1},{2,18},{18,2},{3,19},{19,3},{4,20},{20... | collective-permute-start | bytes 786440 | tf_op jit(solution)/shard_map/ppermute | solution.py:802
  118.4 239.4 %collective-permute-start.5 = (bf16[8,64,1152]{2,1,0:T(8,128)(2,1)}, bf16[8,64,1152]{2,1,0:T(8,128)(2,1)}, u32[]{:S(2)}, u32[]{:S(2)}) collective-permute-start(bf16[8,64,1152]{2,1,0:T(8,128)(2,1)} %get-tuple-element.51), channel_id=1, source_target_pairs={{0,4},{4,0},{1,5},{5,1},{2,6},{6,2},{3,7},{7,3},{8,12},{12,8},{9,1... | collective-permute-start | bytes 3538952 | tf_op jit(solution)/shard_map/ppermute | solution.py:806
  120.8 266.7 %collective-permute-start.6 = (bf16[8,64,1152]{2,1,0:T(8,128)(2,1)}, bf16[8,64,1152]{2,1,0:T(8,128)(2,1)}, u32[]{:S(2)}, u32[]{:S(2)}) collective-permute-start(bf16[8,64,1152]{2,1,0:T(8,128)(2,1)} %get-tuple-element.51), channel_id=1, source_target_pairs={{0,16},{16,0},{1,17},{17,1},{2,18},{18,2},{3,19},{19,3},{4,20},{20... | collective-permute-start | bytes 3538952 | tf_op jit(solution)/shard_map/ppermute | solution.py:802
  125.3 92.3 %collective-permute-start = (f32[4,64,64]{1,2,0:T(8,128)}, f32[4,64,64]{1,2,0:T(8,128)S(1)}, u32[]{:S(2)}, u32[]{:S(2)}) collective-permute-start(f32[4,64,64]{1,2,0:T(8,128)} %broadcast_select_fusion.12), channel_id=1, source_target_pairs={{0,8},{8,0},{1,9},{9,1},{2,10},{10,2},{3,11},{11,3},{4,12},{12,4},... | collective-permute-start | bytes 196616 | tf_op jit(solution)/shard_map/ppermute | solution.py:802
  130.3 29.1 %copy-start.118 = (f32[1024]{0:T(1024)}, f32[1024]{0:T(1024)S(1)}, u32[]{:S(2)}) copy-start(f32[1024]{0:T(1024)S(1)} %get-tuple-element.180) | copy-start | bytes 12292
  141.5 58.9 %copy-start.86 = (f32[2048]{0:T(1024)}, f32[2048]{0:T(1024)S(1)}, u32[]{:S(2)}) copy-start(f32[2048]{0:T(1024)S(1)} %add.465) | copy-start | bytes 24580
  141.6 58.9 %copy-start.79 = (f32[2048]{0:T(1024)}, f32[2048]{0:T(1024)S(1)}, u32[]{:S(2)}) copy-start(f32[2048]{0:T(1024)S(1)} %mul.841) | copy-start | bytes 24580
  141.7 58.7 %copy-start.96 = (f32[2048]{0:T(1024)}, f32[2048]{0:T(1024)S(1)}, u32[]{:S(2)}) copy-start(f32[2048]{0:T(1024)S(1)} %mul.849) | copy-start | bytes 24580
  141.8 58.6 %copy-start.98 = (f32[2048]{0:T(1024)}, f32[2048]{0:T(1024)S(1)}, u32[]{:S(2)}) copy-start(f32[2048]{0:T(1024)S(1)} %mul.866) | copy-start | bytes 24580
  176.3 39.5 %copy-start.5 = (f32[2,4,128,4,64]{2,4,3,1,0:T(8,128)}, f32[2,4,128,4,64]{2,4,3,1,0:T(8,128)S(1)}, u32[]{:S(2)}) copy-start(f32[2,4,128,4,64]{2,4,3,1,0:T(8,128)S(1)} %copy.169) | copy-start | bytes 3145732
  186.3 31.3 %copy-start.103 = (f32[4,64]{1,0:T(4,128)}, f32[4,64]{1,0:T(4,128)S(1)}, u32[]{:S(2)}) copy-start(f32[4,64]{1,0:T(4,128)S(1)} %get-tuple-element.186) | copy-start | bytes 3076
  187.7 23.3 %copy-start.64 = (f32[128,4,64]{0,2,1:T(8,128)}, f32[128,4,64]{0,2,1:T(8,128)S(1)}, u32[]{:S(2)}) copy-start(f32[128,4,64]{0,2,1:T(8,128)S(1)} %multiply_exponential_fusion.1) | copy-start | bytes 393220
  210.9 21.4 %copy-start.92 = (f32[2,4,128,4]{2,3,1,0:T(4,128)}, f32[2,4,128,4]{2,3,1,0:T(4,128)S(1)}, u32[]{:S(2)}) copy-start(f32[2,4,128,4]{2,3,1,0:T(4,128)S(1)} %get-tuple-element.141) | copy-start | bytes 49156
  217.9 9.9 collective-permute-start.1
  227.9 121.4 %collective-permute-start.8 = (bf16[224,2048]{1,0:T(8,128)(2,1)}, bf16[224,2048]{1,0:T(8,128)(2,1)}, u32[]{:S(2)}, u32[]{:S(2)}) collective-permute-start(bf16[224,2048]{1,0:T(8,128)(2,1)} %param.50), channel_id=1, source_target_pairs={{0,4},{4,0},{1,5},{5,1},{2,6},{6,2},{3,7},{7,3},{8,12},{12,8},{9,1... | collective-permute-start | bytes 2752520 | tf_op jit(solution)/shard_map/ppermute | solution.py:806
  249.2 133.9 %reduce-scatter.5.cloned.1.call-start = ((), (), s32[]{:S(2)}) async-start(), calls=%async_computation.3 | async-start | bytes 589824 | tf_op jit(solution)/shard_map/reduce_scatter | solution.py:945
  249.3 8.3 collective-permute-start.4
  256.3 128.3 %collective-permute-start.9 = (bf16[224,2048]{1,0:T(8,128)(2,1)}, bf16[224,2048]{1,0:T(8,128)(2,1)}, u32[]{:S(2)}, u32[]{:S(2)}) collective-permute-start(bf16[224,2048]{1,0:T(8,128)(2,1)} %param.50), channel_id=1, source_target_pairs={{0,16},{16,0},{1,17},{17,1},{2,18},{18,2},{3,19},{19,3},{4,20},{20... | collective-permute-start | bytes 2752520 | tf_op jit(solution)/shard_map/ppermute | solution.py:802
  263.3 51.6 %copy-start.20 = (bf16[1,128,2048]{2,1,0:T(8,128)(2,1)S(1)}, bf16[1,128,2048]{2,1,0:T(8,128)(2,1)}, u32[]{:S(2)}) copy-start(bf16[1,128,2048]{2,1,0:T(8,128)(2,1)} %param.27) | copy-start | bytes 1572868
  263.3 51.6 %copy-start.146 = (f32[128]{0:T(128)S(1)}, f32[128]{0:T(128)}, u32[]{:S(2)}) copy-start(f32[128]{0:T(128)} %broadcast_multiply_fusion.9) | copy-start | bytes 1540
  263.3 53.4 %copy-start.100 = (f32[2048]{0:T(1024)S(1)}, f32[2048]{0:T(1024)}, u32[]{:S(2)}) copy-start(f32[2048]{0:T(1024)} %mul.914) | copy-start | bytes 24580
  263.3 53.4 %copy-start.124 = (f32[2048]{0:T(1024)S(1)}, f32[2048]{0:T(1024)}, u32[]{:S(2)}) copy-start(f32[2048]{0:T(1024)} %add.502) | copy-start | bytes 24580
  349.3 35.3 %collective-permute-start.10 = (bf16[224,2048]{1,0:T(8,128)(2,1)}, bf16[224,2048]{1,0:T(8,128)(2,1)}, u32[]{:S(2)}, u32[]{:S(2)}) collective-permute-start(bf16[224,2048]{1,0:T(8,128)(2,1)} %collective-permute-done.8), channel_id=1, source_target_pairs={{0,16},{16,0},{1,17},{17,1},{2,18},{18,2},{3,19},{19,3},{4,20},{20... | collective-permute-start | bytes 2752520 | tf_op jit(solution)/shard_map/ppermute | solution.py:802
  357.8 39.8 %collective-permute-start.7 = (bf16[8,64,1152]{2,1,0:T(8,128)(2,1)}, bf16[8,64,1152]{2,1,0:T(8,128)(2,1)}, u32[]{:S(2)}, u32[]{:S(2)}) collective-permute-start(bf16[8,64,1152]{2,1,0:T(8,128)(2,1)} %collective-permute-done.5), channel_id=1, source_target_pairs={{0,16},{16,0},{1,17},{17,1},{2,18},{18,2},{3,19},{19,3},{4,20},{20... | collective-permute-start | bytes 3538952 | tf_op jit(solution)/shard_map/ppermute | solution.py:802
  387.4 21.9 %copy-start.58 = (bf16[4,224,2048]{2,1,0:T(8,128)(2,1)}, bf16[4,224,2048]{2,1,0:T(8,128)(2,1)S(1)}, u32[]{:S(2)}) copy-start(bf16[4,224,2048]{2,1,0:T(8,128)(2,1)S(1)} %pad_maximum_fusion.5) | copy-start | bytes 11010052
  401.4 42.0 %copy-start.26 = (bf16[2,2,2,2,2,64,1152]{6,5,4,3,1,2,0:T(8,128)(2,1)}, bf16[2,2,2,2,2,64,1152]{6,5,4,3,1,2,0:T(8,128)(2,1)S(1)}, u32[]{:S(2)}) copy-start(bf16[2,2,2,2,2,64,1152]{6,5,4,3,1,2,0:T(8,128)(2,1)S(1)} %copy.191) | copy-start | bytes 14155780
  448.5 23.0 %copy-start.171 = (f32[1024,896]{1,0:T(8,128)S(1)}, f32[1024,896]{1,0:T(8,128)}, u32[]{:S(2)}) copy-start(f32[1024,896]{1,0:T(8,128)} %copy-done.170) | copy-start | bytes 11010052
  527.2 32.7 %copy-start.70 = (bf16[1,128,2048]{2,1,0:T(8,128)(2,1)S(1)}, bf16[1,128,2048]{2,1,0:T(8,128)(2,1)}, u32[]{:S(2)}) copy-start(bf16[1,128,2048]{2,1,0:T(8,128)(2,1)} %param.28) | copy-start | bytes 1572868
  557.5 35.5 %copy-start.73 = (bf16[1024,256]{1,0:T(8,128)(2,1)S(1)}, bf16[1024,256]{1,0:T(8,128)(2,1)}, u32[]{:S(2)}) copy-start(bf16[1024,256]{1,0:T(8,128)(2,1)} %copy-done.72) | copy-start | bytes 1572868
  562.8 34.9 %copy-start.56 = (bf16[4,64,2048]{2,1,0:T(8,128)(2,1)S(1)}, bf16[4,64,2048]{2,1,0:T(8,128)(2,1)}, u32[]{:S(2)}) copy-start(bf16[4,64,2048]{2,1,0:T(8,128)(2,1)} %copy-done.55) | copy-start | bytes 3145732
  562.8 34.9 %copy-start.148 = (f32[1,256]{1,0:T(1,128)S(1)}, f32[1,256]{1,0:T(1,128)}, u32[]{:S(2)}) copy-start(f32[1,256]{1,0:T(1,128)} %get-tuple-element.203) | copy-start | bytes 3076
  562.8 34.9 %copy-start.154 = (f32[1,256]{1,0:T(1,128)S(1)}, f32[1,256]{1,0:T(1,128)}, u32[]{:S(2)}) copy-start(f32[1,256]{1,0:T(1,128)} %get-tuple-element.202) | copy-start | bytes 3076
  612.9 40.7 %copy-start.94 = (f32[2,4,128,4]{2,3,1,0:T(4,128)}, f32[2,4,128,4]{2,3,1,0:T(4,128)S(1)}, u32[]{:S(2)}) copy-start(f32[2,4,128,4]{2,3,1,0:T(4,128)S(1)} %get-tuple-element.82) | copy-start | bytes 49156
  623.1 198.0 %collective-permute-start.25 = (bf16[2,224,2048]{2,1,0:T(8,128)(2,1)}, bf16[2,224,2048]{2,1,0:T(8,128)(2,1)}, u32[]{:S(2)}, u32[]{:S(2)}) collective-permute-start(bf16[2,224,2048]{2,1,0:T(8,128)(2,1)} %dynamic-slice_bitcast_fusion.2), channel_id=1, source_target_pairs={{0,16},{16,0},{1,17},{17,1},{2,18},{18,2},{3,19},{19,3},{4,20},{20... | collective-permute-start | bytes 5505032 | tf_op jit(solution)/shard_map/ppermute | solution.py:802
  637.6 191.8 %collective-permute-start.16 = (bf16[2,8,64,1152]{3,2,1,0:T(8,128)(2,1)}, bf16[2,8,64,1152]{3,2,1,0:T(8,128)(2,1)}, u32[]{:S(2)}, u32[]{:S(2)}) collective-permute-start(bf16[2,8,64,1152]{3,2,1,0:T(8,128)(2,1)} %dynamic-slice_bitcast_fusion), channel_id=1, source_target_pairs={{0,16},{16,0},{1,17},{17,1},{2,18},{18,2},{3,19},{19,3},{4,20},{20... | collective-permute-start | bytes 7077896 | tf_op jit(solution)/shard_map/ppermute | solution.py:802
  639.8 178.9 %collective-permute-start.14 = (bf16[2,64,2048]{2,1,0:T(8,128)(2,1)}, bf16[2,64,2048]{2,1,0:T(8,128)(2,1)}, u32[]{:S(2)}, u32[]{:S(2)}) collective-permute-start(bf16[2,64,2048]{2,1,0:T(8,128)(2,1)} %dynamic-slice_bitcast_fusion.6), channel_id=1, source_target_pairs={{0,16},{16,0},{1,17},{17,1},{2,18},{18,2},{3,19},{19,3},{4,20},{20... | collective-permute-start | bytes 1572872 | tf_op jit(solution)/shard_map/ppermute | solution.py:802
  641.3 31.5 %collective-permute-start.11 = (f32[2,4,64,64]{2,3,1,0:T(8,128)}, f32[2,4,64,64]{2,3,1,0:T(8,128)}, u32[]{:S(2)}, u32[]{:S(2)}) collective-permute-start(f32[2,4,64,64]{2,3,1,0:T(8,128)} %fusion.139), channel_id=1, source_target_pairs={{4,0},{5,1},{6,2},{7,3},{12,8},{13,9},{14,10},{15,11},{20,16},{21,... | collective-permute-start | bytes 393224 | tf_op jit(solution)/shard_map/ppermute | solution.py:796
  753.2 72.1 %collective-permute-start.12 = (bf16[2,8,64,1024]{3,2,1,0:T(8,128)(2,1)}, bf16[2,8,64,1024]{3,2,1,0:T(8,128)(2,1)}, u32[]{:S(2)}, u32[]{:S(2)}) collective-permute-start(bf16[2,8,64,1024]{3,2,1,0:T(8,128)(2,1)} %dynamic-slice_bitcast_fusion.1), channel_id=1, source_target_pairs={{0,16},{16,0},{1,17},{17,1},{2,18},{18,2},{3,19},{19,3},{4,20},{20... | collective-permute-start | bytes 6291464 | tf_op jit(solution)/shard_map/ppermute | solution.py:802
  781.4 30.5 %copy-start.21 = (bf16[1,128,2048]{2,1,0:T(8,128)(2,1)S(1)}, bf16[1,128,2048]{2,1,0:T(8,128)(2,1)}, u32[]{:S(2)}) copy-start(bf16[1,128,2048]{2,1,0:T(8,128)(2,1)} %param.27) | copy-start | bytes 1572868
  781.4 30.5 %copy-start.147 = (f32[128]{0:T(128)S(1)}, f32[128]{0:T(128)}, u32[]{:S(2)}) copy-start(f32[128]{0:T(128)} %broadcast_multiply_fusion.9) | copy-start | bytes 1540
  781.4 30.5 %copy-start.151 = (f32[128]{0:T(128)S(1)}, f32[128]{0:T(128)}, u32[]{:S(2)}) copy-start(f32[128]{0:T(128)} %add_rsqrt_fusion.2) | copy-start | bytes 1540
  781.4 32.4 %copy-start.137 = (f32[2,2,64]{2,1,0:T(2,128)S(1)}, f32[2,2,64]{2,1,0:T(2,128)}, u32[]{:S(2)}) copy-start(f32[2,2,64]{2,1,0:T(2,128)} %broadcast_in_dim.176) | copy-start | bytes 3076
  781.5 32.4 %copy-start.138 = (f32[2,2,64]{2,1,0:T(2,128)S(1)}, f32[2,2,64]{2,1,0:T(2,128)}, u32[]{:S(2)}) copy-start(f32[2,2,64]{2,1,0:T(2,128)} %broadcast_in_dim.179) | copy-start | bytes 3076
  781.5 32.4 %copy-start.139 = (f32[2,2,64]{2,1,0:T(2,128)S(1)}, f32[2,2,64]{2,1,0:T(2,128)}, u32[]{:S(2)}) copy-start(f32[2,2,64]{2,1,0:T(2,128)} %broadcast_in_dim.182) | copy-start | bytes 3076
  781.5 32.4 %copy-start.152 = (pred[32]{0:T(512)(128)(4,1)S(1)}, pred[32]{0:T(512)(128)(4,1)}, u32[]{:S(2)}) copy-start(pred[32]{0:T(512)(128)(4,1)} %broadcast_in_dim.170) | copy-start | bytes 100
  781.5 33.0 %copy-start.114 = (f32[1,32,64]{2,0,1:T(1,128)S(1)}, f32[1,32,64]{2,0,1:T(1,128)}, u32[]{:S(2)}) copy-start(f32[1,32,64]{2,0,1:T(1,128)} %stack.253) | copy-start | bytes 24580
  781.5 33.0 %copy-start.115 = (f32[1,32,64]{2,0,1:T(1,128)S(1)}, f32[1,32,64]{2,0,1:T(1,128)}, u32[]{:S(2)}) copy-start(f32[1,32,64]{2,0,1:T(1,128)} %stack.254) | copy-start | bytes 24580
  781.5 33.0 %copy-start.116 = (f32[1,32,64]{2,0,1:T(1,128)S(1)}, f32[1,32,64]{2,0,1:T(1,128)}, u32[]{:S(2)}) copy-start(f32[1,32,64]{2,0,1:T(1,128)} %stack.255) | copy-start | bytes 24580
  781.5 33.0 %copy-start.117 = (f32[1,32,64]{2,0,1:T(1,128)S(1)}, f32[1,32,64]{2,0,1:T(1,128)}, u32[]{:S(2)}) copy-start(f32[1,32,64]{2,0,1:T(1,128)} %stack.256) | copy-start | bytes 24580
  781.5 34.1 %copy-start.38 = (f32[128,2048]{1,0:T(8,128)S(1)}, f32[128,2048]{1,0:T(8,128)}, u32[]{:S(2)}) copy-start(f32[128,2048]{1,0:T(8,128)} %get-tuple-element.87) | copy-start | bytes 3145732
  820.0 83.2 %collective-permute-start.15 = (bf16[64,2048]{1,0:T(8,128)(2,1)S(1)}, bf16[64,2048]{1,0:T(8,128)(2,1)S(1)}, u32[]{:S(2)}, u32[]{:S(2)}) collective-permute-start(bf16[64,2048]{1,0:T(8,128)(2,1)S(1)} %dynamic-slice_bitcast_fusion.7), channel_id=1, source_target_pairs={{0,4},{4,0},{1,5},{5,1},{2,6},{6,2},{3,7},{7,3},{8,12},{12,8},{9,1... | collective-permute-start | bytes 786440 | tf_op jit(solution)/shard_map/ppermute | solution.py:806
  823.5 99.3 %collective-permute-start.26 = (bf16[224,2048]{1,0:T(8,128)(2,1)S(1)}, bf16[224,2048]{1,0:T(8,128)(2,1)S(1)}, u32[]{:S(2)}, u32[]{:S(2)}) collective-permute-start(bf16[224,2048]{1,0:T(8,128)(2,1)S(1)} %dynamic-slice_bitcast_fusion.5), channel_id=1, source_target_pairs={{0,4},{4,0},{1,5},{5,1},{2,6},{6,2},{3,7},{7,3},{8,12},{12,8},{9,1... | collective-permute-start | bytes 2752520 | tf_op jit(solution)/shard_map/ppermute | solution.py:806
  828.0 117.3 %collective-permute-start.13 = (bf16[8,64,1024]{2,1,0:T(8,128)(2,1)S(1)}, bf16[8,64,1024]{2,1,0:T(8,128)(2,1)S(1)}, u32[]{:S(2)}, u32[]{:S(2)}) collective-permute-start(bf16[8,64,1024]{2,1,0:T(8,128)(2,1)S(1)} %dynamic-slice_bitcast_fusion.4), channel_id=1, source_target_pairs={{0,4},{4,0},{1,5},{5,1},{2,6},{6,2},{3,7},{7,3},{8,12},{12,8},{9,1... | collective-permute-start | bytes 3145736 | tf_op jit(solution)/shard_map/ppermute | solution.py:806
  832.9 181.7 %collective-permute-start.17 = (bf16[8,64,1152]{2,1,0:T(8,128)(2,1)}, bf16[8,64,1152]{2,1,0:T(8,128)(2,1)}, u32[]{:S(2)}, u32[]{:S(2)}) collective-permute-start(bf16[8,64,1152]{2,1,0:T(8,128)(2,1)} %dynamic-slice_bitcast_fusion.3), channel_id=1, source_target_pairs={{0,4},{4,0},{1,5},{5,1},{2,6},{6,2},{3,7},{7,3},{8,12},{12,8},{9,1... | collective-permute-start | bytes 3538952 | tf_op jit(solution)/shard_map/ppermute | solution.py:806
  1016.3 4.3 collective-permute-start.18
  1017.0 6.7 collective-permute-start.19
  1017.1 8.9 collective-permute-start.20
  1018.9 7.1 collective-permute-start.21
  1020.3 13.5 %collective-permute-start.22 = (bf16[64,1152]{1,0:T(8,128)(2,1)S(1)}, bf16[64,1152]{1,0:T(8,128)(2,1)S(1)}, u32[]{:S(2)}, u32[]{:S(2)}) collective-permute-start(bf16[64,1152]{1,0:T(8,128)(2,1)S(1)} %get-tuple-element.123), channel_id=1, source_target_pairs={{0,9},{1,8},{2,11},{3,10},{8,1},{9,0},{10,3},{11,2},{4,13},{5,12},... | collective-permute-start | bytes 442376 | tf_op jit(solution)/shard_map/ppermute | solution.py:848
  1020.6 13.3 %collective-permute-start.23 = (bf16[64,1152]{1,0:T(8,128)(2,1)S(1)}, bf16[64,1152]{1,0:T(8,128)(2,1)S(1)}, u32[]{:S(2)}, u32[]{:S(2)}) collective-permute-start(bf16[64,1152]{1,0:T(8,128)(2,1)S(1)} %get-tuple-element.122), channel_id=1, source_target_pairs={{0,10},{1,11},{2,8},{3,9},{8,2},{9,3},{10,0},{11,1},{4,14},{5,15},... | collective-permute-start | bytes 442376 | tf_op jit(solution)/shard_map/ppermute | solution.py:848
  1023.7 10.2 collective-permute-start.24
  (147 other events, 1012.1 us)
Sparse Core Ops, SparseCore 0:
  249.3 43.2 reduce-scatter.2
  349.9 33.1 reduce-scatter.4

commit v3 on v2

v3 whole, which is shorter than its diff:
```python
import jax
import jax.numpy as jnp
from jax import lax
from jax.experimental import pallas as pl
from jax.experimental.pallas import tpu as pltpu
from jax.sharding import Mesh, PartitionSpec as P

TEAM = ("b", "l", "c")
TEAMS = ("a", "h")
SEQ = ("h", "l", "c")
ALL = ("a", "b", "h", "l", "c")
HEAD = 64
CHUNK = 128
EPS = 1e-05
GROUP_EPS = 0.00064
BF = jnp.bfloat16
F32 = jnp.float32


MESH = pl.DeviceIdType.MESH
DMA = pltpu.SemaphoreType.DMA
VMEM_BYTES = 60 << 20


def coords():
    return {name: lax.axis_index(name) for name in ALL}


def rank_of(b, l, c):
    return (b * 2 + l) * 2 + c


def remote(src, dst, sent, landed, to):
    return pltpu.make_async_remote_copy(
        src_ref=src,
        dst_ref=dst,
        send_sem=sent,
        recv_sem=landed,
        device_id=to,
        device_id_type=MESH,
    )


def mates(me):
    for m in range(1, 8):
        yield m, {"b": me["b"] ^ (m >> 2), "l": me["l"] ^ ((m >> 1) & 1), "c": me["c"] ^ (m & 1)}


def greet(me, H, column, across):
    sem = pltpu.get_barrier_semaphore()
    count = 0
    for dh in range(H if column else 1):
        h = lax.rem(me["h"] + dh, H)
        for m in range(8):
            if dh == 0 and m == 0:
                continue
            to = {
                "b": me["b"] ^ (m >> 2),
                "h": h if column else me["h"],
                "l": me["l"] ^ ((m >> 1) & 1),
                "c": me["c"] ^ (m & 1),
            }
            pl.semaphore_signal(sem, inc=1, device_id=to, device_id_type=MESH)
            count += 1
    if across:
        pl.semaphore_signal(sem, inc=1, device_id={"a": 1 - me["a"]}, device_id_type=MESH)
        count += 1
    pl.semaphore_wait(sem, count)


class Copies:
    def __init__(self, sems):
        self.sems, self.k, self.open = sems, 0, []

    def go(self, src, dst, landed, to):
        copy = remote(src, dst, self.sems.at[self.k], landed, to)
        self.k += 1
        copy.start()
        self.open.append(copy)

    def drain(self):
        for copy in self.open:
            copy.wait_send()


def landed(ref, sem):
    remote(ref, ref, sem, sem, {"c": 1 - lax.axis_index("c")}).wait_recv()


def upper(ref, half):
    n = ref.shape[0] // 2
    return ref.at[pl.ds(half * n, n)]


class TeamGather:
    def __init__(self, me, own, view, send, recv, via=("xz", "zx")):
        self.me, self.own, self.view, self.recv, self.via = me, own, view, recv, via
        self.copies = Copies(send)
        self.tx, self.tz, self.ts = {"b": 1 - me["b"]}, {"l": 1 - me["l"]}, {"c": 1 - me["c"]}

    def put(self, src, p, half, to):
        self.copies.go(src, upper(self.view(p), half), self.recv.at[p, half], to)

    def start(self):
        mine = rank_of(self.me["b"], self.me["l"], self.me["c"])
        order = [(half, self.tx if self.via[half] == "xz" else self.tz) for half in range(2)]
        order += [(half, self.tz if self.via[half] == "xz" else self.tx) for half in range(2)]
        order += [(0, self.ts), (1, self.ts)]
        for half, to in order:
            self.put(upper(self.own, half), mine, half, to)

    def finish(self):
        b, l, c = self.me["b"], self.me["l"], self.me["c"]
        px, pz, pd = rank_of(1 - b, l, c), rank_of(b, 1 - l, c), rank_of(1 - b, 1 - l, c)
        order = [
            (px, half, self.tz) if self.via[half] == "xz" else (pz, half, self.tx)
            for half in range(2)
        ]
        order += [
            (pz, half, None) if self.via[half] == "xz" else (px, half, None) for half in range(2)
        ]
        for p, half, on in order + [(pd, 0, None), (pd, 1, None)]:
            block = upper(self.view(p), half)
            landed(block, self.recv.at[p, half])
            if on is not None:
                self.put(block, p, half, on)
            self.put(block, p, half, self.ts)
        for q in range(4):
            p = q * 2 + 1 - c
            for half in range(2):
                landed(upper(self.view(p), half), self.recv.at[p, half])
        self.copies.drain()


class TeamSum:
    def __init__(self, me, part, near, acc, mid, far, send, recv, via=("xz", "zx")):
        self.me, self.part, self.near, self.acc, self.mid, self.far = me, part, near, acc, mid, far
        self.recv, self.via = recv, via
        self.copies = Copies(send)

    def start(self):
        b, l, c = self.me["b"], self.me["l"], self.me["c"]
        self.spots = [(b, l), (1 - b, l), (b, 1 - l), (1 - b, 1 - l)]
        for i in (3, 1, 2, 0):
            bb, ll = self.spots[i]
            self.copies.go(
                self.part(rank_of(bb, ll, 1 - c)), self.near.at[i], self.recv.at[i], {"c": 1 - c}
            )

    def tiles(self, rows, body):
        step = max(16, 65536 // self.near.shape[2])

        @pl.loop(0, rows // step)
        def _(t):
            body(pl.ds(pl.multiple_of(t * step, step), step))

    def pair(self, i, write):
        bb, ll = self.spots[i]
        landed(self.near.at[i], self.recv.at[i])
        mine = self.part(rank_of(bb, ll, self.me["c"]))
        self.tiles(
            self.near.shape[1], lambda at: write(at, mine[at].astype(F32) + self.near[i, at].astype(F32))
        )

    def finish(self, write):
        b, l = self.me["b"], self.me["l"]
        tx, tz = {"b": 1 - b}, {"l": 1 - l}
        acc, mid, far, recv, go = self.acc, self.mid, self.far, self.recv, self.copies.go
        n = mid.shape[1]
        hops = [
            (tx, 0, tz, 1) if self.via[half] == "xz" else (tz, 1, tx, 0) for half in range(2)
        ]
        for i in (3, 1, 2):

            def put(at, v):
                acc[i - 1, at] = v.astype(BF)

            self.pair(i, put)
            for half, (one, direct, _, _) in enumerate(hops):
                if i == 3:
                    go(upper(acc.at[2], half), mid.at[half], recv.at[4 + half], one)
                elif i - 1 == direct:
                    go(
                        upper(acc.at[direct], half),
                        upper(far.at[direct], half),
                        recv.at[6 + half],
                        one,
                    )
        for half, (_, _, two, other) in enumerate(hops):
            landed(mid.at[half], recv.at[4 + half])
            into, came = upper(acc.at[other], half), mid.at[half]

            def add(at):
                into[at] = (into[at].astype(F32) + came[at].astype(F32)).astype(BF)

            self.tiles(n, add)
            go(into, upper(far.at[other], half), recv.at[8 + half], two)
        for half, (_, direct, _, other) in enumerate(hops):
            landed(upper(far.at[direct], half), recv.at[6 + half])
            landed(upper(far.at[other], half), recv.at[8 + half])

        def last(at, v):
            write(at, v + far[0, at].astype(F32) + far[1, at].astype(F32))

        self.pair(0, last)
        self.copies.drain()

    @staticmethod
    def scratch(R, C):
        return [
            pltpu.VMEM((4, R, C), BF),
            pltpu.VMEM((3, R, C), BF),
            pltpu.VMEM((2, R // 2, C), BF),
            pltpu.VMEM((2, R, C), BF),
            DMA((10,)),
            DMA((10,)),
        ]


class TeamsGather:
    def __init__(self, me, H, source, out, send, near, far, team=None):
        self.me, self.H, self.source, self.out = me, H, source, out
        self.near, self.far, self.team = near, far, team
        self.copies = Copies(send)

    @staticmethod
    def sems(H):
        return [DMA((9 + 4 * (H - 1),)), DMA((8,)), DMA((2 * H, 2))]

    def groups(self):
        b = self.me["b"]
        return ((0, b), (1, 1 - b))

    def start(self):
        me = self.me
        a, b, h, l, c = (me[n] for n in ALL)
        for m, to in mates(me):
            p = rank_of(to["b"], to["l"], to["c"])
            mine = rank_of(b, l, c)
            self.copies.go(self.source(p), self.out.at[a, b, h, l * 2 + c], self.near.at[mine], to)

    def spread(self, local=None):
        me = self.me
        a, b, h, l, c = (me[n] for n in ALL)
        if local is not None:
            local.wait()
        for g, bb in self.groups():
            block = self.out.at[a, bb, h]
            src = block
            if self.team is not None:
                src = self.team.at[pl.ds(bb * 4, 4)]
            else:
                for m in range(1 - g, 4):
                    ll, cc = l ^ (m >> 1), c ^ (m & 1)
                    landed(self.out.at[a, bb, h, ll * 2 + cc], self.near.at[rank_of(bb, ll, cc)])
            for dh in range(1, self.H):
                to = lax.rem(h + dh, self.H)
                self.copies.go(src, block, self.far.at[dh, g], {"h": to})
            self.copies.go(src, block, self.far.at[0, g], {"a": 1 - a})

    def forward(self, only=(0, 1)):
        a, h, H = self.me["a"], self.me["h"], self.H
        for g, bb in self.groups():
            if g not in only:
                continue
            for dh in range(1, H):
                block = self.out.at[a, bb, lax.rem(h - dh + H, H)]
                landed(block, self.far.at[dh, g])
                self.copies.go(block, block, self.far.at[H - 1 + dh, g], {"a": 1 - a})

    def finish(self):
        a, h, H = self.me["a"], self.me["h"], self.H
        for g, bb in self.groups():
            landed(self.out.at[1 - a, bb, h], self.far.at[0, g])
            for dh in range(1, H):
                block = self.out.at[1 - a, bb, lax.rem(h - dh + H, H)]
                landed(block, self.far.at[H - 1 + dh, g])
        self.copies.drain()


class Halo:
    def __init__(self, me, H, own, out, send, recv):
        self.me, self.H, self.own, self.out, self.send, self.recv = me, H, own, out, send, recv
        self.last = (me["l"] == 1) & (me["c"] == 1) & (me["h"] < H - 1)

    def each(self):
        me = self.me
        n = self.own.shape[0]
        for p in range(8):
            to = {
                "b": p >> 2,
                "h": jnp.minimum(me["h"] + 1, self.H - 1),
                "l": (p >> 1) & 1,
                "c": p & 1,
            }
            src = self.own.at[pl.ds(n - 16, 16)]
            yield remote(src, self.out.at[me["b"]], self.send.at[p], self.recv.at[me["b"]], to)

    def start(self):
        if self.H == 1:
            return

        @pl.when(self.last)
        def _():
            for copy in self.each():
                copy.start()

    def finish(self):
        if self.H == 1:
            return

        @pl.when(self.me["h"] > 0)
        def _():
            for b in range(2):
                landed(self.out.at[b], self.recv.at[b])

        @pl.when(self.last)
        def _():
            for copy in self.each():
                copy.wait_send()


class Edge:
    def __init__(self, me, H, first, got, send, recv):
        self.me, self.H, self.first, self.got, self.send, self.recv = me, H, first, got, send, recv

    def each(self):
        me = self.me
        mine = rank_of(me["b"], me["l"], me["c"])
        for b in range(2):
            to = {"b": b, "h": jnp.maximum(me["h"] - 1, 0), "l": 1, "c": 1}
            yield remote(self.first.at[b], self.got.at[mine], self.send.at[b], self.recv.at[mine], to)

    def start(self):
        if self.H == 1:
            return

        @pl.when(self.me["h"] > 0)
        def _():
            for copy in self.each():
                copy.start()

    def finish(self, out):
        if self.H == 1:
            return
        me = self.me

        @pl.when((me["l"] == 1) & (me["c"] == 1) & (me["h"] < self.H - 1))
        def _():
            for p in range(8):
                landed(self.got.at[p], self.recv.at[p])
            total = self.got[0, 0:1].astype(F32)
            for p in range(1, 8):
                total = total + self.got[p, 0:1].astype(F32)
            n = out.shape[0]
            out[n - 1 : n] = out[n - 1 : n] + total

        @pl.when(me["h"] > 0)
        def _():
            for copy in self.each():
                copy.wait_send()


class Exchange:
    def __init__(self, me, source, out, send, recv):
        self.me, self.source, self.out, self.recv = me, source, out, recv
        self.copies = Copies(send)

    def start(self):
        mine = rank_of(self.me["b"], self.me["l"], self.me["c"])
        for m, to in mates(self.me):
            p = rank_of(to["b"], to["l"], to["c"])
            self.copies.go(self.source(p), self.out(mine), self.recv.at[mine], to)

    def finish(self):
        for m, to in mates(self.me):
            p = rank_of(to["b"], to["l"], to["c"])
            landed(self.out(p), self.recv.at[p])
        self.copies.drain()


ANY = pl.BlockSpec(memory_space=pl.ANY)
VM = pl.BlockSpec(memory_space=pltpu.VMEM)


def comm_call(body, outs, in_specs, out_specs, scratch, cid):
    return pl.pallas_call(
        body,
        out_shape=outs,
        in_specs=in_specs,
        out_specs=out_specs,
        scratch_shapes=scratch,
        compiler_params=pltpu.CompilerParams(
            collective_id=cid, has_side_effects=True, vmem_limit_bytes=VMEM_BYTES
        ),
    )


def dot_nn(a, b):
    return jnp.dot(a, b, preferred_element_type=F32)


def dot_nt(a, b):
    return lax.dot_general(a, b, (((1,), (1,)), ((), ())), preferred_element_type=F32)


def dot_tn(a, b):
    return lax.dot_general(a, b, (((0,), (0,)), ((), ())), preferred_element_type=F32)


MIX = 32


def rows_at(i, n):
    return pl.ds(pl.multiple_of(i * n, n), n)


class RowsGather:
    def __init__(self, me, H, own, out, send, recv, at=None):
        self.me, self.H, self.own, self.out, self.recv, self.at = me, H, own, out, recv, at
        self.copies = Copies(send)

    @staticmethod
    def sems(H):
        return [DMA((2 * H - 1,)), DMA((2 * H,))]

    def block(self, a, h):
        return self.out.at[a, h] if self.at is None else self.out.at[a, h, self.at]

    def start(self):
        a, h = self.me["a"], self.me["h"]
        block = self.block(a, h)
        for dh in range(1, self.H):
            to = lax.rem(h + dh, self.H)
            self.copies.go(self.own, block, self.recv.at[dh], {"h": to})
        self.copies.go(self.own, block, self.recv.at[0], {"a": 1 - a})

    def forward(self):
        a, h, H = self.me["a"], self.me["h"], self.H
        for dh in range(1, H):
            block = self.block(a, lax.rem(h - dh + H, H))
            landed(block, self.recv.at[dh])
            self.copies.go(block, block, self.recv.at[H - 1 + dh], {"a": 1 - a})

    def finish(self):
        a, h, H = self.me["a"], self.me["h"], self.H
        landed(self.block(1 - a, h), self.recv.at[0])
        for dh in range(1, H):
            landed(self.block(1 - a, lax.rem(h - dh + H, H)), self.recv.at[H - 1 + dh])
        self.copies.drain()


def join_lanes(pieces, width):
    per = 128 // width
    out = []
    for g in range(0, len(pieces), per):
        acc = pieces[g]
        for k in range(1, per):
            acc = acc + pltpu.roll(pieces[g + k], width * k, axis=1)
        out.append(acc)
    return jnp.concatenate(out, axis=1) if len(out) > 1 else out[0]


def norm_rows(v):
    mean = jnp.mean(v, axis=-1, keepdims=True)
    cent = v - mean
    rstd = lax.rsqrt(jnp.mean(cent * cent, axis=-1, keepdims=True) + EPS)
    return cent * rstd, rstd


def mix_rows(read, first, carry, shares, write, tiles, rows):
    per = tiles // 2

    @pl.loop(0, tiles)
    def _(p):
        n = read(p)
        prev = jnp.where(lax.rem(p, per) == 0, first(p // per), carry[...])
        row = lax.broadcasted_iota(jnp.int32, n.shape, 0)
        before = jnp.where(row == 0, prev, pltpu.roll(n, 1, axis=0))
        carry[...] = n[rows - 1 : rows]
        diff = n - before
        for i, s in enumerate(shares):
            write(i, p, (before + s * diff).astype(BF))
        write(None, p, diff.astype(BF))


def opening(lay, vecs, x, up, w, later, w_o, w_cv, early):
    H, A = lay.H, lay.A
    grid = (A, 2, H, 4)
    rows, D = x.shape
    T = 8 * rows
    m = D // 8
    w_row = D // lay.n
    kk = D // (2 * A)
    bring_o = lay.strided
    wo_shape = (A, H, w_o.shape[0], D) if bring_o else w_o.shape

    def body(*refs):
        vecs, x, up, w, later, w_o, w_cv = refs[:7]
        full, mine_v, mixed, diff, rkv, gate, upc, w_out, team, wo, wcv = refs[7:18]
        va, xg, halo, hn, carry, mx, df, wa = refs[18:26]
        vs, vn, vf, xs, xr, hs, hr, us, ur, ws, wn, wf, qs, qr, os_, or_, es, er, ls = refs[26:]
        me = coords()
        a, b, h, l, c = (me[n] for n in ALL)
        mine = rank_of(b, l, c)

        def cols(ref, p):
            return ref.at[:, pl.ds(pl.multiple_of(p * m, m), m)]

        local = [
            pltpu.make_async_copy(w.at[mine], wa.at[a, b, h, l * 2 + c], ls.at[0]),
            pltpu.make_async_copy(vecs, va.at[a, b, h, l * 2 + c], ls.at[1]),
            pltpu.make_async_copy(x, xg.at[rows_at(mine, rows)], ls.at[2]),
            pltpu.make_async_copy(cols(up, mine), upc.at[mine], ls.at[3]),
            pltpu.make_async_copy(later.at[mine], team.at[mine], ls.at[4]),
            pltpu.make_async_copy(w_o, wo.at[a, h] if bring_o else wo, ls.at[5]),
        ]
        if early:
            first = w_cv.at[pl.ds(0, early)]
            local.append(pltpu.make_async_copy(first, wcv.at[a, h], ls.at[6]))
        for copy in local:
            copy.start()
        greet(me, H, True, True)
        gw = TeamsGather(me, H, lambda p: w.at[p], wa, ws, wn, wf)
        gv = TeamsGather(me, H, lambda p: vecs, va, vs, vn, vf)
        gx = TeamGather(me, x, lambda p: xg.at[rows_at(p, rows)], xs, xr, ("zx", "zx"))
        gh = Halo(me, H, x, halo, hs, hr)
        gu = Exchange(me, lambda p: cols(up, p), lambda p: upc.at[p], us, ur)
        gq = Exchange(me, lambda p: later.at[p], lambda p: team.at[p], qs, qr)
        if bring_o:
            go = RowsGather(me, H, w_o, wo, os_, or_)
        gv.start()
        gw.start()
        gv.spread(local[1])
        gv.forward()
        gw.spread(local[0])
        gx.start()
        gv.finish()
        local[2].wait()
        gx.finish()
        gh.start()
        gw.forward((0,))
        gu.start()
        if early:
            ge = RowsGather(me, H, first, wcv, es, er)
            ge.start()
        gh.finish()

        def piece(*at):
            return va[at].astype(F32)

        flat = [
            piece(i, j, k, q) for i in range(A) for j in range(2) for k in range(H) for q in range(4)
        ]
        full[...] = join_lanes(flat, w_row)
        if lay.strided:
            own = [piece(i, b, k, l * 2 + c) for i in range(A) for k in range(H)]
            mine_v[...] = join_lanes(own, w_row)
        else:
            mine_v[...] = full[:, pl.ds(pl.multiple_of(mine * m, m), m)]
        gain, bias = full[0:1], full[1:2]
        for s in range(2):
            row = (norm_rows(halo[s].astype(F32))[0] * gain + bias)[15:16]
            hn[s] = jnp.where(h > 0, row, jnp.zeros_like(row))

        def write(i, p, v):
            if i is None:
                df[rows_at(p, MIX)] = v
            else:
                mx[i, rows_at(p, MIX)] = v

        mix_rows(
            lambda p: norm_rows(xg[rows_at(p, MIX)].astype(F32))[0] * gain + bias,
            lambda s: hn[s],
            carry,
            [full[2 + i : 3 + i] for i in range(4)],
            write,
            T // MIX,
            MIX,
        )
        keep = [
            pltpu.make_async_copy(mx, mixed, ls.at[7]),
            pltpu.make_async_copy(df, diff, ls.at[8]),
        ]
        for copy in keep:
            copy.start()
        gw.forward((1,))
        gq.start()
        if bring_o:
            go.start()
        if early:
            ge.forward()
        gw.finish()
        keep.append(pltpu.make_async_copy(wa, w_out, ls.at[9]))
        keep[-1].start()
        for j in range(4):

            @pl.loop(0, 4)
            def _(t):
                at = rows_at(t, T // 4)
                acc = jnp.zeros((T // 4, m), F32)
                for i in range(A):
                    for k in range(2):
                        lo = (i * 2 + k) * kk
                        wt = wa[i, k, :, :, :, j * m : (j + 1) * m].reshape(kk, m)
                        acc = acc + dot_nn(mx[j, at, lo : lo + kk], wt)
                if j < 3:
                    rkv[j, at] = acc.astype(BF)
                else:
                    gate[at] = acc

        gu.finish()
        gq.finish()
        if bring_o:
            go.forward()
            go.finish()
        if early:
            ge.finish()
        for copy in local[3:] + keep:
            copy.wait()

    gsems = TeamsGather.sems(H)
    return comm_call(
        body,
        (
            jax.ShapeDtypeStruct((16, D), F32),
            jax.ShapeDtypeStruct((16, m), F32),
            jax.ShapeDtypeStruct((4, T, D), BF),
            jax.ShapeDtypeStruct((T, D), BF),
            jax.ShapeDtypeStruct((3, T, m), BF),
            jax.ShapeDtypeStruct((T, m), F32),
            jax.ShapeDtypeStruct((8, rows, m), BF),
            jax.ShapeDtypeStruct((*grid, *w.shape[1:]), BF),
            jax.ShapeDtypeStruct(later.shape, BF),
            jax.ShapeDtypeStruct(wo_shape, BF),
            jax.ShapeDtypeStruct((A, H, max(early, 16), D), BF),
        ),
        [ANY] * 7,
        (VM, VM, ANY, ANY, VM, VM, ANY, ANY, ANY, ANY, ANY),
        [
            pltpu.VMEM((*grid, *vecs.shape), BF),
            pltpu.VMEM((T, D), BF),
            pltpu.VMEM((2, 16, D), BF),
            pltpu.VMEM((2, 1, D), F32),
            pltpu.VMEM((1, D), F32),
            pltpu.VMEM((4, T, D), BF),
            pltpu.VMEM((T, D), BF),
            pltpu.VMEM((*grid, *w.shape[1:]), BF),
            *gsems,
            DMA((14,)),
            DMA((8, 2)),
            DMA((8,)),
            DMA((2,)),
            DMA((7,)),
            DMA((8,)),
            *gsems,
            DMA((7,)),
            DMA((8,)),
            *RowsGather.sems(H),
            *RowsGather.sems(H),
            DMA((10,)),
        ],
        0,
    )(vecs, x, up, w, later, w_o, w_cv)


def block_ones(m):
    row = lax.broadcasted_iota(jnp.int32, (m, m), 0) // HEAD
    col = lax.broadcasted_iota(jnp.int32, (m, m), 1) // HEAD
    return jnp.where(row == col, 1.0, 0.0).astype(F32)


def dot_exact(a, b):
    return jnp.dot(a, b, preferred_element_type=F32, precision=lax.Precision.HIGHEST)


class Decay:
    def __init__(self, lam):
        m = lam.shape[1]
        i = lax.broadcasted_iota(jnp.int32, (CHUNK, m), 0).astype(F32)
        self.i = i
        self.down = jnp.exp(-lam * i)
        self.up = jnp.exp(lam * (i + 1.0))
        self.tail = jnp.exp(-lam * (CHUNK - 1.0 - i))
        self.span = jnp.exp(-lam * CHUNK)


def stacked_heads(v):
    m = v.shape[1]
    lane = lax.broadcasted_iota(jnp.int32, v.shape, 1) // HEAD
    zero = jnp.zeros_like(v)
    return jnp.concatenate([jnp.where(lane == g, v, zero) for g in range(m // HEAD)], axis=0)


def own_heads(v):
    m = v.shape[1]
    lane = lax.broadcasted_iota(jnp.int32, (CHUNK, m), 1) // HEAD
    out = v[:CHUNK]
    for g in range(1, m // HEAD):
        out = jnp.where(lane == g, v[g * CHUNK : (g + 1) * CHUNK], out)
    return out


def triangle(heads, low):
    shape = (heads * CHUNK, CHUNK)
    row = lax.rem(lax.broadcasted_iota(jnp.int32, shape, 0), CHUNK)
    col = lax.broadcasted_iota(jnp.int32, shape, 1)
    return row > col if low else row < col


def squeeze(s0, s1):
    def fold(s):
        out = s[:, :128]
        for g in range(1, s.shape[1] // 128):
            out = out + s[:, g * 128 : (g + 1) * 128]
        return out + pltpu.roll(out, HEAD, axis=1)

    lane = lax.broadcasted_iota(jnp.int32, (s0.shape[0], 128), 1)
    return jnp.where(lane < HEAD, fold(s0), fold(s1))


def widen(p, second, ones):
    lane = lax.broadcasted_iota(jnp.int32, p.shape, 1)
    keep = (lane >= HEAD) if second else (lane < HEAD)
    both = jnp.where(keep, p, pltpu.roll(p, HEAD, axis=1))
    return jnp.concatenate([both] * (ones.shape[1] // 128), axis=1) * ones


class Chain:
    def __init__(self, me, H, ahead, out_box, in_box, send, recv):
        h = me["h"]
        self.h, self.H = h, H
        nxt = jnp.minimum(h + 1, H - 1) if ahead else jnp.maximum(h - 1, 0)
        self.has_next = (h < H - 1) if ahead else (h > 0)
        self.has_prev = (h > 0) if ahead else (h < H - 1)
        self.out_box, self.in_box = out_box, in_box
        self.copy = remote(out_box, in_box, send, recv, {"h": nxt})

    def run(self, state, closing, span_all, ones):
        if self.H == 1:
            return

        @pl.when(self.has_prev)
        def _():
            self.copy.wait_recv()
            p = self.in_box[...]
            for s in range(2):
                state[s] = widen(p, s == 1, ones)

        @pl.when(self.has_next)
        def _():
            self.out_box[...] = squeeze(*(span_all * state[s] + closing[s] for s in range(2)))
            self.copy.start()

    def finish(self):
        if self.H == 1:
            return

        @pl.when(self.has_next)
        def _():
            self.copy.wait_send()


def time_mix(lay, rkv, gate, mv, full, start, x, wo, w_cv, wcv_first, early, team):
    H, A = lay.H, lay.A
    rows, D = x.shape
    T = 8 * rows
    m = D // 8
    heads = m // HEAD
    per = T // 2 // CHUNK
    grid = (A, 2, H, 4)
    rest = w_cv.shape[0] - early

    def body(*refs):
        rkv, gate, mv, full, start, x, wo, w_cv, wcv_first, team = refs[:10]
        gated, ghat, grstd, states, fin, middle, n2, halo, wcv, wf = refs[10:20]
        (adds, st, cl, obox, ibox, own, part) = refs[20:27]
        near, acc, mid, far, ss, sr = refs[27:33]
        cs, cr, vs, vr, ws, wn, wfar, gs, gr, hs, hr, ls = refs[33:]
        me = coords()
        a, b, h, l, c = (me[n] for n in ALL)
        mine = rank_of(b, l, c)
        tail = pl.ds(early, rest)
        local = [
            pltpu.make_async_copy(team.at[pl.ds(0, 4)], wf.at[a, 0, h], ls.at[0]),
            pltpu.make_async_copy(team.at[pl.ds(4, 4)], wf.at[a, 1, h], ls.at[1]),
            pltpu.make_async_copy(w_cv.at[tail], wcv.at[a, h, tail], ls.at[2]),
        ]
        if early:
            head = wcv.at[:, :, pl.ds(0, early)]
            local.append(pltpu.make_async_copy(wcv_first, head, ls.at[3]))
        for copy in local:
            copy.start()
        greet(me, H, True, True)
        gw = TeamsGather(me, H, None, wf, ws, wn, wfar, team)
        gv = RowsGather(me, H, w_cv.at[tail], wcv, vs, vr, tail)
        ones = block_ones(m)
        dec = Decay(mv[6:7])
        u = mv[7:8]
        span_all = jnp.exp(-mv[6:7] * (T // 2))

        def tile(i, s, n):
            return rkv[i, rows_at(s * per + n, CHUNK)].astype(F32)

        cl[...] = jnp.zeros_like(cl)

        @pl.loop(0, per)
        def _(n):
            for s in range(2):
                kt = (tile(1, s, n) * dec.tail).astype(BF)
                v = rkv[2, rows_at(s * per + n, CHUNK)]
                add = dot_tn(v, kt) * ones
                adds[s, n] = add
                cl[s] = dec.span * cl[s] + add

        for s in range(2):
            st[s] = jnp.where(h > 0, jnp.zeros_like(start[s]), start[s])
        chain = Chain(me, H, True, obox, ibox, cs, cr)
        chain.run(st, cl, span_all, ones)
        gw.spread()
        low = triangle(heads, True)

        @pl.loop(0, per)
        def _(n):
            for s in range(2):
                at = rows_at(s * per + n, CHUNK)
                r, k, v = (tile(i, s, n) for i in range(3))
                vb = rkv[2, at]
                rd = (r * dec.down).astype(BF)
                kg = (k * dec.up).astype(BF)
                state = st[s]
                states[s, n] = state
                att = jnp.where(low, dot_nt(stacked_heads(rd), kg), 0.0).astype(BF)
                y = own_heads(dot_nn(att, vb)) + dot_nt(rd, state.astype(BF))
                y = y + dot_exact(r * u * k, ones) * v
                st[s] = dec.span * state + adds[s, n]
                mean = dot_exact(y, ones) * (1.0 / HEAD)
                cent = y - mean
                rstd = lax.rsqrt(dot_exact(cent * cent, ones) * (1.0 / HEAD) + GROUP_EPS)
                hat = cent * rstd
                ghat[at] = hat
                grstd[at] = rstd
                g = gate[at]
                silu = g / (1.0 + jnp.exp(-g))
                gated[at] = ((hat * mv[8:9] + mv[9:10]) * silu).astype(BF)

        for s in range(2):
            fin[s] = st[s]
        chain.finish()

        @pl.loop(0, 8)
        def _(p):
            g = gated[rows_at(p, rows)]
            w = wo[...].reshape(m, D)
            for q in range(4):
                lo = q * (D // 4)
                part[p, :, lo : lo + D // 4] = dot_nn(g, w[:, lo : lo + D // 4]).astype(BF)

        sums = TeamSum(me, lambda p: part.at[p], near, acc, mid, far, ss, sr, ("xz", "xz"))
        sums.start()

        def put(at, v):
            v = x[at].astype(F32) + v
            middle[at] = v
            own[at] = (norm_rows(v)[0] * full[10:11] + full[11:12]).astype(BF)

        sums.finish(put)
        keep = pltpu.make_async_copy(own, n2.at[mine], ls.at[4])
        keep.start()
        gx = TeamGather(me, own, lambda p: n2.at[p], gs, gr, ("zx", "zx"))
        gx.start()
        gh = Halo(me, H, own, halo, hs, hr)
        gh.start()
        gv.start()
        gw.forward((0,))
        gx.finish()
        gh.finish()
        keep.wait()
        gw.forward((1,))
        gv.forward()
        gw.finish()
        gv.finish()
        for copy in local:
            copy.wait()

    return comm_call(
        body,
        (
            jax.ShapeDtypeStruct((T, m), BF),
            jax.ShapeDtypeStruct((T, m), F32),
            jax.ShapeDtypeStruct((T, m), F32),
            jax.ShapeDtypeStruct((2, per, m, m), F32),
            jax.ShapeDtypeStruct((2, m, m), F32),
            jax.ShapeDtypeStruct((rows, D), F32),
            jax.ShapeDtypeStruct((8, rows, D), BF),
            jax.ShapeDtypeStruct((2, 16, D), BF),
            jax.ShapeDtypeStruct((A, H, *w_cv.shape), BF),
            jax.ShapeDtypeStruct((*grid, *team.shape[1:]), BF),
        ),
        [VM, VM, VM, VM, VM, VM, VM, ANY, ANY, ANY],
        (VM, VM, VM, VM, VM, VM, ANY, ANY, ANY, ANY),
        [
            pltpu.VMEM((2, per, m, m), F32),
            pltpu.VMEM((2, m, m), F32),
            pltpu.VMEM((2, m, m), F32),
            pltpu.VMEM((m, 128), F32),
            pltpu.VMEM((m, 128), F32),
            pltpu.VMEM((rows, D), BF),
            pltpu.VMEM((8, rows, D), BF),
            *TeamSum.scratch(rows, D),
            DMA,
            DMA,
            *RowsGather.sems(H),
            *TeamsGather.sems(H),
            DMA((14,)),
            DMA((8, 2)),
            DMA((8,)),
            DMA((2,)),
            DMA((5,)),
        ],
        1,
    )(rkv, gate, mv, full, start, x, wo, w_cv, wcv_first, team)


def time_mix_back(lay, d_br, wo, gated, ghat, grstd, gate, rkv, states, mv, items):
    H, A = lay.H, lay.A
    T, m = gate.shape
    D = d_br.shape[-1]
    heads = m // HEAD
    per = T // 2 // CHUNK

    bg = Background(items, H)
    nb = len(items)

    def body(*refs):
        d_br, wo, gated, ghat, grstd, gate, rkv, states, mv = refs[:9]
        srcs, refs = refs[9 : 9 + nb], refs[9 + nb :]
        g_o, d_all, sums = refs[:3]
        dsts, refs = refs[3 : 3 + nb], refs[3 + nb :]
        dy, adds, cl, st, obox, ibox, cs, cr = refs[:8]
        me = coords()
        h = me["h"]
        greet(me, H, True, True)
        ones = block_ones(m)
        dec = Decay(mv[6:7])
        u = mv[7:8]
        span_all = jnp.exp(-mv[6:7] * (T // 2))
        lowT = triangle(heads, False)
        low = triangle(heads, True)
        sums[...] = jnp.zeros_like(sums)

        @pl.loop(0, 2 * per)
        def _(t):
            at = rows_at(t, CHUNK)
            d_gated = dot_nt(d_br[t], wo[...].reshape(m, D))
            g = gate[at]
            sig = 1.0 / (1.0 + jnp.exp(-g))
            hat, rstd = ghat[at], grstd[at]
            dn = d_gated * (g * sig)
            sums[2:3] += jnp.sum(dn * hat, axis=0, keepdims=True)
            sums[3:4] += jnp.sum(dn, axis=0, keepdims=True)
            n = hat * mv[8:9] + mv[9:10]
            d_all[at, 3 * m :] = (d_gated * n * sig * (1.0 + g * (1.0 - sig))).astype(BF)
            e = dn * mv[8:9]
            m1 = dot_exact(e, ones) * (1.0 / HEAD)
            m2 = dot_exact(e * hat, ones) * (1.0 / HEAD)
            dy[at] = (e - m1 - hat * m2) * rstd

        cl[...] = jnp.zeros_like(cl)

        @pl.loop(0, per)
        def _(q):
            n = per - 1 - q
            for s in range(2):
                at = rows_at(s * per + n, CHUNK)
                rd = (rkv[0, at].astype(F32) * dec.down).astype(BF)
                add = dot_tn(dy[at].astype(BF), rd) * ones
                adds[s, n] = add
                cl[s] = dec.span * cl[s] + add

        st[...] = jnp.zeros_like(st)
        chain = Chain(me, H, False, obox, ibox, cs, cr)
        chain.run(st, cl, span_all, ones)
        bg.start(me, srcs, dsts, refs[8:])

        @pl.loop(0, per)
        def _(q):
            n = per - 1 - q
            for s in range(2):
                at = rows_at(s * per + n, CHUNK)
                r, k, v = (rkv[i, at].astype(F32) for i in range(3))
                vb = rkv[2, at]
                rd, kg, kt = r * dec.down, k * dec.up, k * dec.tail
                rdb, kgb, ktb = rd.astype(BF), kg.astype(BF), kt.astype(BF)
                dyt = dy[at]
                dyb = dyt.astype(BF)
                state, end = states[s, n], st[s]
                endb = end.astype(BF)
                datt = jnp.where(low, dot_nt(stacked_heads(dyb), vb), 0.0).astype(BF)
                dattT = jnp.where(lowT, dot_nt(stacked_heads(vb), dyb), 0.0).astype(BF)
                attT = jnp.where(lowT, dot_nt(stacked_heads(kgb), rdb), 0.0).astype(BF)
                ddiag = dot_exact(dyt * v, ones)
                diag = dot_exact(r * u * k, ones)
                d_rd = own_heads(dot_nn(datt, kgb)) + dot_nn(dyb, state.astype(BF))
                d_kg = own_heads(dot_nn(dattT, rdb))
                d_kt = dot_nn(vb, endb)
                d_v = own_heads(dot_nn(attT, dyb)) + diag * dyt + dot_nt(ktb, endb)
                d_r = d_rd * dec.down + ddiag * u * k
                d_k = d_kg * dec.up + d_kt * dec.tail + ddiag * u * r
                d_all[at, :m] = d_r.astype(BF)
                d_all[at, m : 2 * m] = d_k.astype(BF)
                d_all[at, 2 * m : 3 * m] = d_v.astype(BF)
                sums[1:2] += jnp.sum(ddiag * r * k, axis=0, keepdims=True)
                d_l = jnp.sum(
                    (dec.i + 1.0) * kg * d_kg
                    - dec.i * rd * d_rd
                    - (CHUNK - 1.0 - dec.i) * kt * d_kt,
                    axis=0,
                    keepdims=True,
                )
                d_l = d_l - CHUNK * dec.span * jnp.sum(state * end, axis=0, keepdims=True)
                sums[0:1] += d_l
                st[s] = dec.span * end + adds[s, n]

        nw = D // 4
        for q in range(4):
            w = jnp.concatenate([d_br[p, :, q * nw : (q + 1) * nw] for p in range(8)], axis=0)
            g = dot_tn(gated[...], w).astype(BF)
            g_o[:, :, :, q * nw : (q + 1) * nw] = g.reshape(*g_o.shape[:3], nw)
        chain.finish()
        bg.finish()

    out = comm_call(
        body,
        (
            jax.ShapeDtypeStruct(wo.shape, BF),
            jax.ShapeDtypeStruct((T, 4 * m), BF),
            jax.ShapeDtypeStruct((8, m), F32),
            *bg.outs(),
        ),
        [VM] * 9 + [ANY] * nb,
        (VM, VM, VM, *[ANY] * nb),
        [
            pltpu.VMEM((T, m), F32),
            pltpu.VMEM((2, per, m, m), F32),
            pltpu.VMEM((2, m, m), F32),
            pltpu.VMEM((2, m, m), F32),
            pltpu.VMEM((m, 128), F32),
            pltpu.VMEM((m, 128), F32),
            DMA,
            DMA,
            *bg.sems(),
        ],
        5,
    )(d_br, wo, gated, ghat, grstd, gate, rkv, states, mv, *bg.arrays())
    return out[0], out[1], out[2], out[3:]


class Background:
    def __init__(self, items, H):
        self.items, self.H = items, H

    def arrays(self):
        return [v for v, _ in self.items]

    def outs(self):
        shapes = []
        for v, kind in self.items:
            lead = {"h": (max(self.H - 1, 1),), "a": (), "t": (8,)}[kind]
            shapes.append(jax.ShapeDtypeStruct((*lead, *v.shape[1:]), BF))
        return shapes

    def sems(self):
        out = []
        for _, kind in self.items:
            n = {"h": max(self.H - 1, 1), "a": 1, "t": 8}[kind]
            out += [DMA((n,)), DMA((n,))] + ([DMA] if kind == "t" else [])
        return out

    def start(self, me, srcs, dsts, sems):
        self.open = []
        sems = list(sems)
        h, H = me["h"], self.H
        mine = rank_of(me["b"], me["l"], me["c"])
        for (_, kind), src, dst in zip(self.items, srcs, dsts):
            ss, sr = sems.pop(0), sems.pop(0)
            copies = Copies(ss)
            if kind == "h":
                for dh in range(1, H):
                    to = lax.rem(h + dh, H)
                    copies.go(src.at[to], dst.at[dh - 1], sr.at[dh - 1], {"h": to})
                    self.open.append((dst.at[dh - 1], sr.at[dh - 1]))
            elif kind == "a":
                copies.go(src.at[1 - me["a"]], dst, sr.at[0], {"a": 1 - me["a"]})
                self.open.append((dst, sr.at[0]))
            else:
                keep = pltpu.make_async_copy(src.at[mine], dst.at[mine], sems.pop(0))
                keep.start()
                self.open.append(keep)
                for m, to in mates(me):
                    p = rank_of(to["b"], to["l"], to["c"])
                    copies.go(src.at[p], dst.at[mine], sr.at[mine], to)
                    self.open.append((dst.at[p], sr.at[p]))
            self.open.append(copies)

    def finish(self):
        for item in self.open:
            if isinstance(item, tuple):
                landed(*item)
            elif isinstance(item, Copies):
                item.drain()
            else:
                item.wait()


def back_rows(T, tile, chunk, shares, diff, part, first, sums):
    per = T // 2 // tile

    def step(q, carry):
        t = 2 * per - 1 - q
        ds = chunk(t)
        dif = diff(t)
        late = jnp.zeros_like(ds[0])
        here = jnp.zeros_like(ds[0])
        for i, (d, s) in enumerate(zip(ds, shares)):
            sums[i][...] = sums[i][...] + jnp.sum(d * dif, axis=0, keepdims=True)
            late = late + (1.0 - s) * d
            here = here + s * d
        carry = jnp.where(lax.rem(t, per) == per - 1, jnp.zeros_like(carry), carry)
        row = lax.broadcasted_iota(jnp.int32, late.shape, 0)
        part(t, here + jnp.where(row == tile - 1, carry, pltpu.roll(late, tile - 1, axis=0)))

        @pl.when(lax.rem(t, per) == 0)
        def _():
            first(t // per, late[:16].astype(BF))

        return late[:1]

    zero = jnp.zeros((1, diff(0).shape[1]), F32)
    lax.fori_loop(0, 2 * per, step, zero)


def channel_mix(lay, n2, halo, full, wcv, wf, upc, middle, up):
    H, A = lay.H, lay.A
    rows, D = middle.shape
    T = 8 * rows
    F, m = wcv.shape[0], D // 8
    nk, kk, _ = wf.shape
    w_cv = F // (A * H)
    tile = T // 4
    dq = D // 4

    def body(n2, halo, full, wcv, wf, upc, middle, up, *rest):
        d_mid, d_br, moved, s_cv, got_cv, g_f, got_f, sums = rest[:8]
        (big, m2, df, carry, relu, act, sg, d_pg, d_val, dval, gcv, cvbuf, stage) = rest[8:21]
        (dn2, own, add, first, edge) = rest[21:26]
        cn, ca, cm, cf, c_s, c_r = rest[26:32]
        rn, ra, rm, rf, r_s, r_r = rest[32:38]
        ds, dr, bs, br, es, er, ms, mr, vs, vr, fs, fr, ls = rest[38:]
        d_pre = act
        me = coords()
        a, b, h, l, c = (me[n] for n in ALL)
        mine = rank_of(b, l, c)
        loads = [
            pltpu.make_async_copy(n2.at[p], big.at[pl.ds(p * rows, rows)], ls.at[p]) for p in range(8)
        ]
        for copy in loads:
            copy.start()
        greet(me, H, True, True)
        for copy in loads:
            copy.wait()

        def write(i, p, v):
            if i is None:
                df[rows_at(p, MIX)] = v
            else:
                m2[i, rows_at(p, MIX)] = v

        def before(s):
            row = halo[s].astype(F32)[15:16]
            return jnp.where(h > 0, row, jnp.zeros_like(row))

        s_ck, s_cr = full[12:13], full[13:14]
        mix_rows(
            lambda p: big[rows_at(p, MIX)].astype(F32),
            before,
            carry,
            [s_ck, s_cr],
            write,
            T // MIX,
            MIX,
        )

        @pl.loop(0, 4)
        def _(t):
            at = rows_at(t, tile)
            acc = jnp.zeros((tile, F), F32)
            for i in range(nk):
                acc = acc + dot_nn(m2[0, at, i * kk : (i + 1) * kk], wf[i, :, :F])
            pos = jnp.maximum(acc, 0.0)
            relu[at] = pos.astype(BF)
            act[at] = (pos * pos).astype(BF)

        @pl.loop(0, 4)
        def _(t):
            at = rows_at(t, tile)
            for q in range(4):
                lo = q * dq
                big[at, lo : lo + dq] = dot_nn(act[at], wcv[:, lo : lo + dq]).astype(BF)

        def cols(ref):
            return lambda p: ref.at[:, pl.ds(pl.multiple_of(p * m, m), m)]

        total = TeamSum(me, cols(big), cn, ca, cm, cf, c_s, c_r)
        total.start()

        @pl.loop(0, 4)
        def _(t):
            at = rows_at(t, tile)
            acc = jnp.zeros((tile, m), F32)
            for i in range(nk):
                acc = acc + dot_nn(m2[1, at, i * kk : (i + 1) * kk], wf[i, :, F:])
            sg[at] = 1.0 / (1.0 + jnp.exp(-acc))

        def gate_back(at, val):
            sig = sg[at]
            upv = upc[at].astype(F32)
            d_val[at] = (sig * upv).astype(BF)
            d_pg[at] = (upv * val * sig * (1.0 - sig)).astype(BF)
            add[at] = (sig * val).astype(BF)

        total.finish(gate_back)
        keep_val = pltpu.make_async_copy(d_val, cols(dval)(mine), ls.at[8])
        keep_val.start()
        gv = TeamGather(me, d_val, cols(dval), ds, dr)
        gv.start()
        gv.finish()
        keep_val.wait()

        @pl.loop(0, 8)
        def _(q):
            at = pl.ds(pl.multiple_of(q * m, m), m)
            g = dot_tn(act[...], dval[:, at])
            for i in range(A):
                for j in range(H):
                    lo = (i * H + j) * w_cv
                    gcv[i, j, :, at] = g[lo : lo + w_cv].astype(BF)

        cv = Copies(vs)
        cv.go(gcv.at[1 - a], cvbuf, vr.at[0], {"a": 1 - a})

        @pl.loop(0, 4)
        def _(t):
            at = rows_at(t, tile)
            d_pre[at] = (dot_nt(dval[at], wcv[...]) * 2.0 * relu[at].astype(F32)).astype(BF)

        ff = Copies(fs)
        sums[...] = jnp.zeros_like(sums)

        def chunk_of(i):
            lo = i * kk

            def chunk(t):
                at = rows_at(t, tile)
                return (dot_nt(d_pre[at], wf[i, :, :F]), dot_nt(d_pg[at], wf[i, :, F:]))

            def put(t, v):
                big[rows_at(t, tile), lo : lo + kk] = v.astype(BF)

            def put_first(s, v):
                first[s, :, lo : lo + kk] = v

            back_rows(
                T,
                tile,
                chunk,
                (s_ck[:, lo : lo + kk], s_cr[:, lo : lo + kk]),
                lambda t: df[rows_at(t, tile), lo : lo + kk].astype(F32),
                put,
                put_first,
                [sums.at[k : k + 1, lo : lo + kk] for k in range(2)],
            )

        def grads(i):
            lo = i * kk
            for k in range(2):
                at = slice(lo + k * kk // 2, lo + (k + 1) * kk // 2)
                to = slice(k * kk // 2, (k + 1) * kk // 2)
                stage[to, :F] = dot_tn(m2[0, :, at], d_pre[...]).astype(BF)
                stage[to, F:] = dot_tn(m2[1, :, at], d_pg[...]).astype(BF)
            copy = pltpu.make_async_copy(stage, g_f.at[i // 2, i % 2], ls.at[9])
            copy.start()
            return copy

        for i in range(nk):
            copy = grads(i)
            chunk_of(i)
            copy.wait()
        ff.go(g_f.at[1 - a], got_f, fr.at[0], {"a": 1 - a})
        total = TeamSum(me, lambda p: big.at[pl.ds(pl.multiple_of(p * rows, rows), rows)], rn, ra, rm, rf, r_s, r_r)
        total.start()
        e = Edge(me, H, first, edge, es, er)
        e.start()

        def put_dn(at, v):
            dn2[at] = v

        total.finish(put_dn)
        e.finish(dn2)

        @pl.loop(0, rows // MIX)
        def _(t):
            at = rows_at(t, MIX)
            d = dn2[at]
            hat, rstd = norm_rows(middle[at])
            sums[2:3] = sums[2:3] + jnp.sum(d * hat, axis=0, keepdims=True)
            sums[3:4] = sums[3:4] + jnp.sum(d, axis=0, keepdims=True)
            dm = up[at].astype(F32) + norm_back(d * full[10:11], hat, rstd)
            d_mid[at] = dm
            own[at] = dm.astype(BF)

        keep = [
            pltpu.make_async_copy(own, d_br.at[mine], ls.at[10]),
            pltpu.make_async_copy(add.at[rows_at(mine, rows)], moved.at[mine], ls.at[11]),
        ]
        for copy in keep:
            copy.start()
        gx = TeamGather(me, own, lambda p: d_br.at[p], bs, br)
        gx.start()
        landed(cvbuf, vr.at[0])

        @pl.loop(0, H)
        def _(j):
            gcv[a, j] = (gcv[a, j].astype(F32) + cvbuf[j].astype(F32)).astype(BF)

        for dh in range(1, H):
            to = lax.rem(h + dh, H)
            cv.go(gcv.at[a, to], got_cv.at[dh - 1], vr.at[dh], {"h": to})
        keep.append(pltpu.make_async_copy(gcv.at[a, h], s_cv, ls.at[12]))
        keep[-1].start()
        gx.finish()
        gm = Exchange(me, lambda p: add.at[rows_at(p, rows)], lambda p: moved.at[p], ms, mr)
        gm.start()
        gm.finish()
        landed(got_f, fr.at[0])
        ff.drain()
        for dh in range(1, H):
            landed(got_cv.at[dh - 1], vr.at[dh])
        cv.drain()
        for copy in keep:
            copy.wait()

    return comm_call(
        body,
        (
            jax.ShapeDtypeStruct((rows, D), F32),
            jax.ShapeDtypeStruct((8, rows, D), BF),
            jax.ShapeDtypeStruct((8, rows, m), BF),
            jax.ShapeDtypeStruct((w_cv, D), BF),
            jax.ShapeDtypeStruct((max(H - 1, 1), w_cv, D), BF),
            jax.ShapeDtypeStruct((A, nk // A, kk, F + m), BF),
            jax.ShapeDtypeStruct((nk // A, kk, F + m), BF),
            jax.ShapeDtypeStruct((8, D), F32),
        ),
        [ANY, VM, VM, VM, VM, VM, VM, VM],
        (VM, ANY, ANY, ANY, ANY, ANY, ANY, VM),
        [
            pltpu.VMEM((T, D), BF),
            pltpu.VMEM((2, T, D), BF),
            pltpu.VMEM((T, D), BF),
            pltpu.VMEM((1, D), F32),
            pltpu.VMEM((T, F), BF),
            pltpu.VMEM((T, F), BF),
            pltpu.VMEM((T, m), F32),
            pltpu.VMEM((T, m), BF),
            pltpu.VMEM((T, m), BF),
            pltpu.VMEM((T, D), BF),
            pltpu.VMEM((A, H, w_cv, D), BF),
            pltpu.VMEM((H, w_cv, D), BF),
            pltpu.VMEM((kk, F + m), BF),
            pltpu.VMEM((rows, D), F32),
            pltpu.VMEM((rows, D), BF),
            pltpu.VMEM((T, m), BF),
            pltpu.VMEM((2, 16, D), BF),
            pltpu.VMEM((8, 16, D), BF),
            *TeamSum.scratch(T, m),
            *TeamSum.scratch(rows, D),
            DMA((14,)),
            DMA((8, 2)),
            DMA((14,)),
            DMA((8, 2)),
            DMA((2,)),
            DMA((8,)),
            DMA((7,)),
            DMA((8,)),
            DMA((H,)),
            DMA((H,)),
            DMA((1,)),
            DMA((1,)),
            DMA((13,)),
        ],
        2,
    )(n2, halo, full, wcv, wf, upc, middle, up)


def time_in_back(lay, d_all, mixed, diff, w4, full, x, d_mid, items):
    H, A = lay.H, lay.A
    rows, D = x.shape
    T = 8 * rows
    m = D // 8
    nk, kk, _ = w4.shape
    tile = T // 4
    hk = kk // H
    bg = Background(items, H)
    nb = len(items)

    def body(*refs):
        refs = list(refs)
        d_all, mixed, diff, w4, full, x, d_mid = refs[:7]
        srcs, refs = refs[7 : 7 + nb], refs[7 + nb :]
        in_grad, g_out, sums = refs[:3]
        dsts, refs = refs[3 : 3 + nb], refs[3 + nb :]
        part, g4, got, late, dn1, first, edge = refs[:7]
        rn, ra, rm, rf, r_s, r_r = refs[7:13]
        es, er, gs, gr = refs[13:17]
        me = coords()
        a, h = me["a"], me["h"]
        greet(me, H, True, True)
        bg.start(me, srcs, dsts, refs[17:])
        sums[...] = jnp.zeros_like(sums)
        cg = Copies(gs)

        for step in range(A):
            i = lax.rem(a + 1 + step, A)
            for k in range(2):
                lo = pl.ds(pl.multiple_of((i * 2 + k) * kk, kk), kk)
                for j in range(4):
                    g = dot_tn(mixed[j, :, lo], d_all[:, j * m : (j + 1) * m])
                    g4[i * 2 + k, :, j * m : (j + 1) * m] = g.astype(BF)
                if step < A - 1:
                    cg.go(g4.at[i * 2 + k], got.at[k], gr.at[k], {"a": 1 - a})

        def chunk_of(i):
            lo = i * kk

            def chunk(t):
                at = rows_at(t, tile)
                return tuple(
                    dot_nt(d_all[at, j * m : (j + 1) * m], w4[i, :, j * m : (j + 1) * m])
                    for j in range(4)
                )

            def put(t, v):
                part[rows_at(t, tile), lo : lo + kk] = v.astype(BF)

            def put_first(s, v):
                first[s, :, lo : lo + kk] = v

            back_rows(
                T,
                tile,
                chunk,
                tuple(full[2 + j : 3 + j, lo : lo + kk] for j in range(4)),
                lambda t: diff[rows_at(t, tile), lo : lo + kk].astype(F32),
                put,
                put_first,
                [sums.at[j : j + 1, lo : lo + kk] for j in range(4)],
            )

        for i in range(nk):
            chunk_of(i)
        total = TeamSum(me, lambda p: part.at[pl.ds(pl.multiple_of(p * rows, rows), rows)], rn, ra, rm, rf, r_s, r_r)
        total.start()
        e = Edge(me, H, first, edge, es, er)
        e.start()
        for k in range(2):
            landed(got.at[k], gr.at[k])
            g4[a * 2 + k] = (g4[a * 2 + k].astype(F32) + got[k].astype(F32)).astype(BF)
            for dh in range(1, H):
                to = lax.rem(h + dh, H)
                n = (dh - 1) * 2 + k
                cg.go(
                    g4.at[a * 2 + k, pl.ds(pl.multiple_of(to * hk, hk), hk)],
                    late.at[dh - 1, k],
                    gr.at[2 + n],
                    {"h": to},
                )

        def put_dn(at, v):
            dn1[at] = v

        total.finish(put_dn)
        e.finish(dn1)

        @pl.loop(0, rows // MIX)
        def _(t):
            at = rows_at(t, MIX)
            d = dn1[at]
            hat, rstd = norm_rows(x[at].astype(F32))
            sums[4:5] = sums[4:5] + jnp.sum(d * hat, axis=0, keepdims=True)
            sums[5:6] = sums[5:6] + jnp.sum(d, axis=0, keepdims=True)
            in_grad[at] = d_mid[at] + norm_back(d * full[0:1], hat, rstd)

        for k in range(2):
            g = g4[a * 2 + k, pl.ds(pl.multiple_of(h * hk, hk), hk)].astype(F32)
            for dh in range(1, H):
                landed(late.at[dh - 1, k], gr.at[2 + (dh - 1) * 2 + k])
                g = g + late[dh - 1, k].astype(F32)
            g_out[k] = g.astype(BF)
        cg.drain()
        bg.finish()

    out = comm_call(
        body,
        (
            jax.ShapeDtypeStruct((rows, D), F32),
            jax.ShapeDtypeStruct((2, hk, 4 * m), BF),
            jax.ShapeDtypeStruct((8, D), F32),
            *bg.outs(),
        ),
        [VM] * 7 + [ANY] * nb,
        (VM, VM, VM, *[ANY] * nb),
        [
            pltpu.VMEM((T, D), BF),
            pltpu.VMEM((nk, kk, 4 * m), BF),
            pltpu.VMEM((2, kk, 4 * m), BF),
            pltpu.VMEM((max(H - 1, 1), 2, hk, 4 * m), BF),
            pltpu.VMEM((rows, D), F32),
            pltpu.VMEM((2, 16, D), BF),
            pltpu.VMEM((8, 16, D), BF),
            *TeamSum.scratch(rows, D),
            DMA((2,)),
            DMA((8,)),
            DMA((2 + 2 * max(H - 1, 1),)),
            DMA((2 + 2 * max(H - 1, 1),)),
            *bg.sems(),
        ],
        6,
    )(d_all, mixed, diff, w4, full, x, d_mid, *bg.arrays())
    return out[0], out[1], out[2], out[3:]


def closing(lay, small, items):
    H, A, n = lay.H, lay.A, lay.n
    bg = Background(items, H)
    nb = len(items)

    def body(*refs):
        small, srcs, refs = refs[0], refs[1 : 1 + nb], refs[1 + nb :]
        total, dsts, refs = refs[0], refs[1 : 1 + nb], refs[1 + nb :]
        got, ss, sr = refs[:3]
        me = coords()
        a, b, h, l, c = (me[k] for k in ALL)
        sem = pltpu.get_barrier_semaphore()
        others = []
        for i in range(1, n):
            k = i
            dc, k = k % 2, k // 2
            dl, k = k % 2, k // 2
            dh, k = k % H, k // H
            db, da = k % 2, k // 2
            to = {
                "a": lax.rem(a + da, A),
                "b": b ^ db,
                "h": lax.rem(h + dh, H),
                "l": l ^ dl,
                "c": c ^ dc,
            }
            others.append((i, to))
            pl.semaphore_signal(sem, inc=1, device_id=to, device_id_type=MESH)
        pl.semaphore_wait(sem, n - 1)
        bg.start(me, srcs, dsts, refs[3:])
        copies = Copies(ss)

        def at(d):
            return (((d["a"] * 2 + d["b"]) * H + d["h"]) * 2 + d["l"]) * 2 + d["c"]

        for i, to in others:
            copies.go(small.at[at(to)], got.at[i], sr.at[i], to)
        acc = small[at(me)]
        for i, _ in others:
            landed(got.at[i], sr.at[i])
            acc = acc + got[i]
        total[...] = acc
        copies.drain()
        bg.finish()

    out = comm_call(
        body,
        (jax.ShapeDtypeStruct(small.shape[1:], F32), *bg.outs()),
        [VM] + [ANY] * nb,
        (VM, *[ANY] * nb),
        [pltpu.VMEM(small.shape, F32), DMA((n,)), DMA((n,)), *bg.sems()],
        7,
    )(small, *bg.arrays())
    return out[0], out[1:]


def dot(a, b, dims):
    return lax.dot_general(a, b, (dims, ((), ())), preferred_element_type=F32)


def mm(a, b):
    return dot(a, b, ((1,), (0,)))


def mm_nt(a, b):
    return dot(a, b, ((1,), (1,)))


def mm_tn(a, b):
    return dot(a, b, ((0,), (0,)))


class Layout:
    def __init__(self, mesh_shape):
        self.A, self.B, self.H, self.L, self.C = mesh_shape
        self.team = self.B * self.L * self.C
        self.n = self.team * self.A * self.H

    def of(self, D):
        self.strided = (D // self.n) % HEAD == 0
        return self

    def spread(self, v, whole):
        w = v.shape[-1] // self.n
        lead = v.shape[:-1]
        if w % whole:
            return v.reshape(*lead, self.team, -1)
        k = len(lead)
        v = v.reshape(*lead, self.A, self.B, self.H, self.L, self.C, w)
        v = v.transpose(*range(k), k + 1, k + 3, k + 4, k, k + 2, k + 5)
        return v.reshape(*lead, self.team, -1)

    def unspread(self, v, whole):
        lead = v.shape[:-2]
        w = v.shape[-1] * self.team // self.n
        if w % whole:
            return v.reshape(*lead, -1)
        k = len(lead)
        v = v.reshape(*lead, self.B, self.L, self.C, self.A, self.H, w)
        v = v.transpose(*range(k), k + 3, k, k + 4, k + 1, k + 2, k + 5)
        return v.reshape(*lead, -1)

    def rows_in(self, g):
        m = g.shape[-1]
        g = g.reshape(self.A, self.H, self.B, self.L, self.C, -1, m)
        return g.transpose(0, 2, 1, 3, 4, 5, 6).reshape(-1, m)

    def rows_out(self, g):
        m = g.shape[-1]
        g = g.reshape(self.A, self.B, self.H, self.L, self.C, -1, m)
        return g.transpose(0, 2, 1, 3, 4, 5, 6).reshape(self.A * self.H, self.team, -1, m)


def normed(v):
    mean = jnp.mean(v, axis=-1, keepdims=True)
    cent = v - mean
    rstd = lax.rsqrt(jnp.mean(cent * cent, axis=-1, keepdims=True) + EPS)
    return cent * rstd, rstd


def norm_back(e, xhat, rstd):
    m1 = jnp.mean(e, axis=-1, keepdims=True)
    m2 = jnp.mean(e * xhat, axis=-1, keepdims=True)
    return (e - m1 - xhat * m2) * rstd


def with_before(rows, halo, segs):
    v = rows.reshape(segs, -1, rows.shape[-1])
    return jnp.concatenate([halo, v[:, :-1]], axis=1).reshape(rows.shape)


def with_after(rows, segs):
    v = rows.reshape(segs, -1, rows.shape[-1])
    return (
        jnp.concatenate([v[:, 1:], jnp.zeros_like(v[:, :1])], axis=1).reshape(rows.shape),
        v[:, :1],
    )


def swap(v, axis):
    return lax.ppermute(v, axis, [(0, 1), (1, 0)])


def per_device(lay, *args):
    (x_in, up_in, start_in) = args[:3]
    vec = args[3:13]
    w_r, w_k, w_v, w_g, w_o = args[13:18]
    vec2 = args[18:22]
    w_ck, w_cv, w_cr = args[22:]
    a_at, b_at, h_at = (lax.axis_index(n) for n in ("a", "b", "h"))
    rank = (b_at * lay.L + lax.axis_index("l")) * lay.C + lax.axis_index("c")
    H = lay.H
    segs = lay.B
    D = x_in.shape[-1]
    x_own = x_in[0]
    rows = x_own.shape[0]
    T = rows * lay.team
    dcol = D // lay.team
    heads = dcol // HEAD
    half = lay.L * lay.C
    w_row = D // lay.n
    lay.of(D)
    hid = w_ck.shape[1] // lay.team

    stacked = jnp.stack([*vec, *vec2])
    nv = stacked.shape[0]
    stacked = jnp.pad(stacked, ((0, 16 - nv), (0, 128 - w_row)))
    spread4 = jnp.concatenate(
        [lay.spread(w, HEAD) for w in (w_r, w_k, w_v, w_g)], axis=-1
    ).transpose(1, 0, 2)
    ffn = jnp.concatenate([lay.spread(w_ck, 1), lay.spread(w_cr, D)], axis=-1).transpose(1, 0, 2)
    o_own = w_o
    if not lay.strided:
        o_own = lax.all_gather(w_o, ALL, axis=0, tiled=True)
        o_own = lax.dynamic_slice_in_dim(o_own, rank * dcol, dcol, 0)
        o_own = o_own.reshape(lay.A, H, -1, D)
    early = w_cv.shape[0] // 3 // 16 * 16 if w_cv.shape[0] % 16 == 0 else 0
    every, my_vecs, mixed, diff1, rkv, gate, upc, W4, team, W_o, cv_first = opening(
        lay, stacked, x_own, up_in[0], spread4, ffn, o_own, w_cv, early
    )
    nh = start_in.shape[1]
    head_ids = jnp.arange(nh * HEAD, dtype=jnp.int32)

    def heads_of(p):
        ids = lax.dynamic_index_in_dim(lay.spread(head_ids, HEAD), p, 0, False)
        return ids[::HEAD] // HEAD

    my_heads = heads_of(rank)
    own_start = jnp.take(start_in[0], my_heads, axis=0)
    got_start = swap(jnp.take(start_in[0], heads_of(rank ^ 4), axis=0), "b")
    start = jnp.where(b_at == 0, jnp.stack([own_start, got_start]), jnp.stack([got_start, own_start]))
    eye = jnp.eye(heads, dtype=F32)
    start = jnp.einsum("sgcv,gj->sgvjc", start, eye).reshape(segs, dcol, dcol)
    gated, ghat, grstd, states, fin, middle, n2, halo_2, W_cv, ffn_all = time_mix(
        lay, rkv, gate, my_vecs, every, start, x_own, W_o, w_cv, cv_first, early, team
    )
    W_cv = W_cv.reshape(hid, D)
    s_out = jnp.einsum("sgvgc->sgcv", fin.reshape(segs, heads, HEAD, heads, HEAD))

    placed = jnp.zeros((segs, nh, HEAD, HEAD), BF)
    s_fin = jnp.where(h_at == lay.H - 1, s_out, 0.0).astype(BF)
    placed = placed.at[:, my_heads].set(s_fin)
    final = lax.psum_scatter(placed, "b", scatter_dimension=0, tiled=True)
    final = lax.psum_scatter(final, SEQ, scatter_dimension=1, tiled=True).astype(F32)

    wf = ffn_all.reshape(2 * lay.A, D // (2 * lay.A), -1)
    d_mid, d_br, moved, s_cv, got_cv, g_f, got_f, cm_sums = channel_mix(
        lay, n2, halo_2, every, W_cv, wf, upc.reshape(T, dcol), middle, up_in[0]
    )
    layer_output = (middle + moved.transpose(1, 0, 2).reshape(rows, D).astype(F32)).astype(BF)
    g_cv = s_cv.astype(F32) + jnp.sum(got_cv.astype(F32), axis=0)

    def own_half(g, got):
        part = lax.dynamic_index_in_dim(g, a_at, 0, False).astype(F32) + got.astype(F32)
        part = part.astype(BF).reshape(part.shape[0], H, -1, part.shape[-1])
        return part.transpose(1, 0, 2, 3)

    def total(part, got):
        own = lax.dynamic_index_in_dim(part, h_at, 0, False).astype(F32)
        return own + jnp.sum(got.astype(F32), axis=0)

    s_f = own_half(g_f, got_f)
    g_o, d_all, tm_sums, (got_f2,) = time_mix_back(
        lay, d_br, W_o, gated, ghat, grstd, gate, rkv, states, my_vecs, [(s_f, "h")]
    )
    d_l, d_u, g_gs, g_gb = tm_sums[:4]
    t_f = total(s_f, got_f2).astype(BF).reshape(lay.team, -1, hid + dcol)
    w4 = W4.reshape(2 * lay.A, D // (2 * lay.A), -1)
    items = [(t_f, "t")] + ([(g_o, "a")] if lay.strided else [])
    input_grad, g_4, ti_sums, (moved_f, *got_o) = time_in_back(
        lay, d_all, mixed, diff1, w4, every, x_own, d_mid, items
    )
    if lay.strided:
        s_o = lax.dynamic_index_in_dim(g_o, a_at, 0, False).astype(F32) + got_o[0].astype(F32)
        s_o = s_o.astype(BF)
    else:
        g_o = jnp.zeros((D, D), BF).at[rank * dcol + jnp.arange(dcol)].set(g_o.reshape(dcol, D))
        g_o = lax.psum_scatter(g_o, ALL, scatter_dimension=0, tiled=True).astype(F32)

    def in_place(v):
        spread = jnp.where(jnp.arange(lay.team)[:, None] == rank, v.reshape(1, -1), 0.0)
        return lay.unspread(spread, HEAD)

    small = jnp.stack(
        [*ti_sums[4:6], *ti_sums[:4], in_place(d_l), in_place(d_u), in_place(g_gs), in_place(g_gb)]
        + [*cm_sums[2:4], *cm_sums[:2]]
    )
    small = small.reshape(nv, lay.n, w_row).transpose(1, 0, 2)
    small = jnp.pad(small, ((0, 0), (0, 16 - nv), (0, 128 - w_row)))
    items = [(g_4.reshape(lay.team, -1, 4 * dcol), "t")] + ([(s_o, "h")] if lay.strided else [])
    small, (g_4, *got_o) = closing(lay, small, items)
    if lay.strided:
        g_o = total(s_o, got_o[0])
    small = small[:nv, :w_row]

    def columns(got, lo, hi, unit):
        return lay.unspread(got[:, :, lo:hi].transpose(1, 0, 2), unit).astype(F32)

    g_r, g_k, g_v, g_w = (columns(g_4, i * dcol, (i + 1) * dcol, HEAD) for i in range(4))
    g_ck, g_cr = columns(moved_f, 0, hid, 1), columns(moved_f, hid, hid + dcol, D)
    return (
        layer_output[None],
        input_grad[None],
        final,
        *(small[i] for i in range(10)),
        g_r,
        g_k,
        g_v,
        g_w,
        g_o,
        *(small[i] for i in range(10, 14)),
        g_ck,
        g_cv,
        g_cr,
    )


def solution(mesh):
    n_seg, n_seq = mesh.devices.shape
    shape = (n_seg // 2, 2, n_seq // 4, 2, 2)
    view = Mesh(mesh.devices.reshape(shape), ALL)
    lay = Layout(shape)
    seg = ("a", "b")
    vec, mat = P(ALL), P(ALL, None)
    tok = P(seg, SEQ, None)

    def step(*args):
        return per_device(lay, *args)

    return jax.shard_map(
        step,
        mesh=view,
        in_specs=(tok, tok, P(seg, None, None, None), *[vec] * 10, *[mat] * 5, *[vec] * 4, *[mat] * 3),
        out_specs=(tok, tok, P(seg, SEQ, None, None), *[vec] * 10, *[mat] * 5, *[vec] * 4, *[mat] * 3),
        check_vma=False,
    )
```

time: 1070 us -> 751 us (0.70)
  Pallas kernels: 343 us -> 644 us
  matrix products: 161 us -> 0 us
  waiting for transfers between devices: 154 us -> 0.04 us
  other arithmetic: 168 us -> 23.5 us
  local copies, waits for them, and re-layouts: 185 us -> 60.4 us
  starting transfers between devices: 29.5 us -> 3.02 us
    pallas_call x9 -> x6, Pallas kernels: 343 us -> 644 us  [the longest x1 168 us: channel_mix(): comm_call(body, (jax.ShapeDtypeStruct((rows, D), F32), jax.ShapeDtypeStru...]
    dot_general x36 -> x0, matrix products: 161 us -> none  [the longest x24 127 us: dot(): return lax.dot_general(a, b, (dims, ((), ())), preferred_element_type=F32)]
    ppermute x16 -> x0, waiting for transfers between devices: 121 us -> none  [the longest x7 108 us: shifted(): return lax.ppermute(v, 'h', [(i, (i + dh) % H) for i in range(H)])]
    convert_element_type x18 -> x4, other arithmetic: 87.4 us -> 8.64 us  [the longest x1 2.94 us: own_half(): part = part.astype(BF).reshape(part.shape[0], H, -1, part.shape[-1])]
    reduce_scatter x1, waiting for transfers between devices: 23.2 us -> 0.01 us  [per_device(): lax.psum_scatter(final, SEQ, scatter_dimension=1, tiled=True).astype(F32)]
    reshape x12 -> x3, local copies, waits for them, and re-layouts: 26.4 us -> 3.47 us  [the longest x1 1.61 us: own_half(): part = part.astype(BF).reshape(part.shape[0], H, -1, part.shape[-1])]
    concatenate x4 -> x0, local copies, waits for them, and re-layouts: 22.1 us -> none  [the longest x2 13.1 us: shares_out(): whole = jnp.concatenate([g.astype(BF) for g in pieces], axis=1)]
    reduce_sum x15 -> x1, other arithmetic: 19.1 us -> 0.39 us  [per_device(): jnp.einsum('sgvgc->sgcv', fin.reshape(segs, heads, HEAD, heads, HEAD))]
  transfers between devices with their start and end apart: 29 -> 3, of which waited for: 8 -> 0; matrix products, arithmetic and copies ran while one was open for 33% -> 8% of each run, Pallas kernels for 14% -> 20%
where the time goes in v3:
time: 751 us; the launch traced here: 746 us
  Pallas kernels  644 us (86%)
  local copies, waits for them, and re-layouts  60.4 us (8%)
  other arithmetic  23.5 us (3%)
  between operations  15.3 us (2%)
    pallas_call x1, Pallas kernels, channel_mix(): comm_call(body, (jax.ShapeDtypeStruct((rows, D), F32), jax.ShapeDtypeStru...  168 us
    pallas_call x1, Pallas kernels, time_mix(): comm_call(body, (jax.ShapeDtypeStruct((T, m), BF), jax.ShapeDtypeStruct((...  145 us
    pallas_call x1, Pallas kernels, opening(): comm_call(body, (jax.ShapeDtypeStruct((16, D), F32), jax.ShapeDtypeStruct...  115 us
    pallas_call x1, Pallas kernels, time_in_back(): comm_call(body, (jax.ShapeDtypeStruct((rows, D), F32), jax.ShapeDtypeStru...  106 us
    pallas_call x1, Pallas kernels, time_mix_back(): comm_call(body, (jax.ShapeDtypeStruct(wo.shape, BF), jax.ShapeDtypeStruct...  78.9 us
    pallas_call x1, Pallas kernels, closing(): comm_call(body, (jax.ShapeDtypeStruct(small.shape[1:], F32), *bg.outs()),...  31.1 us
    convert_element_type x16, local copies, waits for them, and re-layouts, columns(): return lay.unspread(got[:, :, lo:hi].transpose(1, 0, 2), unit).astype(F32)  28.8 us
  transfers between devices with their start and end apart: 3, of which 0 were waited for; matrix products, arithmetic and copies ran while one was open for 8% of the time, Pallas kernels for 20%

profile of v3, /device:TPU:0, one launch (start us, length us, event | category | flops | bytes accessed | tf_op | source)
XLA Modules:
  0.0 746.0 jit_solution(3422951105349863793)
XLA Ops:
  8.4 0.6 gather_fusion.1
  9.0 0.7 broadcast_select_fusion
  9.7 2.9 collective-permute-start
  12.8 0.6 gather_fusion
  13.4 1.0 copy.117
  14.3 1.5 reshape.414
  15.8 0.4 copy.116
  16.6 0.5 reshape.416
  17.1 0.4 copy.115
  17.9 0.5 reshape.418
  18.4 0.4 copy.114
  19.2 0.5 reshape.420
  20.5 4.9 reshape.422
  25.4 0.8 copy.112
  26.2 0.8 reshape.423
  27.0 1.6 stack.85
  28.6 0.6 pad.8.refs_0_
  29.2 1.1 maximum_bitcast_fusion.refs_4_
  30.4 1.1 maximum_bitcast_fusion.1.refs_3_
  31.5 115.0 %shard_map.432 = (f32[16,2048]{1,0:T(8,128)}, f32[16,256]{1,0:T(8,128)}, bf16[4,1024,2048]{2,1,0:T(8,128)(2,1)}, bf16[1024,2048]{1,0:T(8,128)(2,1)}, bf16[3,1024...) custom-call(bf16[16,128]{1,0:T(8,128)(2,1)} %pad.8.refs_0_, ...), custom_call_target="tpu_custom_call" | custom-call | tf_op jit(solution)/shard_map/pallas_call | solution.py:623
  146.5 1.0 fusion.4
  147.9 1.4 reshape.445.refs_4_
  149.3 144.8 %shard_map.433 = (bf16[1024,256]{1,0:T(8,128)(2,1)}, f32[1024,256]{1,0:T(8,128)}, f32[1024,256]{1,0:T(8,128)}, f32[2,4,256,256]{3,2,1,0:T(8,128)}, f32[2,256,256...) custom-call(bf16[3,1024,256]{2,1,0:T(8,128)(2,1)} %get-tuple-element, ...), custom_call_target="tpu_custom_call" | custom-call | tf_op jit(solution)/shard_map/pallas_call | solution.py:886
  294.1 167.6 %shard_map.434 = (f32[128,2048]{1,0:T(8,128)}, bf16[8,128,2048]{2,1,0:T(8,128)(2,1)}, bf16[8,128,256]{2,1,0:T(8,128)(2,1)}, bf16[224,2048]{1,0:T(8,128)(2,1)}, b...) custom-call(bf16[8,128,2048]{2,1,0:T(8,128)(2,1)} %get-tuple-element, ...), custom_call_target="tpu_custom_call" | custom-call | tf_op jit(solution)/shard_map/pallas_call | solution.py:1353
  461.7 2.9 fusion
  464.6 1.6 copy.111
  466.3 78.9 %shard_map.435 = (bf16[2,2,64,2048]{3,2,1,0:T(8,128)(2,1)}, bf16[1024,1024]{1,0:T(8,128)(2,1)}, f32[8,256]{1,0:T(8,128)}, bf16[1,2,256,1152]{3,2,1,0:T(8,128)(2,1)}) custom-call(bf16[8,128,2048]{2,1,0:T(8,128)(2,1)} %get-tuple-element.81.refs_0_, bf16[2,2,64,2048]{3,2,1,0:T(8,128)(2,1)} %get-tuple-element.71.refs_6_.refs_1_, ...), custom_call_target="tpu_custom_call" | custom-call | tf_op jit(solution)/shard_map/pallas_call | solution.py:1033
  545.3 2.6 fusion.1.refs_7_
  547.9 106.4 %shard_map.436 = (f32[128,2048]{1,0:T(8,128)}, bf16[2,256,1024]{2,1,0:T(8,128)(2,1)}, f32[8,2048]{1,0:T(8,128)}, bf16[8,64,1152]{2,1,0:T(8,128)(2,1)}, bf16[2,64,2048]{2,1,0:T(8,128)(2,1)}) custom-call(bf16[1024,1024]{1,0:T(8,128)(2,1)} %get-tuple-element.88.refs_0_, bf16[4,1024,2048]{2,1,0:T(8,128)(2,1)} %get-tuple-element.89.refs_1_, ...), custom_call_target="tpu_custom_call" | custom-call | tf_op jit(solution)/shard_map/pallas_call | solution.py:1513
  654.2 0.8 unstack.30
  655.1 0.8 unstack.31
  655.9 0.5 reshape.451
  657.2 0.7 scatter_fusion
  658.0 1.0 copy-done.2
  659.3 1.2 convert_bitcast_fusion.1
  660.5 2.0 fusion.2.refs_2_
  663.1 1.4 convert_bitcast_fusion
  664.9 0.7 pad.9.refs_0_
  665.6 31.1 %shard_map.437 = (f32[16,128]{1,0:T(8,128)}, bf16[8,64,1024]{2,1,0:T(8,128)(2,1)}, bf16[1,64,2048]{2,1,0:T(8,128)(2,1)}) custom-call(f32[32,16,128]{2,1,0:T(8,128)} %pad.9.refs_0_, bf16[8,64,1024]{2,1,0:T(8,128)(2,1)} %bitcast.180, bf16[2,64,2048]{2,1,0:T(8,128)(2,1)} %fusion.2.refs_2_), custom_call_target="tpu_custom_call" | custom-call | tf_op jit(solution)/shard_map/pallas_call | solution.py:1588
  696.7 2.7 convert_bitcast_fusion.2
  699.4 1.0 convert_bitcast_fusion.6
  700.4 0.9 add_bitcast_fusion
  701.3 1.5 convert_add_fusion.2
  702.8 0.6 slice_bitcast_fusion
  703.8 1.3 copy.89
  705.1 0.8 copy.103
  705.9 4.8 reshape.469
  710.7 3.0 copy.100
  713.6 5.2 reshape.462
  718.9 0.6 reshape.468
  719.5 0.8 copy.99
  720.3 1.8 reshape.461
  722.1 0.6 reshape.467
  722.7 0.8 copy.98
  723.5 1.8 reshape.460
  725.3 0.6 reshape.466
  725.9 0.8 copy.97
  726.8 1.8 reshape.459
  728.5 0.6 reshape.465
  729.2 1.8 copy.96
  731.0 3.1 reshape.458
  734.0 0.9 fusion.3
  734.9 1.5 convert_element_type.170
  736.4 2.3 copy.120
  (108 shorter events, 6.1 us)
Async XLA Ops:
  7.2 1.2 copy-start
  7.2 9.4 %copy-start.15 = (bf16[64,2048]{1,0:T(8,128)(2,1)S(1)}, bf16[64,2048]{1,0:T(8,128)(2,1)}, u32[]{:S(2)}) copy-start(bf16[64,2048]{1,0:T(8,128)(2,1)} %param.41) | copy-start | bytes 786436
  7.2 695.6 %reduce-scatter.3.cloned.1.call-start = ((), (), s32[]{:S(2)}) async-start(), calls=%async_computation.2 | async-start | bytes 1572864 | tf_op jit(solution)/shard_map/reduce_scatter | solution.py:1745
  9.7 136.8 %collective-permute-start = (f32[4,64,64]{2,1,0:T(8,128)}, f32[4,64,64]{2,1,0:T(8,128)}, u32[]{:S(2)}, u32[]{:S(2)}) collective-permute-start(f32[4,64,64]{2,1,0:T(8,128)} %broadcast_select_fusion), channel_id=1, source_target_pairs={{0,8},{8,0},{1,9},{9,1},{2,10},{10,2},{3,11},{11,3},{4,12},{12,4},... | collective-permute-start | bytes 196616 | tf_op jit(solution)/shard_map/ppermute | solution.py:1683
  15.8 2.1 copy-start.16
  17.1 2.1 copy-start.17
  547.9 108.1 %copy-start.14 = (f32[2,256,256]{2,1,0:T(8,128)S(1)}, f32[2,256,256]{2,1,0:T(8,128)}, u32[]{:S(2)}) copy-start(f32[2,256,256]{2,1,0:T(8,128)} %get-tuple-element.96) | copy-start | bytes 1572868
  656.4 2.7 copy-start.19
  657.0 3.5 copy-start.6
  658.0 1.0 copy-start.2
  658.0 4.5 copy-start.21
  659.0 4.1 copy-start.11
  659.0 75.9 %reduce-scatter.5.cloned.1.call-start = ((), (), s32[]{:S(2)}) async-start(), calls=%async_computation.3 | async-start | bytes 589824 | tf_op jit(solution)/shard_map/reduce_scatter | solution.py:1746
  696.6 3.8 copy-start.5
  696.7 3.8 copy-start.18
  696.7 4.6 copy-start.12
  696.7 4.6 copy-start.13
  701.3 1.6 copy-start.20
  713.6 5.2 copy-start.10
  719.5 2.6 copy-start.9
  722.7 2.6 copy-start.8
  725.9 2.6 copy-start.7
  729.1 4.9 copy-start.3
  729.1 4.9 copy-start.4
  730.9 7.8 %copy-start.1 = (f32[1,32,64,64]{3,2,1,0:T(8,128)S(1)}, f32[1,32,64,64]{3,2,1,0:T(8,128)}, u32[]{:S(2)}) copy-start(f32[1,32,64,64]{3,2,1,0:T(8,128)} %param.29) | copy-start | bytes 1572868
Sparse Core Ops, SparseCore 0:
  659.1 24.0 reduce-scatter.2
  703.0 28.7 reduce-scatter.4

commit v4 on v3

v4 whole, which is shorter than its diff:
```python
import jax
import jax.numpy as jnp
from jax import lax
from jax.experimental import pallas as pl
from jax.experimental.pallas import tpu as pltpu
from jax.sharding import Mesh, PartitionSpec as P

TEAM = ("b", "l", "c")
TEAMS = ("a", "h")
SEQ = ("h", "l", "c")
ALL = ("a", "b", "h", "l", "c")
HEAD = 64
CHUNK = 128
EPS = 1e-05
GROUP_EPS = 0.00064
BF = jnp.bfloat16
F32 = jnp.float32


MESH = pl.DeviceIdType.MESH
DMA = pltpu.SemaphoreType.DMA
VMEM_BYTES = 62 << 20


def coords():
    return {name: lax.axis_index(name) for name in ALL}


def rank_of(b, l, c):
    return (b * 2 + l) * 2 + c


def remote(src, dst, sent, landed, to):
    return pltpu.make_async_remote_copy(
        src_ref=src,
        dst_ref=dst,
        send_sem=sent,
        recv_sem=landed,
        device_id=to,
        device_id_type=MESH,
    )


def mates(me):
    for m in range(1, 8):
        yield m, {"b": me["b"] ^ (m >> 2), "l": me["l"] ^ ((m >> 1) & 1), "c": me["c"] ^ (m & 1)}


def greet(me, H, column, across):
    sem = pltpu.get_barrier_semaphore()
    count = 0
    for dh in range(H if column else 1):
        h = lax.rem(me["h"] + dh, H)
        for m in range(8):
            if dh == 0 and m == 0:
                continue
            to = {
                "b": me["b"] ^ (m >> 2),
                "h": h if column else me["h"],
                "l": me["l"] ^ ((m >> 1) & 1),
                "c": me["c"] ^ (m & 1),
            }
            pl.semaphore_signal(sem, inc=1, device_id=to, device_id_type=MESH)
            count += 1
    if across:
        pl.semaphore_signal(sem, inc=1, device_id={"a": 1 - me["a"]}, device_id_type=MESH)
        count += 1
    pl.semaphore_wait(sem, count)


class Copies:
    def __init__(self, sems):
        self.sems, self.k, self.open = sems, 0, []

    def go(self, src, dst, landed, to):
        copy = remote(src, dst, self.sems.at[self.k], landed, to)
        self.k += 1
        copy.start()
        self.open.append(copy)

    def drain(self):
        for copy in self.open:
            copy.wait_send()


def landed(ref, sem):
    remote(ref, ref, sem, sem, {"c": 1 - lax.axis_index("c")}).wait_recv()


def upper(ref, half):
    n = ref.shape[0] // 2
    return ref.at[pl.ds(half * n, n)]


class TeamGather:
    def __init__(self, me, own, view, send, recv, via=("xz", "zx")):
        self.me, self.own, self.view, self.recv, self.via = me, own, view, recv, via
        self.copies = Copies(send)
        self.tx, self.tz, self.ts = {"b": 1 - me["b"]}, {"l": 1 - me["l"]}, {"c": 1 - me["c"]}

    def put(self, src, p, half, to):
        self.copies.go(src, upper(self.view(p), half), self.recv.at[p, half], to)

    def start(self):
        mine = rank_of(self.me["b"], self.me["l"], self.me["c"])
        order = [(half, self.tx if self.via[half] == "xz" else self.tz) for half in range(2)]
        order += [(half, self.tz if self.via[half] == "xz" else self.tx) for half in range(2)]
        order += [(0, self.ts), (1, self.ts)]
        for half, to in order:
            self.put(upper(self.own, half), mine, half, to)

    def finish(self):
        b, l, c = self.me["b"], self.me["l"], self.me["c"]
        px, pz, pd = rank_of(1 - b, l, c), rank_of(b, 1 - l, c), rank_of(1 - b, 1 - l, c)
        order = [
            (px, half, self.tz) if self.via[half] == "xz" else (pz, half, self.tx)
            for half in range(2)
        ]
        order += [
            (pz, half, None) if self.via[half] == "xz" else (px, half, None) for half in range(2)
        ]
        for p, half, on in order + [(pd, 0, None), (pd, 1, None)]:
            block = upper(self.view(p), half)
            landed(block, self.recv.at[p, half])
            if on is not None:
                self.put(block, p, half, on)
            self.put(block, p, half, self.ts)
        for q in range(4):
            p = q * 2 + 1 - c
            for half in range(2):
                landed(upper(self.view(p), half), self.recv.at[p, half])
        self.copies.drain()


class TeamSum:
    def __init__(self, me, part, near, acc, mid, far, send, recv, via=("xz", "zx")):
        self.me, self.part, self.near, self.acc, self.mid, self.far = me, part, near, acc, mid, far
        self.recv, self.via = recv, via
        self.copies = Copies(send)

    def start(self):
        b, l, c = self.me["b"], self.me["l"], self.me["c"]
        self.spots = [(b, l), (1 - b, l), (b, 1 - l), (1 - b, 1 - l)]
        for i in (3, 1, 2, 0):
            bb, ll = self.spots[i]
            self.copies.go(
                self.part(rank_of(bb, ll, 1 - c)), self.near.at[i], self.recv.at[i], {"c": 1 - c}
            )

    def tiles(self, rows, body):
        step = max(16, 65536 // self.near.shape[2])

        @pl.loop(0, rows // step)
        def _(t):
            body(pl.ds(pl.multiple_of(t * step, step), step))

    def pair(self, i, write):
        bb, ll = self.spots[i]
        landed(self.near.at[i], self.recv.at[i])
        mine = self.part(rank_of(bb, ll, self.me["c"]))
        self.tiles(
            self.near.shape[1], lambda at: write(at, mine[at].astype(F32) + self.near[i, at].astype(F32))
        )

    def finish(self, write, then=lambda: None):
        b, l = self.me["b"], self.me["l"]
        tx, tz = {"b": 1 - b}, {"l": 1 - l}
        acc, mid, far, recv, go = self.acc, self.mid, self.far, self.recv, self.copies.go
        n = mid.shape[1]
        hops = [
            (tx, 0, tz, 1) if self.via[half] == "xz" else (tz, 1, tx, 0) for half in range(2)
        ]
        for i in (3, 1, 2):

            def put(at, v):
                acc[i - 1, at] = v.astype(BF)

            self.pair(i, put)
            if i == 3:
                for half, (one, _, _, _) in enumerate(hops):
                    go(upper(acc.at[2], half), mid.at[half], recv.at[4 + half], one)
        for half, (one, direct, two, other) in enumerate(hops):
            landed(mid.at[half], recv.at[4 + half])
            into, came = upper(acc.at[other], half), mid.at[half]

            def add(at):
                into[at] = (into[at].astype(F32) + came[at].astype(F32)).astype(BF)

            self.tiles(n, add)
            go(into, upper(far.at[other], half), recv.at[8 + half], two)
            go(upper(acc.at[direct], half), upper(far.at[direct], half), recv.at[6 + half], one)
        then()
        for half, (_, direct, _, other) in enumerate(hops):
            landed(upper(far.at[direct], half), recv.at[6 + half])
            landed(upper(far.at[other], half), recv.at[8 + half])

        def last(at, v):
            write(at, v + far[0, at].astype(F32) + far[1, at].astype(F32))

        self.pair(0, last)
        self.copies.drain()

    @staticmethod
    def scratch(R, C):
        return [
            pltpu.VMEM((4, R, C), BF),
            pltpu.VMEM((3, R, C), BF),
            pltpu.VMEM((2, R // 2, C), BF),
            pltpu.VMEM((2, R, C), BF),
            DMA((10,)),
            DMA((10,)),
        ]


class TeamsGather:
    def __init__(self, me, H, source, out, send, near, far, team=None, count=2):
        self.me, self.H, self.source, self.out = me, H, source, out
        self.near, self.far, self.team, self.count = near, far, team, count
        self.copies = Copies(send)

    @staticmethod
    def sems(H, count=2):
        return [DMA((7 + count * (2 * H - 1),)), DMA((8,)), DMA((2 * H, count))]

    def groups(self, only=None):
        b, n = self.me["b"], 8 // self.count
        for g in range(self.count):
            if only is None or g in only:
                at = g * n
                yield g, (b if at < 4 else 1 - b), at % 4, n

    def block(self, a, bb, h, lo, n):
        return self.out.at[a, bb, h, pl.ds(lo, n)]

    def start(self):
        me = self.me
        a, b, h, l, c = (me[n] for n in ALL)
        for m, to in mates(me):
            p = rank_of(to["b"], to["l"], to["c"])
            mine = rank_of(b, l, c)
            self.copies.go(self.source(p), self.out.at[a, b, h, l * 2 + c], self.near.at[mine], to)

    def spread(self, local=None, only=None):
        me = self.me
        a, b, h, l, c = (me[n] for n in ALL)
        if local is not None:
            local.wait()
        for g, bb, lo, n in self.groups(only):
            block = self.block(a, bb, h, lo, n)
            src = block
            if self.team is not None:
                src = self.team.at[pl.ds(bb * 4 + lo, n)]
            else:
                for m in range(1 - g, 4):
                    ll, cc = l ^ (m >> 1), c ^ (m & 1)
                    landed(self.out.at[a, bb, h, ll * 2 + cc], self.near.at[rank_of(bb, ll, cc)])
            for dh in range(1, self.H):
                to = lax.rem(h + dh, self.H)
                self.copies.go(src, block, self.far.at[dh, g], {"h": to})
            self.copies.go(src, block, self.far.at[0, g], {"a": 1 - a})

    def forward(self, only=None):
        a, h, H = self.me["a"], self.me["h"], self.H
        for g, bb, lo, n in self.groups(only):
            for dh in range(1, H):
                block = self.block(a, bb, lax.rem(h - dh + H, H), lo, n)
                landed(block, self.far.at[dh, g])
                self.copies.go(block, block, self.far.at[H - 1 + dh, g], {"a": 1 - a})

    def finish(self):
        a, h, H = self.me["a"], self.me["h"], self.H
        for g, bb, lo, n in self.groups():
            landed(self.block(1 - a, bb, h, lo, n), self.far.at[0, g])
            for dh in range(1, H):
                block = self.block(1 - a, bb, lax.rem(h - dh + H, H), lo, n)
                landed(block, self.far.at[H - 1 + dh, g])
        self.copies.drain()


class Halo:
    def __init__(self, me, H, own, out, send, recv):
        self.me, self.H, self.own, self.out, self.send, self.recv = me, H, own, out, send, recv
        self.last = (me["l"] == 1) & (me["c"] == 1) & (me["h"] < H - 1)

    def each(self):
        me = self.me
        n = self.own.shape[0]
        for p in range(8):
            to = {
                "b": p >> 2,
                "h": jnp.minimum(me["h"] + 1, self.H - 1),
                "l": (p >> 1) & 1,
                "c": p & 1,
            }
            src = self.own.at[pl.ds(n - 16, 16)]
            yield remote(src, self.out.at[me["b"]], self.send.at[p], self.recv.at[me["b"]], to)

    def start(self):
        if self.H == 1:
            return

        @pl.when(self.last)
        def _():
            for copy in self.each():
                copy.start()

    def finish(self):
        if self.H == 1:
            return

        @pl.when(self.me["h"] > 0)
        def _():
            for b in range(2):
                landed(self.out.at[b], self.recv.at[b])

        @pl.when(self.last)
        def _():
            for copy in self.each():
                copy.wait_send()


class Edge:
    def __init__(self, me, H, first, got, send, recv):
        self.me, self.H, self.first, self.got, self.send, self.recv = me, H, first, got, send, recv

    def each(self):
        me = self.me
        mine = rank_of(me["b"], me["l"], me["c"])
        for b in range(2):
            to = {"b": b, "h": jnp.maximum(me["h"] - 1, 0), "l": 1, "c": 1}
            yield remote(self.first.at[b], self.got.at[mine], self.send.at[b], self.recv.at[mine], to)

    def start(self):
        if self.H == 1:
            return

        @pl.when(self.me["h"] > 0)
        def _():
            for copy in self.each():
                copy.start()

    def finish(self, out):
        if self.H == 1:
            return
        me = self.me

        @pl.when((me["l"] == 1) & (me["c"] == 1) & (me["h"] < self.H - 1))
        def _():
            for p in range(8):
                landed(self.got.at[p], self.recv.at[p])
            total = self.got[0, 0:1].astype(F32)
            for p in range(1, 8):
                total = total + self.got[p, 0:1].astype(F32)
            n = out.shape[0]
            out[n - 1 : n] = out[n - 1 : n] + total

        @pl.when(me["h"] > 0)
        def _():
            for copy in self.each():
                copy.wait_send()


class Exchange:
    def __init__(self, me, source, out, send, recv):
        self.me, self.source, self.out, self.recv = me, source, out, recv
        self.copies = Copies(send)

    def start(self):
        mine = rank_of(self.me["b"], self.me["l"], self.me["c"])
        for m, to in mates(self.me):
            p = rank_of(to["b"], to["l"], to["c"])
            self.copies.go(self.source(p), self.out(mine), self.recv.at[mine], to)

    def finish(self):
        for m, to in mates(self.me):
            p = rank_of(to["b"], to["l"], to["c"])
            landed(self.out(p), self.recv.at[p])
        self.copies.drain()


ANY = pl.BlockSpec(memory_space=pl.ANY)
VM = pl.BlockSpec(memory_space=pltpu.VMEM)


def comm_call(body, outs, in_specs, out_specs, scratch, cid):
    return pl.pallas_call(
        body,
        out_shape=outs,
        in_specs=in_specs,
        out_specs=out_specs,
        scratch_shapes=scratch,
        compiler_params=pltpu.CompilerParams(
            collective_id=cid, has_side_effects=True, vmem_limit_bytes=VMEM_BYTES
        ),
    )


def dot_nn(a, b):
    return jnp.dot(a, b, preferred_element_type=F32)


def dot_nt(a, b):
    return lax.dot_general(a, b, (((1,), (1,)), ((), ())), preferred_element_type=F32)


def dot_tn(a, b):
    return lax.dot_general(a, b, (((0,), (0,)), ((), ())), preferred_element_type=F32)


MIX = 32


def rows_at(i, n):
    return pl.ds(pl.multiple_of(i * n, n), n)


class RowsGather:
    def __init__(self, me, H, own, out, send, recv, at=None):
        self.me, self.H, self.own, self.out, self.recv, self.at = me, H, own, out, recv, at
        self.copies = Copies(send)

    @staticmethod
    def sems(H):
        return [DMA((2 * H - 1,)), DMA((2 * H,))]

    def block(self, a, h):
        return self.out.at[a, h] if self.at is None else self.out.at[a, h, self.at]

    def start(self):
        a, h = self.me["a"], self.me["h"]
        block = self.block(a, h)
        for dh in range(1, self.H):
            to = lax.rem(h + dh, self.H)
            self.copies.go(self.own, block, self.recv.at[dh], {"h": to})
        self.copies.go(self.own, block, self.recv.at[0], {"a": 1 - a})

    def forward(self):
        a, h, H = self.me["a"], self.me["h"], self.H
        for dh in range(1, H):
            block = self.block(a, lax.rem(h - dh + H, H))
            landed(block, self.recv.at[dh])
            self.copies.go(block, block, self.recv.at[H - 1 + dh], {"a": 1 - a})

    def finish(self):
        a, h, H = self.me["a"], self.me["h"], self.H
        landed(self.block(1 - a, h), self.recv.at[0])
        for dh in range(1, H):
            landed(self.block(1 - a, lax.rem(h - dh + H, H)), self.recv.at[H - 1 + dh])
        self.copies.drain()


def join_lanes(pieces, width):
    per = 128 // width
    out = []
    for g in range(0, len(pieces), per):
        acc = pieces[g]
        for k in range(1, per):
            acc = acc + pltpu.roll(pieces[g + k], width * k, axis=1)
        out.append(acc)
    return jnp.concatenate(out, axis=1) if len(out) > 1 else out[0]


def norm_rows(v):
    mean = jnp.mean(v, axis=-1, keepdims=True)
    cent = v - mean
    rstd = lax.rsqrt(jnp.mean(cent * cent, axis=-1, keepdims=True) + EPS)
    return cent * rstd, rstd


def mix_rows(read, first, carry, shares, write, tiles, rows):
    per = tiles // 2

    @pl.loop(0, tiles)
    def _(p):
        n = read(p)
        prev = jnp.where(lax.rem(p, per) == 0, first(p // per), carry[...])
        row = lax.broadcasted_iota(jnp.int32, n.shape, 0)
        before = jnp.where(row == 0, prev, pltpu.roll(n, 1, axis=0))
        carry[...] = n[rows - 1 : rows]
        diff = n - before
        for i, s in enumerate(shares):
            write(i, p, (before + s * diff).astype(BF))
        write(None, p, diff.astype(BF))


def block_ones(m):
    row = lax.broadcasted_iota(jnp.int32, (m, m), 0) // HEAD
    col = lax.broadcasted_iota(jnp.int32, (m, m), 1) // HEAD
    return jnp.where(row == col, 1.0, 0.0).astype(F32)


def dot_exact(a, b):
    return jnp.dot(a, b, preferred_element_type=F32, precision=lax.Precision.HIGHEST)


class Decay:
    def __init__(self, lam):
        m = lam.shape[1]
        i = lax.broadcasted_iota(jnp.int32, (CHUNK, m), 0).astype(F32)
        self.i = i
        self.down = jnp.exp(-lam * i)
        self.up = jnp.exp(lam * (i + 1.0))
        self.tail = jnp.exp(-lam * (CHUNK - 1.0 - i))
        self.span = jnp.exp(-lam * CHUNK)


def stacked_heads(v):
    m = v.shape[1]
    lane = lax.broadcasted_iota(jnp.int32, v.shape, 1) // HEAD
    zero = jnp.zeros_like(v)
    return jnp.concatenate([jnp.where(lane == g, v, zero) for g in range(m // HEAD)], axis=0)


def own_heads(v):
    m = v.shape[1]
    lane = lax.broadcasted_iota(jnp.int32, (CHUNK, m), 1) // HEAD
    out = v[:CHUNK]
    for g in range(1, m // HEAD):
        out = jnp.where(lane == g, v[g * CHUNK : (g + 1) * CHUNK], out)
    return out


def triangle(heads, low):
    shape = (heads * CHUNK, CHUNK)
    row = lax.rem(lax.broadcasted_iota(jnp.int32, shape, 0), CHUNK)
    col = lax.broadcasted_iota(jnp.int32, shape, 1)
    return row > col if low else row < col


def squeeze(s0, s1):
    def fold(s):
        out = s[:, :128]
        for g in range(1, s.shape[1] // 128):
            out = out + s[:, g * 128 : (g + 1) * 128]
        return out + pltpu.roll(out, HEAD, axis=1)

    lane = lax.broadcasted_iota(jnp.int32, (s0.shape[0], 128), 1)
    return jnp.where(lane < HEAD, fold(s0), fold(s1))


def widen(p, second, ones):
    lane = lax.broadcasted_iota(jnp.int32, p.shape, 1)
    keep = (lane >= HEAD) if second else (lane < HEAD)
    both = jnp.where(keep, p, pltpu.roll(p, HEAD, axis=1))
    return jnp.concatenate([both] * (ones.shape[1] // 128), axis=1) * ones


class Chain:
    def __init__(self, me, H, ahead, out_box, in_box, send, recv):
        h = me["h"]
        self.h, self.H = h, H
        nxt = jnp.minimum(h + 1, H - 1) if ahead else jnp.maximum(h - 1, 0)
        self.has_next = (h < H - 1) if ahead else (h > 0)
        self.has_prev = (h > 0) if ahead else (h < H - 1)
        self.out_box, self.in_box = out_box, in_box
        self.copy = remote(out_box, in_box, send, recv, {"h": nxt})

    def run(self, state, closing, span_all, ones):
        if self.H == 1:
            return

        @pl.when(self.has_prev)
        def _():
            self.copy.wait_recv()
            p = self.in_box[...].astype(F32)
            for s in range(2):
                state[s] = widen(p, s == 1, ones)

        @pl.when(self.has_next)
        def _():
            out = squeeze(*(span_all * state[s] + closing[s] for s in range(2)))
            self.out_box[...] = out.astype(BF)
            self.copy.start()

    def finish(self):
        if self.H == 1:
            return

        @pl.when(self.has_next)
        def _():
            self.copy.wait_send()


def window(read, width, s):
    if s < 0:
        return pltpu.roll(read(0, 128).astype(F32), -s, axis=1)
    t, off = s // 128 * 128, s % 128
    if off == 0:
        return read(t, t + 128).astype(F32)
    if t + 256 <= width:
        return pltpu.roll(read(t, t + 256).astype(F32), 256 - off, axis=1)[:, :128]
    return pltpu.roll(read(t, t + 128).astype(F32), 128 - off, axis=1)


def lay_lanes(width, parts, put):
    for lo in range(0, width, 128):
        out = None
        for read, wide, src, dst, n in parts:
            d0, d1 = max(dst - lo, 0), min(dst + n - lo, 128)
            if d0 >= d1:
                continue
            v = window(read, wide, src + lo - dst)
            if out is not None:
                lane = lax.broadcasted_iota(jnp.int32, v.shape, 1)
                v = jnp.where((lane >= d0) & (lane < d1), v, out)
            out = v
        put(lo, out)


def rank_columns(lay, n, whole, p):
    w, m = n // lay.n, n // 8
    if w % whole:
        return [(p * m, 0, m)]
    b, l, c = p >> 2, (p >> 1) & 1, p & 1
    teams = [(i, j) for i in range(lay.A) for j in range(lay.H)]
    return [
        (((((i * 2 + b) * lay.H + j) * 2 + l) * 2 + c) * w, k * w, w) for k, (i, j) in enumerate(teams)
    ]


def front(lay, vecs, x, up, w4, w_ck, w_cr, w_o, w_cv, start):
    H, A = lay.H, lay.A
    grid = (A, 2, H, 4)
    rows, D = x.shape
    T = 8 * rows
    m = D // 8
    w_row = D // lay.n
    kk = D // (2 * A)
    heads = m // HEAD
    per = T // 2 // CHUNK
    bring_o = lay.strided
    wo_shape = (A, H, m // (A * H), D)
    cv_rows = w_cv.shape[0]
    F = w_ck.shape[1]
    nf = F // 8 + m
    k_row = w_ck.shape[0]
    early = cv_rows // 2 // 16 * 16 if cv_rows % 16 == 0 else 0

    def body(*refs):
        vecs, x, up, w_r, w_k, w_v, w_g, w_ck, w_cr, w_o, w_cv, start = refs[:12]
        refs = refs[4:]
        full, mine_v, mixed, diff, rkv, gate, upc, w_out = refs[8:16]
        wo, gated, ghat, grstd, states, fin, middle, n2, halo2, wcv, wf = refs[16:27]
        va, xg, halo, hn, carry, mx, df, wa, wos, team = refs[27:37]
        adds, st, cl, obox, ibox, own = refs[37:43]
        near, acc, mid, far, ss, sr = refs[43:49]
        vs, vn, vf, xs, xr, hs, hr, us, ur, ws, wn, wf_, qs, qr, os_, or_ = refs[49:65]
        es, er, cs, cr, ts, tr, fs, fn, ff, gs, gr, ks, kr, ls = refs[65:79]
        w, later, sbuf, zbuf, bs, br = refs[79:]
        part = xg
        me = coords()
        a, b, h, l, c = (me[n] for n in ALL)
        mine = rank_of(b, l, c)

        def cols(ref, p):
            return ref.at[:, pl.ds(pl.multiple_of(p * m, m), m)]

        for p in range(8):
            for j, ref in enumerate((w_r, w_k, w_v, w_g)):
                read = lambda lo, hi, ref=ref: ref[:, lo:hi]
                parts = [(read, D, *at) for at in rank_columns(lay, D, HEAD, p)]

                def put_w(lo, v, p=p, j=j):
                    w[p, :, j * m + lo : j * m + lo + 128] = v.astype(BF)

                lay_lanes(m, parts, put_w)

        local = [
            pltpu.make_async_copy(w.at[mine], wa.at[a, b, h, l * 2 + c], ls.at[0]),
            pltpu.make_async_copy(x, xg.at[rows_at(mine, rows)], ls.at[2]),
            pltpu.make_async_copy(cols(up, mine), upc.at[mine], ls.at[3]),
            pltpu.make_async_copy(vecs, va.at[a, b, h, l * 2 + c], ls.at[4]),
            pltpu.make_async_copy(w_o, wos.at[a, h] if bring_o else wos, ls.at[5]),
            pltpu.make_async_copy(w_cv, wcv.at[a, h], ls.at[6]),
        ]
        for copy in local:
            copy.start()
        greet(me, H, True, True)
        gw = TeamsGather(me, H, lambda p: w.at[p], wa, ws, wn, wf_)
        gv = TeamsGather(me, H, lambda p: vecs, va, vs, vn, vf)
        gx = TeamGather(me, x, lambda p: xg.at[rows_at(p, rows)], xs, xr, ("zx", "zx"))
        gh = Halo(me, H, x, halo, hs, hr)
        gu = Exchange(me, lambda p: cols(up, p), lambda p: upc.at[p], us, ur)
        gq = Exchange(me, lambda p: later.at[p], lambda p: team.at[p], qs, qr)
        gf = TeamsGather(me, H, None, wf, fs, fn, ff, team, 4)
        if bring_o:
            go = RowsGather(me, H, w_o, wos, os_, or_)
        top, rest = pl.ds(0, early), pl.ds(early, cv_rows - early)
        if early:
            ge = RowsGather(me, H, w_cv.at[top], wcv, es, er, top)
        gc = RowsGather(me, H, w_cv.at[rest], wcv, ts, tr, rest)
        def head(bb, k):
            if lay.strided:
                return (((k // H * 2 + bb) * H + k % H) * 2 + l) * 2 + c
            return rank_of(bb, l, c) * heads + k

        near_states = [
            pltpu.make_async_copy(start.at[head(b, k)], sbuf.at[b, k], ls.at[14 + k]) for k in range(heads)
        ]
        far_states = [
            remote(start.at[head(1 - b, k)], sbuf.at[b, k], bs.at[k], br.at[k], {"b": 1 - b})
            for k in range(heads)
        ]
        gv.start()
        gh.start()
        gw.start()
        for copy in near_states + far_states:
            copy.start()
        gx.start()
        gv.spread(local[3])
        gv.forward()
        gw.spread(local[0])
        gv.finish()
        for p in range(8):
            parts = [(lambda lo, hi: w_ck[:, lo:hi], F, *at) for at in rank_columns(lay, F, 1, p)]

            def put_ck(lo, v, p=p):
                later[p, :, lo : lo + 128] = v.astype(BF)

            lay_lanes(F // 8, parts, put_ck)
            later[p, :, F // 8 :] = w_cr[:, p * m : (p + 1) * m]
        mine_team = pltpu.make_async_copy(later.at[mine], team.at[mine], ls.at[1])
        mine_team.start()
        local[1].wait()
        gx.finish()
        gq.start()
        gu.start()
        gw.forward((0,))
        gh.finish()

        def piece(*at):
            return va[at].astype(F32)

        flat = [
            piece(i, j, k, q) for i in range(A) for j in range(2) for k in range(H) for q in range(4)
        ]
        full[...] = join_lanes(flat, w_row)
        if lay.strided:
            held = [piece(i, b, k, l * 2 + c) for i in range(A) for k in range(H)]
            mine_v[...] = join_lanes(held, w_row)
        else:
            mine_v[...] = full[:, pl.ds(pl.multiple_of(mine * m, m), m)]
        gain, bias = full[0:1], full[1:2]
        for s in range(2):
            row = (norm_rows(halo[s].astype(F32))[0] * gain + bias)[15:16]
            hn[s] = jnp.where(h > 0, row, jnp.zeros_like(row))

        def write(i, p, v):
            if i is None:
                df[rows_at(p, MIX)] = v
            else:
                mx[i, rows_at(p, MIX)] = v

        mix_rows(
            lambda p: norm_rows(xg[rows_at(p, MIX)].astype(F32))[0] * gain + bias,
            lambda s: hn[s],
            carry,
            [full[2 + i : 3 + i] for i in range(4)],
            write,
            T // MIX,
            MIX,
        )
        keep = [
            pltpu.make_async_copy(mx, mixed, ls.at[7]),
            pltpu.make_async_copy(df, diff, ls.at[8]),
        ]
        for copy in keep:
            copy.start()
        gw.forward((1,))
        if bring_o:
            go.start()
        mine_team.wait()
        gq.finish()
        keep += [
            pltpu.make_async_copy(team.at[pl.ds(0, 4)], wf.at[a, 0, h], ls.at[11]),
            pltpu.make_async_copy(team.at[pl.ds(4, 4)], wf.at[a, 1, h], ls.at[12]),
        ]
        for copy in keep[2:]:
            copy.start()
        gf.spread(None, (0,))
        gw.finish()
        keep.append(pltpu.make_async_copy(wa, w_out, ls.at[9]))
        keep[-1].start()
        for j in range(4):

            @pl.loop(0, 4)
            def _(t):
                at = rows_at(t, T // 4)
                acc = jnp.zeros((T // 4, m), F32)
                for i in range(A):
                    for k in range(2):
                        lo = (i * 2 + k) * kk
                        wt = wa[i, k, :, :, :, j * m : (j + 1) * m].reshape(kk, m)
                        acc = acc + dot_nn(mx[j, at, lo : lo + kk], wt)
                if j < 3:
                    rkv[j, at] = acc.astype(BF)
                else:
                    gate[at] = acc

        ones = block_ones(m)
        dec = Decay(mine_v[6:7])
        u = mine_v[7:8]
        span_all = jnp.exp(-mine_v[6:7] * (T // 2))

        def tile(i, s, n):
            return rkv[i, rows_at(s * per + n, CHUNK)].astype(F32)

        cl[...] = jnp.zeros_like(cl)

        @pl.loop(0, per)
        def _(n):
            for s in range(2):
                kt = (tile(1, s, n) * dec.tail).astype(BF)
                v = rkv[2, rows_at(s * per + n, CHUNK)]
                add = dot_tn(v, kt) * ones
                adds[s, n] = add
                cl[s] = dec.span * cl[s] + add

        for copy in near_states:
            copy.wait()
        for copy in far_states:
            copy.wait_send()
        for k in range(heads):
            landed(sbuf.at[1 - b, k], br.at[k])
        odd = lax.rem(lax.broadcasted_iota(jnp.int32, (m, 128), 0) // HEAD, 2) == 1
        zbuf[...] = jnp.zeros_like(zbuf)
        for s in range(2):
            for k in range(heads):
                zbuf[k * HEAD : (k + 1) * HEAD, :HEAD] = sbuf[s, k]
            z = zbuf[...]
            z = jnp.where(odd, pltpu.roll(z, HEAD, axis=1), z)
            z = (jnp.concatenate([z] * (m // 128), axis=1) * ones).T
            st[s] = jnp.where(h > 0, jnp.zeros_like(z), z)
        chain = Chain(me, H, True, obox, ibox, cs, cr)
        chain.run(st, cl, span_all, ones)
        gf.spread(None, (1, 2))
        local[4].wait()
        if bring_o:
            go.forward()
        low = triangle(heads, True)

        @pl.loop(0, per)
        def _(n):
            for s in range(2):
                at = rows_at(s * per + n, CHUNK)
                r, k, v = (tile(i, s, n) for i in range(3))
                vb = rkv[2, at]
                rd = (r * dec.down).astype(BF)
                kg = (k * dec.up).astype(BF)
                state = st[s]
                states[s, n] = state
                att = jnp.where(low, dot_nt(stacked_heads(rd), kg), 0.0).astype(BF)
                y = own_heads(dot_nn(att, vb)) + dot_nt(rd, state.astype(BF))
                y = y + dot_exact(r * u * k, ones) * v
                st[s] = dec.span * state + adds[s, n]
                mean = dot_exact(y, ones) * (1.0 / HEAD)
                cent = y - mean
                rstd = lax.rsqrt(dot_exact(cent * cent, ones) * (1.0 / HEAD) + GROUP_EPS)
                hat = cent * rstd
                ghat[at] = hat
                grstd[at] = rstd
                g = gate[at]
                silu = g / (1.0 + jnp.exp(-g))
                gated[at] = ((hat * mine_v[8:9] + mine_v[9:10]) * silu).astype(BF)

        fin[...] = squeeze(st[0], st[1])
        chain.finish()
        if bring_o:
            go.finish()
        keep.append(pltpu.make_async_copy(wos, wo, ls.at[13]))
        keep[-1].start()

        @pl.loop(0, 8)
        def _(p):
            g = gated[rows_at(p, rows)]
            w = wos[...].reshape(m, D)
            for q in range(4):
                lo = q * (D // 4)
                part[rows_at(p, rows), lo : lo + D // 4] = dot_nn(g, w[:, lo : lo + D // 4]).astype(BF)

        sums = TeamSum(me, lambda p: part.at[rows_at(p, rows)], near, acc, mid, far, ss, sr, ("xz", "xz"))
        sums.start()

        def put(at, v):
            v = x[at].astype(F32) + v
            middle[at] = v
            own[at] = (norm_rows(v)[0] * full[10:11] + full[11:12]).astype(BF)

        sums.finish(put)
        keep.append(pltpu.make_async_copy(own, n2.at[mine], ls.at[10]))
        keep[-1].start()
        gn = TeamGather(me, own, lambda p: n2.at[p], gs, gr, ("zx", "zx"))
        gn.start()
        gk = Halo(me, H, own, halo2, ks, kr)
        gk.start()
        gf.spread(None, (3,))
        if early:
            ge.start()
        gc.start()
        gf.forward((0, 1, 2))
        gn.finish()
        gk.finish()
        gf.forward((3,))
        if early:
            ge.forward()
        gc.forward()
        gu.finish()
        gf.finish()
        if early:
            ge.finish()
        gc.finish()
        for copy in local[2:3] + local[5:] + keep:
            copy.wait()

    gsems = TeamsGather.sems(H)
    team_sems = [DMA((14,)), DMA((8, 2))]
    halo_sems = [DMA((8,)), DMA((2,))]
    move_sems = [DMA((7,)), DMA((8,))]
    return comm_call(
        body,
        (
            jax.ShapeDtypeStruct((16, D), F32),
            jax.ShapeDtypeStruct((16, m), F32),
            jax.ShapeDtypeStruct((4, T, D), BF),
            jax.ShapeDtypeStruct((T, D), BF),
            jax.ShapeDtypeStruct((3, T, m), BF),
            jax.ShapeDtypeStruct((T, m), F32),
            jax.ShapeDtypeStruct((8, rows, m), BF),
            jax.ShapeDtypeStruct((*grid, k_row, 4 * m), BF),
            jax.ShapeDtypeStruct(wo_shape, BF),
            jax.ShapeDtypeStruct((T, m), BF),
            jax.ShapeDtypeStruct((T, m), F32),
            jax.ShapeDtypeStruct((T, m), F32),
            jax.ShapeDtypeStruct((2, per, m, m), F32),
            jax.ShapeDtypeStruct((m, 128), F32),
            jax.ShapeDtypeStruct((rows, D), F32),
            jax.ShapeDtypeStruct((8, rows, D), BF),
            jax.ShapeDtypeStruct((2, 16, D), BF),
            jax.ShapeDtypeStruct((A, H, *w_cv.shape), BF),
            jax.ShapeDtypeStruct((*grid, k_row, nf), BF),
        ),
        [VM] * 11 + [ANY],
        (VM, VM, ANY, ANY, VM, VM, ANY, ANY, ANY, VM, VM, VM, VM, VM, VM, ANY, ANY, ANY, ANY),
        [
            pltpu.VMEM((*grid, *vecs.shape), BF),
            pltpu.VMEM((T, D), BF),
            pltpu.VMEM((2, 16, D), BF),
            pltpu.VMEM((2, 1, D), F32),
            pltpu.VMEM((1, D), F32),
            pltpu.VMEM((4, T, D), BF),
            pltpu.VMEM((T, D), BF),
            pltpu.VMEM((*grid, k_row, 4 * m), BF),
            pltpu.VMEM(wo_shape, BF),
            pltpu.VMEM((8, k_row, nf), BF),
            pltpu.VMEM((2, per, m, m), F32),
            pltpu.VMEM((2, m, m), F32),
            pltpu.VMEM((2, m, m), F32),
            pltpu.VMEM((m, 128), BF),
            pltpu.VMEM((m, 128), BF),
            pltpu.VMEM((rows, D), BF),
            *TeamSum.scratch(rows, D),
            *gsems,
            *team_sems,
            *halo_sems,
            *move_sems,
            *gsems,
            *move_sems,
            *RowsGather.sems(H),
            *RowsGather.sems(H),
            DMA,
            DMA,
            *RowsGather.sems(H),
            *TeamsGather.sems(H, 4),
            *team_sems,
            *halo_sems,
            DMA((14 + heads,)),
            pltpu.VMEM((8, k_row, 4 * m), BF),
            pltpu.VMEM((8, k_row, nf), BF),
            pltpu.VMEM((2, heads, HEAD, HEAD), F32),
            pltpu.VMEM((m, 128), F32),
            DMA((heads,)),
            DMA((heads,)),
        ],
        0,
    )(vecs, x, up, *w4, w_ck, w_cr, w_o, w_cv, start)


class Background:
    def __init__(self, items, H):
        self.items, self.H = items, H

    def arrays(self):
        return [v for v, _ in self.items]

    def outs(self):
        shapes = []
        for v, kind in self.items:
            lead = {"h": (max(self.H - 1, 1),), "a": (), "t": (8,)}[kind]
            shapes.append(jax.ShapeDtypeStruct((*lead, *v.shape[1:]), BF))
        return shapes

    def sems(self):
        out = []
        for _, kind in self.items:
            n = {"h": max(self.H - 1, 1), "a": 1, "t": 8}[kind]
            out += [DMA((n,)), DMA((n,))] + ([DMA] if kind == "t" else [])
        return out

    def start(self, me, srcs, dsts, sems):
        self.open = []
        sems = list(sems)
        h, H = me["h"], self.H
        mine = rank_of(me["b"], me["l"], me["c"])
        for (_, kind), src, dst in zip(self.items, srcs, dsts):
            ss, sr = sems.pop(0), sems.pop(0)
            copies = Copies(ss)
            if kind == "h":
                for dh in range(1, H):
                    to = lax.rem(h + dh, H)
                    copies.go(src.at[to], dst.at[dh - 1], sr.at[dh - 1], {"h": to})
                    self.open.append((dst.at[dh - 1], sr.at[dh - 1]))
            elif kind == "a":
                copies.go(src.at[1 - me["a"]], dst, sr.at[0], {"a": 1 - me["a"]})
                self.open.append((dst, sr.at[0]))
            else:
                keep = pltpu.make_async_copy(src.at[mine], dst.at[mine], sems.pop(0))
                keep.start()
                self.open.append(keep)
                for m, to in mates(me):
                    p = rank_of(to["b"], to["l"], to["c"])
                    copies.go(src.at[p], dst.at[mine], sr.at[mine], to)
                    self.open.append((dst.at[p], sr.at[p]))
            self.open.append(copies)

    def finish(self):
        for item in self.open:
            if isinstance(item, tuple):
                landed(*item)
            elif isinstance(item, Copies):
                item.drain()
            else:
                item.wait()


def back_rows(T, tile, chunk, shares, diff, part, first, sums):
    per = T // 2 // tile

    def step(q, carry):
        t = 2 * per - 1 - q
        ds = chunk(t)
        dif = diff(t)
        late = jnp.zeros_like(ds[0])
        here = jnp.zeros_like(ds[0])
        for i, (d, s) in enumerate(zip(ds, shares)):
            sums[i][...] = sums[i][...] + jnp.sum(d * dif, axis=0, keepdims=True)
            late = late + (1.0 - s) * d
            here = here + s * d
        carry = jnp.where(lax.rem(t, per) == per - 1, jnp.zeros_like(carry), carry)
        row = lax.broadcasted_iota(jnp.int32, late.shape, 0)
        part(t, here + jnp.where(row == tile - 1, carry, pltpu.roll(late, tile - 1, axis=0)))

        @pl.when(lax.rem(t, per) == 0)
        def _():
            first(t // per, late[:16].astype(BF))

        return late[:1]

    zero = jnp.zeros((1, diff(0).shape[1]), F32)
    lax.fori_loop(0, 2 * per, step, zero)


def channel_mix(lay, n2, halo, full, wcv, wf, upc, middle, up, items):
    H, A = lay.H, lay.A
    rows, D = middle.shape
    T = 8 * rows
    F, m = wcv.shape[0], D // 8
    nk, kk, _ = wf.shape
    w_cv = F // (A * H)
    tile = T // 4
    dq = D // 4
    bg = Background(items, H)
    nb = len(items)

    def body(n2, halo, full, wcv, wf, upc, middle, up, *rest):
        srcs, rest = rest[:nb], rest[nb:]
        d_mid, d_br, moved, s_cv, got_cv, g_f, got_f, sums = rest[:8]
        dsts, rest = rest[8 : 8 + nb], rest[:8] + rest[8 + nb :]
        (big, m2, df, carry, relu, act, sg, d_pg, d_val, dval, gcv, cvbuf, stage) = rest[8:21]
        (dn2, own, add, first, edge) = rest[21:26]
        cn, ca, cm, cf, c_s, c_r = rest[26:32]
        rn, ra, rm, rf, r_s, r_r = rest[32:38]
        ds, dr, bs, br, es, er, ms, mr, vs, vr, fs, fr, ls = rest[38:51]
        d_pre = act
        me = coords()
        a, b, h, l, c = (me[n] for n in ALL)
        mine = rank_of(b, l, c)
        loads = [
            pltpu.make_async_copy(n2.at[p], big.at[pl.ds(p * rows, rows)], ls.at[p]) for p in range(8)
        ]
        for copy in loads:
            copy.start()
        greet(me, H, True, True)
        for copy in loads:
            copy.wait()

        def write(i, p, v):
            if i is None:
                df[rows_at(p, MIX)] = v
            else:
                m2[i, rows_at(p, MIX)] = v

        def before(s):
            row = halo[s].astype(F32)[15:16]
            return jnp.where(h > 0, row, jnp.zeros_like(row))

        s_ck, s_cr = full[12:13], full[13:14]
        mix_rows(
            lambda p: big[rows_at(p, MIX)].astype(F32),
            before,
            carry,
            [s_ck, s_cr],
            write,
            T // MIX,
            MIX,
        )

        @pl.loop(0, 4)
        def _(t):
            at = rows_at(t, tile)
            acc = jnp.zeros((tile, F), F32)
            for i in range(nk):
                acc = acc + dot_nn(m2[0, at, i * kk : (i + 1) * kk], wf[i, :, :F])
            pos = jnp.maximum(acc, 0.0)
            relu[at] = pos.astype(BF)
            act[at] = (pos * pos).astype(BF)

        @pl.loop(0, 4)
        def _(t):
            at = rows_at(t, tile)
            for q in range(4):
                lo = q * dq
                big[at, lo : lo + dq] = dot_nn(act[at], wcv[:, lo : lo + dq]).astype(BF)

        def cols(ref):
            return lambda p: ref.at[:, pl.ds(pl.multiple_of(p * m, m), m)]

        total = TeamSum(me, cols(big), cn, ca, cm, cf, c_s, c_r)
        total.start()

        @pl.loop(0, 4)
        def _(t):
            at = rows_at(t, tile)
            acc = jnp.zeros((tile, m), F32)
            for i in range(nk):
                acc = acc + dot_nn(m2[1, at, i * kk : (i + 1) * kk], wf[i, :, F:])
            sg[at] = 1.0 / (1.0 + jnp.exp(-acc))

        def gate_back(at, val):
            sig = sg[at]
            upv = upc[at].astype(F32)
            d_val[at] = (sig * upv).astype(BF)
            d_pg[at] = (upv * val * sig * (1.0 - sig)).astype(BF)
            add[at] = (sig * val).astype(BF)

        total.finish(gate_back)
        keep_val = pltpu.make_async_copy(d_val, cols(dval)(mine), ls.at[8])
        keep_val.start()
        gv = TeamGather(me, d_val, cols(dval), ds, dr)
        gv.start()
        gv.finish()
        keep_val.wait()

        @pl.loop(0, 8)
        def _(q):
            at = pl.ds(pl.multiple_of(q * m, m), m)
            g = dot_tn(act[...], dval[:, at])
            for i in range(A):
                for j in range(H):
                    lo = (i * H + j) * w_cv
                    gcv[i, j, :, at] = g[lo : lo + w_cv].astype(BF)

        cv = Copies(vs)
        cv.go(gcv.at[1 - a], cvbuf, vr.at[0], {"a": 1 - a})

        @pl.loop(0, 4)
        def _(t):
            at = rows_at(t, tile)
            d_pre[at] = (dot_nt(dval[at], wcv[...]) * 2.0 * relu[at].astype(F32)).astype(BF)

        ff = Copies(fs)
        sums[...] = jnp.zeros_like(sums)

        def chunk_of(i):
            lo = i * kk

            def chunk(t):
                at = rows_at(t, tile)
                return (dot_nt(d_pre[at], wf[i, :, :F]), dot_nt(d_pg[at], wf[i, :, F:]))

            def put(t, v):
                big[rows_at(t, tile), lo : lo + kk] = v.astype(BF)

            def put_first(s, v):
                first[s, :, lo : lo + kk] = v

            back_rows(
                T,
                tile,
                chunk,
                (s_ck[:, lo : lo + kk], s_cr[:, lo : lo + kk]),
                lambda t: df[rows_at(t, tile), lo : lo + kk].astype(F32),
                put,
                put_first,
                [sums.at[k : k + 1, lo : lo + kk] for k in range(2)],
            )

        def grads(i):
            lo = i * kk
            for k in range(2):
                at = slice(lo + k * kk // 2, lo + (k + 1) * kk // 2)
                to = slice(k * kk // 2, (k + 1) * kk // 2)
                stage[to, :F] = dot_tn(m2[0, :, at], d_pre[...]).astype(BF)
                stage[to, F:] = dot_tn(m2[1, :, at], d_pg[...]).astype(BF)
            copy = pltpu.make_async_copy(stage, g_f.at[i // 2, i % 2], ls.at[9])
            copy.start()
            return copy

        for i in range(nk):
            copy = grads(i)
            chunk_of(i)
            copy.wait()
        ff.go(g_f.at[1 - a], got_f, fr.at[0], {"a": 1 - a})
        total = TeamSum(me, lambda p: big.at[rows_at(p, rows)], rn, ra, rm, rf, r_s, r_r)
        total.start()
        e = Edge(me, H, first, edge, es, er)
        e.start()

        def put_dn(at, v):
            dn2[at] = v

        halves = 2 if w_cv % 32 == 0 else 1

        def pass_on(g):
            at = pl.ds(g * (w_cv // halves), w_cv // halves)
            for dh in range(1, H):
                to = lax.rem(h + dh, H)
                cv.go(
                    gcv.at[a, to, at],
                    got_cv.at[dh - 1, at],
                    vr.at[1 + (dh - 1) * 2 + g],
                    {"h": to},
                )

        def value_sums():
            landed(cvbuf, vr.at[0])

            @pl.loop(0, H)
            def _(j):
                gcv[a, j] = (gcv[a, j].astype(F32) + cvbuf[j].astype(F32)).astype(BF)

            pass_on(0)

        total.finish(put_dn, value_sums)
        e.finish(dn2)

        @pl.loop(0, rows // MIX)
        def _(t):
            at = rows_at(t, MIX)
            d = dn2[at]
            hat, rstd = norm_rows(middle[at])
            sums[2:3] = sums[2:3] + jnp.sum(d * hat, axis=0, keepdims=True)
            sums[3:4] = sums[3:4] + jnp.sum(d, axis=0, keepdims=True)
            dm = up[at].astype(F32) + norm_back(d * full[10:11], hat, rstd)
            d_mid[at] = dm
            own[at] = dm.astype(BF)

        keep = [
            pltpu.make_async_copy(own, d_br.at[mine], ls.at[10]),
            pltpu.make_async_copy(add.at[rows_at(mine, rows)], moved.at[mine], ls.at[11]),
        ]
        for copy in keep:
            copy.start()
        gx = TeamGather(me, own, lambda p: d_br.at[p], bs, br, ("zx", "zx"))
        gx.start()
        if halves == 2:
            pass_on(1)
        keep.append(pltpu.make_async_copy(gcv.at[a, h], s_cv, ls.at[12]))
        keep[-1].start()
        gx.finish()
        gm = Exchange(me, lambda p: add.at[rows_at(p, rows)], lambda p: moved.at[p], ms, mr)
        gm.start()
        bg.start(me, srcs, dsts, rest[51:])
        gm.finish()
        bg.finish()
        landed(got_f, fr.at[0])
        ff.drain()
        for dh in range(1, H):
            for g in range(halves):
                at = pl.ds(g * (w_cv // halves), w_cv // halves)
                landed(got_cv.at[dh - 1, at], vr.at[1 + (dh - 1) * 2 + g])
        cv.drain()
        for copy in keep:
            copy.wait()

    return comm_call(
        body,
        (
            jax.ShapeDtypeStruct((rows, D), F32),
            jax.ShapeDtypeStruct((8, rows, D), BF),
            jax.ShapeDtypeStruct((8, rows, m), BF),
            jax.ShapeDtypeStruct((w_cv, D), BF),
            jax.ShapeDtypeStruct((max(H - 1, 1), w_cv, D), BF),
            jax.ShapeDtypeStruct((A, nk // A, kk, F + m), BF),
            jax.ShapeDtypeStruct((nk // A, kk, F + m), BF),
            jax.ShapeDtypeStruct((8, D), F32),
            *bg.outs(),
        ),
        [ANY, VM, VM, VM, VM, VM, VM, VM] + [ANY] * nb,
        (VM, ANY, ANY, ANY, ANY, ANY, ANY, VM, *[ANY] * nb),
        [
            pltpu.VMEM((T, D), BF),
            pltpu.VMEM((2, T, D), BF),
            pltpu.VMEM((T, D), BF),
            pltpu.VMEM((1, D), F32),
            pltpu.VMEM((T, F), BF),
            pltpu.VMEM((T, F), BF),
            pltpu.VMEM((T, m), F32),
            pltpu.VMEM((T, m), BF),
            pltpu.VMEM((T, m), BF),
            pltpu.VMEM((T, D), BF),
            pltpu.VMEM((A, H, w_cv, D), BF),
            pltpu.VMEM((H, w_cv, D), BF),
            pltpu.VMEM((kk, F + m), BF),
            pltpu.VMEM((rows, D), F32),
            pltpu.VMEM((rows, D), BF),
            pltpu.VMEM((T, m), BF),
            pltpu.VMEM((2, 16, D), BF),
            pltpu.VMEM((8, 16, D), BF),
            *TeamSum.scratch(T, m),
            *TeamSum.scratch(rows, D),
            DMA((14,)),
            DMA((8, 2)),
            DMA((14,)),
            DMA((8, 2)),
            DMA((2,)),
            DMA((8,)),
            DMA((7,)),
            DMA((8,)),
            DMA((2 * H,)),
            DMA((2 * H,)),
            DMA((1,)),
            DMA((1,)),
            DMA((13,)),
            *bg.sems(),
        ],
        2,
    )(n2, halo, full, wcv, wf, upc, middle, up, *bg.arrays())


def time_back(lay, d_br, wo, gated, ghat, grstd, gate, rkv, states, mv, full, mixed, diff, w4, x, d_mid, cm_sums, s_f, fin):
    H, A, n_dev = lay.H, lay.A, lay.n
    T, m = gate.shape
    rows, D = x.shape
    heads = m // HEAD
    per = T // 2 // CHUNK
    nk, kk, _ = w4.shape
    tile = T // 4
    hk = kk // H
    w_row = D // n_dev
    nf = s_f.shape[-1]
    H1 = max(H - 1, 1)
    strided = lay.strided
    hop = fin is not None
    F = (nf - m) * 8
    k_row = hk // 4

    def body(*refs):
        d_br, wo, gated, ghat, grstd, gate, rkv, states, mv, full, mixed, diff, w4, x, d_mid, cm_sums, s_f = refs[:17]
        if hop:
            fin, refs = refs[17], refs[:17] + refs[18:]
        in_grad, o_out, total_out, fin_out, ck_out, cr_out, *four = refs[17:27]
        refs = refs[5:]
        (big, dy, adds, cl, st, obox, ibox, d_all, tsum, sums) = refs[22:32]
        (mbuf, g4, got, late, t4, first, edge) = refs[32:39]
        dn1 = in_grad
        (g_o, o_got, o_late, f_own, f_got, t_f, small, s_got) = refs[39:47]
        rn, ra, rm, rf, r_s, r_r = refs[47:53]
        cs, cr, es, er, gs, gr, os_, or_, fs, fr, xs, xr, ys, yr, ss, sr, ls, f_out, g_out, hs, hr = refs[53:]
        me = coords()
        a, b, h, l, c = (me[k] for k in ALL)
        mine = rank_of(b, l, c)
        loads = [
            pltpu.make_async_copy(d_br.at[p], big.at[pl.ds(p * rows, rows)], ls.at[p]) for p in range(8)
        ]
        loads.append(pltpu.make_async_copy(s_f.at[h], f_own, ls.at[8]))
        for copy in loads:
            copy.start()

        sem = pltpu.get_barrier_semaphore()
        others = []
        for i in range(1, n_dev):
            k = i
            dc, k = k % 2, k // 2
            dl, k = k % 2, k // 2
            dh, k = k % H, k // H
            db, da = k % 2, k // 2
            to = {
                "a": lax.rem(a + da, A),
                "b": b ^ db,
                "h": lax.rem(h + dh, H),
                "l": l ^ dl,
                "c": c ^ dc,
            }
            others.append((i, to))
            pl.semaphore_signal(sem, inc=1, device_id=to, device_id_type=MESH)
        pl.semaphore_wait(sem, n_dev - 1)
        for copy in loads[:8]:
            copy.wait()

        ones = block_ones(m)
        dec = Decay(mv[6:7])
        u = mv[7:8]
        span_all = jnp.exp(-mv[6:7] * (T // 2))
        low_t = triangle(heads, False)
        low = triangle(heads, True)
        tsum[...] = jnp.zeros_like(tsum)

        @pl.loop(0, 2 * per)
        def _(t):
            at = rows_at(t, CHUNK)
            d_gated = dot_nt(big[at], wo[...].reshape(m, D))
            g = gate[at]
            sig = 1.0 / (1.0 + jnp.exp(-g))
            hat, rstd = ghat[at], grstd[at]
            dn = d_gated * (g * sig)
            tsum[2:3] += jnp.sum(dn * hat, axis=0, keepdims=True)
            tsum[3:4] += jnp.sum(dn, axis=0, keepdims=True)
            nm = hat * mv[8:9] + mv[9:10]
            d_all[at, 3 * m :] = (d_gated * nm * sig * (1.0 + g * (1.0 - sig))).astype(BF)
            e = dn * mv[8:9]
            m1 = dot_exact(e, ones) * (1.0 / HEAD)
            m2 = dot_exact(e * hat, ones) * (1.0 / HEAD)
            dy[at] = (e - m1 - hat * m2) * rstd

        cl[...] = jnp.zeros_like(cl)

        @pl.loop(0, per)
        def _(q):
            n = per - 1 - q
            for s in range(2):
                at = rows_at(s * per + n, CHUNK)
                rd = (rkv[0, at].astype(F32) * dec.down).astype(BF)
                add = dot_tn(dy[at].astype(BF), rd) * ones
                adds[s, n] = add
                cl[s] = dec.span * cl[s] + add

        st[...] = jnp.zeros_like(st)
        chain = Chain(me, H, False, obox, ibox, cs, cr)
        chain.run(st, cl, span_all, ones)
        cf = Copies(fs)
        for dh in range(1, H):
            to = lax.rem(h + dh, H)
            cf.go(s_f.at[to], f_got.at[dh - 1], fr.at[dh - 1], {"h": to})

        if hop:
            mine_fin = fin.at[pl.ds(l * 4, 4)]
            last = h == H - 1
            to_first = remote(mine_fin.at[:, pl.ds(0, HEAD)], fin_out, hs, hr, {"h": 0})
            kept = pltpu.make_async_copy(mine_fin.at[:, pl.ds(HEAD, HEAD)], fin_out, hs)

            @pl.when(last)
            def _():
                to_first.start()

        nw = D // 8

        @pl.loop(0, 8)
        def _(q):
            at = pl.ds(pl.multiple_of(q * nw, nw), nw)
            g = dot_tn(gated[...], big[:, at]).astype(BF)
            g_o[:, :, :, at] = g.reshape(*g_o.shape[:3], nw)

        co = Copies(os_)
        if strided:
            co.go(g_o.at[1 - a], o_got, or_.at[0], {"a": 1 - a})

        @pl.loop(0, per)
        def _(q):
            n = per - 1 - q
            for s in range(2):
                at = rows_at(s * per + n, CHUNK)
                r, k, v = (rkv[i, at].astype(F32) for i in range(3))
                vb = rkv[2, at]
                rd, kg, kt = r * dec.down, k * dec.up, k * dec.tail
                rdb, kgb, ktb = rd.astype(BF), kg.astype(BF), kt.astype(BF)
                dyt = dy[at]
                dyb = dyt.astype(BF)
                state, end = states[s, n], st[s]
                endb = end.astype(BF)
                datt = jnp.where(low, dot_nt(stacked_heads(dyb), vb), 0.0).astype(BF)
                datt_t = jnp.where(low_t, dot_nt(stacked_heads(vb), dyb), 0.0).astype(BF)
                att_t = jnp.where(low_t, dot_nt(stacked_heads(kgb), rdb), 0.0).astype(BF)
                ddiag = dot_exact(dyt * v, ones)
                diag = dot_exact(r * u * k, ones)
                d_rd = own_heads(dot_nn(datt, kgb)) + dot_nn(dyb, state.astype(BF))
                d_kg = own_heads(dot_nn(datt_t, rdb))
                d_kt = dot_nn(vb, endb)
                d_v = own_heads(dot_nn(att_t, dyb)) + diag * dyt + dot_nt(ktb, endb)
                d_r = d_rd * dec.down + ddiag * u * k
                d_k = d_kg * dec.up + d_kt * dec.tail + ddiag * u * r
                d_all[at, :m] = d_r.astype(BF)
                d_all[at, m : 2 * m] = d_k.astype(BF)
                d_all[at, 2 * m : 3 * m] = d_v.astype(BF)
                tsum[1:2] += jnp.sum(ddiag * r * k, axis=0, keepdims=True)
                d_l = jnp.sum(
                    (dec.i + 1.0) * kg * d_kg
                    - dec.i * rd * d_rd
                    - (CHUNK - 1.0 - dec.i) * kt * d_kt,
                    axis=0,
                    keepdims=True,
                )
                d_l = d_l - CHUNK * dec.span * jnp.sum(state * end, axis=0, keepdims=True)
                tsum[0:1] += d_l
                st[s] = dec.span * end + adds[s, n]

        chain.finish()

        cg = Copies(gs)
        units = [(step, k, jj) for step in range(A) for k in range(2) for jj in range(2)]

        def unit(v):
            step, k, jj = units[v]
            i = lax.rem(a + 1 + step, A)
            lo = pl.ds(pl.multiple_of((i * 2 + k) * kk, kk), kk)
            src = mixed.at[pl.ds(jj * 2, 2), :, lo]
            return pltpu.make_async_copy(src, mbuf.at[v % 2], ls.at[9 + v % 2])

        unit(0).start()
        for v, (step, k, jj) in enumerate(units):
            if v + 1 < len(units):
                unit(v + 1).start()
            unit(v).wait()
            i = lax.rem(a + 1 + step, A)
            for q in range(2):
                j = jj * 2 + q
                g = dot_tn(mbuf[v % 2, q], d_all[:, j * m : (j + 1) * m])
                g4[i * 2 + k, :, j * m : (j + 1) * m] = g.astype(BF)
            if step < A - 1 and jj == 1:
                cg.go(g4.at[i * 2 + k], got.at[k], gr.at[k], {"a": 1 - a})

        difs = [
            pltpu.make_async_copy(diff.at[:, pl.ds(i * kk, kk)], mbuf.at[i // 2, i % 2], ls.at[13 + i])
            for i in range(nk)
        ]
        for copy in difs:
            copy.start()
        sums[...] = jnp.zeros_like(sums)

        def chunk_of(i):
            lo = i * kk

            def chunk(t):
                at = rows_at(t, tile)
                return tuple(
                    dot_nt(d_all[at, j * m : (j + 1) * m], w4[i, :, j * m : (j + 1) * m])
                    for j in range(4)
                )

            def put(t, v):
                big[rows_at(t, tile), lo : lo + kk] = v.astype(BF)

            def put_first(s, v):
                first[s, :, lo : lo + kk] = v

            back_rows(
                T,
                tile,
                chunk,
                tuple(full[2 + j : 3 + j, lo : lo + kk] for j in range(4)),
                lambda t: mbuf[i // 2, i % 2, rows_at(t, tile)].astype(F32),
                put,
                put_first,
                [sums.at[j : j + 1, lo : lo + kk] for j in range(4)],
            )

        for i in range(nk):
            difs[i].wait()
            chunk_of(i)
        total = TeamSum(
            me, lambda p: big.at[rows_at(p, rows)], rn, ra, rm, rf, r_s, r_r, ("xz", "xz")
        )
        total.start()
        e = Edge(me, H, first, edge, es, er)
        e.start()

        def pass_on():
            if strided:
                landed(o_got, or_.at[0])

                @pl.loop(0, H)
                def _(j):
                    g_o[a, j] = (g_o[a, j].astype(F32) + o_got[j].astype(F32)).astype(BF)

                for dh in range(1, H):
                    to = lax.rem(h + dh, H)
                    co.go(g_o.at[a, to], o_late.at[dh - 1], or_.at[dh], {"h": to})
            for k in range(2):
                landed(got.at[k], gr.at[k])

                @pl.loop(0, kk // 64)
                def _(q):
                    at = rows_at(q, 64)
                    g4[a * 2 + k, at] = (g4[a * 2 + k, at].astype(F32) + got[k, at].astype(F32)).astype(BF)

                for dh in range(1, H):
                    to = lax.rem(h + dh, H)
                    v = (dh - 1) * 2 + k
                    cg.go(
                        g4.at[a * 2 + k, rows_at(to, hk)], late.at[dh - 1, k], gr.at[2 + v], {"h": to}
                    )

        def put_dn(at, v):
            dn1[at] = v

        total.finish(put_dn, pass_on)
        e.finish(dn1)

        @pl.loop(0, rows // MIX)
        def _(t):
            at = rows_at(t, MIX)
            d = dn1[at]
            hat, rstd = norm_rows(x[at].astype(F32))
            sums[4:5] = sums[4:5] + jnp.sum(d * hat, axis=0, keepdims=True)
            sums[5:6] = sums[5:6] + jnp.sum(d, axis=0, keepdims=True)
            in_grad[at] = d_mid[at] + norm_back(d * full[0:1], hat, rstd)

        small[...] = jnp.zeros_like(small)
        per_lane = 128 // w_row
        for f in range(n_dev):
            g = pl.ds(f // per_lane * 128, 128)
            block = jnp.concatenate([sums[:, g], cm_sums[:, g]], axis=0)
            shift = (128 - w_row * (f % per_lane)) % 128
            small[f] = pltpu.roll(block, shift, axis=1) if shift else block

        if strided:
            for i in range(A):
                for j in range(H):
                    f = (((i * 2 + b) * H + j) * 2 + l) * 2 + c
                    v = (i * H + j) * w_row
                    block = tsum[:, v // 128 * 128 : v // 128 * 128 + 128]
                    shift = (128 - v % 128) % 128
                    block = pltpu.roll(block, shift, axis=1) if shift else block
                    small[f, 12:16] = block[:4]
        else:
            span = n_dev // 8
            for i in range(span):
                v = i * w_row
                block = tsum[:, v // 128 * 128 : v // 128 * 128 + 128]
                shift = (128 - v % 128) % 128
                block = pltpu.roll(block, shift, axis=1) if shift else block
                small[mine * span + i, 12:16] = block[:4]
        cv = Copies(ss)

        def flat(d):
            return (((d["a"] * 2 + d["b"]) * H + d["h"]) * 2 + d["l"]) * 2 + d["c"]

        for i, to in others:
            cv.go(small.at[flat(to)], s_got.at[i], sr.at[i], to)

        loads[8].wait()
        for dh in range(1, H):
            landed(f_got.at[dh - 1], fr.at[dh - 1])
        for k in range(2):
            for q in range(4):
                at = pl.ds(q * (hk // 4), hk // 4)
                v = f_own[k, at].astype(F32)
                for dh in range(1, H):
                    v = v + f_got[dh - 1, k, at].astype(F32)
                t_f[k * 4 + q] = v.astype(BF)
        keep = [pltpu.make_async_copy(t_f.at[mine], f_out.at[mine], ls.at[11])]
        keep[0].start()
        gf = Exchange(me, lambda p: t_f.at[p], lambda p: f_out.at[p], xs, xr)
        gf.start()
        for k in range(2):
            for dh in range(1, H):
                landed(late.at[dh - 1, k], gr.at[2 + (dh - 1) * 2 + k])
            for q in range(4):
                at = pl.ds(pl.multiple_of(h * hk + q * (hk // 4), hk // 4), hk // 4)
                v = g4[a * 2 + k, at].astype(F32)
                for dh in range(1, H):
                    v = v + late[dh - 1, k, pl.ds(q * (hk // 4), hk // 4)].astype(F32)
                t4[k * 4 + q] = v.astype(BF)
        keep.append(pltpu.make_async_copy(t4.at[mine], g_out.at[mine], ls.at[12]))
        keep[1].start()
        gg = Exchange(me, lambda p: t4.at[p], lambda p: g_out.at[p], ys, yr)
        gg.start()
        if strided:
            v = g_o[a, h].astype(F32)
            for dh in range(1, H):
                landed(o_late.at[dh - 1], or_.at[dh])
                v = v + o_late[dh - 1].astype(F32)
            o_out[...] = v
        else:
            o_out[...] = g_o[...]
        acc = small[flat(me)]
        for i, _ in others:
            landed(s_got.at[i], sr.at[i])
            acc = acc + s_got[i]
        total_out[...] = acc
        if hop:

            @pl.when(last)
            def _():
                to_first.wait_send()
                kept.start()
                kept.wait()

            @pl.when(h == 0)
            def _():
                to_first.wait_recv()

        gf.finish()
        for copy in keep:
            copy.wait()

        def from_ranks(ref, lo, n, whole):
            parts = []
            for p in range(8):
                read = lambda i, j, p=p: ref[p, :, lo + i : lo + j]
                for src, dst, many in rank_columns(lay, n, whole, p):
                    parts.append((read, n // 8, dst, src, many))
            return parts

        def into(ref):
            def put(lo, v):
                ref[:, lo : lo + 128] = v

            return put

        lay_lanes(F, from_ranks(f_out, 0, F, 1), into(ck_out))
        for p in range(8):
            cr_out[:, p * m : (p + 1) * m] = f_out[p, :, F // 8 :].astype(F32)
        gg.finish()
        for j, ref in enumerate(four):
            lay_lanes(D, from_ranks(g_out, j * m, D, HEAD), into(ref))
        for copies in (cf, co, cg, cv):
            copies.drain()

    o_shape = wo.shape[2:] if strided else wo.shape
    return comm_call(
        body,
        (
            jax.ShapeDtypeStruct((rows, D), F32),
            jax.ShapeDtypeStruct(o_shape, F32 if strided else BF),
            jax.ShapeDtypeStruct((16, 128), F32),
            jax.ShapeDtypeStruct((4, HEAD, 128), BF),
            jax.ShapeDtypeStruct((k_row, F), F32),
            *[jax.ShapeDtypeStruct((k_row, D), F32)] * 5,
        ),
        [ANY] + [VM] * 9 + [ANY] * 2 + [VM] * 4 + [ANY] * (2 if hop else 1),
        (VM, VM, VM, ANY, *[VM] * 6),
        [
            pltpu.VMEM((T, D), BF),
            pltpu.VMEM((T, m), F32),
            pltpu.VMEM((2, per, m, m), F32),
            pltpu.VMEM((2, m, m), F32),
            pltpu.VMEM((2, m, m), F32),
            pltpu.VMEM((m, 128), BF),
            pltpu.VMEM((m, 128), BF),
            pltpu.VMEM((T, 4 * m), BF),
            pltpu.VMEM((8, m), F32),
            pltpu.VMEM((8, D), F32),
            pltpu.VMEM((2, 2, T, kk), BF),
            pltpu.VMEM((nk, kk, 4 * m), BF),
            pltpu.VMEM((2, kk, 4 * m), BF),
            pltpu.VMEM((H1, 2, hk, 4 * m), BF),
            pltpu.VMEM((8, hk // 4, 4 * m), BF),
            pltpu.VMEM((2, 16, D), BF),
            pltpu.VMEM((8, 16, D), BF),
            pltpu.VMEM(wo.shape, BF),
            pltpu.VMEM(wo.shape[1:], BF),
            pltpu.VMEM((H1, *wo.shape[2:]), BF),
            pltpu.VMEM(s_f.shape[1:], BF),
            pltpu.VMEM((H1, *s_f.shape[1:]), BF),
            pltpu.VMEM((8, hk // 4, nf), BF),
            pltpu.VMEM((n_dev, 16, 128), F32),
            pltpu.VMEM((n_dev, 16, 128), F32),
            *TeamSum.scratch(rows, D),
            DMA,
            DMA,
            DMA((2,)),
            DMA((8,)),
            DMA((2 + 2 * H1,)),
            DMA((2 + 2 * H1,)),
            DMA((H,)),
            DMA((H,)),
            DMA((H1,)),
            DMA((H1,)),
            DMA((7,)),
            DMA((8,)),
            DMA((7,)),
            DMA((8,)),
            DMA((n_dev,)),
            DMA((n_dev,)),
            DMA((13 + nk,)),
            pltpu.VMEM((8, k_row, nf), BF),
            pltpu.VMEM((8, k_row, 4 * m), BF),
            DMA,
            DMA,
        ],
        3,
    )(d_br, wo, gated, ghat, grstd, gate, rkv, states, mv, full, mixed, diff, w4, x, d_mid, cm_sums, s_f, *([fin] if hop else []))


def dot(a, b, dims):
    return lax.dot_general(a, b, (dims, ((), ())), preferred_element_type=F32)


def mm(a, b):
    return dot(a, b, ((1,), (0,)))


def mm_nt(a, b):
    return dot(a, b, ((1,), (1,)))


def mm_tn(a, b):
    return dot(a, b, ((0,), (0,)))


class Layout:
    def __init__(self, mesh_shape):
        self.A, self.B, self.H, self.L, self.C = mesh_shape
        self.team = self.B * self.L * self.C
        self.n = self.team * self.A * self.H

    def of(self, D):
        self.strided = (D // self.n) % HEAD == 0
        return self

    def spread(self, v, whole):
        w = v.shape[-1] // self.n
        lead = v.shape[:-1]
        if w % whole:
            return v.reshape(*lead, self.team, -1)
        k = len(lead)
        v = v.reshape(*lead, self.A, self.B, self.H, self.L, self.C, w)
        v = v.transpose(*range(k), k + 1, k + 3, k + 4, k, k + 2, k + 5)
        return v.reshape(*lead, self.team, -1)

    def unspread(self, v, whole):
        lead = v.shape[:-2]
        w = v.shape[-1] * self.team // self.n
        if w % whole:
            return v.reshape(*lead, -1)
        k = len(lead)
        v = v.reshape(*lead, self.B, self.L, self.C, self.A, self.H, w)
        v = v.transpose(*range(k), k + 3, k, k + 4, k + 1, k + 2, k + 5)
        return v.reshape(*lead, -1)

    def rows_in(self, g):
        m = g.shape[-1]
        g = g.reshape(self.A, self.H, self.B, self.L, self.C, -1, m)
        return g.transpose(0, 2, 1, 3, 4, 5, 6).reshape(-1, m)

    def rows_out(self, g):
        m = g.shape[-1]
        g = g.reshape(self.A, self.B, self.H, self.L, self.C, -1, m)
        return g.transpose(0, 2, 1, 3, 4, 5, 6).reshape(self.A * self.H, self.team, -1, m)


def normed(v):
    mean = jnp.mean(v, axis=-1, keepdims=True)
    cent = v - mean
    rstd = lax.rsqrt(jnp.mean(cent * cent, axis=-1, keepdims=True) + EPS)
    return cent * rstd, rstd


def norm_back(e, xhat, rstd):
    m1 = jnp.mean(e, axis=-1, keepdims=True)
    m2 = jnp.mean(e * xhat, axis=-1, keepdims=True)
    return (e - m1 - xhat * m2) * rstd


def with_before(rows, halo, segs):
    v = rows.reshape(segs, -1, rows.shape[-1])
    return jnp.concatenate([halo, v[:, :-1]], axis=1).reshape(rows.shape)


def with_after(rows, segs):
    v = rows.reshape(segs, -1, rows.shape[-1])
    return (
        jnp.concatenate([v[:, 1:], jnp.zeros_like(v[:, :1])], axis=1).reshape(rows.shape),
        v[:, :1],
    )


def swap(v, axis):
    return lax.ppermute(v, axis, [(0, 1), (1, 0)])


def per_device(lay, *args):
    (x_in, up_in, start_in) = args[:3]
    vec = args[3:13]
    w_r, w_k, w_v, w_g, w_o = args[13:18]
    vec2 = args[18:22]
    w_ck, w_cv, w_cr = args[22:]
    a_at, b_at, h_at = (lax.axis_index(n) for n in ("a", "b", "h"))
    rank = (b_at * lay.L + lax.axis_index("l")) * lay.C + lax.axis_index("c")
    H = lay.H
    segs = lay.B
    D = x_in.shape[-1]
    x_own = x_in[0]
    rows = x_own.shape[0]
    T = rows * lay.team
    dcol = D // lay.team
    heads = dcol // HEAD
    half = lay.L * lay.C
    w_row = D // lay.n
    lay.of(D)
    hid = w_ck.shape[1] // lay.team

    stacked = jnp.stack([*vec, *vec2])
    nv = stacked.shape[0]
    stacked = jnp.pad(stacked, ((0, 16 - nv), (0, 128 - w_row)))
    o_own = w_o
    if not lay.strided:
        o_own = lax.all_gather(w_o, ALL, axis=0, tiled=True)
        o_own = lax.dynamic_slice_in_dim(o_own, rank * dcol, dcol, 0)
        o_own = o_own.reshape(lay.A, H, -1, D)
    (
        every, my_vecs, mixed, diff1, rkv, gate, upc, W4, W_o, gated, ghat, grstd, states, fin, middle, n2, halo_2,
        W_cv, ffn_all,
    ) = front(lay, stacked, x_own, up_in[0], (w_r, w_k, w_v, w_g), w_ck, w_cr, o_own, w_cv, start_in[0])
    W_cv = W_cv.reshape(hid, D)
    direct = lay.strided and H == 2 and lay.A == 2
    items = []
    if direct:
        blocks = fin.astype(BF).reshape(lay.A, H, HEAD, 128).transpose(1, 0, 2, 3)
        blocks = jnp.broadcast_to(blocks.reshape(H, lay.A * HEAD, 128), (4, H, lay.A * HEAD, 128))
        items = [(blocks.reshape(8, lay.A * HEAD, 128), "t")]
    else:
        nh = start_in.shape[1]
        head_ids = lay.spread(jnp.arange(nh * HEAD, dtype=jnp.int32), HEAD)
        my_heads = lax.dynamic_index_in_dim(head_ids, rank, 0, False)[::HEAD] // HEAD
        s_out = fin.reshape(heads, HEAD, 2, HEAD).transpose(2, 0, 3, 1)
        placed = jnp.zeros((segs, nh, HEAD, HEAD), BF)
        s_fin = jnp.where(h_at == lay.H - 1, s_out, 0.0).astype(BF)
        placed = placed.at[:, my_heads].set(s_fin)
        final = lax.psum_scatter(placed, "b", scatter_dimension=0, tiled=True)
        final = lax.psum_scatter(final, SEQ, scatter_dimension=1, tiled=True).astype(F32)

    wf = ffn_all.reshape(2 * lay.A, D // (2 * lay.A), -1)
    d_mid, d_br, moved, s_cv, got_cv, g_f, got_f, cm_sums, *got_fin = channel_mix(
        lay, n2, halo_2, every, W_cv, wf, upc.reshape(T, dcol), middle, up_in[0], items
    )
    layer_output = (middle + moved.transpose(1, 0, 2).reshape(rows, D).astype(F32)).astype(BF)
    g_cv = s_cv.astype(F32) + jnp.sum(got_cv.astype(F32), axis=0)

    def own_half(g, got):
        part = lax.dynamic_index_in_dim(g, a_at, 0, False).astype(F32) + got.astype(F32)
        part = part.astype(BF).reshape(part.shape[0], H, -1, part.shape[-1])
        return part.transpose(1, 0, 2, 3)

    s_f = own_half(g_f, got_f)
    w4 = W4.reshape(2 * lay.A, D // (2 * lay.A), -1)
    input_grad, g_o, small, fin, g_ck, g_cr, g_r, g_k, g_v, g_w = time_back(
        lay, d_br, W_o, gated, ghat, grstd, gate, rkv, states, my_vecs, every, mixed, diff1, w4, x_own, d_mid,
        cm_sums, s_f, got_fin[0] if direct else None,
    )
    if direct:
        fin = jnp.where(b_at == 0, fin[:, :, :HEAD], fin[:, :, HEAD:])
        final = fin.transpose(0, 2, 1)[None].astype(F32)
    if not lay.strided:
        g_o = jnp.zeros((D, D), BF).at[rank * dcol + jnp.arange(dcol)].set(g_o.reshape(dcol, D))
        g_o = lax.psum_scatter(g_o, ALL, scatter_dimension=0, tiled=True).astype(F32)
    small = small[:, :w_row]
    order = (4, 5, 0, 1, 2, 3, 12, 13, 14, 15, 10, 11, 8, 9)
    small = [small[i] for i in order]

    return (
        layer_output[None],
        input_grad[None],
        final,
        *small[:10],
        g_r,
        g_k,
        g_v,
        g_w,
        g_o,
        *small[10:],
        g_ck,
        g_cv,
        g_cr,
    )


def solution(mesh):
    n_seg, n_seq = mesh.devices.shape
    shape = (n_seg // 2, 2, n_seq // 4, 2, 2)
    view = Mesh(mesh.devices.reshape(shape), ALL)
    lay = Layout(shape)
    seg = ("a", "b")
    vec, mat = P(ALL), P(ALL, None)
    tok = P(seg, SEQ, None)

    def step(*args):
        return per_device(lay, *args)

    return jax.shard_map(
        step,
        mesh=view,
        in_specs=(tok, tok, P(seg, None, None, None), *[vec] * 10, *[mat] * 5, *[vec] * 4, *[mat] * 3),
        out_specs=(tok, tok, P(seg, SEQ, None, None), *[vec] * 10, *[mat] * 5, *[vec] * 4, *[mat] * 3),
        check_vma=False,
    )
```

time: 751 us -> 628 us (0.84); the launches traced: 746 us -> 637 us
  local copies, waits for them, and re-layouts: 60.4 us -> 15.5 us
  Pallas kernels: 644 us -> 612 us
  other arithmetic: 23.5 us -> 8.27 us
  between operations: 15.3 us -> 1.01 us
    pallas_call x5 -> x2, Pallas kernels: 476 us -> 409 us  [the longest x1 236 us: front(): comm_call(body, (jax.ShapeDtypeStruct((16, D), F32), jax.ShapeDtypeStruct...]
    pallas_call x1, Pallas kernels: 168 us -> 203 us  [channel_mix(): comm_call(body, (jax.ShapeDtypeStruct((rows, D), F32), jax.ShapeDtypeStru...]
    convert_element_type x17 -> x0, local copies, waits for them, and re-layouts: 28.9 us -> none  [the longest x16 28.8 us: columns(): return lay.unspread(got[:, :, lo:hi].transpose(1, 0, 2), unit).astype(F32)]
    reshape x23 -> x1, local copies, waits for them, and re-layouts: 15.7 us -> 0.01 us  [per_device(): blocks = fin.astype(BF).reshape(lay.A, H, HEAD, 128).transpose(1, 0, 2, 3)]
    convert_element_type x6 -> x2, other arithmetic: 10.2 us -> 1.92 us  [the longest x1 1 us: per_device(): final = fin.transpose(0, 2, 1)[None].astype(F32)]
  transfers between devices with their start and end apart: 3 -> 0, of which waited for: 0 -> 0; matrix products, arithmetic and copies ran while one was open for 8% -> 0% of each run, Pallas kernels for 20% -> 0%
where the time goes in v4:
time: 628 us; the launch traced here: 637 us
  Pallas kernels  612 us (97%)
  local copies, waits for them, and re-layouts  15.5 us (2%)
  other arithmetic  8.27 us (1%)
    pallas_call x1, Pallas kernels, front(): comm_call(body, (jax.ShapeDtypeStruct((16, D), F32), jax.ShapeDtypeStruct...  236 us
    pallas_call x1, Pallas kernels, channel_mix(): comm_call(body, (jax.ShapeDtypeStruct((rows, D), F32), jax.ShapeDtypeStru...  203 us
    pallas_call x1, Pallas kernels, time_back(): comm_call(body, (jax.ShapeDtypeStruct((rows, D), F32), jax.ShapeDtypeStru...  173 us

profile of v4, /device:TPU:0, one launch (start us, length us, event | category | flops | bytes accessed | tf_op | source)
XLA Modules:
  0.0 636.8 jit_solution(12301303428381841086)
XLA Ops:
  0.7 1.6 stack.59
  2.2 0.6 pad.4.refs_0_
  2.8 236.2 %shard_map.432 = (f32[16,2048]{1,0:T(8,128)}, f32[16,256]{1,0:T(8,128)}, bf16[4,1024,2048]{2,1,0:T(8,128)(2,1)}, bf16[1024,2048]{1,0:T(8,128)(2,1)}, bf16[3,1024...) custom-call(bf16[16,128]{1,0:T(8,128)(2,1)} %pad.4.refs_0_, ...), custom_call_target="tpu_custom_call" | custom-call | tf_op jit(solution)/shard_map/pallas_call | solution.py:919
  239.0 0.9 convert_element_type.42
  239.9 0.7 broadcast_in_dim.10
  240.7 202.7 %shard_map.433 = (f32[128,2048]{1,0:T(8,128)}, bf16[8,128,2048]{2,1,0:T(8,128)(2,1)}, bf16[8,128,256]{2,1,0:T(8,128)(2,1)}, bf16[224,2048]{1,0:T(8,128)(2,1)}, b...) custom-call(bf16[8,128,2048]{2,1,0:T(8,128)(2,1)} %get-tuple-element, ...), custom_call_target="tpu_custom_call" | custom-call | tf_op jit(solution)/shard_map/pallas_call | solution.py:1305
  443.4 0.0 copy-start.1
  443.4 3.1 convert_add_fusion.1
  446.6 0.0 copy-done.1
  446.6 2.2 fusion
  448.8 1.6 copy.57
  450.4 0.0 copy-start.4
  450.4 173.1 %shard_map.434 = (f32[128,2048]{1,0:T(8,128)}, f32[64,2048]{1,0:T(8,128)}, f32[16,128]{1,0:T(8,128)}, bf16[4,64,128]{2,1,0:T(8,128)(2,1)}, f32[64,7168]{1,0:T(8,...) custom-call(bf16[8,128,2048]{2,1,0:T(8,128)(2,1)} %get-tuple-element, ...), custom_call_target="tpu_custom_call" | custom-call | tf_op jit(solution)/shard_map/pallas_call | solution.py:1750
  623.5 1.0 convert_bitcast_fusion.1
  624.5 0.8 copy.55
  625.3 1.5 slice_bitcast_fusion
  626.8 0.0 copy-done.4
  626.8 0.1 convert_bitcast_fusion
  626.9 0.0 copy-start
  626.9 0.3 copy.52
  627.3 0.3 copy.53
  627.6 0.5 copy-done
  628.2 0.0 copy-start.3
  628.2 0.0 copy-start.10
  628.2 0.0 copy-start.9
  628.2 0.9 fusion.1
  629.1 0.5 copy-done.3
  629.6 0.0 copy-start.8
  629.6 0.0 copy-start.7
  629.6 1.0 copy.66
  630.5 0.0 copy-done.10
  630.5 0.0 copy-start.6
  630.5 0.8 copy.67
  631.3 0.0 copy-done.9
  631.3 0.0 copy-start.2
  631.3 0.8 copy.68
  632.1 0.0 copy-done.8
  632.1 0.8 copy.69
  632.9 0.0 copy-done.7
  632.9 0.8 copy.70
  633.7 0.0 copy-done.6
  633.7 0.0 copy-start.5
  633.7 0.8 copy.71
  634.5 0.0 copy-done.2
  634.5 1.2 copy.72
  635.8 0.0 copy-done.5
  635.8 0.8 copy.73
  (1 shorter events, 0.0 us)
Async XLA Ops:
  443.4 3.1 copy-start.1
  450.4 176.4 %copy-start.4 = (bf16[8,128,256]{2,1,0:T(8,128)(2,1)S(1)}, bf16[8,128,256]{2,1,0:T(8,128)(2,1)}, u32[]{:S(2)}) copy-start(bf16[8,128,256]{2,1,0:T(8,128)(2,1)} %get-tuple-element.71) | copy-start | bytes 1572868
  626.9 1.2 copy-start
  628.2 1.4 copy-start.3
  628.2 2.4 copy-start.10
  628.2 3.2 copy-start.9
  629.6 2.6 copy-start.8
  629.6 3.4 copy-start.7
  630.5 3.2 copy-start.6
  631.3 3.2 copy-start.2
  633.7 2.0 copy-start.5

commit v5 on v4

--- a/solution.py
+++ b/solution.py
@@ -72,15 +72,23 @@
     def __init__(self, sems):
         self.sems, self.k, self.open = sems, 0, []
 
-    def go(self, src, dst, landed, to):
+    def go(self, src, dst, landed, to, when=None):
         copy = remote(src, dst, self.sems.at[self.k], landed, to)
         self.k += 1
-        copy.start()
+        if when is None:
+            copy.start()
+        else:
+            pl.when(when)(copy.start)
         self.open.append(copy)
+        return copy
 
     def drain(self):
         for copy in self.open:
             copy.wait_send()
+
+
+def inner(me, H):
+    return me["h"] != me["l"] if H == 2 else me["h"] < 0
 
 
 def landed(ref, sem):
@@ -162,7 +170,7 @@
             self.near.shape[1], lambda at: write(at, mine[at].astype(F32) + self.near[i, at].astype(F32))
         )
 
-    def finish(self, write, then=lambda: None):
+    def finish(self, write, then=lambda: None, between=lambda: None):
         b, l = self.me["b"], self.me["l"]
         tx, tz = {"b": 1 - b}, {"l": 1 - l}
         acc, mid, far, recv, go = self.acc, self.mid, self.far, self.recv, self.copies.go
@@ -179,6 +187,7 @@
             if i == 3:
                 for half, (one, _, _, _) in enumerate(hops):
                     go(upper(acc.at[2], half), mid.at[half], recv.at[4 + half], one)
+        between()
         for half, (one, direct, two, other) in enumerate(hops):
             landed(mid.at[half], recv.at[4 + half])
             into, came = upper(acc.at[other], half), mid.at[half]
@@ -216,6 +225,7 @@
     def __init__(self, me, H, source, out, send, near, far, team=None, count=2):
         self.me, self.H, self.source, self.out = me, H, source, out
         self.near, self.far, self.team, self.count = near, far, team, count
+        self.held = []
         self.copies = Copies(send)
 
     @staticmethod
@@ -256,8 +266,15 @@
                     landed(self.out.at[a, bb, h, ll * 2 + cc], self.near.at[rank_of(bb, ll, cc)])
             for dh in range(1, self.H):
                 to = lax.rem(h + dh, self.H)
-                self.copies.go(src, block, self.far.at[dh, g], {"h": to})
+                when = jnp.logical_not(inner(me, self.H))
+                copy = self.copies.go(src, block, self.far.at[dh, g], {"h": to}, when)
+                self.held.append((g, copy))
             self.copies.go(src, block, self.far.at[0, g], {"a": 1 - a})
+
+    def release(self, only=None):
+        for g, copy in self.held:
+            if only is None or g in only:
+                pl.when(inner(self.me, self.H))(copy.start)
 
     def forward(self, only=None):
         a, h, H = self.me["a"], self.me["h"], self.H
@@ -415,8 +432,11 @@
 
 
 class RowsGather:
-    def __init__(self, me, H, own, out, send, recv, at=None):
+    def __init__(self, me, H, own, out, send, recv, at=None, inner_first=False):
         self.me, self.H, self.own, self.out, self.recv, self.at = me, H, own, out, recv, at
+        self.first = inner(me, H)
+        if not inner_first:
+            self.first = jnp.logical_not(self.first)
         self.copies = Copies(send)
 
     @staticmethod
@@ -429,10 +449,15 @@
     def start(self):
         a, h = self.me["a"], self.me["h"]
         block = self.block(a, h)
+        self.held = []
         for dh in range(1, self.H):
             to = lax.rem(h + dh, self.H)
-            self.copies.go(self.own, block, self.recv.at[dh], {"h": to})
+            self.held.append(self.copies.go(self.own, block, self.recv.at[dh], {"h": to}, self.first))
         self.copies.go(self.own, block, self.recv.at[0], {"a": 1 - a})
+
+    def release(self):
+        for copy in self.held:
+            pl.when(jnp.logical_not(self.first))(copy.start)
 
     def forward(self):
         a, h, H = self.me["a"], self.me["h"], self.H
@@ -687,8 +712,8 @@
             go = RowsGather(me, H, w_o, wos, os_, or_)
         top, rest = pl.ds(0, early), pl.ds(early, cv_rows - early)
         if early:
-            ge = RowsGather(me, H, w_cv.at[top], wcv, es, er, top)
-        gc = RowsGather(me, H, w_cv.at[rest], wcv, ts, tr, rest)
+            ge = RowsGather(me, H, w_cv.at[top], wcv, es, er, top, True)
+        gc = RowsGather(me, H, w_cv.at[rest], wcv, ts, tr, rest, True)
         def head(bb, k):
             if lay.strided:
                 return (((k // H * 2 + bb) * H + k % H) * 2 + l) * 2 + c
@@ -706,11 +731,19 @@
         gw.start()
         for copy in near_states + far_states:
             copy.start()
+        if early:
+            ge.start()
+        gc.start()
         gx.start()
         gv.spread(local[3])
+        gv.release()
         gv.forward()
         gw.spread(local[0])
         gv.finish()
+        local[1].wait()
+        gx.finish()
+        gw.release()
+        gu.start()
         for p in range(8):
             parts = [(lambda lo, hi: w_ck[:, lo:hi], F, *at) for at in rank_columns(lay, F, 1, p)]
 
@@ -721,10 +754,7 @@
             later[p, :, F // 8 :] = w_cr[:, p * m : (p + 1) * m]
         mine_team = pltpu.make_async_copy(later.at[mine], team.at[mine], ls.at[1])
         mine_team.start()
-        local[1].wait()
-        gx.finish()
         gq.start()
-        gu.start()
         gw.forward((0,))
         gh.finish()
 
@@ -769,6 +799,7 @@
         gw.forward((1,))
         if bring_o:
             go.start()
+            go.release()
         mine_team.wait()
         gq.finish()
         keep += [
@@ -777,7 +808,8 @@
         ]
         for copy in keep[2:]:
             copy.start()
-        gf.spread(None, (0,))
+        gf.spread(None, (0, 1, 2))
+        gf.release((0,))
         gw.finish()
         keep.append(pltpu.make_async_copy(wa, w_out, ls.at[9]))
         keep[-1].start()
@@ -833,7 +865,7 @@
             st[s] = jnp.where(h > 0, jnp.zeros_like(z), z)
         chain = Chain(me, H, True, obox, ibox, cs, cr)
         chain.run(st, cl, span_all, ones)
-        gf.spread(None, (1, 2))
+        gf.release((1, 2))
         local[4].wait()
         if bring_o:
             go.forward()
@@ -886,17 +918,20 @@
             middle[at] = v
             own[at] = (norm_rows(v)[0] * full[10:11] + full[11:12]).astype(BF)
 
-        sums.finish(put)
+        def more():
+            gf.spread(None, (3,))
+            if early:
+                ge.release()
+            gc.release()
+
+        sums.finish(put, more)
         keep.append(pltpu.make_async_copy(own, n2.at[mine], ls.at[10]))
         keep[-1].start()
         gn = TeamGather(me, own, lambda p: n2.at[p], gs, gr, ("zx", "zx"))
         gn.start()
         gk = Halo(me, H, own, halo2, ks, kr)
         gk.start()
-        gf.spread(None, (3,))
-        if early:
-            ge.start()
-        gc.start()
+        gf.release((3,))
         gf.forward((0, 1, 2))
         gn.finish()
         gk.finish()
@@ -1081,7 +1116,7 @@
     bg = Background(items, H)
     nb = len(items)
 
-    def body(n2, halo, full, wcv, wf, upc, middle, up, *rest):
+    def body(n2, halo, full, wcv_in, wf_in, upc, middle, up, *rest):
         srcs, rest = rest[:nb], rest[nb:]
         d_mid, d_br, moved, s_cv, got_cv, g_f, got_f, sums = rest[:8]
         dsts, rest = rest[8 : 8 + nb], rest[:8] + rest[8 + nb :]
@@ -1090,6 +1125,7 @@
         cn, ca, cm, cf, c_s, c_r = rest[26:32]
         rn, ra, rm, rf, r_s, r_r = rest[32:38]
         ds, dr, bs, br, es, er, ms, mr, vs, vr, fs, fr, ls = rest[38:51]
+        wf, wcv = rest[51 + len(bg.sems()) :]
         d_pre = act
         me = coords()
         a, b, h, l, c = (me[n] for n in ALL)
@@ -1097,10 +1133,12 @@
         loads = [
             pltpu.make_async_copy(n2.at[p], big.at[pl.ds(p * rows, rows)], ls.at[p]) for p in range(8)
         ]
+        loads.append(pltpu.make_async_copy(wf_in, wf, ls.at[14]))
+        loads.append(pltpu.make_async_copy(wcv_in, wcv, ls.at[15]))
         for copy in loads:
             copy.start()
         greet(me, H, True, True)
-        for copy in loads:
+        for copy in loads[:8]:
             copy.wait()
 
         def write(i, p, v):
@@ -1124,6 +1162,8 @@
             MIX,
         )
 
+        loads[8].wait()
+
         @pl.loop(0, 4)
         def _(t):
             at = rows_at(t, tile)
@@ -1134,6 +1174,8 @@
             relu[at] = pos.astype(BF)
             act[at] = (pos * pos).astype(BF)
 
+        loads[9].wait()
+
         @pl.loop(0, 4)
         def _(t):
             at = rows_at(t, tile)
@@ -1169,6 +1211,11 @@
         gv.start()
         gv.finish()
         keep_val.wait()
+        keep_add = pltpu.make_async_copy(add.at[rows_at(mine, rows)], moved.at[mine], ls.at[11])
+        keep_add.start()
+        gm = Exchange(me, lambda p: add.at[rows_at(p, rows)], lambda p: moved.at[p], ms, mr)
+        gm.start()
+        bg.start(me, srcs, dsts, rest[51:-2])
 
         @pl.loop(0, 8)
         def _(q):
@@ -1214,22 +1261,19 @@
                 [sums.at[k : k + 1, lo : lo + kk] for k in range(2)],
             )
 
-        def grads(i):
-            lo = i * kk
-            for k in range(2):
-                at = slice(lo + k * kk // 2, lo + (k + 1) * kk // 2)
-                to = slice(k * kk // 2, (k + 1) * kk // 2)
-                stage[to, :F] = dot_tn(m2[0, :, at], d_pre[...]).astype(BF)
-                stage[to, F:] = dot_tn(m2[1, :, at], d_pg[...]).astype(BF)
-            copy = pltpu.make_async_copy(stage, g_f.at[i // 2, i % 2], ls.at[9])
+        def grads(step, k):
+            i = lax.rem(a + 1 + step, A)
+            for q in range(2):
+                at = pl.ds(pl.multiple_of((i * 2 + k) * kk + q * (kk // 2), kk // 2), kk // 2)
+                to = slice(q * kk // 2, (q + 1) * kk // 2)
+                stage[k, to, :F] = dot_tn(m2[0, :, at], d_pre[...]).astype(BF)
+                stage[k, to, F:] = dot_tn(m2[1, :, at], d_pg[...]).astype(BF)
+            copy = pltpu.make_async_copy(stage.at[k], g_f.at[i, k], ls.at[9 if k == 0 else 13])
             copy.start()
             return copy
 
         for i in range(nk):
-            copy = grads(i)
             chunk_of(i)
-            copy.wait()
-        ff.go(g_f.at[1 - a], got_f, fr.at[0], {"a": 1 - a})
         total = TeamSum(me, lambda p: big.at[rows_at(p, rows)], rn, ra, rm, rf, r_s, r_r)
         total.start()
         e = Edge(me, H, first, edge, es, er)
@@ -1240,15 +1284,21 @@
 
         halves = 2 if w_cv % 32 == 0 else 1
 
+        held = []
+
         def pass_on(g):
             at = pl.ds(g * (w_cv // halves), w_cv // halves)
             for dh in range(1, H):
                 to = lax.rem(h + dh, H)
-                cv.go(
-                    gcv.at[a, to, at],
-                    got_cv.at[dh - 1, at],
-                    vr.at[1 + (dh - 1) * 2 + g],
-                    {"h": to},
+                when = None if g == 0 else jnp.logical_not(inner(me, H))
+                held.append(
+                    cv.go(
+                        gcv.at[a, to, at],
+                        got_cv.at[dh - 1, at],
+                        vr.at[1 + (dh - 1) * 2 + g],
+                        {"h": to},
+                        when,
+                    )
                 )
 
         def value_sums():
@@ -1259,8 +1309,15 @@
                 gcv[a, j] = (gcv[a, j].astype(F32) + cvbuf[j].astype(F32)).astype(BF)
 
             pass_on(0)
-
-        total.finish(put_dn, value_sums)
+            for copy in staged:
+                copy.wait()
+            ff.go(g_f.at[1 - a, 0], got_f, fr.at[0], {"a": 1 - a})
+            staged[:] = [grads(1, 0), grads(1, 1)]
+
+        staged = []
+        total.finish(put_dn, value_sums, lambda: staged.extend([grads(0, 0), grads(0, 1)]))
+        for copy in staged:
+            copy.wait()
         e.finish(dn2)
 
         @pl.loop(0, rows // MIX)
@@ -1276,20 +1333,18 @@
 
         keep = [
             pltpu.make_async_copy(own, d_br.at[mine], ls.at[10]),
-            pltpu.make_async_copy(add.at[rows_at(mine, rows)], moved.at[mine], ls.at[11]),
+            keep_add,
         ]
-        for copy in keep:
-            copy.start()
+        keep[0].start()
         gx = TeamGather(me, own, lambda p: d_br.at[p], bs, br, ("zx", "zx"))
         gx.start()
         if halves == 2:
             pass_on(1)
+            for copy in held[len(held) // 2 :]:
+                pl.when(inner(me, H))(copy.start)
         keep.append(pltpu.make_async_copy(gcv.at[a, h], s_cv, ls.at[12]))
         keep[-1].start()
         gx.finish()
-        gm = Exchange(me, lambda p: add.at[rows_at(p, rows)], lambda p: moved.at[p], ms, mr)
-        gm.start()
-        bg.start(me, srcs, dsts, rest[51:])
         gm.finish()
         bg.finish()
         landed(got_f, fr.at[0])
@@ -1311,11 +1366,11 @@
             jax.ShapeDtypeStruct((w_cv, D), BF),
             jax.ShapeDtypeStruct((max(H - 1, 1), w_cv, D), BF),
             jax.ShapeDtypeStruct((A, nk // A, kk, F + m), BF),
-            jax.ShapeDtypeStruct((nk // A, kk, F + m), BF),
+            jax.ShapeDtypeStruct((kk, F + m), BF),
             jax.ShapeDtypeStruct((8, D), F32),
             *bg.outs(),
         ),
-        [ANY, VM, VM, VM, VM, VM, VM, VM] + [ANY] * nb,
+        [ANY, VM, VM, ANY, ANY, VM, VM, VM] + [ANY] * nb,
         (VM, ANY, ANY, ANY, ANY, ANY, ANY, VM, *[ANY] * nb),
         [
             pltpu.VMEM((T, D), BF),
@@ -1330,7 +1385,7 @@
             pltpu.VMEM((T, D), BF),
             pltpu.VMEM((A, H, w_cv, D), BF),
             pltpu.VMEM((H, w_cv, D), BF),
-            pltpu.VMEM((kk, F + m), BF),
+            pltpu.VMEM((2, kk, F + m), BF),
             pltpu.VMEM((rows, D), F32),
             pltpu.VMEM((rows, D), BF),
             pltpu.VMEM((T, m), BF),
@@ -1350,14 +1405,16 @@
             DMA((2 * H,)),
             DMA((1,)),
             DMA((1,)),
-            DMA((13,)),
+            DMA((16,)),
             *bg.sems(),
+            pltpu.VMEM(wf.shape, BF),
+            pltpu.VMEM(wcv.shape, BF),
         ],
         2,
     )(n2, halo, full, wcv, wf, upc, middle, up, *bg.arrays())
 
 
-def time_back(lay, d_br, wo, gated, ghat, grstd, gate, rkv, states, mv, full, mixed, diff, w4, x, d_mid, cm_sums, s_f, fin):
+def time_back(lay, d_br, wo, gated, ghat, grstd, gate, rkv, states, mv, full, mixed, diff, w4, x, d_mid, cm_sums, s_f, g_f, fin):
     H, A, n_dev = lay.H, lay.A, lay.n
     T, m = gate.shape
     rows, D = x.shape
@@ -1375,7 +1432,8 @@
     k_row = hk // 4
 
     def body(*refs):
-        d_br, wo, gated, ghat, grstd, gate, rkv, states, mv, full, mixed, diff, w4, x, d_mid, cm_sums, s_f = refs[:17]
+        d_br, wo, gated, ghat, grstd, gate, rkv, states, mv, full, mixed, diff, w4_in, x, d_mid, cm_sums, s_f = refs[:17]
+        g_f, refs = refs[17], refs[:17] + refs[18:]
         if hop:
             fin, refs = refs[17], refs[:17] + refs[18:]
         in_grad, o_out, total_out, fin_out, ck_out, cr_out, *four = refs[17:27]
@@ -1385,7 +1443,7 @@
         dn1 = in_grad
         (g_o, o_got, o_late, f_own, f_got, t_f, small, s_got) = refs[39:47]
         rn, ra, rm, rf, r_s, r_r = refs[47:53]
-        cs, cr, es, er, gs, gr, os_, or_, fs, fr, xs, xr, ys, yr, ss, sr, ls, f_out, g_out, hs, hr = refs[53:]
+        cs, cr, es, er, gs, gr, os_, or_, fs, fr, xs, xr, ys, yr, ss, sr, ls, f_out, g_out, hs, hr, f1, f1_got, f1s, f1r, w4 = refs[53:]
         me = coords()
         a, b, h, l, c = (me[k] for k in ALL)
         mine = rank_of(b, l, c)
@@ -1393,6 +1451,8 @@
             pltpu.make_async_copy(d_br.at[p], big.at[pl.ds(p * rows, rows)], ls.at[p]) for p in range(8)
         ]
         loads.append(pltpu.make_async_copy(s_f.at[h], f_own, ls.at[8]))
+        loads.append(pltpu.make_async_copy(g_f.at[a, 1], f1, ls.at[13 + nk]))
+        loads.append(pltpu.make_async_copy(w4_in, w4, ls.at[14 + nk]))
         for copy in loads:
             copy.start()
 
@@ -1414,6 +1474,8 @@
             others.append((i, to))
             pl.semaphore_signal(sem, inc=1, device_id=to, device_id_type=MESH)
         pl.semaphore_wait(sem, n_dev - 1)
+        c1 = Copies(f1s)
+        c1.go(g_f.at[1 - a, 1], f1_got, f1r, {"a": 1 - a})
         for copy in loads[:8]:
             copy.wait()
 
@@ -1458,9 +1520,11 @@
         chain = Chain(me, H, False, obox, ibox, cs, cr)
         chain.run(st, cl, span_all, ones)
         cf = Copies(fs)
+        held = []
         for dh in range(1, H):
             to = lax.rem(h + dh, H)
-            cf.go(s_f.at[to], f_got.at[dh - 1], fr.at[dh - 1], {"h": to})
+            when = jnp.logical_not(inner(me, H))
+            held.append(cf.go(s_f.at[to], f_got.at[dh - 1, 0], fr.at[2 * dh - 2], {"h": to}, when))
 
         if hop:
             mine_fin = fin.at[pl.ds(l * 4, 4)]
@@ -1523,6 +1587,19 @@
                 tsum[0:1] += d_l
                 st[s] = dec.span * end + adds[s, n]
 
+        for copy in held:
+            pl.when(inner(me, H))(copy.start)
+        loads[9].wait()
+        landed(f1_got, f1r)
+
+        @pl.loop(0, kk // 64)
+        def _(q):
+            at = rows_at(q, 64)
+            f1[at] = (f1[at].astype(F32) + f1_got[at].astype(F32)).astype(BF)
+
+        for dh in range(1, H):
+            to = lax.rem(h + dh, H)
+            cf.go(f1.at[rows_at(to, hk)], f_got.at[dh - 1, 1], fr.at[2 * dh - 1], {"h": to})
         chain.finish()
 
         cg = Copies(gs)
@@ -1583,6 +1660,7 @@
                 [sums.at[j : j + 1, lo : lo + kk] for j in range(4)],
             )
 
+        loads[10].wait()
         for i in range(nk):
             difs[i].wait()
             chunk_of(i)
@@ -1618,6 +1696,26 @@
                     cg.go(
                         g4.at[a * 2 + k, rows_at(to, hk)], late.at[dh - 1, k], gr.at[2 + v], {"h": to}
                     )
+
+            loads[8].wait()
+            for dh in range(1, H):
+                for k in range(2):
+                    landed(f_got.at[dh - 1, k], fr.at[2 * dh - 2 + k])
+            for k in range(2):
+                for q in range(4):
+                    at = pl.ds(q * (hk // 4), hk // 4)
+                    if k == 0:
+                        v = f_own[at].astype(F32)
+                    else:
+                        v = f1[pl.ds(pl.multiple_of(h * hk + q * (hk // 4), hk // 4), hk // 4)].astype(F32)
+                    for dh in range(1, H):
+                        v = v + f_got[dh - 1, k, at].astype(F32)
+                    t_f[k * 4 + q] = v.astype(BF)
+            keep_f.start()
+            gf.start()
+
+        keep_f = pltpu.make_async_copy(t_f.at[mine], f_out.at[mine], ls.at[11])
+        gf = Exchange(me, lambda p: t_f.at[p], lambda p: f_out.at[p], xs, xr)
 
         def put_dn(at, v):
             dn1[at] = v
@@ -1667,20 +1765,6 @@
         for i, to in others:
             cv.go(small.at[flat(to)], s_got.at[i], sr.at[i], to)
 
-        loads[8].wait()
-        for dh in range(1, H):
-            landed(f_got.at[dh - 1], fr.at[dh - 1])
-        for k in range(2):
-            for q in range(4):
-                at = pl.ds(q * (hk // 4), hk // 4)
-                v = f_own[k, at].astype(F32)
-                for dh in range(1, H):
-                    v = v + f_got[dh - 1, k, at].astype(F32)
-                t_f[k * 4 + q] = v.astype(BF)
-        keep = [pltpu.make_async_copy(t_f.at[mine], f_out.at[mine], ls.at[11])]
-        keep[0].start()
-        gf = Exchange(me, lambda p: t_f.at[p], lambda p: f_out.at[p], xs, xr)
-        gf.start()
         for k in range(2):
             for dh in range(1, H):
                 landed(late.at[dh - 1, k], gr.at[2 + (dh - 1) * 2 + k])
@@ -1690,7 +1774,7 @@
                 for dh in range(1, H):
                     v = v + late[dh - 1, k, pl.ds(q * (hk // 4), hk // 4)].astype(F32)
                 t4[k * 4 + q] = v.astype(BF)
-        keep.append(pltpu.make_async_copy(t4.at[mine], g_out.at[mine], ls.at[12]))
+        keep = [keep_f, pltpu.make_async_copy(t4.at[mine], g_out.at[mine], ls.at[12])]
         keep[1].start()
         gg = Exchange(me, lambda p: t4.at[p], lambda p: g_out.at[p], ys, yr)
         gg.start()
@@ -1743,7 +1827,7 @@
         gg.finish()
         for j, ref in enumerate(four):
             lay_lanes(D, from_ranks(g_out, j * m, D, HEAD), into(ref))
-        for copies in (cf, co, cg, cv):
+        for copies in (c1, cf, co, cg, cv):
             copies.drain()
 
     o_shape = wo.shape[2:] if strided else wo.shape
@@ -1757,7 +1841,7 @@
             jax.ShapeDtypeStruct((k_row, F), F32),
             *[jax.ShapeDtypeStruct((k_row, D), F32)] * 5,
         ),
-        [ANY] + [VM] * 9 + [ANY] * 2 + [VM] * 4 + [ANY] * (2 if hop else 1),
+        [ANY] + [VM] * 9 + [ANY] * 3 + [VM] * 3 + [ANY] * (3 if hop else 2),
         (VM, VM, VM, ANY, *[VM] * 6),
         [
             pltpu.VMEM((T, D), BF),
@@ -1781,7 +1865,7 @@
             pltpu.VMEM(wo.shape[1:], BF),
             pltpu.VMEM((H1, *wo.shape[2:]), BF),
             pltpu.VMEM(s_f.shape[1:], BF),
-            pltpu.VMEM((H1, *s_f.shape[1:]), BF),
+            pltpu.VMEM((H1, 2, *s_f.shape[1:]), BF),
             pltpu.VMEM((8, hk // 4, nf), BF),
             pltpu.VMEM((n_dev, 16, 128), F32),
             pltpu.VMEM((n_dev, 16, 128), F32),
@@ -1794,22 +1878,27 @@
             DMA((2 + 2 * H1,)),
             DMA((H,)),
             DMA((H,)),
-            DMA((H1,)),
-            DMA((H1,)),
+            DMA((2 * H1,)),
+            DMA((2 * H1,)),
             DMA((7,)),
             DMA((8,)),
             DMA((7,)),
             DMA((8,)),
             DMA((n_dev,)),
             DMA((n_dev,)),
-            DMA((13 + nk,)),
+            DMA((15 + nk,)),
             pltpu.VMEM((8, k_row, nf), BF),
             pltpu.VMEM((8, k_row, 4 * m), BF),
             DMA,
             DMA,
+            pltpu.VMEM((kk, nf), BF),
+            pltpu.VMEM((kk, nf), BF),
+            DMA((1,)),
+            DMA,
+            pltpu.VMEM(w4.shape, BF),
         ],
         3,
-    )(d_br, wo, gated, ghat, grstd, gate, rkv, states, mv, full, mixed, diff, w4, x, d_mid, cm_sums, s_f, *([fin] if hop else []))
+    )(d_br, wo, gated, ghat, grstd, gate, rkv, states, mv, full, mixed, diff, w4, x, d_mid, cm_sums, s_f, g_f, *([fin] if hop else []))
 
 
 def dot(a, b, dims):
@@ -1957,16 +2046,12 @@
     layer_output = (middle + moved.transpose(1, 0, 2).reshape(rows, D).astype(F32)).astype(BF)
     g_cv = s_cv.astype(F32) + jnp.sum(got_cv.astype(F32), axis=0)
 
-    def own_half(g, got):
-        part = lax.dynamic_index_in_dim(g, a_at, 0, False).astype(F32) + got.astype(F32)
-        part = part.astype(BF).reshape(part.shape[0], H, -1, part.shape[-1])
-        return part.transpose(1, 0, 2, 3)
-
-    s_f = own_half(g_f, got_f)
+    s_f = lax.dynamic_index_in_dim(g_f[:, 0], a_at, 0, False).astype(F32) + got_f.astype(F32)
+    s_f = s_f.astype(BF).reshape(H, -1, s_f.shape[-1])
     w4 = W4.reshape(2 * lay.A, D // (2 * lay.A), -1)
     input_grad, g_o, small, fin, g_ck, g_cr, g_r, g_k, g_v, g_w = time_back(
         lay, d_br, W_o, gated, ghat, grstd, gate, rkv, states, my_vecs, every, mixed, diff1, w4, x_own, d_mid,
-        cm_sums, s_f, got_fin[0] if direct else None,
+        cm_sums, s_f, g_f, got_fin[0] if direct else None,
     )
     if direct:
         fin = jnp.where(b_at == 0, fin[:, :, :HEAD], fin[:, :, HEAD:])

time: 628 us -> 595 us (0.947); the launches traced: 637 us -> 592 us
  Pallas kernels: 612 us -> 568 us
    pallas_call x1, Pallas kernels: 203 us -> 176 us  [channel_mix(): comm_call(body, (jax.ShapeDtypeStruct((rows, D), F32), jax.ShapeDtypeStru...]
    pallas_call x1, Pallas kernels: 173 us -> 162 us  [time_back(): comm_call(body, (jax.ShapeDtypeStruct((rows, D), F32), jax.ShapeDtypeStru...]
    pallas_call x1, Pallas kernels: 236 us -> 230 us  [front(): comm_call(body, (jax.ShapeDtypeStruct((16, D), F32), jax.ShapeDtypeStruct...]
where the time goes in v5:
time: 595 us; the launch traced here: 592 us
  Pallas kernels  568 us (95%)
  local copies, waits for them, and re-layouts  15.9 us (3%)
  other arithmetic  7.19 us (1%)
    pallas_call x1, Pallas kernels, front(): comm_call(body, (jax.ShapeDtypeStruct((16, D), F32), jax.ShapeDtypeStruct...  230 us
    pallas_call x1, Pallas kernels, channel_mix(): comm_call(body, (jax.ShapeDtypeStruct((rows, D), F32), jax.ShapeDtypeStru...  176 us
    pallas_call x1, Pallas kernels, time_back(): comm_call(body, (jax.ShapeDtypeStruct((rows, D), F32), jax.ShapeDtypeStru...  162 us

profile of v5, /device:TPU:0, one launch (start us, length us, event | category | flops | bytes accessed | tf_op | source)
XLA Modules:
  0.0 591.7 jit_solution(13337806967027992285)
XLA Ops:
  0.7 1.6 stack.59
  2.2 0.6 pad.4.refs_0_
  2.8 229.6 %shard_map.432 = (f32[16,2048]{1,0:T(8,128)}, f32[16,256]{1,0:T(8,128)}, bf16[4,1024,2048]{2,1,0:T(8,128)(2,1)}, bf16[1024,2048]{1,0:T(8,128)(2,1)}, bf16[3,1024...) custom-call(bf16[16,128]{1,0:T(8,128)(2,1)} %pad.4.refs_0_, ...), custom_call_target="tpu_custom_call" | custom-call | tf_op jit(solution)/shard_map/pallas_call | solution.py:954
  232.4 0.9 convert_element_type.42
  233.3 0.7 broadcast_in_dim.10
  234.1 176.2 %shard_map.433 = (f32[128,2048]{1,0:T(8,128)}, bf16[8,128,2048]{2,1,0:T(8,128)(2,1)}, bf16[8,128,256]{2,1,0:T(8,128)(2,1)}, bf16[224,2048]{1,0:T(8,128)(2,1)}, b...) custom-call(bf16[8,128,2048]{2,1,0:T(8,128)(2,1)} %get-tuple-element, ...), custom_call_target="tpu_custom_call" | custom-call | tf_op jit(solution)/shard_map/pallas_call | solution.py:1360
  410.3 3.0 convert_add_fusion.1
  413.3 0.0 copy-start.2
  413.3 1.9 slice.66
  415.3 0.0 copy-done.2
  415.3 1.3 fusion
  416.6 0.0 copy-start.4
  416.6 161.9 %shard_map.434 = (f32[128,2048]{1,0:T(8,128)}, f32[64,2048]{1,0:T(8,128)}, f32[16,128]{1,0:T(8,128)}, bf16[4,64,128]{2,1,0:T(8,128)(2,1)}, f32[64,7168]{1,0:T(8,...) custom-call(bf16[8,128,2048]{2,1,0:T(8,128)(2,1)} %get-tuple-element, ...), custom_call_target="tpu_custom_call" | custom-call | tf_op jit(solution)/shard_map/pallas_call | solution.py:1834
  578.5 1.0 convert_bitcast_fusion.1
  579.5 0.8 copy.54
  580.2 1.5 slice_bitcast_fusion
  581.8 0.0 copy-done.4
  581.8 0.1 convert_bitcast_fusion
  581.9 0.0 copy-start
  581.9 0.3 copy.52
  582.2 0.3 copy.53
  582.6 0.5 copy-done
  583.1 0.0 copy-start.3
  583.1 0.0 copy-start.10
  583.1 0.0 copy-start.9
  583.1 0.9 fusion.1
  584.0 0.5 copy-done.3
  584.5 0.0 copy-start.8
  584.5 0.0 copy-start.7
  584.5 1.0 copy.63
  585.5 0.0 copy-done.10
  585.5 0.0 copy-start.6
  585.5 0.8 copy.64
  586.3 0.0 copy-done.9
  586.3 0.0 copy-start.1
  586.3 0.8 copy.65
  587.1 0.0 copy-done.8
  587.1 0.8 copy.66
  587.9 0.0 copy-done.7
  587.9 0.8 copy.67
  588.7 0.0 copy-done.6
  588.7 0.0 copy-start.5
  588.7 0.8 copy.68
  589.5 0.0 copy-done.1
  589.5 1.2 copy.69
  590.7 0.0 copy-done.5
  590.7 0.8 copy.70
  (1 shorter events, 0.0 us)
Async XLA Ops:
  413.3 2.0 copy-start.2
  416.6 165.2 %copy-start.4 = (bf16[8,128,256]{2,1,0:T(8,128)(2,1)S(1)}, bf16[8,128,256]{2,1,0:T(8,128)(2,1)}, u32[]{:S(2)}) copy-start(bf16[8,128,256]{2,1,0:T(8,128)(2,1)} %get-tuple-element.71) | copy-start | bytes 1572868
  581.9 1.2 copy-start
  583.1 1.4 copy-start.3
  583.1 2.4 copy-start.10
  583.1 3.2 copy-start.9
  584.5 2.6 copy-start.8
  584.5 3.4 copy-start.7
  585.5 3.2 copy-start.6
  586.3 3.2 copy-start.1
  588.7 2.0 copy-start.5

commit v6 on v5

--- a/solution.py
+++ b/solution.py
@@ -72,14 +72,18 @@
     def __init__(self, sems):
         self.sems, self.k, self.open = sems, 0, []
 
-    def go(self, src, dst, landed, to, when=None):
+    def plan(self, src, dst, landed, to):
         copy = remote(src, dst, self.sems.at[self.k], landed, to)
         self.k += 1
+        self.open.append(copy)
+        return copy
+
+    def go(self, src, dst, landed, to, when=None):
+        copy = self.plan(src, dst, landed, to)
         if when is None:
             copy.start()
         else:
             pl.when(when)(copy.start)
-        self.open.append(copy)
         return copy
 
     def drain(self):
@@ -459,12 +463,27 @@
         for copy in self.held:
             pl.when(jnp.logical_not(self.first))(copy.start)
 
-    def forward(self):
+    def forward(self, early=None):
         a, h, H = self.me["a"], self.me["h"], self.H
+        if early:
+            self.passed = []
         for dh in range(1, H):
             block = self.block(a, lax.rem(h - dh + H, H))
-            landed(block, self.recv.at[dh])
-            self.copies.go(block, block, self.recv.at[H - 1 + dh], {"a": 1 - a})
+            if early is None:
+                landed(block, self.recv.at[dh])
+                self.copies.go(block, block, self.recv.at[H - 1 + dh], {"a": 1 - a})
+                continue
+            if early:
+                on = self.copies.plan(block, block, self.recv.at[H - 1 + dh], {"a": 1 - a})
+                self.passed.append(on)
+            on = self.passed[dh - 1]
+            now = jnp.logical_not(self.first) if H == 2 else self.first
+            now = now if early else jnp.logical_not(now)
+
+            @pl.when(now)
+            def _():
+                landed(block, self.recv.at[dh])
+                on.start()
 
     def finish(self):
         a, h, H = self.me["a"], self.me["h"], self.H
@@ -866,9 +885,15 @@
         chain = Chain(me, H, True, obox, ibox, cs, cr)
         chain.run(st, cl, span_all, ones)
         gf.release((1, 2))
+        if early:
+            ge.release()
         local[4].wait()
         if bring_o:
             go.forward()
+        gf.forward((0,))
+        if early:
+            ge.forward(True)
+        gc.forward(True)
         low = triangle(heads, True)
 
         @pl.loop(0, per)
@@ -919,9 +944,8 @@
             own[at] = (norm_rows(v)[0] * full[10:11] + full[11:12]).astype(BF)
 
         def more():
+            gf.forward((1, 2))
             gf.spread(None, (3,))
-            if early:
-                ge.release()
             gc.release()
 
         sums.finish(put, more)
@@ -932,13 +956,12 @@
         gk = Halo(me, H, own, halo2, ks, kr)
         gk.start()
         gf.release((3,))
-        gf.forward((0, 1, 2))
+        if early:
+            ge.forward(False)
         gn.finish()
         gk.finish()
         gf.forward((3,))
-        if early:
-            ge.forward()
-        gc.forward()
+        gc.forward(False)
         gu.finish()
         gf.finish()
         if early:

time: 595 us -> 585 us (0.983)
  Pallas kernels: 568 us -> 555 us
    pallas_call x1, Pallas kernels: 230 us -> 210 us  [front(): comm_call(body, (jax.ShapeDtypeStruct((16, D), F32), jax.ShapeDtypeStruct...]
    pallas_call x1, Pallas kernels: 176 us -> 187 us  [channel_mix(): comm_call(body, (jax.ShapeDtypeStruct((rows, D), F32), jax.ShapeDtypeStru...]
where the time goes in v6:
time: 585 us; the launch traced here: 579 us
  Pallas kernels  555 us (95%)
  local copies, waits for them, and re-layouts  15.9 us (3%)
  other arithmetic  7.19 us (1%)
    pallas_call x1, Pallas kernels, front(): comm_call(body, (jax.ShapeDtypeStruct((16, D), F32), jax.ShapeDtypeStruct...  210 us
    pallas_call x1, Pallas kernels, channel_mix(): comm_call(body, (jax.ShapeDtypeStruct((rows, D), F32), jax.ShapeDtypeStru...  187 us
    pallas_call x1, Pallas kernels, time_back(): comm_call(body, (jax.ShapeDtypeStruct((rows, D), F32), jax.ShapeDtypeStru...  158 us

profile of v6, /device:TPU:0, one launch (start us, length us, event | category | flops | bytes accessed | tf_op | source)
XLA Modules:
  0.0 578.7 jit_solution(10450042936255962687)
XLA Ops:
  0.7 1.6 stack.59
  2.2 0.6 pad.4.refs_0_
  2.8 209.5 %shard_map.432 = (f32[16,2048]{1,0:T(8,128)}, f32[16,256]{1,0:T(8,128)}, bf16[4,1024,2048]{2,1,0:T(8,128)(2,1)}, bf16[1024,2048]{1,0:T(8,128)(2,1)}, bf16[3,1024...) custom-call(bf16[16,128]{1,0:T(8,128)(2,1)} %pad.4.refs_0_, ...), custom_call_target="tpu_custom_call" | custom-call | tf_op jit(solution)/shard_map/pallas_call | solution.py:977
  212.4 0.9 convert_element_type.42
  213.3 0.7 broadcast_in_dim.10
  214.0 187.3 %shard_map.433 = (f32[128,2048]{1,0:T(8,128)}, bf16[8,128,2048]{2,1,0:T(8,128)(2,1)}, bf16[8,128,256]{2,1,0:T(8,128)(2,1)}, bf16[224,2048]{1,0:T(8,128)(2,1)}, b...) custom-call(bf16[8,128,2048]{2,1,0:T(8,128)(2,1)} %get-tuple-element, ...), custom_call_target="tpu_custom_call" | custom-call | tf_op jit(solution)/shard_map/pallas_call | solution.py:1383
  401.3 3.0 convert_add_fusion.1
  404.3 0.0 copy-start.2
  404.3 1.9 slice.66
  406.3 0.0 copy-done.2
  406.3 1.3 fusion
  407.6 0.0 copy-start.4
  407.6 157.9 %shard_map.434 = (f32[128,2048]{1,0:T(8,128)}, f32[64,2048]{1,0:T(8,128)}, f32[16,128]{1,0:T(8,128)}, bf16[4,64,128]{2,1,0:T(8,128)(2,1)}, f32[64,7168]{1,0:T(8,...) custom-call(bf16[8,128,2048]{2,1,0:T(8,128)(2,1)} %get-tuple-element, ...), custom_call_target="tpu_custom_call" | custom-call | tf_op jit(solution)/shard_map/pallas_call | solution.py:1857
  565.5 1.0 convert_bitcast_fusion.1
  566.5 0.8 copy.54
  567.2 1.5 slice_bitcast_fusion
  568.8 0.0 copy-done.4
  568.8 0.1 convert_bitcast_fusion
  568.9 0.0 copy-start
  568.9 0.3 copy.52
  569.2 0.3 copy.53
  569.6 0.5 copy-done
  570.1 0.0 copy-start.3
  570.1 0.0 copy-start.10
  570.1 0.0 copy-start.9
  570.1 0.9 fusion.1
  571.0 0.5 copy-done.3
  571.5 0.0 copy-start.8
  571.5 0.0 copy-start.7
  571.5 1.0 copy.63
  572.5 0.0 copy-done.10
  572.5 0.0 copy-start.6
  572.5 0.8 copy.64
  573.3 0.0 copy-done.9
  573.3 0.0 copy-start.1
  573.3 0.8 copy.65
  574.1 0.0 copy-done.8
  574.1 0.8 copy.66
  574.9 0.0 copy-done.7
  574.9 0.8 copy.67
  575.7 0.0 copy-done.6
  575.7 0.0 copy-start.5
  575.7 0.8 copy.68
  576.5 0.0 copy-done.1
  576.5 1.2 copy.69
  577.7 0.0 copy-done.5
  577.7 0.8 copy.70
  (1 shorter events, 0.0 us)
Async XLA Ops:
  404.3 2.0 copy-start.2
  407.6 161.2 %copy-start.4 = (bf16[8,128,256]{2,1,0:T(8,128)(2,1)S(1)}, bf16[8,128,256]{2,1,0:T(8,128)(2,1)}, u32[]{:S(2)}) copy-start(bf16[8,128,256]{2,1,0:T(8,128)(2,1)} %get-tuple-element.71) | copy-start | bytes 1572868
  568.9 1.2 copy-start
  570.1 1.4 copy-start.3
  570.1 2.4 copy-start.10
  570.1 3.2 copy-start.9
  571.5 2.6 copy-start.8
  571.5 3.4 copy-start.7
  572.5 3.2 copy-start.6
  573.3 3.2 copy-start.1
  575.7 2.0 copy-start.5

commit v7 on v6

--- a/solution.py
+++ b/solution.py
@@ -887,6 +887,7 @@
         gf.release((1, 2))
         if early:
             ge.release()
+        gc.release()
         local[4].wait()
         if bring_o:
             go.forward()
@@ -946,7 +947,6 @@
         def more():
             gf.forward((1, 2))
             gf.spread(None, (3,))
-            gc.release()
 
         sums.finish(put, more)
         keep.append(pltpu.make_async_copy(own, n2.at[mine], ls.at[10]))
@@ -958,10 +958,10 @@
         gf.release((3,))
         if early:
             ge.forward(False)
+        gc.forward(False)
         gn.finish()
         gk.finish()
         gf.forward((3,))
-        gc.forward(False)
         gu.finish()
         gf.finish()
         if early:
@@ -2069,7 +2069,8 @@
     layer_output = (middle + moved.transpose(1, 0, 2).reshape(rows, D).astype(F32)).astype(BF)
     g_cv = s_cv.astype(F32) + jnp.sum(got_cv.astype(F32), axis=0)
 
-    s_f = lax.dynamic_index_in_dim(g_f[:, 0], a_at, 0, False).astype(F32) + got_f.astype(F32)
+    s_f = lax.dynamic_slice(g_f, (a_at, 0, 0, 0), (1, 1, *g_f.shape[2:]))[0, 0]
+    s_f = s_f.astype(F32) + got_f.astype(F32)
     s_f = s_f.astype(BF).reshape(H, -1, s_f.shape[-1])
     w4 = W4.reshape(2 * lay.A, D // (2 * lay.A), -1)
     input_grad, g_o, small, fin, g_ck, g_cr, g_r, g_k, g_v, g_w = time_back(

time: 585 us -> 582 us (level); the launches traced: 579 us -> 582 us
    pallas_call x1, Pallas kernels: 187 us -> 175 us  [channel_mix(): comm_call(body, (jax.ShapeDtypeStruct((rows, D), F32), jax.ShapeDtypeStru...]
    pallas_call x1, Pallas kernels: 158 us -> 166 us  [time_back(): comm_call(body, (jax.ShapeDtypeStruct((rows, D), F32), jax.ShapeDtypeStru...]
    pallas_call x1, Pallas kernels: 210 us -> 217 us  [front(): comm_call(body, (jax.ShapeDtypeStruct((16, D), F32), jax.ShapeDtypeStruct...]
where the time goes in v7:
time: 582 us
  Pallas kernels  559 us (96%)
  local copies, waits for them, and re-layouts  14.1 us (2%)
  other arithmetic  8.55 us (1%)
    pallas_call x1, Pallas kernels, front(): comm_call(body, (jax.ShapeDtypeStruct((16, D), F32), jax.ShapeDtypeStruct...  217 us
    pallas_call x1, Pallas kernels, channel_mix(): comm_call(body, (jax.ShapeDtypeStruct((rows, D), F32), jax.ShapeDtypeStru...  175 us
    pallas_call x1, Pallas kernels, time_back(): comm_call(body, (jax.ShapeDtypeStruct((rows, D), F32), jax.ShapeDtypeStru...  166 us

profile of v7, /device:TPU:0, one launch (start us, length us, event | category | flops | bytes accessed | tf_op | source)
XLA Modules:
  0.0 582.2 jit_solution(7906584726956507650)
XLA Ops:
  0.7 1.6 stack.59
  2.2 0.6 pad.4.refs_0_
  2.8 217.2 %shard_map.432 = (f32[16,2048]{1,0:T(8,128)}, f32[16,256]{1,0:T(8,128)}, bf16[4,1024,2048]{2,1,0:T(8,128)(2,1)}, bf16[1024,2048]{1,0:T(8,128)(2,1)}, bf16[3,1024...) custom-call(bf16[16,128]{1,0:T(8,128)(2,1)} %pad.4.refs_0_, ...), custom_call_target="tpu_custom_call" | custom-call | tf_op jit(solution)/shard_map/pallas_call | solution.py:977
  220.1 0.9 convert_element_type.42
  221.0 0.7 broadcast_in_dim.10
  221.7 174.9 %shard_map.433 = (f32[128,2048]{1,0:T(8,128)}, bf16[8,128,2048]{2,1,0:T(8,128)(2,1)}, bf16[8,128,256]{2,1,0:T(8,128)(2,1)}, bf16[224,2048]{1,0:T(8,128)(2,1)}, b...) custom-call(bf16[8,128,2048]{2,1,0:T(8,128)(2,1)} %get-tuple-element, ...), custom_call_target="tpu_custom_call" | custom-call | tf_op jit(solution)/shard_map/pallas_call | solution.py:1383
  396.6 0.0 copy-start.2
  396.6 3.1 convert_add_fusion.1
  399.7 0.0 copy-done.2
  399.7 2.6 fusion
  402.3 0.0 copy-start.4
  402.3 166.4 %shard_map.434 = (f32[128,2048]{1,0:T(8,128)}, f32[64,2048]{1,0:T(8,128)}, f32[16,128]{1,0:T(8,128)}, bf16[4,64,128]{2,1,0:T(8,128)(2,1)}, f32[64,7168]{1,0:T(8,...) custom-call(bf16[8,128,2048]{2,1,0:T(8,128)(2,1)} %get-tuple-element, ...), custom_call_target="tpu_custom_call" | custom-call | tf_op jit(solution)/shard_map/pallas_call | solution.py:1857
  568.7 1.0 convert_bitcast_fusion.1
  569.7 0.8 copy.54
  570.5 1.5 slice_bitcast_fusion
  572.1 0.0 copy-done.4
  572.1 0.1 convert_bitcast_fusion
  572.2 0.0 copy-start
  572.2 0.3 copy.52
  572.5 0.3 copy.53
  572.9 0.5 copy-done
  573.4 0.0 copy-start.3
  573.4 0.0 copy-start.10
  573.4 0.9 fusion.1
  574.3 0.5 copy-done.3
  574.8 0.0 copy-start.9
  574.8 0.0 copy-start.8
  574.8 1.0 copy.63
  575.8 0.0 copy-done.10
  575.8 0.0 copy-start.7
  575.8 0.0 copy-start.6
  575.8 0.8 copy.64
  576.6 0.0 copy-done.9
  576.6 0.0 copy-start.1
  576.6 0.8 copy.65
  577.4 0.0 copy-done.8
  577.4 0.8 copy.66
  578.2 0.0 copy-done.7
  578.2 0.8 copy.67
  579.0 0.0 copy-done.6
  579.0 0.8 copy.68
  579.8 0.0 copy-done.1
  579.8 0.0 copy-start.5
  579.8 1.2 copy.69
  581.0 0.2 copy-done.5
  581.2 0.8 copy.70
  (1 shorter events, 0.0 us)
Async XLA Ops:
  396.6 3.1 copy-start.2
  402.3 169.8 %copy-start.4 = (bf16[8,128,256]{2,1,0:T(8,128)(2,1)S(1)}, bf16[8,128,256]{2,1,0:T(8,128)(2,1)}, u32[]{:S(2)}) copy-start(bf16[8,128,256]{2,1,0:T(8,128)(2,1)} %get-tuple-element.71) | copy-start | bytes 1572868
  572.2 1.2 copy-start
  573.4 1.4 copy-start.3
  573.4 2.4 copy-start.10
  574.8 1.8 copy-start.9
  574.8 2.6 copy-start.8
  575.8 2.4 copy-start.7
  575.8 3.2 copy-start.6
  576.6 3.2 copy-start.1
  579.8 1.4 copy-start.5
